TPU v7x, 32 devices: a whole 2x2x4 slice. The times are simulated.
32 devices in a mesh: blk: 16 (over z, y, x), tp: 2 (over core).
Axes of the slice: x: 2, y: 2, z: 4, core: 2. Of those that a mesh axis runs over, the one named last changes fastest.
Arguments:
- tokens: bfloat16 [2048, 2048], P('blk'), may hold values from -6 to 6
- w_qkv: bfloat16 [3, 2048, 2048], P(None, 'blk', 'tp'), may hold values from -0.125 to 0.125
- b_qkv: bfloat16 [3, 16, 128], P(None, 'tp', 'blk'), may hold values from -2 to 2
- w_out: bfloat16 [2048, 2048], P('tp', 'blk'), may hold values from -2 to 2
- b_out: bfloat16 [16, 128], P(None, 'blk'), may hold values from -2 to 2
- w_in: bfloat16 [2048, 8192], P('blk', 'tp'), may hold values from -0.125 to 0.125
- b_in: bfloat16 [64, 128], P('tp', 'blk'), may hold values from -3 to 3
- w_out2: bfloat16 [8192, 2048], P('tp', 'blk'), may hold values from -0.0625 to 0.0625
- b_out2: bfloat16 [16, 128], P(None, 'blk'), may hold values from -2 to 2
- norm_gain: bfloat16 [2, 16, 128], P(None, None, 'blk'), may hold values from 0.099609375 to 1.8984375
- norm_shift: bfloat16 [2, 16, 128], P(None, None, 'blk'), may hold values from -2 to 2
- doc_start: int32 [2048], P('blk'), may hold values from 0 to 2047, as said below
- live: int32 [2048], P('blk'), may hold values from 0 to 1, as said below
- cotangent: bfloat16 [2048, 2048], P('blk'), may hold values from -6 to 6
Outputs:
- mixed: bfloat16 [2048, 2048], P('blk')
- tokens_grad: bfloat16 [2048, 2048], P('blk')
- w_qkv_grad: float32 [3, 2048, 2048], P(None, 'blk', 'tp')
- b_qkv_grad: float32 [3, 16, 128], P(None, 'tp', 'blk')
- w_out_grad: float32 [2048, 2048], P('tp', 'blk')
- b_out_grad: float32 [16, 128], P(None, 'blk')
- w_in_grad: float32 [2048, 8192], P('blk', 'tp')
- b_in_grad: float32 [64, 128], P('tp', 'blk')
- w_out2_grad: float32 [8192, 2048], P('tp', 'blk')
- b_out2_grad: float32 [16, 128], P(None, 'blk')
- norm_gain_grad: float32 [2, 16, 128], P(None, None, 'blk')
- norm_shift_grad: float32 [2, 16, 128], P(None, None, 'blk')
Inputs may be any that keep to these rules, and one draw needn't show every extreme that they name: `doc_start`: each token's value is the index of the first token of its document, so tokens with equal values form one run and the first token has 0; the last token is a document of its own. Short documents lie in the first block of 128 tokens; then one document runs up to the second-to-last token. `live`: pad tokens are the last tokens of the pack, from a quarter to a half of 2048 of them; all others are 1.
All inputs are finite; a program needn't handle non-finite values.
Results may differ from a plain program's by a relative error of at most 0.013.
Values may be sent and summed in bfloat16 or wider, within the bound.
No kernel may reach another device: no remote copies, remote signals or barrier semaphores. Data moves between devices by JAX's collectives and lax.ppermute only.
A program may use at most 256 MiB of HBM per device.

v0:
```python
import math

import jax
import jax.numpy as jnp
from jax import lax
from jax.sharding import PartitionSpec as P

HEADS = 8
HEAD = 256
ROT = 64


EPSILON = 1e-05
NEGATIVE = -1e30


def layer_norm(values, gain, shift):
    center = values - jnp.mean(values, axis=-1, keepdims=True)
    spread = jnp.mean(center * center, axis=-1, keepdims=True)
    return center * lax.rsqrt(spread + EPSILON) * gain + shift


def exact_gelu(values):
    return jax.nn.gelu(values, approximate=False)


def rotary_tables(positions, width):
    steps = jnp.arange(width // 2, dtype=jnp.float32)
    inverse = 10000.0 ** (-2.0 * steps / width)
    angle = positions.astype(jnp.float32)[:, None] * inverse[None, :]
    return (jnp.cos(angle), jnp.sin(angle))


def rotate(values, cosine, sine):
    half = cosine.shape[-1]
    first = values[..., :half]
    second = values[..., half : 2 * half]
    cosine = cosine[:, None, :]
    sine = sine[:, None, :]
    return jnp.concatenate(
        [first * cosine - second * sine, second * cosine + first * sine, values[..., 2 * half :]],
        axis=-1,
    )


def allowed(query_index, query_start, key_index, key_start, key_live):
    same = query_start[:, None] == key_start[None, :]
    causal = key_index[None, :] <= query_index[:, None]
    usable = (key_live[None, :] == 1) | (key_index[None, :] == query_index[:, None])
    return same & causal & usable


def blocked(arrays, count):
    size = math.gcd(count, 512)
    return tuple((array.reshape((count // size, size) + array.shape[1:]) for array in arrays))


def body(
    tokens,
    w_qkv,
    b_qkv,
    w_out,
    b_out,
    w_in,
    b_in,
    w_out2,
    b_out2,
    norm_gain,
    norm_shift,
    doc_start,
    live,
    cotangent,
):
    rows, width = tokens.shape
    local_heads = HEADS // lax.axis_size("tp")
    scale = 1.0 / math.sqrt(HEAD)
    here = lax.axis_index("blk") * rows + jnp.arange(rows, dtype=jnp.int32)
    gathered = (
        lax.all_gather(w_qkv, "blk", axis=1, tiled=True),
        lax.all_gather(b_qkv, "blk", axis=2, tiled=True),
        lax.all_gather(w_out, "blk", axis=1, tiled=True),
        lax.all_gather(b_out, "blk", axis=1, tiled=True),
        lax.all_gather(w_in, "blk", axis=0, tiled=True),
        lax.all_gather(b_in, "blk", axis=1, tiled=True),
        lax.all_gather(w_out2, "blk", axis=1, tiled=True),
        lax.all_gather(b_out2, "blk", axis=1, tiled=True),
        lax.all_gather(norm_gain, "blk", axis=2, tiled=True),
        lax.all_gather(norm_shift, "blk", axis=2, tiled=True),
    )
    (
        triple_weight,
        triple_bias,
        output_weight,
        output_bias,
        expand_weight,
        expand_bias,
        shrink_weight,
        shrink_bias,
        gain_rows,
        shift_rows,
    ) = gathered
    gains = gain_rows.reshape(2, width).astype(jnp.float32)
    shifts = shift_rows.reshape(2, width).astype(jnp.float32)
    triple_shift = triple_bias.reshape(3, -1).astype(jnp.float32)
    expand_shift = expand_bias.reshape(-1).astype(jnp.float32)
    residual_shift = output_bias.reshape(-1).astype(jnp.float32) + shrink_bias.reshape(-1).astype(
        jnp.float32
    )
    inputs = tokens.astype(jnp.float32)
    normed_attend = layer_norm(inputs, gains[0], shifts[0]).astype(jnp.bfloat16)
    normed_feed = layer_norm(inputs, gains[1], shifts[1]).astype(jnp.bfloat16)
    linear = (
        jnp.einsum("td,sde->ste", normed_attend, triple_weight, preferred_element_type=jnp.float32)
        + triple_shift[:, None, :]
    )
    cosine, sine = rotary_tables(here - doc_start, ROT)
    split = linear.reshape(3, rows, local_heads, HEAD)
    queries = rotate(split[0], cosine, sine).astype(jnp.bfloat16)
    keys = rotate(split[1], cosine, sine).astype(jnp.bfloat16)
    values = split[2].astype(jnp.bfloat16)
    start_state = (
        jnp.full((local_heads, rows), NEGATIVE, jnp.float32),
        jnp.zeros((local_heads, rows), jnp.float32),
        jnp.zeros((local_heads, rows, HEAD), jnp.float32),
    )
    carry = start_state
    piece_keys = lax.all_gather(keys, "blk", axis=0, tiled=True)
    piece_values = lax.all_gather(values, "blk", axis=0, tiled=True)
    piece_starts = lax.all_gather(doc_start, "blk", axis=0, tiled=True)
    piece_live = lax.all_gather(live, "blk", axis=0, tiled=True)
    count = piece_keys.shape[0]
    key_index = jnp.arange(count, dtype=jnp.int32)

    def attend_step(state, block):
        top, total, weighted = state
        block_keys, block_values, block_starts, block_live, block_index = block
        scores = (
            jnp.einsum("qhd,khd->hqk", queries, block_keys, preferred_element_type=jnp.float32)
            * scale
        )
        mask = allowed(here, doc_start, block_index, block_starts, block_live)[None]
        masked = jnp.where(mask, scores, NEGATIVE)
        new_top = jnp.maximum(top, jnp.max(masked, axis=-1))
        weight = jnp.where(mask, jnp.exp(masked - new_top[..., None]), 0.0)
        fade = jnp.exp(top - new_top)
        total = total * fade + jnp.sum(weight, axis=-1)
        weighted = weighted * fade[..., None] + jnp.einsum(
            "hqk,khd->hqd",
            weight.astype(jnp.bfloat16),
            block_values,
            preferred_element_type=jnp.float32,
        )
        return ((new_top, total, weighted), None)

    carry, unused = lax.scan(
        attend_step,
        carry,
        blocked((piece_keys, piece_values, piece_starts, piece_live, key_index), count),
    )
    top, total, weighted = carry
    attended = weighted / total[..., None]
    log_total = top + jnp.log(total)
    attended_tokens = jnp.transpose(attended, (1, 0, 2))
    attended_rows = attended_tokens.reshape(rows, -1).astype(jnp.bfloat16)
    attend_part = jnp.dot(attended_rows, output_weight, preferred_element_type=jnp.float32)
    expanded = (
        jnp.dot(normed_feed, expand_weight, preferred_element_type=jnp.float32) + expand_shift
    )
    activated = exact_gelu(expanded).astype(jnp.bfloat16)
    feed_part = jnp.dot(activated, shrink_weight, preferred_element_type=jnp.float32)
    branches = lax.psum((attend_part + feed_part).astype(jnp.bfloat16), "tp").astype(jnp.float32)
    mixed = (inputs + branches + residual_shift).astype(jnp.bfloat16)
    triple_weight, output_weight, expand_weight, shrink_weight = (
        lax.all_gather(w_qkv, "blk", axis=1, tiled=True),
        lax.all_gather(w_out, "blk", axis=1, tiled=True),
        lax.all_gather(w_in, "blk", axis=0, tiled=True),
        lax.all_gather(w_out2, "blk", axis=1, tiled=True),
    )
    incoming = cotangent.astype(jnp.float32)
    grad_output = jnp.einsum(
        "tk,td->kd", attended_rows, cotangent, preferred_element_type=jnp.float32
    )
    grad_shrink = jnp.einsum("tk,td->kd", activated, cotangent, preferred_element_type=jnp.float32)
    grad_residual_bias = jnp.sum(incoming, axis=0)
    grad_activated = jnp.einsum(
        "td,kd->tk", cotangent, shrink_weight, preferred_element_type=jnp.float32
    )
    unused, gelu_pull = jax.vjp(exact_gelu, expanded)
    grad_expanded = gelu_pull(grad_activated)[0].astype(jnp.bfloat16)
    grad_expand = jnp.einsum(
        "tk,tf->kf", normed_feed, grad_expanded, preferred_element_type=jnp.float32
    )
    grad_expand_bias = jnp.sum(grad_expanded.astype(jnp.float32), axis=0)
    grad_normed_feed = jnp.einsum(
        "tf,kf->tk", grad_expanded, expand_weight, preferred_element_type=jnp.float32
    )
    residual_rows = grad_residual_bias.reshape(output_bias.shape)
    expand_rows = grad_expand_bias.reshape(expand_bias.shape)
    grad_attended = (
        jnp.einsum("td,kd->tk", cotangent, output_weight, preferred_element_type=jnp.float32)
        .reshape(rows, local_heads, HEAD)
        .astype(jnp.bfloat16)
    )
    delta = jnp.sum(grad_attended.astype(jnp.float32) * attended_tokens, axis=-1)
    delta_heads = jnp.transpose(delta)
    carry = jnp.zeros((rows, local_heads, HEAD), jnp.float32)
    piece_keys = lax.all_gather(keys, "blk", axis=0, tiled=True)
    piece_values = lax.all_gather(values, "blk", axis=0, tiled=True)
    piece_starts = lax.all_gather(doc_start, "blk", axis=0, tiled=True)
    piece_live = lax.all_gather(live, "blk", axis=0, tiled=True)
    count = piece_keys.shape[0]
    key_index = jnp.arange(count, dtype=jnp.int32)

    def query_step(state, block):
        block_keys, block_values, block_starts, block_live, block_index = block
        scores = (
            jnp.einsum("qhd,khd->hqk", queries, block_keys, preferred_element_type=jnp.float32)
            * scale
        )
        mask = allowed(here, doc_start, block_index, block_starts, block_live)[None]
        prob = jnp.where(
            mask, jnp.exp(jnp.where(mask, scores, NEGATIVE) - log_total[..., None]), 0.0
        )
        push = jnp.einsum(
            "qhd,khd->hqk", grad_attended, block_values, preferred_element_type=jnp.float32
        )
        slope = (prob * (push - delta_heads[..., None])).astype(jnp.bfloat16)
        return (
            state
            + jnp.einsum("hqk,khd->qhd", slope, block_keys, preferred_element_type=jnp.float32),
            None,
        )

    carry, unused_rows = lax.scan(
        query_step,
        carry,
        blocked((piece_keys, piece_values, piece_starts, piece_live, key_index), count),
    )
    grad_queries = carry
    grad_queries = grad_queries * scale
    row_log, row_delta = (
        lax.all_gather(jnp.transpose(log_total), "blk", axis=0, tiled=True),
        lax.all_gather(delta, "blk", axis=0, tiled=True),
    )
    empty_keys = jnp.zeros((rows, local_heads, HEAD), jnp.float32)
    carry = (empty_keys, empty_keys)
    piece_queries = lax.all_gather(queries, "blk", axis=0, tiled=True)
    piece_grads = lax.all_gather(grad_attended, "blk", axis=0, tiled=True)
    piece_starts = lax.all_gather(doc_start, "blk", axis=0, tiled=True)
    count = piece_queries.shape[0]
    query_index = jnp.arange(count, dtype=jnp.int32)

    def key_step(state, block):
        grad_keys, grad_values = state
        block_queries, block_grads, block_starts, block_index, block_log, block_delta = block
        scores = (
            jnp.einsum("qhd,khd->hqk", block_queries, keys, preferred_element_type=jnp.float32)
            * scale
        )
        mask = allowed(block_index, block_starts, here, doc_start, live)[None]
        prob = jnp.where(
            mask,
            jnp.exp(jnp.where(mask, scores, NEGATIVE) - jnp.transpose(block_log)[..., None]),
            0.0,
        )
        grad_values = grad_values + jnp.einsum(
            "hqk,qhd->khd",
            prob.astype(jnp.bfloat16),
            block_grads,
            preferred_element_type=jnp.float32,
        )
        push = jnp.einsum("qhd,khd->hqk", block_grads, values, preferred_element_type=jnp.float32)
        slope = (prob * (push - jnp.transpose(block_delta)[..., None])).astype(jnp.bfloat16)
        grad_keys = grad_keys + jnp.einsum(
            "hqk,qhd->khd", slope, block_queries, preferred_element_type=jnp.float32
        )
        return ((grad_keys, grad_values), None)

    carry, unused_rows = lax.scan(
        key_step,
        carry,
        blocked((piece_queries, piece_grads, piece_starts, query_index, row_log, row_delta), count),
    )
    grad_keys, grad_values = carry
    grad_keys = grad_keys * scale

    def rotate_here(part):
        return rotate(part, cosine, sine)

    unused_value, rotate_pull = jax.vjp(rotate_here, split[0])
    grad_linear = (
        jnp.stack([rotate_pull(grad_queries)[0], rotate_pull(grad_keys)[0], grad_values])
        .reshape(3, rows, -1)
        .astype(jnp.bfloat16)
    )
    grad_triple = jnp.einsum(
        "td,ste->sde", normed_attend, grad_linear, preferred_element_type=jnp.float32
    )
    grad_triple_bias = jnp.sum(grad_linear.astype(jnp.float32), axis=1)
    grad_normed_attend = jnp.einsum(
        "ste,sde->td", grad_linear, triple_weight, preferred_element_type=jnp.float32
    )
    summed_attend, summed_feed = (
        lax.psum(grad_normed_attend.astype(jnp.bfloat16), "tp").astype(jnp.float32),
        lax.psum(grad_normed_feed.astype(jnp.bfloat16), "tp").astype(jnp.float32),
    )
    unused_attend, pull_attend = jax.vjp(layer_norm, inputs, gains[0], shifts[0])
    back_attend, gain_attend, shift_attend = pull_attend(summed_attend)
    unused_feed, pull_feed = jax.vjp(layer_norm, inputs, gains[1], shifts[1])
    back_feed, gain_feed, shift_feed = pull_feed(summed_feed)
    tokens_grad = (incoming + back_attend + back_feed).astype(jnp.bfloat16)
    gain_grads = jnp.stack([gain_attend, gain_feed]).reshape(gain_rows.shape)
    shift_grads = jnp.stack([shift_attend, shift_feed]).reshape(shift_rows.shape)
    triple_rows = grad_triple_bias.reshape(triple_bias.shape)
    scattered = (
        lax.psum_scatter(grad_triple, "blk", scatter_dimension=1, tiled=True),
        lax.psum_scatter(triple_rows, "blk", scatter_dimension=2, tiled=True),
        lax.psum_scatter(grad_output, "blk", scatter_dimension=1, tiled=True),
        lax.psum_scatter(residual_rows, "blk", scatter_dimension=1, tiled=True),
        lax.psum_scatter(grad_expand, "blk", scatter_dimension=0, tiled=True),
        lax.psum_scatter(expand_rows, "blk", scatter_dimension=1, tiled=True),
        lax.psum_scatter(grad_shrink, "blk", scatter_dimension=1, tiled=True),
        lax.psum_scatter(residual_rows, "blk", scatter_dimension=1, tiled=True),
        lax.psum_scatter(gain_grads, "blk", scatter_dimension=2, tiled=True),
        lax.psum_scatter(shift_grads, "blk", scatter_dimension=2, tiled=True),
    )
    (
        triple_grad,
        triple_bias_grad,
        output_grad,
        output_bias_grad,
        expand_grad,
        expand_bias_grad,
        shrink_grad,
        shrink_bias_grad,
        gain_grad,
        shift_grad,
    ) = scattered
    return (
        mixed,
        tokens_grad,
        triple_grad,
        triple_bias_grad,
        output_grad,
        output_bias_grad,
        expand_grad,
        expand_bias_grad,
        shrink_grad,
        shrink_bias_grad,
        gain_grad,
        shift_grad,
    )


def solution(mesh):
    placed = (
        P("blk", None),
        P(None, "blk", "tp"),
        P(None, "tp", "blk"),
        P("tp", "blk"),
        P(None, "blk"),
        P("blk", "tp"),
        P("tp", "blk"),
        P("tp", "blk"),
        P(None, "blk"),
        P(None, None, "blk"),
        P(None, None, "blk"),
        P("blk"),
        P("blk"),
        P("blk", None),
    )
    return jax.shard_map(
        body,
        mesh=mesh,
        in_specs=placed,
        out_specs=(
            P("blk", None),
            P("blk", None),
            P(None, "blk", "tp"),
            P(None, "tp", "blk"),
            P("tp", "blk"),
            P(None, "blk"),
            P("blk", "tp"),
            P("tp", "blk"),
            P("tp", "blk"),
            P(None, "blk"),
            P(None, None, "blk"),
            P(None, None, "blk"),
        ),
        check_vma=False,
    )
```

profile of v0, /device:TPU:11, one launch (start us, length us, event | category | flops | bytes accessed | tf_op | source)
XLA Modules:
  0.0 3203.8 jit_solution(2106831396695865319)
XLA Ops:
  9.4 25.1 all_gather.65
  35.3 34.5 %all_gather.66 = bf16[2,16,128]{1,0,2:T(2,128)(2,1)S(1)} all-gather(bf16[2,16,8]{1,0,2:T(2,128)(2,1)S(1)} %copy.183), channel_id=1, replica_groups=mesh['blk'=16,'tp'=2] {'blk'}, dimensions={2}, use_global_device_ids=true | all-gather | bytes 8704 | tf_op jit(solution)/shard_map/all_gather | solution.py:88
  70.6 30.0 all_gather.68
  102.3 61.9 %all-gather.11.cloned.1.call-done = bf16[3,2048,1024]{2,1,0:T(8,128)(2,1)} async-done(((bf16[3,128,1024]{2,1,0:T(8,128)(2,1)}), bf16[3,2048,1024]{2,1,0:T(8,128)(2,1)}) %all-gather.11.cloned.1.call-update) | async-done | bytes 12582928 | tf_op jit(solution)/shard_map/all_gather | solution.py:79
  164.1 6.5 add_bitcast_fusion
  176.6 77.6 %all-gather.17.cloned.1.call-done = bf16[1024,2048]{1,0:T(8,128)(2,1)} async-done(((bf16[1024,128]{1,0:T(8,128)(2,1)}), bf16[1024,2048]{1,0:T(8,128)(2,1)}) %all-gather.17.cloned.1.call-update) | async-done | bytes 4194320 | tf_op jit(solution)/shard_map/all_gather | solution.py:81
  254.2 3.7 convolution_convert_fusion.1
  261.6 25.8 all-gather
  288.5 31.8 all-gather.1
  321.6 28.0 all_gather.73
  351.9 4.6 copy.193
  356.5 55.2 %all-gather.15.cloned.1.call-done = bf16[2048,4,256]{2,1,0:T(4,128)(2,1)} async-done(((bf16[128,4,256]{2,1,0:T(4,128)(2,1)}), bf16[2048,4,256]{2,1,0:T(4,128)(2,1)}) %all-gather.15.cloned.1.call-update) | async-done | bytes 4194320 | tf_op jit(solution)/shard_map/all_gather | solution.py:128
  411.6 4.9 copy.194
  416.5 19.3 while.39
  419.6 1.8 convolution_add_fusion.4
  422.4 1.8 fusion.169
  424.4 1.8 convolution_add_fusion.4
  429.3 1.8 convolution_add_fusion.4
  434.1 1.8 convolution_add_fusion.4
  439.0 23.7 while.40
  440.7 1.9 fusion.177
  442.6 2.4 fusion.178
  446.7 1.8 fusion.177
  448.5 2.4 fusion.178
  452.6 1.8 fusion.177
  454.4 2.4 fusion.178
  458.5 1.8 fusion.177
  460.3 2.4 fusion.178
  463.7 43.0 %all_gather.80 = f32[2048,4]{1,0:T(8,128)S(1)} all-gather(f32[128,4]{1,0:T(8,128)S(1)} %copy.239), channel_id=1, replica_groups=mesh['blk'=16,'tp'=2] {'blk'}, dimensions={0}, use_global_device_ids=true | all-gather | bytes 34816 | tf_op jit(solution)/shard_map/all_gather | solution.py:243
  507.1 27.8 all_gather.78
  534.9 44.0 %all-gather.23.cloned.1.call-done = bf16[2048,4,256]{2,0,1:T(8,128)(2,1)} async-done(((bf16[128,4,256]{2,0,1:T(8,128)(2,1)}), bf16[2048,4,256]{2,0,1:T(8,128)(2,1)}) %all-gather.23.cloned.1.call-update) | async-done | bytes 4194320 | tf_op jit(solution)/shard_map/all_gather | solution.py:247
  578.9 28.6 while.41
  581.7 1.8 fusion.188
  583.5 2.5 fusion.187
  588.8 1.9 fusion.188
  590.7 2.6 fusion.187
  596.1 1.8 fusion.188
  597.9 2.5 fusion.187
  601.4 1.8 fusion.186
  603.2 1.8 fusion.188
  605.0 2.5 fusion.187
  613.4 157.4 %all-gather.19.cloned.1.call-done = bf16[2048,4096]{1,0:T(8,128)(2,1)} async-done(((bf16[128,4096]{1,0:T(8,128)(2,1)}), bf16[2048,4096]{1,0:T(8,128)(2,1)}) %all-gather.19.cloned.1.call-update) | async-done | bytes 16777232 | tf_op jit(solution)/shard_map/all_gather | solution.py:83
  770.8 9.6 convolution_add_fusion.1
  780.4 240.1 %all-gather.21.cloned.1.call-done = bf16[4096,2048]{1,0:T(8,128)(2,1)} async-done(((bf16[4096,128]{1,0:T(8,128)(2,1)}), bf16[4096,2048]{1,0:T(8,128)(2,1)}) %all-gather.21.cloned.1.call-update) | async-done | bytes 16777232 | tf_op jit(solution)/shard_map/all_gather | solution.py:85
  1020.5 17.5 convert_reduce_fusion
  1038.0 2.4 multiply_convert_fusion
  1040.5 3.5 fusion.117
  1043.9 12.6 convolution_convert_fusion
  1056.6 3.8 fusion.71
  1060.4 9.6 fusion.72
  1070.2 25.3 all_gather.75
  1095.5 31.7 all_gather.76
  1128.1 2.0 fusion.96
  1132.6 3.6 convert_reduce_fusion.5
  1136.3 10.3 convolution_bitcast_fusion.1
  1146.6 4.6 fusion.118
  1152.4 13.3 fusion.119
  1166.9 13.3 fusion.109
  1182.1 79.3 %all-reduce.16.cloned.1.call-done = (f32[3,8,128]{2,1,0:T(8,128)}, f32[16,128]{1,0:T(8,128)}, f32[32,128]{1,0:T(8,128)}, f32[2,16,128]{1,0,2:T(2,128)}, f32[2,16,128]{1,0,2:T(2,128)}) async-done(((f32[3,8,128]{2,1,0:T(8,128)}, f32[16,128]{1,0:T(8,128)}, f32[32,128]{1,0:T(8,128)}, f32[2,16,128]{1,0,2:T(2,128)}, f32[2,16,128]{1,0,2:T(2,128)}), (f32[3,8,128]{2,1,0:T(8,128)}, f32[16,128]{1,0:T(8,128)}, ...) | async-done | bytes 69648
  1267.6 361.5 %reduce-scatter.8.cloned.1.call-done = f32[3,128,1024]{1,2,0:T(8,128)} async-done(((f32[3,2048,1024]{1,2,0:T(8,128)}), f32[3,128,1024]{1,2,0:T(8,128)}) %reduce-scatter.8.cloned.1.call-update) | async-done | bytes 1572880 | tf_op jit(solution)/shard_map/reduce_scatter | solution.py:316
  1629.1 3.0 copy.218
  1632.2 180.9 %reduce-scatter.10.cloned.1.call-done = f32[1024,128]{1,0:T(8,128)} async-done(((f32[1024,2048]{1,0:T(8,128)}), f32[1024,128]{1,0:T(8,128)}) %reduce-scatter.10.cloned.1.call-update) | async-done | bytes 524304 | tf_op jit(solution)/shard_map/reduce_scatter | solution.py:318
  1813.1 691.3 %reduce-scatter.14.cloned.1.call-done = f32[4096,128]{1,0:T(8,128)} async-done(((f32[4096,2048]{1,0:T(8,128)}), f32[4096,128]{1,0:T(8,128)}) %reduce-scatter.14.cloned.1.call-update) | async-done | bytes 2097168 | tf_op jit(solution)/shard_map/reduce_scatter | solution.py:322
  2504.4 691.9 %reduce-scatter.12.cloned.1.call-done = f32[128,4096]{1,0:T(8,128)} async-done(((f32[2048,4096]{1,0:T(8,128)}), f32[128,4096]{1,0:T(8,128)}) %reduce-scatter.12.cloned.1.call-update) | async-done | bytes 2097168 | tf_op jit(solution)/shard_map/reduce_scatter | solution.py:320
  (305 shorter events, 69.9 us)
Async XLA Ops:
  7.2 93.6 %copy-start = (bf16[128,2048]{1,0:T(8,128)(2,1)S(1)}, bf16[128,2048]{1,0:T(8,128)(2,1)}, u32[]{:S(2)}) copy-start(bf16[128,2048]{1,0:T(8,128)(2,1)} %param.20) | copy-start | bytes 1572868
  7.2 94.1 %copy-start.32 = (s32[128]{0:T(128)S(1)}, s32[128]{0:T(128)}, u32[]{:S(2)}) copy-start(s32[128]{0:T(128)} %param.31) | copy-start | bytes 1540
  7.2 156.9 %all-gather.11.cloned.1.call-start = ((), (), s32[]{:S(2)}) async-start(), calls=%async_computation.4 | async-start | bytes 13369344 | tf_op jit(solution)/shard_map/all_gather | solution.py:79
  7.9 246.2 %all-gather.17.cloned.1.call-start = ((), (), s32[]{:S(2)}) async-start(), calls=%async_computation.7 | async-start | bytes 4456448 | tf_op jit(solution)/shard_map/all_gather | solution.py:81
  8.7 343.2 %all-gather.13.cloned.1.call-start = ((), (), s32[]{:S(2)}) async-start(), calls=%async_computation.5 | async-start | bytes 4456448 | tf_op jit(solution)/shard_map/all_gather | solution.py:127
  101.0 69.7 %copy-start.38 = (f32[128]{0:T(128)}, f32[128]{0:T(128)S(1)}, u32[]{:S(2)}) copy-start(f32[128]{0:T(128)S(1)} %broadcast_multiply_fusion.2) | copy-start | bytes 1540
  101.2 69.4 %copy-start.47 = (f32[128]{0:T(128)}, f32[128]{0:T(128)S(1)}, u32[]{:S(2)}) copy-start(f32[128]{0:T(128)S(1)} %fusion.95) | copy-start | bytes 1540
  101.3 69.4 %copy-start.40 = (f32[128]{0:T(128)}, f32[128]{0:T(128)S(1)}, u32[]{:S(2)}) copy-start(f32[128]{0:T(128)S(1)} %fusion.108) | copy-start | bytes 1540
  101.3 69.4 %copy-start.28 = (f32[2048]{0:T(1024)}, f32[2048]{0:T(1024)S(1)}, u32[]{:S(2)}) copy-start(f32[2048]{0:T(1024)S(1)} %get-tuple-element.732) | copy-start | bytes 24580
  101.9 68.8 %copy-start.35 = (f32[2048]{0:T(1024)}, f32[2048]{0:T(1024)S(1)}, u32[]{:S(2)}) copy-start(f32[2048]{0:T(1024)S(1)} %get-tuple-element.734) | copy-start | bytes 24580
  102.2 71.5 %copy-start.21 = (f32[128,32]{1,0:T(8,128)}, f32[128,32]{1,0:T(8,128)S(1)}, u32[]{:S(2)}) copy-start(f32[128,32]{1,0:T(8,128)S(1)} %get-tuple-element.736) | copy-start | bytes 49156
  102.2 71.5 %copy-start.23 = (f32[128,32]{1,0:T(8,128)}, f32[128,32]{1,0:T(8,128)S(1)}, u32[]{:S(2)}) copy-start(f32[128,32]{1,0:T(8,128)S(1)} %get-tuple-element.737) | copy-start | bytes 49156
  173.7 80.4 %copy-start.7 = (bf16[128,2048]{1,0:T(8,128)(2,1)S(1)}, bf16[128,2048]{1,0:T(8,128)(2,1)}, u32[]{:S(2)}) copy-start(bf16[128,2048]{1,0:T(8,128)(2,1)} %param.33) | copy-start | bytes 1572868
  175.5 236.1 %all-gather.15.cloned.1.call-start = ((), (), s32[]{:S(2)}) async-start(), calls=%async_computation.6 | async-start | bytes 4456448 | tf_op jit(solution)/shard_map/all_gather | solution.py:128
  176.5 82.4 %copy-start.25 = (bf16[128,4,32]{2,0,1:T(8,128)(2,1)S(1)}, bf16[128,4,32]{2,0,1:T(8,128)(2,1)}, u32[]{:S(2)}) copy-start(bf16[128,4,32]{2,0,1:T(8,128)(2,1)} %get-tuple-element.718) | copy-start | bytes 98308
  176.6 358.4 %all-gather.25.cloned.1.call-start = ((), (), s32[]{:S(2)}) async-start(), calls=%async_computation.11 | async-start | bytes 4456448 | tf_op jit(solution)/shard_map/all_gather | solution.py:248
  258.6 29.9 copy-start.49
  258.6 63.0 %copy-start.44 = (bf16[32,8]{0,1:T(8,128)(2,1)S(1)}, bf16[32,8]{0,1:T(8,128)(2,1)}, u32[]{:S(2)}) copy-start(bf16[32,8]{0,1:T(8,128)(2,1)} %param.26) | copy-start | bytes 1540
  258.7 320.2 %all-gather.23.cloned.1.call-start = ((), (), s32[]{:S(2)}) async-start(), calls=%async_computation.10 | async-start | bytes 4456448 | tf_op jit(solution)/shard_map/all_gather | solution.py:247
  258.9 92.2 %copy-start.19 = (bf16[128,4,256]{2,1,0:T(4,128)(2,1)S(1)}, bf16[128,4,256]{2,1,0:T(4,128)(2,1)}, u32[]{:S(2)}) copy-start(bf16[128,4,256]{2,1,0:T(4,128)(2,1)} %convert_element_type.136) | copy-start | bytes 786436
  260.0 510.8 %all-gather.19.cloned.1.call-start = ((), (), s32[]{:S(2)}) async-start(), calls=%async_computation.8 | async-start | bytes 17825792 | tf_op jit(solution)/shard_map/all_gather | solution.py:83
  260.7 759.8 %all-gather.21.cloned.1.call-start = ((), (), s32[]{:S(2)}) async-start(), calls=%async_computation.9 | async-start | bytes 17825792 | tf_op jit(solution)/shard_map/all_gather | solution.py:85
  261.5 866.6 %all-reduce.18.cloned.1.call-start = ((), (), s32[]{:S(2)}) async-start(), calls=%async_computation.17 | async-start | bytes 3145728 | tf_op jit(solution)/shard_map/psum | solution.py:171
  416.5 22.4 copy-start.5
  435.9 0.6 copy-start.30
  436.1 2.9 copy-start.9
  462.7 116.2 %copy-start.2 = (f32[128,4,256]{0,2,1:T(8,128)S(1)}, f32[128,4,256]{0,2,1:T(8,128)}, u32[]{:S(2)}) copy-start(f32[128,4,256]{0,2,1:T(8,128)} %custom-call.4) | copy-start | bytes 1572868
  462.7 116.2 %copy-start.6 = (bf16[128,4,256]{2,0,1:T(8,128)(2,1)S(1)}, bf16[128,4,256]{2,0,1:T(8,128)(2,1)}, u32[]{:S(2)}) copy-start(bf16[128,4,256]{2,0,1:T(8,128)(2,1)} %copy.210) | copy-start | bytes 786436
  462.7 116.2 %copy-start.50 = (s32[128]{0:T(128)S(1)}, s32[128]{0:T(128)}, u32[]{:S(2)}) copy-start(s32[128]{0:T(128)} %param.32) | copy-start | bytes 1540
  578.9 28.8 copy-start.20
  607.7 0.8 copy-start.22
  607.7 0.9 copy-start.24
  609.4 3.3 copy-start.10
  609.4 3.2 copy-start.34
  610.3 160.5 %copy-start.39 = (f32[128]{0:T(128)S(1)}, f32[128]{0:T(128)}, u32[]{:S(2)}) copy-start(f32[128]{0:T(128)} %copy-done.38) | copy-start | bytes 1540
  610.6 160.2 %copy-start.26 = (f32[2048]{0:T(1024)S(1)}, f32[2048]{0:T(1024)}, u32[]{:S(2)}) copy-start(f32[2048]{0:T(1024)} %get-tuple-element.735) | copy-start | bytes 24580
  610.6 160.1 %copy-start.37 = (f32[4096]{0:T(1024)S(1)}, f32[4096]{0:T(1024)}, u32[]{:S(2)}) copy-start(f32[4096]{0:T(1024)} %bitcast_convert_fusion.1) | copy-start | bytes 49156
  610.7 160.1 %copy-start.41 = (f32[128]{0:T(128)S(1)}, f32[128]{0:T(128)}, u32[]{:S(2)}) copy-start(f32[128]{0:T(128)} %copy-done.40) | copy-start | bytes 1540
  770.8 249.7 %copy-start.8 = (bf16[128,2048]{1,0:T(8,128)(2,1)S(1)}, bf16[128,2048]{1,0:T(8,128)(2,1)}, u32[]{:S(2)}) copy-start(bf16[128,2048]{1,0:T(8,128)(2,1)} %param.33) | copy-start | bytes 1572868
  1020.5 19.9 copy-start.1
  1040.5 3.5 copy-start.3
  1043.9 12.6 copy-start.14
  1043.9 12.6 copy-start.15
  1056.6 3.8 copy-start.16
  1056.6 3.8 copy-start.17
  1056.6 3.8 copy-start.18
  1060.4 9.7 copy-start.45
  1060.4 35.1 %copy-start.46 = (bf16[16,8]{0,1:T(8,128)(2,1)S(1)}, bf16[16,8]{0,1:T(8,128)(2,1)}, u32[]{:S(2)}) copy-start(bf16[16,8]{0,1:T(8,128)(2,1)} %param.28) | copy-start | bytes 772
  1070.1 58.0 %copy-start.29 = (f32[2048]{0:T(1024)S(1)}, f32[2048]{0:T(1024)}, u32[]{:S(2)}) copy-start(f32[2048]{0:T(1024)} %copy-done.28) | copy-start | bytes 24580
  1070.1 60.7 %copy-start.48 = (f32[128]{0:T(128)S(1)}, f32[128]{0:T(128)}, u32[]{:S(2)}) copy-start(f32[128]{0:T(128)} %copy-done.47) | copy-start | bytes 1540
  1070.1 60.8 %copy-start.42 = (f32[128]{0:T(128)S(1)}, f32[128]{0:T(128)}, u32[]{:S(2)}) copy-start(f32[128]{0:T(128)} %copy-done.40) | copy-start | bytes 1540
  1070.1 191.3 %all-reduce.16.cloned.1.call-start = ((), (), s32[]{:S(2)}) async-start(), calls=%async_computation.16 | async-start | bytes 598016
  1128.1 2.8 copy-start.11
  1128.1 2.8 copy-start.12
  1131.8 4.5 copy-start.36
  1136.2 492.9 %reduce-scatter.8.cloned.1.call-start = ((), (), s32[]{:S(2)}) async-start(), calls=%async_computation.12 | async-start | bytes 26738688 | tf_op jit(solution)/shard_map/reduce_scatter | solution.py:316
  1146.6 666.5 %reduce-scatter.10.cloned.1.call-start = ((), (), s32[]{:S(2)}) async-start(), calls=%async_computation.13 | async-start | bytes 8912896 | tf_op jit(solution)/shard_map/reduce_scatter | solution.py:318
  1151.2 1.2 copy-start.4
  1151.2 1353.2 %reduce-scatter.14.cloned.1.call-start = ((), (), s32[]{:S(2)}) async-start(), calls=%async_computation.15 | async-start | bytes 35651584 | tf_op jit(solution)/shard_map/reduce_scatter | solution.py:322
  1165.7 1.2 copy-start.13
  1165.7 1.2 copy-start.27
  1165.7 2030.5 %reduce-scatter.12.cloned.1.call-start = ((), (), s32[]{:S(2)}) async-start(), calls=%async_computation.14 | async-start | bytes 35651584 | tf_op jit(solution)/shard_map/reduce_scatter | solution.py:320
  1180.2 0.7 copy-start.51
  1266.3 1930.6 %copy-start.43 = (f32[16,8]{0,1:T(8,128)}, f32[16,8]{0,1:T(8,128)S(1)}, u32[]{:S(2)}) copy-start(f32[16,8]{0,1:T(8,128)S(1)} %copy.219) | copy-start | bytes 1540
  (2 other events, 1.2 us)
Sparse Core Ops, SparseCore 0:
  10.8 153.2 all-gather.10
  166.8 87.3 all-gather.16
  257.5 76.1 all-gather.12
  336.9 74.6 all-gather.14
  414.8 80.6 all-gather.24
  498.7 80.1 all-gather.22
  581.7 189.0 all-gather.18
  773.5 246.9 all-gather.20
  1070.2 22.5 all-reduce.17
  1136.3 124.9 all-reduce.15
  1267.1 361.9 reduce-scatter.7
  1631.9 181.1 reduce-scatter.9
  1816.0 688.3 reduce-scatter.13
  2507.2 689.0 reduce-scatter.11
where the time goes:
time: 3210 us; the launch traced here: 3200 us
  waiting for transfers between devices  2640 us (82%)
  blocking collectives  303 us (9%)
  matrix products  163 us (5%)
  local copies, waits for them, and re-layouts  48 us (1%)
    reduce_scatter x1, waiting for transfers between devices, body(): lax.psum_scatter(grad_expand, 'blk', scatter_dimension=0, tiled=True)  692 us
    reduce_scatter x1, waiting for transfers between devices, body(): lax.psum_scatter(grad_shrink, 'blk', scatter_dimension=1, tiled=True)  691 us
    reduce_scatter x1, waiting for transfers between devices, body(): lax.psum_scatter(grad_triple, 'blk', scatter_dimension=1, tiled=True)  361 us
    all_gather x1, waiting for transfers between devices, body(): lax.all_gather(w_out2, 'blk', axis=1, tiled=True)  240 us
    reduce_scatter x1, waiting for transfers between devices, body(): lax.psum_scatter(grad_output, 'blk', scatter_dimension=1, tiled=True)  181 us
    all_gather x1, waiting for transfers between devices, body(): lax.all_gather(w_in, 'blk', axis=0, tiled=True)  157 us
    unnamed x15, waiting for transfers between devices  82.2 us
    all_gather x1, waiting for transfers between devices, body(): lax.all_gather(w_out, 'blk', axis=1, tiled=True)  77.6 us
  transfers between devices with their start and end apart: 14, of which 11 were waited for; matrix products, arithmetic and copies ran while one was open for 6% of the time, Pallas kernels for 0%

commit v1 on v0

v1 whole, which is shorter than its diff:
```python
import math

import jax
import jax.numpy as jnp
from jax import lax
from jax.sharding import PartitionSpec as P

HEADS = 8
HEAD = 256
ROT = 64

EPSILON = 1e-05
NEGATIVE = -1e30
BF = jnp.bfloat16
F32 = jnp.float32


def dot(left, right, dims):
    return lax.dot_general(left, right, (dims, ((), ())), preferred_element_type=F32)


def swap_cores(value):
    return lax.ppermute(value, "tp", [(0, 1), (1, 0)])


def from_peer(value, mask):
    count = lax.axis_size("blk")
    return lax.ppermute(value, "blk", [(i, i ^ mask) for i in range(count)])


def spread(value, masks):
    return jnp.stack([value] + [from_peer(value, mask) for mask in masks])


def collect(parts, masks):
    total = parts[0].astype(F32)
    for at, mask in enumerate(masks):
        total = total + from_peer(parts[at + 1], mask).astype(F32)
    return total


def by_core(core, mine, other):
    first = core == 0
    return jnp.where(first, mine, other), jnp.where(first, other, mine)


def gelu_and_slope(values):
    cumulative = 0.5 * (1.0 + lax.erf(values * (1.0 / math.sqrt(2.0))))
    density = jnp.exp(-0.5 * values * values) * (1.0 / math.sqrt(2.0 * math.pi))
    return values * cumulative, cumulative + values * density


def turn(values, cosine, sine):
    half = ROT // 2
    first, second = values[:, :half], values[:, half:ROT]
    return jnp.concatenate(
        [first * cosine - second * sine, second * cosine + first * sine, values[:, ROT:]],
        axis=1,
    )


def body(
    tokens,
    w_qkv,
    b_qkv,
    w_out,
    b_out,
    w_in,
    b_in,
    w_out2,
    b_out2,
    norm_gain,
    norm_shift,
    doc_start,
    live,
    cotangent,
):
    blocks = lax.axis_size("blk")
    cores = lax.axis_size("tp")
    me, core = lax.axis_index("blk"), lax.axis_index("tp")
    rows, width = tokens.shape
    depth = w_in.shape[0]
    part = rows // cores
    quarter = part // 2
    group = blocks // HEADS
    columns = HEAD // group
    units = w_in.shape[1] // blocks
    cut = depth // cores
    near = columns // cores
    scale = 1.0 / math.sqrt(HEAD)

    masks_x = list(range(1, group))
    masks_y = [group]
    masks_z = [2 * group * i for i in range(1, blocks // (2 * group))]
    size_x, size_y, size_z = group, 2, len(masks_z) + 1

    def gather(value):
        over_z = spread(value, masks_z)
        one = spread(spread(over_z[:, :quarter], masks_y), masks_x)
        two = spread(spread(over_z[:, quarter:], masks_x), masks_y)
        return one.reshape(-1, value.shape[-1]), two.reshape(-1, value.shape[-1])

    def scatter(one, two):
        one = one.reshape(size_x, size_y, size_z, quarter, width)
        two = two.reshape(size_y, size_x, size_z, quarter, width)
        one = collect(collect(one, masks_x).astype(BF), masks_y)
        two = collect(collect(two, masks_y).astype(BF), masks_x)
        return collect(jnp.concatenate([one, two], axis=1).astype(BF), masks_z)

    small = jnp.concatenate(
        [
            norm_gain.reshape(-1),
            norm_shift.reshape(-1),
            b_out.reshape(-1),
            b_out2.reshape(-1),
            b_qkv.reshape(-1),
            b_in.reshape(-1),
            (doc_start // 256).astype(BF),
            (doc_start % 256).astype(BF),
            live.astype(BF),
        ]
    )
    small_rows = -(-small.size // 2048) * 16
    small = jnp.pad(small, (0, small_rows * 128 - small.size)).reshape(small_rows * 128 // columns, columns)
    lines = small.shape[0]

    own_heads = HEADS // cores * group
    triple = w_qkv.reshape(3, cores, cut, own_heads, columns).transpose(1, 3, 0, 2, 4)
    triple = triple.reshape(cores, own_heads, 3 * cut, columns)
    outward = w_out.reshape(own_heads, cores, near, depth).transpose(1, 0, 2, 3)
    outward = outward.reshape(cores, own_heads, near * depth // columns, columns)
    dealt = jnp.concatenate([triple, outward], axis=2)
    keep = lax.dynamic_index_in_dim(dealt, core, 0, keepdims=False)
    give = lax.dynamic_index_in_dim(dealt, 1 - core, 0, keepdims=False)
    got = swap_cores(give)
    heads_low, heads_high = by_core(core, keep, got)
    deal = jnp.concatenate(
        [
            jnp.concatenate([heads_low, heads_high]),
            jnp.broadcast_to(small, (blocks,) + small.shape),
        ],
        axis=1,
    )
    here = lax.all_to_all(deal, "blk", 0, 0, tiled=True)
    there = swap_cores(here)
    both = jnp.stack(by_core(core, here, there))

    expand_deal = w_in.reshape(depth, blocks, units).transpose(1, 0, 2)
    expand_mine = lax.all_to_all(expand_deal, "blk", 0, 0, tiled=True).reshape(width, units)
    expand_other = swap_cores(expand_mine)
    shrink_mine = lax.all_to_all(
        w_out2.reshape(blocks, units, depth), "blk", 0, 0, tiled=True
    )
    shrink_other = swap_cores(shrink_mine)
    w_expand = jnp.concatenate([expand_mine, expand_other], axis=1)
    w_shrink = jnp.concatenate([shrink_mine, shrink_other], axis=1)
    w_shrink = w_shrink.transpose(1, 0, 2).reshape(2 * units, width)

    my_tokens = lax.dynamic_slice_in_dim(tokens, core * part, part, 0)
    my_cotangent = lax.dynamic_slice_in_dim(cotangent, core * part, part, 0)
    all_tokens = jnp.concatenate(gather(my_tokens))
    all_cotangent = jnp.concatenate(gather(my_cotangent))
    count = all_tokens.shape[0]

    at = 3 * cut
    mid = at + near * depth // columns
    w_triple = both[:, :, :at].reshape(cores, blocks, 3, cut, columns)
    w_triple = w_triple.transpose(1, 0, 3, 2, 4).reshape(width, 3 * columns)
    w_near = both[:, :, at:mid].reshape(cores, blocks, near, depth)
    w_near = w_near.transpose(0, 2, 1, 3).reshape(columns, width)
    w_head = spread(w_near, masks_x).reshape(HEAD, width)
    flat = both[:, :, mid:].reshape(cores, blocks, -1)

    def take(offset, like):
        return flat[:, :, offset : offset + like.size].reshape((cores, blocks) + like.shape), offset + like.size

    offset = 0
    gain_all, offset = take(offset, norm_gain)
    shift_all, offset = take(offset, norm_shift)
    out_all, offset = take(offset, b_out)
    out2_all, offset = take(offset, b_out2)
    triple_all, offset = take(offset, b_qkv)
    expand_all, offset = take(offset, b_in)
    start_high, offset = take(offset, doc_start)
    start_low, offset = take(offset, doc_start)
    live_all, offset = take(offset, live)
    gains = gain_all[0].transpose(1, 2, 0, 3).reshape(2, width).astype(F32)
    shifts = shift_all[0].transpose(1, 2, 0, 3).reshape(2, width).astype(F32)
    residual_shift = (out_all[0].astype(F32) + out2_all[0].astype(F32)).transpose(1, 0, 2).reshape(width)
    triple_shift = triple_all.astype(F32).transpose(2, 0, 3, 1, 4).reshape(3, width)
    triple_shift = lax.dynamic_slice_in_dim(triple_shift, me * columns, columns, 1).reshape(-1)
    expand_shift = expand_all.astype(F32).transpose(0, 2, 1, 3).reshape(cores, -1)
    expand_shift = lax.dynamic_slice_in_dim(expand_shift, me * units, units, 1)
    expand_shift = jnp.concatenate(by_core(core, expand_shift[0], expand_shift[1]))
    starts = (start_high[0].astype(F32) * 256.0 + start_low[0].astype(F32)).astype(jnp.int32)
    lives = live_all[0].astype(jnp.int32)

    x_at = jnp.arange(size_x)[:, None, None]
    y_at = group * jnp.arange(size_y)[None, :, None]
    z_at = 2 * group * jnp.arange(size_z)[None, None, :]
    order = (x_at + y_at + z_at) ^ me
    inside = jnp.arange(quarter, dtype=jnp.int32)

    def index_of(which):
        base = order[..., None] * rows + which * part + inside
        one, two = base, base + quarter
        return jnp.concatenate(
            [one.reshape(size_x, -1), two.reshape(size_x, -1)], axis=1
        )

    def heads_order(value):
        tail = value.shape[1:]
        one = value[: count // 2].reshape((size_x, -1) + tail)
        two = value[count // 2 :].reshape((size_y, size_x, -1) + tail)
        two = jnp.swapaxes(two, 0, 1).reshape((size_x, -1) + tail)
        return jnp.concatenate([one, two], axis=1)

    def gathered_order(value):
        tail = value.shape[2:]
        middle = value.shape[1] // 2
        one = value[:, :middle].reshape((count // 2,) + tail)
        two = value[:, middle:].reshape((size_x, size_y, -1) + tail)
        two = jnp.swapaxes(two, 0, 1).reshape((count // 2,) + tail)
        return jnp.concatenate([one, two])

    index_mine, index_other = index_of(core), index_of(1 - core)
    index = jnp.concatenate([index_mine.reshape(-1), index_other.reshape(-1)])
    token_start = starts.reshape(-1)[index]
    token_live = lives.reshape(-1)[index]

    inputs = all_tokens.astype(F32)
    center = inputs - jnp.mean(inputs, axis=-1, keepdims=True)
    inverse = lax.rsqrt(jnp.mean(center * center, axis=-1, keepdims=True) + EPSILON)
    normal = center * inverse
    normed_attend = (normal * gains[0] + shifts[0]).astype(BF)
    normed_feed = (normal * gains[1] + shifts[1]).astype(BF)

    linear = dot(normed_attend, w_triple, ((1,), (0,))) + triple_shift
    linear = heads_order(linear).reshape(count, 3, columns)
    steps = jnp.arange(ROT // 2, dtype=F32)
    speed = 10000.0 ** (-2.0 * steps / ROT)
    place = (index - token_start).astype(F32)
    angle = place[:count, None] * speed[None, :]
    cosine, sine = jnp.cos(angle), jnp.sin(angle)
    slot = me % group

    def turn_pieces(pieces, cosine, sine):
        if columns >= ROT:
            return jnp.stack(
                [
                    turn(
                        pieces[r],
                        jnp.where(slot == r, cosine, 1.0),
                        jnp.where(slot == r, sine, 0.0),
                    )
                    for r in range(group)
                ]
            )
        place_of = jnp.arange(group) ^ slot
        whole = jnp.swapaxes(pieces[place_of], 0, 1).reshape(pieces.shape[1], HEAD)
        whole = turn(whole, cosine, sine).reshape(-1, group, columns)
        return jnp.swapaxes(whole, 0, 1)[place_of]

    if columns >= ROT:
        own_cosine = jnp.where(slot == 0, cosine, 1.0)
        own_sine = jnp.where(slot == 0, sine, 0.0)
        queries = turn(linear[:, 0], own_cosine, own_sine)
        keys = turn(linear[:, 1], own_cosine, own_sine)
    else:
        queries, keys = linear[:, 0], linear[:, 1]
    mine = jnp.concatenate([queries, keys, linear[:, 2]], axis=1).astype(BF)

    def align(value, r):
        return value.reshape((size_x, -1) + value.shape[1:])[jnp.arange(size_x) ^ r].reshape(value.shape)

    pieces = [mine] + [align(from_peer(mine, r), r) for r in masks_x]
    pieces = jnp.stack(pieces).reshape(group, count, 3, columns)
    if columns < ROT:
        turned = [turn_pieces(pieces[:, :, s].astype(F32), cosine, sine).astype(BF) for s in (0, 1)]
        pieces = jnp.stack(turned + [pieces[:, :, 2]], axis=2)
    own_triple = pieces.transpose(2, 1, 0, 3).reshape(3, count, HEAD)
    other_triple = swap_cores(own_triple)
    queries, keys, values = jnp.concatenate([own_triple, other_triple], axis=1)

    cotangent_x = heads_order(all_cotangent)
    grad_attended = dot(all_cotangent, w_head, ((1,), (1,))).astype(BF)
    grad_attended = heads_order(grad_attended).reshape(count, HEAD)
    grad_attended = jnp.concatenate([grad_attended, swap_cores(grad_attended)])

    share = count // size_x
    mine_index, mine_start, mine_live = index[:share], token_start[:share], token_live[:share]

    def allowed(query_index, query_start, key_index, key_start, key_live):
        same = query_start == key_start
        causal = key_index <= query_index
        usable = (key_live == 1) | (key_index == query_index)
        return same & causal & usable

    mask = allowed(mine_index[:, None], mine_start[:, None], index[None], token_start[None], token_live[None])
    scores = dot(queries[:share], keys, ((1,), (1,))) * scale
    masked = jnp.where(mask, scores, NEGATIVE)
    top = jnp.max(masked, axis=-1, keepdims=True)
    weight = jnp.where(mask, jnp.exp(masked - top), 0.0)
    total = jnp.sum(weight, axis=-1, keepdims=True)
    prob = weight / total
    attended = dot(prob.astype(BF), values, ((1,), (0,)))
    log_total = top + jnp.log(total)
    delta = jnp.sum(grad_attended[:share].astype(F32) * attended, axis=-1, keepdims=True)
    push = dot(grad_attended[:share], values, ((1,), (1,)))
    slope = (prob * (push - delta)).astype(BF)
    grad_queries = dot(slope, keys, ((1,), (0,))) * scale
    attended = attended.astype(BF)

    marks = jnp.concatenate([log_total, delta], axis=1).T
    marks = spread(marks, masks_x).transpose(1, 0, 2).reshape(2, count)
    marks = jnp.concatenate([marks, swap_cores(marks)], axis=1)
    mask = allowed(index[None], token_start[None], mine_index[:, None], mine_start[:, None], mine_live[:, None])
    scores = dot(keys[:share], queries, ((1,), (1,))) * scale
    prob = jnp.where(mask, jnp.exp(jnp.where(mask, scores, NEGATIVE) - marks[0][None]), 0.0)
    grad_values = dot(prob.astype(BF), grad_attended, ((1,), (0,)))
    push = dot(values[:share], grad_attended, ((1,), (1,)))
    slope = (prob * (push - marks[1][None])).astype(BF)
    grad_keys = dot(slope, queries, ((1,), (0,))) * scale

    expanded = dot(normed_feed, w_expand, ((1,), (0,))) + expand_shift
    activated, bend = gelu_and_slope(expanded)
    activated = activated.astype(BF)
    grad_activated = dot(all_cotangent, w_shrink, ((1,), (1,)))
    grad_expanded = (bend * grad_activated).astype(BF)

    branch = dot(activated, w_shrink, ((1,), (0,)))
    attend_part = dot(attended, w_head, ((1,), (0,)))
    rest = jnp.zeros((size_x - 1,) + attend_part.shape, F32)
    attend_part = gathered_order(jnp.concatenate([attend_part[None], rest]))
    branch = (branch + attend_part).astype(BF)
    branch = scatter(branch[: count // 2], branch[count // 2 :])
    my_inputs = my_tokens.astype(F32)
    my_mixed = (my_inputs + branch.reshape(part, width) + residual_shift).astype(BF)

    def whole_block(value):
        low, high = by_core(core, value, swap_cores(value))
        return jnp.concatenate([low, high])

    mixed = whole_block(my_mixed)

    grad_shrink = dot(activated, all_cotangent, ((0,), (0,)))
    grad_expand = dot(normed_feed, grad_expanded, ((0,), (0,)))
    grad_shrink = grad_shrink[:units] + swap_cores(grad_shrink[units:].astype(BF)).astype(F32)
    grad_expand = grad_expand[:, :units] + swap_cores(grad_expand[:, units:].astype(BF)).astype(F32)
    shrink_deal = grad_shrink.astype(BF).reshape(units, blocks, depth).transpose(1, 0, 2)
    expand_deal = grad_expand.astype(BF).reshape(blocks, depth, units)
    shrink_grad = lax.all_to_all(shrink_deal, "blk", 0, 0, tiled=True)
    shrink_grad = shrink_grad.reshape(-1, depth).astype(F32)
    expand_grad = lax.all_to_all(expand_deal, "blk", 0, 0, tiled=True)
    expand_grad = expand_grad.transpose(1, 0, 2).reshape(depth, -1).astype(F32)

    def by_pieces(value):
        return value.reshape(share, group, columns).transpose(1, 0, 2)

    own_cosine, own_sine = cosine[:share], -sine[:share]
    back = [
        turn_pieces(by_pieces(grad_queries), own_cosine, own_sine),
        turn_pieces(by_pieces(grad_keys), own_cosine, own_sine),
        by_pieces(grad_values),
    ]
    back = jnp.concatenate(back, axis=2).astype(BF)
    back = jnp.concatenate([back, by_pieces(attended)], axis=2)
    back = jnp.stack([back[0]] + [from_peer(back[r], r) for r in masks_x])
    back = gathered_order(back)
    grad_linear, attended_near = back[:, : 3 * columns], back[:, 3 * columns :]
    grad_triple = dot(normed_attend, grad_linear, ((0,), (0,)))
    grad_out = dot(attended_near, all_cotangent, ((0,), (0,)))
    grad_triple = grad_triple.reshape(blocks, cores, cut, 3, columns).transpose(1, 0, 3, 2, 4)
    grad_triple = grad_triple.reshape(cores, blocks, 3 * cut, columns)
    grad_out = grad_out.reshape(cores, near, blocks, depth).transpose(0, 2, 1, 3)
    grad_out = grad_out.reshape(cores, blocks, near * depth // columns, columns)
    dealt = jnp.concatenate([grad_triple, grad_out], axis=2)
    keep = lax.dynamic_index_in_dim(dealt, core, 0, keepdims=False)
    give = lax.dynamic_index_in_dim(dealt, 1 - core, 0, keepdims=False)
    dealt = (keep + swap_cores(give.astype(BF)).astype(F32)).astype(BF)
    dealt = lax.all_to_all(dealt, "blk", 0, 0, tiled=True)
    dealt = dealt.reshape((cores, own_heads) + dealt.shape[1:])
    keep = lax.dynamic_index_in_dim(dealt, core, 0, keepdims=False)
    give = lax.dynamic_index_in_dim(dealt, 1 - core, 0, keepdims=False)
    dealt = jnp.stack(by_core(core, keep, swap_cores(give)))
    triple_grad = dealt[:, :, :at].reshape(cores, own_heads, 3, cut, columns)
    triple_grad = triple_grad.transpose(2, 0, 3, 1, 4).reshape(3, depth, -1).astype(F32)
    output_grad = dealt[:, :, at:].reshape(cores, own_heads, near, depth)
    output_grad = output_grad.transpose(1, 0, 2, 3).reshape(-1, depth).astype(F32)

    grad_attend_norm = dot(grad_linear, w_triple, ((1,), (1,)))
    grad_feed_norm = dot(grad_expanded, w_expand, ((1,), (1,)))
    combined = (gains[0] * grad_attend_norm + gains[1] * grad_feed_norm).astype(BF)
    combined = scatter(combined[: count // 2], combined[count // 2 :]).reshape(part, width)
    my_center = my_inputs - jnp.mean(my_inputs, axis=-1, keepdims=True)
    my_inverse = lax.rsqrt(jnp.mean(my_center * my_center, axis=-1, keepdims=True) + EPSILON)
    my_normal = my_center * my_inverse
    my_grad = my_inverse * (
        combined
        - jnp.mean(combined, axis=-1, keepdims=True)
        - my_normal * jnp.mean(combined * my_normal, axis=-1, keepdims=True)
    )
    tokens_grad = whole_block((my_cotangent.astype(F32) + my_grad).astype(BF))

    sums = [
        jnp.sum(normal * grad_attend_norm, axis=0),
        jnp.sum(normal * grad_feed_norm, axis=0),
        jnp.sum(grad_attend_norm, axis=0),
        jnp.sum(grad_feed_norm, axis=0),
        jnp.sum(all_cotangent.astype(F32), axis=0),
        jnp.sum(grad_expanded.astype(F32), axis=0),
        jnp.sum(grad_linear.astype(F32), axis=0),
    ]
    sums = jnp.concatenate(sums)
    other = swap_cores(sums)
    added = sums + other
    norm_sums = added[: 4 * width].reshape(4, width // 128, blocks, -1).transpose(2, 0, 1, 3)
    residual_sum = added[4 * width : 5 * width].reshape(width // 128, 128)
    lanes = 128 // blocks
    residual_grad = lax.dynamic_slice_in_dim(residual_sum, me * lanes, lanes, 1)
    unit_sum = sums[5 * width : 5 * width + units] + other[5 * width + units : 5 * width + 2 * units]
    unit_sums = lax.dynamic_update_slice_in_dim(
        jnp.zeros((w_in.shape[1],), F32), unit_sum, me * units, 0
    )
    unit_sums = unit_sums.reshape(-1, blocks, lanes).transpose(1, 0, 2)
    line_sum = added[5 * width + 2 * units :].reshape(3, columns)
    line_sums = lax.dynamic_update_slice_in_dim(
        jnp.zeros((3, width), F32), line_sum, me * columns, 1
    )
    line_sums = lax.dynamic_slice_in_dim(line_sums, core * (width // cores), width // cores, 1)
    line_sums = line_sums.reshape(3, -1, blocks, lanes).transpose(2, 0, 1, 3)
    tiny = jnp.concatenate(
        [norm_sums.reshape(blocks, -1), unit_sums.reshape(blocks, -1), line_sums.reshape(blocks, -1)],
        axis=1,
    )
    tiny = jnp.sum(lax.all_to_all(tiny, "blk", 0, 0, tiled=True), axis=0)
    first = norm_gain.size
    gain_grad = tiny[:first].reshape(norm_gain.shape)
    shift_grad = tiny[first : 2 * first].reshape(norm_shift.shape)
    expand_bias_grad = tiny[2 * first : 2 * first + b_in.size].reshape(b_in.shape)
    triple_bias_grad = tiny[2 * first + b_in.size :].reshape(b_qkv.shape)
    return (
        mixed,
        tokens_grad,
        triple_grad,
        triple_bias_grad,
        output_grad,
        residual_grad,
        expand_grad,
        expand_bias_grad,
        shrink_grad,
        residual_grad,
        gain_grad,
        shift_grad,
    )


def solution(mesh):
    placed = (
        P("blk", None),
        P(None, "blk", "tp"),
        P(None, "tp", "blk"),
        P("tp", "blk"),
        P(None, "blk"),
        P("blk", "tp"),
        P("tp", "blk"),
        P("tp", "blk"),
        P(None, "blk"),
        P(None, None, "blk"),
        P(None, None, "blk"),
        P("blk"),
        P("blk"),
        P("blk", None),
    )
    return jax.shard_map(
        body,
        mesh=mesh,
        in_specs=placed,
        out_specs=(
            P("blk", None),
            P("blk", None),
            P(None, "blk", "tp"),
            P(None, "tp", "blk"),
            P("tp", "blk"),
            P(None, "blk"),
            P("blk", "tp"),
            P("tp", "blk"),
            P("tp", "blk"),
            P(None, "blk"),
            P(None, None, "blk"),
            P(None, None, "blk"),
        ),
        check_vma=False,
    )
```

time: 3210 us -> 582 us (0.18)
  waiting for transfers between devices: 2640 us -> 157 us
  blocking collectives: 303 us -> 0 us
  local copies, waits for them, and re-layouts: 48 us -> 146 us
  starting transfers between devices: 0.57 us -> 97.6 us
  matrix products: 163 us -> 78.2 us
  other arithmetic: 28.6 us -> 90.5 us
    reduce_scatter x4 -> x0, waiting for transfers between devices: 1930 us -> none  [the longest x1 692 us: body(): lax.psum_scatter(grad_expand, 'blk', scatter_dimension=0, tiled=True)]
    all_gather x8 -> x0, waiting for transfers between devices: 636 us -> none  [the longest x1 240 us: body(): lax.all_gather(w_out2, 'blk', axis=1, tiled=True)]
    all_gather x10 -> x0, blocking collectives: 303 us -> none  [the longest x1 43 us: body(): lax.all_gather(delta, 'blk', axis=0, tiled=True)]
    ppermute x0 -> x46, waiting for transfers between devices: none -> 155 us  [the longest x32 155 us: from_peer(): return lax.ppermute(value, 'blk', [(i, i ^ mask) for i in range(count)])]
    dot_general x40 -> x18, matrix products: 163 us -> 78.2 us  [dot(): lax.dot_general(left, right, (dims, ((), ())), preferred_element_type=F32)]
    unnamed x15 -> x0, waiting for transfers between devices: 82.2 us -> none
    ppermute x0 -> x46, starting transfers between devices: none -> 57.2 us  [the longest x32 32.6 us: from_peer(): return lax.ppermute(value, 'blk', [(i, i ^ mask) for i in range(count)])]
    all_to_all x0 -> x7, starting transfers between devices: none -> 40.4 us  [the longest x1 7.15 us: body(): dealt = lax.all_to_all(dealt, 'blk', 0, 0, tiled=True)]
  transfers between devices with their start and end apart: 14 -> 53, of which waited for: 11 -> 14; matrix products, arithmetic and copies ran while one was open for 6% -> 51% of each run, Pallas kernels for 0% -> 0%
where the time goes in v1:
time: 582 us; the launch traced here: 573 us
  waiting for transfers between devices  157 us (27%)
  local copies, waits for them, and re-layouts  146 us (25%)
  starting transfers between devices  97.6 us (17%)
  other arithmetic  90.5 us (16%)
  matrix products  78.2 us (13%)
    ppermute x32, waiting for transfers between devices, from_peer(): return lax.ppermute(value, 'blk', [(i, i ^ mask) for i in range(count)])  155 us
    dot_general x18, matrix products, dot(): lax.dot_general(left, right, (dims, ((), ())), preferred_element_type=F32)  78.2 us
    ppermute x32, starting transfers between devices, from_peer(): return lax.ppermute(value, 'blk', [(i, i ^ mask) for i in range(count)])  32.6 us
    ppermute x14, starting transfers between devices, swap_cores(): return lax.ppermute(value, 'tp', [(0, 1), (1, 0)])  24.6 us
    another operation x13, other arithmetic, spread(): return jnp.stack([value] + [from_peer(value, mask) for mask in masks])  17 us
    unnamed x238, local copies, waits for them, and re-layouts  16.1 us
    concatenate x11, local copies, waits for them, and re-layouts, body(): mine = jnp.concatenate([queries, keys, linear[:, 2]], axis=1).astype(BF)  14.4 us
    gather x1, local copies, waits for them, and re-layouts, body(): token_start = starts.reshape(-1)[index]  11.8 us
  transfers between devices with their start and end apart: 53, of which 14 were waited for; matrix products, arithmetic and copies ran while one was open for 51% of the time, Pallas kernels for 0%

profile of v1, /device:TPU:11, one launch (start us, length us, event | category | flops | bytes accessed | tf_op | source)
XLA Modules:
  0.0 573.3 jit_solution(3833562631406307455)
XLA Ops:
  8.9 5.5 all-to-all-start.2
  20.0 3.7 collective-permute-start.7
  23.6 3.4 collective-permute-done.2
  31.1 12.2 %collective-permute-done.23 = bf16[64,2048]{1,0:T(8,128)(2,1)S(1)} collective-permute-done((bf16[64,2048]{1,0:T(8,128)(2,1)S(1)}, bf16[64,2048]{1,0:T(8,128)(2,1)S(1)}, u32[]{:S(2)}, u32[]{:S(2)}) %collective-permute-start.23) | collective-permute-done | bytes 262176 | tf_op jit(solution)/shard_map/ppermute | solution.py:28
  43.3 28.6 %collective-permute-done.24 = bf16[64,2048]{1,0:T(8,128)(2,1)S(1)} collective-permute-done((bf16[64,2048]{1,0:T(8,128)(2,1)S(1)}, bf16[64,2048]{1,0:T(8,128)(2,1)S(1)}, u32[]{:S(2)}, u32[]{:S(2)}) %collective-permute-start.24) | collective-permute-done | bytes 262176 | tf_op jit(solution)/shard_map/ppermute | solution.py:28
  73.4 5.6 all-to-all-start
  84.2 2.5 fusion.143
  87.6 13.9 %collective-permute-done.25 = bf16[4,32,2048]{2,1,0:T(8,128)(2,1)S(1)} collective-permute-done((bf16[4,32,2048]{2,1,0:T(8,128)(2,1)S(1)}, bf16[4,32,2048]{2,1,0:T(8,128)(2,1)S(1)}, u32[]{:S(2)}, u32[]{:S(2)}) %collective-permute-start.25) | collective-permute-done | bytes 524320 | tf_op jit(solution)/shard_map/ppermute | solution.py:28
  107.7 18.1 %collective-permute-done.4 = bf16[2,4,32,2048]{3,2,1,0:T(8,128)(2,1)} collective-permute-done((bf16[2,4,32,2048]{3,2,1,0:T(8,128)(2,1)S(1)}, bf16[2,4,32,2048]{3,2,1,0:T(8,128)(2,1)}, u32[]{:S(2)}, u32[]{:S(2)}) %collective-permute-start.4) | collective-permute-done | bytes 1048608 | tf_op jit(solution)/shard_map/ppermute | solution.py:28
  127.6 6.3 %all-to-all-start.1 = ((bf16[16,128,256]{1,2,0:T(8,128)(2,1)}), bf16[16,128,256]{1,2,0:T(8,128)(2,1)}, u32[]{:S(2)}, u32[]{:S(2)}) async-start(bf16[16,128,256]{1,2,0:T(8,128)(2,1)} %bitcast.458), calls=%async_computation.1 | async-start | bytes 2097152 | tf_op jit(solution)/shard_map/all_to_all | solution.py:149
  136.2 17.7 %collective-permute-done.26 = bf16[2,4,32,2048]{3,2,1,0:T(8,128)(2,1)} collective-permute-done((bf16[2,4,32,2048]{3,2,1,0:T(8,128)(2,1)}, bf16[2,4,32,2048]{3,2,1,0:T(8,128)(2,1)}, u32[]{:S(2)}, u32[]{:S(2)}) %collective-permute-start.26) | collective-permute-done | bytes 1048608 | tf_op jit(solution)/shard_map/ppermute | solution.py:28
  157.6 6.4 %collective-permute-start.10 = (bf16[16,256,128]{2,1,0:T(8,128)(2,1)}, bf16[16,256,128]{2,1,0:T(8,128)(2,1)}, u32[]{:S(2)}, u32[]{:S(2)}) collective-permute-start(bf16[16,256,128]{2,1,0:T(8,128)(2,1)} %all-to-all-done.2), channel_id=1, source_target_pairs={{0,1},{1,0},{2,3},{3,2},{4,5},{5,4},{6,7},{7,6},{8,9},{9,8},{10,11... | collective-permute-start | bytes 3145736 | tf_op jit(solution)/shard_map/ppermute | solution.py:23
  165.3 2.8 fusion.12
  170.9 3.1 maximum_bitcast_fusion
  174.0 4.0 copy.246
  182.8 2.4 fusion.39
  195.5 3.0 copy.249
  198.6 7.9 %fusion.7 = (bf16[1024,2048]{1,0:T(8,128)(2,1)}, bf16[1024,2048]{1,0:T(8,128)(2,1)S(1)}) fusion(f32[2048]{0:T(1024)S(1)} %add.374, f32[2048]{0:T(1024)S(1)} %copy-done.79, f32[1024]{0:T(1024)S(1)} %add_rsqrt_fusion, f32[1024]{0:T(1024)S(1)} %broadcast_multiply_fusion, bf16[512,2048]{1,0:T(8,128)(2,1)S(1)} %bitcast.431, bf16[512,2048]{1,0:T(8,128)(2,1)S(1)} %bitcast.427, ...), kind=kLoop, calls=%fused_computation.14 | loop fusion | flops 25165824 | bytes 12623872 | tf_op jit(solution)/shard_map/convert_element_type | solution.py:236
  206.5 2.4 fusion.44
  210.3 3.7 copy.253
  214.0 3.4 reshape.659
  226.2 3.7 fusion.48
  229.9 2.4 fusion.152
  235.5 5.9 %convert_reduce_fusion.2 = (f32[512]{0:T(512)}, bf16[1024,512]{1,0:T(8,128)(2,1)}) fusion(bf16[512,2048]{0,1:T(8,128)(2,1)S(1)} %bitcast.479, bf16[512,2048]{1,0:T(8,128)(2,1)S(1)} %bitcast.447, bf16[512,2048]{1,0:T(8,128)(2,1)S(1)} %bitcast.442, f32[1024,512]{1,0:T(8,128)S(1)} %fusion.48, f32[512]{0:T(512)S(1)} %pad_maximum_fusion.39), kind=kOutput, calls=%fused_computation.80 | convolution fusion | flops 2162687488 | bytes 9441280 | tf_op jit(solution)/shard_map/dot_general | solution.py:19
  241.4 11.8 %gather_fusion = s32[2048]{0:T(1024)S(1)} fusion(s32[2048]{0:T(1024)S(1)} %get-tuple-element.157, s32[2048]{0:T(1024)S(1)} %broadcast_clamp_fusion), kind=kCustom, calls=%fused_computation | custom fusion | bytes 24576 | tf_op jit(solution)/shard_map/gather | solution.py:228
  260.7 4.1 concatenate.179
  269.7 4.9 fusion.170
  282.8 3.3 concatenate.178
  287.3 11.8 %gather_fusion.1 = s32[2048]{0:T(1024)S(1)} fusion(s32[2048]{0:T(1024)S(1)} %fusion.118, s32[2048]{0:T(1024)S(1)} %broadcast_clamp_fusion), kind=kCustom, calls=%fused_computation.1 | custom fusion | bytes 24576 | tf_op jit(solution)/shard_map/gather | solution.py:229
  300.8 2.8 gather_fusion.2
  303.6 3.0 copy.269
  306.6 3.2 stack.191
  322.9 3.2 bitcast_bitcast_fusion
  326.1 5.1 all-to-all-start.6
  331.2 3.1 fusion.30
  334.4 3.3 fusion.14
  337.7 3.0 fusion.16
  340.7 3.8 multiply_reduce_fusion
  345.6 2.8 pad_slice_fusion.1
  350.7 6.7 %fusion.51 = f32[512,256]{0,1:T(8,128)} fusion(f32[512]{0:T(512)S(1)} %get-tuple-element.144, bf16[2,256,256]{1,2,0:T(8,128)(2,1)S(1)} %copy-done.55, bf16[2,256,256]{1,2,0:T(8,128)(2,1)S(1)} %copy-done.52, bf16[3,1024,256]{1,2,0:T(8,128)(2,1)} %bitcast.66, bf16[3,1024,256]{1,2,0:T(8,128)(2,1)} %collective-permute-done.12, f32[512,2048]{1,0:T(8,128)} %copy-done.28, ...), kind=kOutput, calls=%fused_computation.117 | convolution fusion | flops 1093271552 | bytes 11563008 | tf_op jit(solution)/shard_map/dot_general | solution.py:19
  357.4 9.1 %fusion.13 = bf16[1024,2048]{1,0:T(8,128)(2,1)} fusion(f32[512,2048]{1,0:T(8,128)} %bitcast.457, f32[512,2048]{1,0:T(8,128)} %bitcast.456, bf16[512,2048]{0,1:T(8,128)(2,1)} %bitcast.478, f32[1024,512]{1,0:T(8,128)} %copy-done.103, f32[512]{0:T(512)S(1)} %copy-done.99), kind=kOutput, calls=%fused_computation.21 | convolution fusion | flops 2156920832 | bytes 16779264 | tf_op jit(solution)/shard_map/dot_general | solution.py:19
  369.3 5.7 exponential_select_fusion
  375.0 5.0 fusion.52
  383.1 3.1 fusion.53
  392.9 7.1 %collective-permute-done.32 = bf16[512,512]{0,1:T(8,128)(2,1)S(1)} collective-permute-done((bf16[512,512]{0,1:T(8,128)(2,1)S(1)}, bf16[512,512]{0,1:T(8,128)(2,1)S(1)}, u32[]{:S(2)}, u32[]{:S(2)}) %collective-permute-start.32) | collective-permute-done | bytes 524320 | tf_op jit(solution)/shard_map/ppermute | solution.py:28
  402.7 3.1 convolution_bitcast_fusion.1
  406.1 4.1 fusion.169
  410.2 5.7 %fusion.40 = f32[1024,2048]{1,0:T(8,128)} fusion(bf16[1024,384]{1,0:T(8,128)(2,1)S(1)} %get-tuple-element.67, bf16[256,8,3,128]{3,2,1,0:T(4,128)(2,1)S(1)} %bitcast.453), kind=kOutput, calls=%fused_computation.88 | convolution fusion | flops 1610612736 | bytes 10747904 | tf_op jit(solution)/shard_map/dot_general | solution.py:19
  416.5 6.2 %reshape.681 = f32[16,2,64,3,128]{4,3,2,1,0:T(4,128)} reshape(f32[2048,384]{1,0:T(8,128)} %fusion.169) | data formatting | bytes 6291456 | tf_op jit(solution)/shard_map/reshape | solution.py:373
  422.7 2.6 copy.281
  429.1 7.2 %fusion.155 = (f32[2048]{0:T(1024)S(1)}, f32[2048]{0:T(1024)S(1)}, bf16[1024,2048]{1,0:T(8,128)(2,1)S(1)}, f32[2048]{0:T(1024)S(1)}, f32[2048]{0:T(1024)S(1)}) fusion(f32[1024]{0:T(1024)S(1)} %copy-done.84, f32[1024]{0:T(1024)S(1)} %copy-done.73, bf16[512,2048]{1,0:T(8,128)(2,1)S(1)} %bitcast.432, bf16[512,2048]{1,0:T(8,128)(2,1)S(1)} %bitcast.428, ...), kind=kOutput, calls=%fused_computation.385 | convolution fusion | flops 2185224192 | bytes 19980288 | tf_op jit(solution)/shard_map/dot_general | solution.py:19
  449.6 6.3 %all-to-all-start.5 = ((bf16[16,128,256]{2,1,0:T(8,128)(2,1)}), bf16[16,128,256]{2,1,0:T(8,128)(2,1)}, u32[]{:S(2)}, u32[]{:S(2)}) async-start(bf16[16,128,256]{2,1,0:T(8,128)(2,1)} %bitcast.181), calls=%async_computation.5 | async-start | bytes 2097152 | tf_op jit(solution)/shard_map/all_to_all | solution.py:354
  455.9 2.7 bitcast_convert_fusion
  458.6 26.3 %collective-permute-done.17 = bf16[4,32,2048]{2,1,0:T(8,128)(2,1)} collective-permute-done((bf16[4,32,2048]{2,1,0:T(8,128)(2,1)}, bf16[4,32,2048]{2,1,0:T(8,128)(2,1)}, u32[]{:S(2)}, u32[]{:S(2)}) %collective-permute-start.17) | collective-permute-done | bytes 524320 | tf_op jit(solution)/shard_map/ppermute | solution.py:28
  495.9 5.2 collective-permute-done.36
  501.3 2.4 collective-permute-done.34
  507.3 4.5 all-to-all-start.4
  513.1 2.6 fusion.28
  515.8 3.5 collective-permute-start.20
  519.3 7.2 %all-to-all-start.3 = ((bf16[16,256,128]{2,1,0:T(8,128)(2,1)}), bf16[16,256,128]{2,1,0:T(8,128)(2,1)S(1)}, u32[]{:S(2)}, u32[]{:S(2)}) async-start(bf16[16,256,128]{2,1,0:T(8,128)(2,1)} %fusion.28), calls=%async_computation.3 | async-start | bytes 2097152 | tf_op jit(solution)/shard_map/all_to_all | solution.py:381
  526.5 15.8 %collective-permute-done.39 = bf16[64,2048]{1,0:T(8,128)(2,1)} collective-permute-done((bf16[64,2048]{1,0:T(8,128)(2,1)}, bf16[64,2048]{1,0:T(8,128)(2,1)}, u32[]{:S(2)}, u32[]{:S(2)}) %collective-permute-start.39) | collective-permute-done | bytes 262176 | tf_op jit(solution)/shard_map/ppermute | solution.py:28
  543.9 4.1 collective-permute-done.20
  549.5 6.5 %collective-permute-start.40 = (bf16[64,2048]{1,0:T(8,128)(2,1)S(1)}, bf16[64,2048]{1,0:T(8,128)(2,1)S(1)}, u32[]{:S(2)}, u32[]{:S(2)}) collective-permute-start(bf16[64,2048]{1,0:T(8,128)(2,1)S(1)} %get-tuple-element.150), channel_id=1, source_target_pairs={{0,1},{1,0},{2,3},{3,2},{4,5},{5,4},{6,7},{7,6},{8,9},{9,8},{10,11... | collective-permute-start | bytes 786440 | tf_op jit(solution)/shard_map/ppermute | solution.py:23
  564.2 3.0 collective-permute-start.42
  (542 shorter events, 176.8 us)
Async XLA Ops:
  1.8 16.8 %collective-permute-start = (bf16[64,2048]{1,0:T(8,128)(2,1)S(1)}, bf16[64,2048]{1,0:T(8,128)(2,1)S(1)}, u32[]{:S(2)}, u32[]{:S(2)}) collective-permute-start(bf16[64,2048]{1,0:T(8,128)(2,1)S(1)} %get-tuple-element.70), channel_id=1, source_target_pairs={{0,8},{2,10},{4,12},{6,14},{8,0},{10,2},{12,4},{14,6},{16,24},{18,... | collective-permute-start | bytes 786440 | tf_op jit(solution)/shard_map/ppermute | solution.py:28
  2.1 17.9 %collective-permute-start.1 = (bf16[64,2048]{1,0:T(8,128)(2,1)S(1)}, bf16[64,2048]{1,0:T(8,128)(2,1)}, u32[]{:S(2)}, u32[]{:S(2)}) collective-permute-start(bf16[64,2048]{1,0:T(8,128)(2,1)S(1)} %get-tuple-element.70), channel_id=1, source_target_pairs={{0,16},{2,18},{4,20},{6,22},{8,24},{10,26},{12,28},{14,30},{16,0},... | collective-permute-start | bytes 786440 | tf_op jit(solution)/shard_map/ppermute | solution.py:28
  4.4 22.6 %collective-permute-start.2 = (bf16[64,2048]{1,0:T(8,128)(2,1)S(1)}, bf16[64,2048]{1,0:T(8,128)(2,1)}, u32[]{:S(2)}, u32[]{:S(2)}) collective-permute-start(bf16[64,2048]{1,0:T(8,128)(2,1)S(1)} %get-tuple-element.70), channel_id=1, source_target_pairs={{0,24},{2,26},{4,28},{6,30},{8,16},{10,18},{12,20},{14,22},{16,8},... | collective-permute-start | bytes 786440 | tf_op jit(solution)/shard_map/ppermute | solution.py:28
  5.5 25.4 %collective-permute-start.22 = (bf16[64,2048]{1,0:T(8,128)(2,1)S(1)}, bf16[64,2048]{1,0:T(8,128)(2,1)S(1)}, u32[]{:S(2)}, u32[]{:S(2)}) collective-permute-start(bf16[64,2048]{1,0:T(8,128)(2,1)S(1)} %constant_dynamic-slice_fusion.2), channel_id=1, source_target_pairs={{0,8},{2,10},{4,12},{6,14},{8,0},{10,2},{12,4},{14,6},{16,24},{18,... | collective-permute-start | bytes 786440 | tf_op jit(solution)/shard_map/ppermute | solution.py:28
  6.7 36.6 %collective-permute-start.23 = (bf16[64,2048]{1,0:T(8,128)(2,1)S(1)}, bf16[64,2048]{1,0:T(8,128)(2,1)S(1)}, u32[]{:S(2)}, u32[]{:S(2)}) collective-permute-start(bf16[64,2048]{1,0:T(8,128)(2,1)S(1)} %constant_dynamic-slice_fusion.2), channel_id=1, source_target_pairs={{0,16},{2,18},{4,20},{6,22},{8,24},{10,26},{12,28},{14,30},{16,0},... | collective-permute-start | bytes 786440 | tf_op jit(solution)/shard_map/ppermute | solution.py:28
  8.9 64.5 %all-to-all-start.2 = ((bf16[16,256,128]{2,1,0:T(8,128)(2,1)}), bf16[16,256,128]{2,1,0:T(8,128)(2,1)}, u32[]{:S(2)}, u32[]{:S(2)}) async-start(bf16[16,256,128]{2,1,0:T(8,128)(2,1)} %bitcast.492), calls=%async_computation.2 | async-start | bytes 2097152 | tf_op jit(solution)/shard_map/all_to_all | solution.py:151
  18.7 53.2 %collective-permute-start.24 = (bf16[64,2048]{1,0:T(8,128)(2,1)S(1)}, bf16[64,2048]{1,0:T(8,128)(2,1)S(1)}, u32[]{:S(2)}, u32[]{:S(2)}) collective-permute-start(bf16[64,2048]{1,0:T(8,128)(2,1)S(1)} %constant_dynamic-slice_fusion.2), channel_id=1, source_target_pairs={{0,24},{2,26},{4,28},{6,30},{8,16},{10,18},{12,20},{14,22},{16,8},... | collective-permute-start | bytes 786440 | tf_op jit(solution)/shard_map/ppermute | solution.py:28
  20.0 52.0 %collective-permute-start.7 = (bf16[8,256,128]{2,1,0:T(8,128)(2,1)S(1)}, bf16[8,256,128]{2,1,0:T(8,128)(2,1)S(1)}, u32[]{:S(2)}, u32[]{:S(2)}) collective-permute-start(bf16[8,256,128]{2,1,0:T(8,128)(2,1)S(1)} %fusion.85), channel_id=1, source_target_pairs={{0,1},{1,0},{2,3},{3,2},{4,5},{5,4},{6,7},{7,6},{8,9},{9,8},{10,11... | collective-permute-start | bytes 1572872 | tf_op jit(solution)/shard_map/ppermute | solution.py:23
  29.6 51.2 %collective-permute-start.3 = (bf16[4,32,2048]{2,1,0:T(8,128)(2,1)}, bf16[4,32,2048]{2,1,0:T(8,128)(2,1)}, u32[]{:S(2)}, u32[]{:S(2)}) collective-permute-start(bf16[4,32,2048]{2,1,0:T(8,128)(2,1)} %get-tuple-element.123), channel_id=1, source_target_pairs={{0,4},{2,6},{4,0},{6,2},{8,12},{10,14},{12,8},{14,10},{16,20},{18,... | collective-permute-start | bytes 1572872 | tf_op jit(solution)/shard_map/ppermute | solution.py:28
  30.9 53.3 %collective-permute-start.5 = (bf16[4,32,2048]{2,1,0:T(8,128)(2,1)}, bf16[4,32,2048]{2,1,0:T(8,128)(2,1)}, u32[]{:S(2)}, u32[]{:S(2)}) collective-permute-start(bf16[4,32,2048]{2,1,0:T(8,128)(2,1)} %get-tuple-element.122), channel_id=1, source_target_pairs={{0,2},{2,0},{4,6},{6,4},{8,10},{10,8},{12,14},{14,12},{16,18},{18,... | collective-permute-start | bytes 1572872 | tf_op jit(solution)/shard_map/ppermute | solution.py:28
  73.4 54.2 %all-to-all-start = ((bf16[16,272,128]{2,1,0:T(8,128)(2,1)}), bf16[16,272,128]{2,1,0:T(8,128)(2,1)S(1)}, u32[]{:S(2)}, u32[]{:S(2)}) async-start(bf16[16,272,128]{2,1,0:T(8,128)(2,1)} %pad_maximum_fusion.10), calls=%async_computation | async-start | bytes 2228224 | tf_op jit(solution)/shard_map/all_to_all | solution.py:144
  79.3 22.2 %collective-permute-start.25 = (bf16[4,32,2048]{2,1,0:T(8,128)(2,1)S(1)}, bf16[4,32,2048]{2,1,0:T(8,128)(2,1)S(1)}, u32[]{:S(2)}, u32[]{:S(2)}) collective-permute-start(bf16[4,32,2048]{2,1,0:T(8,128)(2,1)S(1)} %get-tuple-element.112), channel_id=1, source_target_pairs={{0,4},{2,6},{4,0},{6,2},{8,12},{10,14},{12,8},{14,10},{16,20},{18,... | collective-permute-start | bytes 1572872 | tf_op jit(solution)/shard_map/ppermute | solution.py:28
  80.5 22.8 %collective-permute-start.27 = (bf16[4,32,2048]{2,1,0:T(8,128)(2,1)S(1)}, bf16[4,32,2048]{2,1,0:T(8,128)(2,1)S(1)}, u32[]{:S(2)}, u32[]{:S(2)}) collective-permute-start(bf16[4,32,2048]{2,1,0:T(8,128)(2,1)S(1)} %get-tuple-element.111), channel_id=1, source_target_pairs={{0,2},{2,0},{4,6},{6,4},{8,10},{10,8},{12,14},{14,12},{16,18},{18,... | collective-permute-start | bytes 1572872 | tf_op jit(solution)/shard_map/ppermute | solution.py:28
  83.0 42.8 %collective-permute-start.4 = (bf16[2,4,32,2048]{3,2,1,0:T(8,128)(2,1)S(1)}, bf16[2,4,32,2048]{3,2,1,0:T(8,128)(2,1)}, u32[]{:S(2)}, u32[]{:S(2)}) collective-permute-start(bf16[2,4,32,2048]{3,2,1,0:T(8,128)(2,1)S(1)} %get-tuple-element.119), channel_id=1, source_target_pairs={{0,2},{2,0},{4,6},{6,4},{8,10},{10,8},{12,14},{14,12},{16,18},{18,... | collective-permute-start | bytes 3145736 | tf_op jit(solution)/shard_map/ppermute | solution.py:28
  86.7 47.1 %collective-permute-start.6 = (bf16[2,4,32,2048]{3,2,1,0:T(8,128)(2,1)}, bf16[2,4,32,2048]{3,2,1,0:T(8,128)(2,1)}, u32[]{:S(2)}, u32[]{:S(2)}) collective-permute-start(bf16[2,4,32,2048]{3,2,1,0:T(8,128)(2,1)} %get-tuple-element.125), channel_id=1, source_target_pairs={{0,4},{2,6},{4,0},{6,2},{8,12},{10,14},{12,8},{14,10},{16,20},{18,... | collective-permute-start | bytes 3145736 | tf_op jit(solution)/shard_map/ppermute | solution.py:28
  103.0 50.9 %collective-permute-start.26 = (bf16[2,4,32,2048]{3,2,1,0:T(8,128)(2,1)}, bf16[2,4,32,2048]{3,2,1,0:T(8,128)(2,1)}, u32[]{:S(2)}, u32[]{:S(2)}) collective-permute-start(bf16[2,4,32,2048]{3,2,1,0:T(8,128)(2,1)} %get-tuple-element.108), channel_id=1, source_target_pairs={{0,2},{2,0},{4,6},{6,4},{8,10},{10,8},{12,14},{14,12},{16,18},{18,... | collective-permute-start | bytes 3145736 | tf_op jit(solution)/shard_map/ppermute | solution.py:28
  104.8 51.1 %collective-permute-start.28 = (bf16[2,4,32,2048]{3,2,1,0:T(8,128)(2,1)}, bf16[2,4,32,2048]{3,2,1,0:T(8,128)(2,1)}, u32[]{:S(2)}, u32[]{:S(2)}) collective-permute-start(bf16[2,4,32,2048]{3,2,1,0:T(8,128)(2,1)} %get-tuple-element.114), channel_id=1, source_target_pairs={{0,4},{2,6},{4,0},{6,2},{8,12},{10,14},{12,8},{14,10},{16,20},{18,... | collective-permute-start | bytes 3145736 | tf_op jit(solution)/shard_map/ppermute | solution.py:28
  127.5 36.4 %copy-start.26 = (bf16[16,272,128]{2,1,0:T(8,128)(2,1)}, bf16[16,272,128]{2,1,0:T(8,128)(2,1)S(1)}, u32[]{:S(2)}) copy-start(bf16[16,272,128]{2,1,0:T(8,128)(2,1)S(1)} %all-to-all-done) | copy-start | bytes 3342340
  127.6 40.6 %all-to-all-start.1 = ((bf16[16,128,256]{1,2,0:T(8,128)(2,1)}), bf16[16,128,256]{1,2,0:T(8,128)(2,1)}, u32[]{:S(2)}, u32[]{:S(2)}) async-start(bf16[16,128,256]{1,2,0:T(8,128)(2,1)} %bitcast.458), calls=%async_computation.1 | async-start | bytes 2097152 | tf_op jit(solution)/shard_map/all_to_all | solution.py:149
  135.6 29.8 %copy-start = (bf16[2,2,4,32,2048]{4,3,2,1,0:T(8,128)(2,1)}, bf16[2,2,4,32,2048]{4,3,2,1,0:T(8,128)(2,1)S(1)}, u32[]{:S(2)}) copy-start(bf16[2,2,4,32,2048]{4,3,2,1,0:T(8,128)(2,1)S(1)} %pad_maximum_fusion.3) | copy-start | bytes 6291460
  157.6 13.3 %collective-permute-start.10 = (bf16[16,256,128]{2,1,0:T(8,128)(2,1)}, bf16[16,256,128]{2,1,0:T(8,128)(2,1)}, u32[]{:S(2)}, u32[]{:S(2)}) collective-permute-start(bf16[16,256,128]{2,1,0:T(8,128)(2,1)} %all-to-all-done.2), channel_id=1, source_target_pairs={{0,1},{1,0},{2,3},{3,2},{4,5},{5,4},{6,7},{7,6},{8,9},{9,8},{10,11... | collective-permute-start | bytes 3145736 | tf_op jit(solution)/shard_map/ppermute | solution.py:23
  164.0 14.0 %collective-permute-start.8 = (bf16[16,272,128]{2,1,0:T(8,128)(2,1)S(1)}, bf16[16,272,128]{2,1,0:T(8,128)(2,1)}, u32[]{:S(2)}, u32[]{:S(2)}) collective-permute-start(bf16[16,272,128]{2,1,0:T(8,128)(2,1)S(1)} %all-to-all-done), channel_id=1, source_target_pairs={{0,1},{1,0},{2,3},{3,2},{4,5},{5,4},{6,7},{7,6},{8,9},{9,8},{10,11... | collective-permute-start | bytes 3342344 | tf_op jit(solution)/shard_map/ppermute | solution.py:23
  165.3 33.2 %copy-start.72 = (f32[1024]{0:T(1024)}, f32[1024]{0:T(1024)S(1)}, u32[]{:S(2)}) copy-start(f32[1024]{0:T(1024)S(1)} %broadcast_multiply_fusion) | copy-start | bytes 12292
  168.2 30.4 %copy-start.83 = (f32[1024]{0:T(1024)}, f32[1024]{0:T(1024)S(1)}, u32[]{:S(2)}) copy-start(f32[1024]{0:T(1024)S(1)} %add_rsqrt_fusion) | copy-start | bytes 12292
  170.4 55.7 %collective-permute-start.9 = (bf16[2048,256]{1,0:T(8,128)(2,1)}, bf16[2048,256]{1,0:T(8,128)(2,1)}, u32[]{:S(2)}, u32[]{:S(2)}) collective-permute-start(bf16[2048,256]{1,0:T(8,128)(2,1)} %bitcast.493), channel_id=1, source_target_pairs={{0,1},{1,0},{2,3},{3,2},{4,5},{5,4},{6,7},{7,6},{8,9},{9,8},{10,11... | collective-permute-start | bytes 3145736 | tf_op jit(solution)/shard_map/ppermute | solution.py:23
  233.5 89.4 %collective-permute-start.45 = (bf16[256,2048]{1,0:T(8,128)(2,1)}, bf16[256,2048]{1,0:T(8,128)(2,1)}, u32[]{:S(2)}, u32[]{:S(2)}) collective-permute-start(bf16[256,2048]{1,0:T(8,128)(2,1)} %slice.909), channel_id=1, source_target_pairs={{0,1},{1,0},{2,3},{3,2},{4,5},{5,4},{6,7},{7,6},{8,9},{9,8},{10,11... | collective-permute-start | bytes 3145736 | tf_op jit(solution)/shard_map/ppermute | solution.py:23
  264.9 35.9 %collective-permute-start.11 = (bf16[1024,384]{1,0:T(8,128)(2,1)}, bf16[1024,384]{1,0:T(8,128)(2,1)}, u32[]{:S(2)}, u32[]{:S(2)}) collective-permute-start(bf16[1024,384]{1,0:T(8,128)(2,1)} %concatenate.179), channel_id=1, source_target_pairs={{0,2},{2,0},{4,6},{6,4},{8,10},{10,8},{12,14},{14,12},{16,18},{18,... | collective-permute-start | bytes 2359304 | tf_op jit(solution)/shard_map/ppermute | solution.py:28
  268.2 31.2 %collective-permute-start.13 = (bf16[128,2048]{1,0:T(8,128)(2,1)}, bf16[128,2048]{1,0:T(8,128)(2,1)}, u32[]{:S(2)}, u32[]{:S(2)}) collective-permute-start(bf16[128,2048]{1,0:T(8,128)(2,1)} %bitcast.423), channel_id=1, source_target_pairs={{0,2},{2,0},{4,6},{6,4},{8,10},{10,8},{12,14},{14,12},{16,18},{18,... | collective-permute-start | bytes 1572872 | tf_op jit(solution)/shard_map/ppermute | solution.py:28
  277.8 53.5 %collective-permute-start.44 = (bf16[2048,256]{1,0:T(8,128)(2,1)}, bf16[2048,256]{1,0:T(8,128)(2,1)}, u32[]{:S(2)}, u32[]{:S(2)}) collective-permute-start(bf16[2048,256]{1,0:T(8,128)(2,1)} %slice.910), channel_id=1, source_target_pairs={{0,1},{1,0},{2,3},{3,2},{4,5},{5,4},{6,7},{7,6},{8,9},{9,8},{10,11... | collective-permute-start | bytes 3145736 | tf_op jit(solution)/shard_map/ppermute | solution.py:23
  312.8 21.6 %collective-permute-start.12 = (bf16[3,1024,256]{1,2,0:T(8,128)(2,1)}, bf16[3,1024,256]{1,2,0:T(8,128)(2,1)}, u32[]{:S(2)}, u32[]{:S(2)}) collective-permute-start(bf16[3,1024,256]{1,2,0:T(8,128)(2,1)} %bitcast.66), channel_id=1, source_target_pairs={{0,1},{1,0},{2,3},{3,2},{4,5},{5,4},{6,7},{7,6},{8,9},{9,8},{10,11... | collective-permute-start | bytes 4718600 | tf_op jit(solution)/shard_map/ppermute | solution.py:23
  322.9 52.1 %collective-permute-start.31 = (bf16[1024,256]{1,0:T(8,128)(2,1)}, bf16[1024,256]{1,0:T(8,128)(2,1)}, u32[]{:S(2)}, u32[]{:S(2)}) collective-permute-start(bf16[1024,256]{1,0:T(8,128)(2,1)} %bitcast.486), channel_id=1, source_target_pairs={{0,1},{1,0},{2,3},{3,2},{4,5},{5,4},{6,7},{7,6},{8,9},{9,8},{10,11... | collective-permute-start | bytes 1572872 | tf_op jit(solution)/shard_map/ppermute | solution.py:23
  326.1 123.5 %all-to-all-start.6 = ((bf16[16,256,128]{2,1,0:T(8,128)(2,1)}), bf16[16,256,128]{2,1,0:T(8,128)(2,1)}, u32[]{:S(2)}, u32[]{:S(2)}) async-start(bf16[16,256,128]{2,1,0:T(8,128)(2,1)} %bitcast_bitcast_fusion), calls=%async_computation.6 | async-start | bytes 2097152 | tf_op jit(solution)/shard_map/all_to_all | solution.py:352
  344.6 22.0 %collective-permute-start.29 = (f32[2,512]{1,0:T(2,128)S(1)}, f32[2,512]{1,0:T(2,128)S(1)}, u32[]{:S(2)}, u32[]{:S(2)}) collective-permute-start(f32[2,512]{1,0:T(2,128)S(1)} %get-tuple-element.178), channel_id=1, source_target_pairs={{0,2},{2,0},{4,6},{6,4},{8,10},{10,8},{12,14},{14,12},{16,18},{18,... | collective-permute-start | bytes 12296 | tf_op jit(solution)/shard_map/ppermute | solution.py:28
  366.6 2.7 collective-permute-start.30
  386.3 13.7 %collective-permute-start.32 = (bf16[512,512]{0,1:T(8,128)(2,1)S(1)}, bf16[512,512]{0,1:T(8,128)(2,1)S(1)}, u32[]{:S(2)}, u32[]{:S(2)}) collective-permute-start(bf16[512,512]{0,1:T(8,128)(2,1)S(1)} %get-tuple-element.106), channel_id=1, source_target_pairs={{0,2},{2,0},{4,6},{6,4},{8,10},{10,8},{12,14},{14,12},{16,18},{18,... | collective-permute-start | bytes 1572872 | tf_op jit(solution)/shard_map/ppermute | solution.py:28
  390.6 53.4 %collective-permute-start.16 = (bf16[2,4,32,2048]{3,2,1,0:T(8,128)(2,1)}, bf16[2,4,32,2048]{3,2,1,0:T(8,128)(2,1)}, u32[]{:S(2)}, u32[]{:S(2)}) collective-permute-start(bf16[2,4,32,2048]{3,2,1,0:T(8,128)(2,1)} %bitcast.83), channel_id=1, source_target_pairs={{0,4},{2,6},{4,0},{6,2},{8,12},{10,14},{12,8},{14,10},{16,20},{18,... | collective-permute-start | bytes 3145736 | tf_op jit(solution)/shard_map/ppermute | solution.py:28
  391.8 55.0 %collective-permute-start.14 = (bf16[2,4,32,2048]{3,2,1,0:T(8,128)(2,1)}, bf16[2,4,32,2048]{3,2,1,0:T(8,128)(2,1)}, u32[]{:S(2)}, u32[]{:S(2)}) collective-permute-start(bf16[2,4,32,2048]{3,2,1,0:T(8,128)(2,1)} %bitcast.79), channel_id=1, source_target_pairs={{0,2},{2,0},{4,6},{6,4},{8,10},{10,8},{12,14},{14,12},{16,18},{18,... | collective-permute-start | bytes 3145736 | tf_op jit(solution)/shard_map/ppermute | solution.py:28
  427.4 84.4 %collective-permute-start.41 = (bf16[16,256,128]{2,1,0:T(8,128)(2,1)}, bf16[16,256,128]{2,1,0:T(8,128)(2,1)}, u32[]{:S(2)}, u32[]{:S(2)}) collective-permute-start(bf16[16,256,128]{2,1,0:T(8,128)(2,1)} %fusion.59), channel_id=1, source_target_pairs={{0,1},{1,0},{2,3},{3,2},{4,5},{5,4},{6,7},{7,6},{8,9},{9,8},{10,11... | collective-permute-start | bytes 3145736 | tf_op jit(solution)/shard_map/ppermute | solution.py:23
  436.4 4.1 collective-permute-start.43
  439.3 48.2 %collective-permute-start.35 = (bf16[2,4,32,2048]{3,2,1,0:T(8,128)(2,1)}, bf16[2,4,32,2048]{3,2,1,0:T(8,128)(2,1)}, u32[]{:S(2)}, u32[]{:S(2)}) collective-permute-start(bf16[2,4,32,2048]{3,2,1,0:T(8,128)(2,1)} %bitcast.152), channel_id=1, source_target_pairs={{0,4},{2,6},{4,0},{6,2},{8,12},{10,14},{12,8},{14,10},{16,20},{18,... | collective-permute-start | bytes 3145736 | tf_op jit(solution)/shard_map/ppermute | solution.py:28
  440.5 50.1 %collective-permute-start.33 = (bf16[2,4,32,2048]{3,2,1,0:T(8,128)(2,1)}, bf16[2,4,32,2048]{3,2,1,0:T(8,128)(2,1)}, u32[]{:S(2)}, u32[]{:S(2)}) collective-permute-start(bf16[2,4,32,2048]{3,2,1,0:T(8,128)(2,1)} %bitcast.148), channel_id=1, source_target_pairs={{0,2},{2,0},{4,6},{6,4},{8,10},{10,8},{12,14},{14,12},{16,18},{18,... | collective-permute-start | bytes 3145736 | tf_op jit(solution)/shard_map/ppermute | solution.py:28
  444.0 128.5 %copy-start.85 = (f32[16,8]{0,1:T(8,128)}, f32[16,8]{0,1:T(8,128)S(1)}, u32[]{:S(2)}) copy-start(f32[16,8]{0,1:T(8,128)S(1)} %copy.293) | copy-start | bytes 1540
  446.5 38.4 %collective-permute-start.17 = (bf16[4,32,2048]{2,1,0:T(8,128)(2,1)}, bf16[4,32,2048]{2,1,0:T(8,128)(2,1)}, u32[]{:S(2)}, u32[]{:S(2)}) collective-permute-start(bf16[4,32,2048]{2,1,0:T(8,128)(2,1)} %slice_bitcast_fusion.5), channel_id=1, source_target_pairs={{0,2},{2,0},{4,6},{6,4},{8,10},{10,8},{12,14},{14,12},{16,18},{18,... | collective-permute-start | bytes 1572872 | tf_op jit(solution)/shard_map/ppermute | solution.py:28
  449.3 36.8 %collective-permute-start.15 = (bf16[4,32,2048]{2,1,0:T(8,128)(2,1)}, bf16[4,32,2048]{2,1,0:T(8,128)(2,1)}, u32[]{:S(2)}, u32[]{:S(2)}) collective-permute-start(bf16[4,32,2048]{2,1,0:T(8,128)(2,1)} %slice_bitcast_fusion.7), channel_id=1, source_target_pairs={{0,4},{2,6},{4,0},{6,2},{8,12},{10,14},{12,8},{14,10},{16,20},{18,... | collective-permute-start | bytes 1572872 | tf_op jit(solution)/shard_map/ppermute | solution.py:28
  449.6 57.7 %all-to-all-start.5 = ((bf16[16,128,256]{2,1,0:T(8,128)(2,1)}), bf16[16,128,256]{2,1,0:T(8,128)(2,1)}, u32[]{:S(2)}, u32[]{:S(2)}) async-start(bf16[16,128,256]{2,1,0:T(8,128)(2,1)} %bitcast.181), calls=%async_computation.5 | async-start | bytes 2097152 | tf_op jit(solution)/shard_map/all_to_all | solution.py:354
  458.6 28.9 %copy-start.36 = (bf16[256,2048]{1,0:T(8,128)(2,1)S(1)}, bf16[256,2048]{1,0:T(8,128)(2,1)}, u32[]{:S(2)}) copy-start(bf16[256,2048]{1,0:T(8,128)(2,1)} %get-tuple-element.82) | copy-start | bytes 3145732
  489.4 11.8 %collective-permute-start.36 = (bf16[4,32,2048]{2,1,0:T(8,128)(2,1)S(1)}, bf16[4,32,2048]{2,1,0:T(8,128)(2,1)S(1)}, u32[]{:S(2)}, u32[]{:S(2)}) collective-permute-start(bf16[4,32,2048]{2,1,0:T(8,128)(2,1)S(1)} %slice_bitcast_fusion), channel_id=1, source_target_pairs={{0,2},{2,0},{4,6},{6,4},{8,10},{10,8},{12,14},{14,12},{16,18},{18,... | collective-permute-start | bytes 1572872 | tf_op jit(solution)/shard_map/ppermute | solution.py:28
  492.2 11.5 %collective-permute-start.34 = (bf16[4,32,2048]{2,1,0:T(8,128)(2,1)S(1)}, bf16[4,32,2048]{2,1,0:T(8,128)(2,1)S(1)}, u32[]{:S(2)}, u32[]{:S(2)}) collective-permute-start(bf16[4,32,2048]{2,1,0:T(8,128)(2,1)S(1)} %slice_bitcast_fusion.2), channel_id=1, source_target_pairs={{0,4},{2,6},{4,0},{6,2},{8,12},{10,14},{12,8},{14,10},{16,20},{18,... | collective-permute-start | bytes 1572872 | tf_op jit(solution)/shard_map/ppermute | solution.py:28
  493.5 50.3 %collective-permute-start.18 = (bf16[64,2048]{1,0:T(8,128)(2,1)}, bf16[64,2048]{1,0:T(8,128)(2,1)}, u32[]{:S(2)}, u32[]{:S(2)}) collective-permute-start(bf16[64,2048]{1,0:T(8,128)(2,1)} %get-tuple-element.115), channel_id=1, source_target_pairs={{0,8},{2,10},{4,12},{6,14},{8,0},{10,2},{12,4},{14,6},{16,24},{18,... | collective-permute-start | bytes 786440 | tf_op jit(solution)/shard_map/ppermute | solution.py:28
  493.8 50.1 %collective-permute-start.19 = (bf16[64,2048]{1,0:T(8,128)(2,1)}, bf16[64,2048]{1,0:T(8,128)(2,1)}, u32[]{:S(2)}, u32[]{:S(2)}) collective-permute-start(bf16[64,2048]{1,0:T(8,128)(2,1)} %get-tuple-element.117), channel_id=1, source_target_pairs={{0,16},{2,18},{4,20},{6,22},{8,24},{10,26},{12,28},{14,30},{16,0},... | collective-permute-start | bytes 786440 | tf_op jit(solution)/shard_map/ppermute | solution.py:28
  504.9 10.8 %collective-permute-start.37 = (bf16[64,2048]{1,0:T(8,128)(2,1)}, bf16[64,2048]{1,0:T(8,128)(2,1)S(1)}, u32[]{:S(2)}, u32[]{:S(2)}) collective-permute-start(bf16[64,2048]{1,0:T(8,128)(2,1)} %get-tuple-element.100), channel_id=1, source_target_pairs={{0,8},{2,10},{4,12},{6,14},{8,0},{10,2},{12,4},{14,6},{16,24},{18,... | collective-permute-start | bytes 786440 | tf_op jit(solution)/shard_map/ppermute | solution.py:28
  505.2 21.3 %collective-permute-start.38 = (bf16[64,2048]{1,0:T(8,128)(2,1)}, bf16[64,2048]{1,0:T(8,128)(2,1)}, u32[]{:S(2)}, u32[]{:S(2)}) collective-permute-start(bf16[64,2048]{1,0:T(8,128)(2,1)} %get-tuple-element.102), channel_id=1, source_target_pairs={{0,16},{2,18},{4,20},{6,22},{8,24},{10,26},{12,28},{14,30},{16,0},... | collective-permute-start | bytes 786440 | tf_op jit(solution)/shard_map/ppermute | solution.py:28
  507.3 12.0 %all-to-all-start.4 = ((f32[16,1,960]{2,1,0:T(1,128)}), f32[16,1,960]{2,1,0:T(1,128)S(1)}, u32[]{:S(2)}, u32[]{:S(2)}) async-start(f32[16,1,960]{2,1,0:T(1,128)} %all_to_all.28), calls=%async_computation.4 | async-start | bytes 131072 | tf_op jit(solution)/shard_map/all_to_all | solution.py:436
  511.8 30.5 %collective-permute-start.39 = (bf16[64,2048]{1,0:T(8,128)(2,1)}, bf16[64,2048]{1,0:T(8,128)(2,1)}, u32[]{:S(2)}, u32[]{:S(2)}) collective-permute-start(bf16[64,2048]{1,0:T(8,128)(2,1)} %get-tuple-element.101), channel_id=1, source_target_pairs={{0,24},{2,26},{4,28},{6,30},{8,16},{10,18},{12,20},{14,22},{16,8},... | collective-permute-start | bytes 786440 | tf_op jit(solution)/shard_map/ppermute | solution.py:28
  515.7 26.6 %copy-start.25 = (bf16[4,32,2048]{2,1,0:T(8,128)(2,1)S(1)}, bf16[4,32,2048]{2,1,0:T(8,128)(2,1)}, u32[]{:S(2)}) copy-start(bf16[4,32,2048]{2,1,0:T(8,128)(2,1)} %copy-done.24) | copy-start | bytes 1572868
  515.7 26.6 %copy-start.90 = (f32[64]{0:T(128)S(1)}, f32[64]{0:T(128)}, u32[]{:S(2)}) copy-start(f32[64]{0:T(128)} %copy-done.89) | copy-start | bytes 772
  515.7 26.6 %copy-start.94 = (f32[64]{0:T(128)S(1)}, f32[64]{0:T(128)}, u32[]{:S(2)}) copy-start(f32[64]{0:T(128)} %add_rsqrt_fusion.1) | copy-start | bytes 772
  515.8 32.2 %copy-start.19 = (bf16[4,32,2048]{2,1,0:T(8,128)(2,1)S(1)}, bf16[4,32,2048]{2,1,0:T(8,128)(2,1)}, u32[]{:S(2)}) copy-start(bf16[4,32,2048]{2,1,0:T(8,128)(2,1)} %copy-done.18) | copy-start | bytes 1572868
  515.8 32.2 %copy-start.21 = (bf16[4,32,2048]{2,1,0:T(8,128)(2,1)S(1)}, bf16[4,32,2048]{2,1,0:T(8,128)(2,1)}, u32[]{:S(2)}) copy-start(bf16[4,32,2048]{2,1,0:T(8,128)(2,1)} %copy-done.20) | copy-start | bytes 1572868
  515.8 32.2 %collective-permute-start.20 = (bf16[64,2048]{1,0:T(8,128)(2,1)}, bf16[64,2048]{1,0:T(8,128)(2,1)}, u32[]{:S(2)}, u32[]{:S(2)}) collective-permute-start(bf16[64,2048]{1,0:T(8,128)(2,1)} %get-tuple-element.116), channel_id=1, source_target_pairs={{0,24},{2,26},{4,28},{6,30},{8,16},{10,18},{12,20},{14,22},{16,8},... | collective-permute-start | bytes 786440 | tf_op jit(solution)/shard_map/ppermute | solution.py:28
  519.3 44.8 %all-to-all-start.3 = ((bf16[16,256,128]{2,1,0:T(8,128)(2,1)}), bf16[16,256,128]{2,1,0:T(8,128)(2,1)S(1)}, u32[]{:S(2)}, u32[]{:S(2)}) async-start(bf16[16,256,128]{2,1,0:T(8,128)(2,1)} %fusion.28), calls=%async_computation.3 | async-start | bytes 2097152 | tf_op jit(solution)/shard_map/all_to_all | solution.py:381
  549.5 12.5 %collective-permute-start.40 = (bf16[64,2048]{1,0:T(8,128)(2,1)S(1)}, bf16[64,2048]{1,0:T(8,128)(2,1)S(1)}, u32[]{:S(2)}, u32[]{:S(2)}) collective-permute-start(bf16[64,2048]{1,0:T(8,128)(2,1)S(1)} %get-tuple-element.150), channel_id=1, source_target_pairs={{0,1},{1,0},{2,3},{3,2},{4,5},{5,4},{6,7},{7,6},{8,9},{9,8},{10,11... | collective-permute-start | bytes 786440 | tf_op jit(solution)/shard_map/ppermute | solution.py:23
  562.0 5.3 collective-permute-start.21
  564.2 4.8 collective-permute-start.42
  (94 other events, 542.2 us)

commit v2 on v1

--- a/solution.py
+++ b/solution.py
@@ -3,6 +3,8 @@
 import jax
 import jax.numpy as jnp
 from jax import lax
+from jax.experimental import pallas as pl
+from jax.experimental.pallas import tpu as pltpu
 from jax.sharding import PartitionSpec as P
 
 HEADS = 8
@@ -59,7 +61,7 @@
     )
 
 
-def body(
+def general_body(
     tokens,
     w_qkv,
     b_qkv,
@@ -271,7 +273,8 @@
     mine = jnp.concatenate([queries, keys, linear[:, 2]], axis=1).astype(BF)
 
     def align(value, r):
-        return value.reshape((size_x, -1) + value.shape[1:])[jnp.arange(size_x) ^ r].reshape(value.shape)
+        slabs = value.reshape((size_x, -1) + value.shape[1:])
+        return jnp.stack([slabs[x ^ r] for x in range(size_x)]).reshape(value.shape)
 
     pieces = [mine] + [align(from_peer(mine, r), r) for r in masks_x]
     pieces = jnp.stack(pieces).reshape(group, count, 3, columns)
@@ -455,6 +458,719 @@
     )
 
 
+VMEM = pl.BlockSpec(memory_space=pltpu.VMEM)
+SMEM = pl.BlockSpec(memory_space=pltpu.SMEM)
+GRANT = 50 * 1024 * 1024
+MARK_COS, MARK_SIN = 32, 64
+
+
+def run_kernel(kernel, outs, grid=None, ins=None, out_specs=None, scratch=(), flops=0, moved=0):
+    outs = [jax.ShapeDtypeStruct(shape, kind) for shape, kind in outs]
+    single = len(outs) == 1
+    out_specs = out_specs or [VMEM] * len(outs)
+    extra = {} if grid is None else {"grid": grid}
+    return pl.pallas_call(
+        kernel,
+        out_shape=outs[0] if single else outs,
+        in_specs=ins,
+        out_specs=out_specs[0] if single else out_specs,
+        scratch_shapes=list(scratch),
+        compiler_params=pltpu.CompilerParams(vmem_limit_bytes=GRANT),
+        cost_estimate=pl.CostEstimate(flops=int(flops), bytes_accessed=int(moved), transcendentals=0),
+        **extra,
+    )
+
+
+def chunk_bits(half, at, lanes):
+    z = at % lanes
+    low, high = (at // lanes) % 2, at // (2 * lanes)
+    x, y = (high, low) if half == 0 else (low, high)
+    return x + 2 * y + 4 * z
+
+
+class Rows:
+    def __init__(self, blocks, cores, rows):
+        self.blocks, self.rows = blocks, rows
+        self.part = rows // cores
+        self.chunk = self.part // 2
+        self.half = blocks * self.chunk
+        self.count = 2 * self.half
+        self.share = self.half
+        self.sizes_z = blocks // 4
+
+    def natural(self, me, core, half, at):
+        block = me ^ chunk_bits(half, at, self.sizes_z)
+        return block * self.rows + core * self.part + half * self.chunk
+
+    def x_rows(self, x):
+        h, q = self.half // 2, self.half // 4
+        return [
+            (x * h, 0, h),
+            (self.half + x * q, h, q),
+            (self.half + 2 * q + x * q, h + q, q),
+        ]
+
+    def pairs(self):
+        mine, peer = self.x_rows(0), self.x_rows(1)
+        both = [(a[0], b[0], a[2]) for a, b in zip(mine, peer)]
+        return both + [(b, a, n) for a, b, n in both]
+
+
+def nn(left, right):
+    return lax.dot_general(left, right, (((1,), (0,)), ((), ())), preferred_element_type=F32)
+
+
+def nt(left, right):
+    return lax.dot_general(left, right, (((1,), (1,)), ((), ())), preferred_element_type=F32)
+
+
+def lane_of(shape):
+    return lax.broadcasted_iota(jnp.int32, shape, len(shape) - 1)
+
+
+def turn_lanes(values, table, active, sign):
+    lane = lane_of(values.shape)
+    first, second = lane < ROT // 2, lane < ROT
+    to_first = 128 - MARK_COS
+    cosine = jnp.where(first, pltpu.roll(table, to_first, 1), table)
+    sine_first = pltpu.roll(table, 128 - MARK_SIN, 1)
+    sine_second = pltpu.roll(table, 128 - MARK_SIN + ROT // 2, 1)
+    sine = jnp.where(first, -sine_first, sine_second) * sign
+    cosine = jnp.where(second & active, cosine, 1.0)
+    sine = jnp.where(second & active, sine, 0.0)
+    partner = jnp.where(first, pltpu.roll(values, 128 - ROT // 2, 1), pltpu.roll(values, ROT // 2, 1))
+    return values * cosine + partner * sine
+
+
+def deal_kernel(cut, blocks, ids, here, there, triple, near):
+    core = ids[1]
+    for source in range(blocks):
+        for who, ref in ((core, here), (1 - core, there)):
+            at = pl.multiple_of(source * 2 * cut + who * cut, cut)
+            for s in range(3):
+                triple[pl.ds(at, cut), s * 128 : (s + 1) * 128] = ref[source, s * cut : (s + 1) * cut, :]
+            at = pl.multiple_of(who * cut, cut)
+            near[pl.ds(at, cut), source * 128 : (source + 1) * 128] = ref[source, 3 * cut : 4 * cut, :]
+
+
+def shrink_kernel(blocks, units, mine, other, out):
+    for source in range(blocks):
+        out[:units, source * 128 : (source + 1) * 128] = mine[source]
+        out[units:, source * 128 : (source + 1) * 128] = other[source]
+
+
+def norm_kernel(r, ids, t0, t1, t2, t3, norms, weight, bias, marks, attend, feed, normal, mine, tile, table):
+    i = pl.program_id(0)
+    me, core = ids[0], ids[1]
+    for k, ref in enumerate((t0, t1, t2, t3)):
+
+        @pl.when(i == k)
+        def _(ref=ref):
+            tile[...] = ref[...]
+
+    for half in (0, 1):
+
+        @pl.when(i // 2 == half)
+        def _(half=half):
+            for q in range(8):
+                at = r.natural(me, core, half, (i % 2) * 8 + q)
+                table[q * r.chunk : (q + 1) * r.chunk, :] = marks[pl.ds(pl.multiple_of(at, r.chunk), r.chunk), :]
+
+    step = 16
+
+    @pl.loop(0, tile.shape[0] // step)
+    def _(j):
+        rows = pl.ds(pl.multiple_of(j * step, step), step)
+        values = tile[rows, :].astype(F32)
+        center = values - jnp.mean(values, axis=-1, keepdims=True)
+        spread = jnp.mean(center * center, axis=-1, keepdims=True)
+        value = center * lax.rsqrt(spread + EPSILON)
+        normal[rows, :] = value.astype(BF)
+        attend[rows, :] = (value * norms[0:1, :] + norms[2:3, :]).astype(BF)
+        feed[rows, :] = (value * norms[1:2, :] + norms[3:4, :]).astype(BF)
+
+    linear = nn(attend[...], weight[...]) + bias[...]
+    active = me % 2 == 0
+    for s in (0, 1):
+        cols = slice(s * 128, (s + 1) * 128)
+        mine[:, cols] = turn_lanes(linear[:, cols], table[...], active, 1.0).astype(BF)
+    mine[:, 256:] = linear[:, 256:].astype(BF)
+
+
+def cotangent_kernel(t0, t1, t2, t3, near, peer, whole, grads, sums):
+    i = pl.program_id(0)
+    for k, ref in enumerate((t0, t1, t2, t3)):
+
+        @pl.when(i == k)
+        def _(ref=ref):
+            whole[...] = ref[...]
+
+    grads[:, :128] = nt(whole[...], near[...]).astype(BF)
+    grads[:, 128:] = nt(whole[...], peer[...]).astype(BF)
+
+    @pl.when(i == 0)
+    def _():
+        sums[...] = jnp.zeros_like(sums)
+
+    sums[0:1, :] += jnp.sum(whole[...].astype(F32), axis=0, keepdims=True)
+
+
+def gather_columns(r, out, low, high, column):
+    cols = slice(column * 128, (column + 1) * 128)
+    out[:, :128] = low[:, cols]
+    for here, there, size in r.pairs():
+        out[here : here + size, 128:] = high[there : there + size, cols]
+
+
+def gather_marks(r, ids, marks, table, line):
+    me, core = ids[0], ids[1]
+    for w in (0, 1):
+        who = core if w == 0 else 1 - core
+        for half in (0, 1):
+            for q in range(16):
+                at = r.natural(me, who, half, q)
+                to = w * r.count + half * r.half + q * r.chunk
+                table[to : to + r.chunk, :] = marks[pl.ds(pl.multiple_of(at, r.chunk), r.chunk), :]
+    for b in range(2 * r.count // 128):
+        line[:, b * 128 : (b + 1) * 128] = table[b * 128 : (b + 1) * 128, :].T[:8, :]
+
+
+def own_rows(r, out, ref, columns=slice(None)):
+    for row, place, size in r.x_rows(0):
+        out[place : place + size, :] = ref[row : row + size, columns]
+
+
+def query_kernel(r, scale, ids, a00, a01, a10, a11, grads, marks, attended, keep, send, lines,
+                 keys, values, queries, pushes, table, line, mine):
+    i = pl.program_id(0)
+    me = ids[0]
+    count, tile = r.count, r.share // 2
+
+    @pl.when(i == 0)
+    def _():
+        gather_columns(r, keys.at[:count], a00, a01, 1)
+        gather_columns(r, keys.at[count:], a10, a11, 1)
+        gather_columns(r, values.at[:count], a00, a01, 2)
+        gather_columns(r, values.at[count:], a10, a11, 2)
+        for row, place, size in r.x_rows(0):
+            queries[place : place + size, :128] = a00[row : row + size, :128]
+        for (row, place, size), (there, _, _) in zip(r.x_rows(0), r.x_rows(1)):
+            queries[place : place + size, 128:] = a01[there : there + size, :128]
+        own_rows(r, pushes, grads)
+        gather_marks(r, ids, marks, table, line)
+        own_rows(r, mine, table.at[:count])
+
+    rows = pl.ds(pl.multiple_of(i * tile, tile), tile)
+    mark = mine[rows, :]
+    q_at, q_start = mark[:, 0:1], mark[:, 2:3]
+    k_at, k_live = line[0:1, :], line[1:2, :]
+    mask = ((k_live >= q_start) & (k_at <= q_at)) | (k_at == q_at)
+    scores = jnp.where(mask, nt(queries[rows, :], keys[...]) * scale, NEGATIVE)
+    top = jnp.max(scores, axis=-1, keepdims=True)
+    weight = jnp.where(mask, jnp.exp(scores - top), 0.0)
+    total = jnp.sum(weight, axis=-1, keepdims=True)
+    prob = weight * (1.0 / total)
+    result = nn(prob.astype(BF), values[...])
+    grad = pushes[rows, :]
+    delta = jnp.sum(grad.astype(F32) * result, axis=-1, keepdims=True)
+    slope = (prob * (nt(grad, values[...]) - delta)).astype(BF)
+    back = nn(slope, keys[...]) * scale
+    result = result.astype(BF)
+    attended[...] = result
+    for k, ref in enumerate((keep, send)):
+        cols = slice(k * 128, (k + 1) * 128)
+        ref[:, :128] = turn_lanes(back[:, cols], mark, me % 2 == k, -1.0).astype(BF)
+        ref[:, 128:] = result[:, cols]
+    lane = lane_of((tile, 128))
+    both = jnp.where(lane == 0, top + jnp.log(total), jnp.where(lane == 1, delta, 0.0))
+    for b in range(tile // 128):
+        lines[:, b * 128 : (b + 1) * 128] = both[b * 128 : (b + 1) * 128, :].T[:8, :]
+
+
+def key_kernel(r, scale, ids, a00, a01, a10, a11, grads, other_grads, l00, l01, l10, l11, marks, keep, send,
+               queries, pushes, keys, values, table, line, mine, tops):
+    i = pl.program_id(0)
+    me = ids[0]
+    count, tile = r.count, r.share // 2
+
+    @pl.when(i == 0)
+    def _():
+        gather_columns(r, queries.at[:count], a00, a01, 0)
+        gather_columns(r, queries.at[count:], a10, a11, 0)
+        pushes[:count, :] = grads[...]
+        pushes[count:, :] = other_grads[...]
+        for k, out in ((1, keys), (2, values)):
+            cols = slice(k * 128, (k + 1) * 128)
+            for row, place, size in r.x_rows(0):
+                out[place : place + size, :128] = a00[row : row + size, cols]
+            for (row, place, size), (there, _, _) in zip(r.x_rows(0), r.x_rows(1)):
+                out[place : place + size, 128:] = a01[there : there + size, cols]
+        gather_marks(r, ids, marks, table, line)
+        own_rows(r, mine, table.at[:count])
+        for base, low, high in ((0, l00, l01), (count, l10, l11)):
+            for x, ref in ((0, low), (1, high)):
+                for row, place, size in r.x_rows(x):
+                    tops[:, base + row : base + row + size] = ref[:, place : place + size]
+
+    rows = pl.ds(pl.multiple_of(i * tile, tile), tile)
+    mark = mine[rows, :]
+    k_at, k_live = mark[:, 0:1], mark[:, 1:2]
+    q_at, q_start = line[0:1, :], line[2:3, :]
+    mask = ((k_live >= q_start) & (k_at <= q_at)) | (k_at == q_at)
+    scores = nt(keys[rows, :], queries[...]) * scale
+    prob = jnp.where(mask, jnp.exp(scores - tops[0:1, :]), 0.0)
+    grad_values = nn(prob.astype(BF), pushes[...])
+    slope = (prob * (nt(values[rows, :], pushes[...]) - tops[1:2, :])).astype(BF)
+    back = nn(slope, queries[...]) * scale
+    for k, ref in enumerate((keep, send)):
+        cols = slice(k * 128, (k + 1) * 128)
+        ref[:, :128] = turn_lanes(back[:, cols], mark, me % 2 == k, -1.0).astype(BF)
+        ref[:, 128:] = grad_values[:, cols].astype(BF)
+
+
+def feed_kernel(units, normed, cotangent, expand, shrink, bias, act0, act1, grad0, grad1, sums):
+    i = pl.program_id(0)
+    expanded = nn(normed[...], expand[...]) + bias[...]
+    activated, bend = gelu_and_slope(expanded)
+    activated = activated.astype(BF)
+    act0[...] = activated[:, :units]
+    act1[...] = activated[:, units:]
+    grad = (bend * nt(cotangent[...], shrink[...])).astype(BF)
+    grad0[...] = grad[:, :units]
+    grad1[...] = grad[:, units:]
+
+    @pl.when(i == 0)
+    def _():
+        sums[...] = jnp.zeros_like(sums)
+
+    sums[0:1, :] += jnp.sum(grad.astype(F32), axis=0, keepdims=True)
+
+
+def branch_kernel(r, act0, act1, attended, shrink, near, peer, o0, o1, o2, o3, rows):
+    i = pl.program_id(0)
+    units = act0.shape[1]
+
+    @pl.when(i == 0)
+    def _():
+        rows[...] = jnp.zeros_like(rows)
+        for row, place, size in r.x_rows(0):
+            rows[row : row + size, :] = attended[place : place + size, :]
+
+    tile = act0.shape[0]
+    here = pl.ds(pl.multiple_of(i * tile, tile), tile)
+    result = nn(act0[...], shrink[:units, :]) + nn(act1[...], shrink[units:, :])
+    result = result + nn(rows[here, :128], near[...]) + nn(rows[here, 128:], peer[...])
+    result = result.astype(BF)
+    for k, ref in enumerate((o0, o1, o2, o3)):
+
+        @pl.when(i == k)
+        def _(ref=ref):
+            ref[...] = result
+
+
+def inputs_kernel(r, keep1, keep2, got1, got2, grad0, grad1, normal, triple, expand, gains,
+                  o0, o1, o2, o3, linear, near, sums, line_sums, rows):
+    i = pl.program_id(0)
+    units = grad0.shape[1]
+    tile = grad0.shape[0]
+
+    @pl.when(i == 0)
+    def _():
+        sums[...] = jnp.zeros_like(sums)
+        line_sums[...] = jnp.zeros_like(line_sums)
+        for x, one, two in ((0, keep1, keep2), (1, got1, got2)):
+            for row, place, size in r.x_rows(x):
+                rows[row : row + size, :128] = one[place : place + size, :128]
+                rows[row : row + size, 128:384] = two[place : place + size, :]
+                near[row : row + size, :] = one[place : place + size, 128:]
+
+    here = pl.ds(pl.multiple_of(i * tile, tile), tile)
+    line = rows[here, :]
+    linear[...] = line
+    line_sums[0:1, :] += jnp.sum(line.astype(F32), axis=0, keepdims=True)
+    wide = 256
+    for j in range(normal.shape[1] // wide):
+        cols = slice(j * wide, (j + 1) * wide)
+        attend = nt(line, triple[cols, :])
+        feed = nt(grad0[...], expand[cols, :units]) + nt(grad1[...], expand[cols, units:])
+        value = normal[:, cols].astype(F32)
+        sums[0:1, cols] += jnp.sum(value * attend, axis=0, keepdims=True)
+        sums[1:2, cols] += jnp.sum(value * feed, axis=0, keepdims=True)
+        sums[2:3, cols] += jnp.sum(attend, axis=0, keepdims=True)
+        sums[3:4, cols] += jnp.sum(feed, axis=0, keepdims=True)
+        both = (gains[0:1, cols] * attend + gains[1:2, cols] * feed).astype(BF)
+        for k, ref in enumerate((o0, o1, o2, o3)):
+
+            @pl.when(i == k)
+            def _(ref=ref, cols=cols, both=both):
+                ref[:, cols] = both
+
+
+def pack_kernel(cut, blocks, ids, triple, outward, keep, give):
+    core = ids[1]
+    for b in range(blocks):
+        for who, out in ((core, keep), (1 - core, give)):
+            at = pl.multiple_of(b * 2 * cut + who * cut, cut)
+            for s in range(3):
+                out[b, s * cut : (s + 1) * cut, :] = triple[pl.ds(at, cut), s * 128 : (s + 1) * 128].astype(out.dtype)
+            at = pl.multiple_of(who * cut, cut)
+            out[b, 3 * cut :, :] = outward[pl.ds(at, cut), b * 128 : (b + 1) * 128].astype(out.dtype)
+
+
+def unpack_kernel(cut, heads, ids, mine, other, triple, outward):
+    core = ids[1]
+    for who, ref in ((core, mine), (1 - core, other)):
+        at = pl.multiple_of(who * cut, cut)
+        for k in range(heads):
+            for s in range(3):
+                triple[s, pl.ds(at, cut), k * 128 : (k + 1) * 128] = ref[k, s * cut : (s + 1) * cut, :].astype(F32)
+            to = pl.multiple_of(k * 2 * cut + who * cut, cut)
+            outward[pl.ds(to, cut), :] = ref[k, 3 * cut :, :].astype(F32)
+
+
+def body(
+    tokens,
+    w_qkv,
+    b_qkv,
+    w_out,
+    b_out,
+    w_in,
+    b_in,
+    w_out2,
+    b_out2,
+    norm_gain,
+    norm_shift,
+    doc_start,
+    live,
+    cotangent,
+):
+    blocks = lax.axis_size("blk")
+    cores = lax.axis_size("tp")
+    me, core = lax.axis_index("blk"), lax.axis_index("tp")
+    ids = jnp.stack([me, core]).astype(jnp.int32)
+    rows, width = tokens.shape
+    depth = w_in.shape[0]
+    r = Rows(blocks, cores, rows)
+    part, count, share = r.part, r.count, r.share
+    quarter = count // 4
+    units = w_in.shape[1] // blocks
+    cut = depth // cores
+    scale = 1.0 / math.sqrt(HEAD)
+    masks_z = [4 * i for i in range(1, blocks // 4)]
+
+    def gather(value):
+        over_z = spread(value, masks_z)
+        one, two = over_z[:, : r.chunk], over_z[:, r.chunk :]
+        one, two = spread(one, [2]), spread(two, [1])
+        return [
+            piece.reshape(quarter, width)
+            for piece in (one, from_peer(one, 1), two, from_peer(two, 2))
+        ]
+
+    def scatter(quarters):
+        def fold(keep, send, mask):
+            got = from_peer(send, mask).astype(F32)
+            half = keep.shape[0] // 2
+            keep = keep.astype(F32)
+            return (keep[:half] + got[:half]).astype(BF), (keep[half:] + got[half:]).astype(BF)
+
+        one = fold(quarters[0], quarters[1], 1)
+        two = fold(quarters[2], quarters[3], 2)
+        one = one[0].astype(F32) + from_peer(one[1], 2).astype(F32)
+        two = two[0].astype(F32) + from_peer(two[1], 1).astype(F32)
+        one = one.reshape(-1, r.chunk, width)
+        two = two.reshape(-1, r.chunk, width)
+        return collect([jnp.concatenate([a, b]).astype(BF) for a, b in zip(one, two)], masks_z)
+
+    my_tokens = lax.dynamic_slice_in_dim(tokens, core * part, part, 0)
+    my_cotangent = lax.dynamic_slice_in_dim(cotangent, core * part, part, 0)
+    all_tokens = gather(my_tokens)
+    all_cotangent = gather(my_cotangent)
+
+    lanes = norm_gain.shape[-1]
+    small = [norm_gain, norm_shift, b_out, b_out2, b_qkv, b_in]
+    sizes = [value.size // lanes for value in small]
+    small = jnp.concatenate([value.reshape(-1) for value in small])
+    start_high, start_low = doc_start // 256, doc_start % 256
+    places = jnp.stack([start_high, start_low, live]).astype(BF)
+    small = jnp.pad(small, (0, -small.size % 128)).reshape(-1, 128)
+    small_lines = small.shape[0]
+    small = jnp.concatenate([small, places])
+    small = jnp.pad(small, ((0, -small.shape[0] % 16), (0, 0)))
+
+    own_heads = HEADS // cores * 2
+    triple = w_qkv.reshape(3, cores, cut, own_heads, 128).transpose(1, 3, 0, 2, 4)
+    triple = triple.reshape(cores, own_heads, 3 * cut, 128)
+    outward = w_out.reshape(own_heads, cores, cut, 128).transpose(1, 0, 2, 3)
+    dealt = jnp.concatenate([triple, outward], axis=2)
+    keep = lax.dynamic_index_in_dim(dealt, core, 0, keepdims=False)
+    give = lax.dynamic_index_in_dim(dealt, 1 - core, 0, keepdims=False)
+    heads_low, heads_high = by_core(core, keep, swap_cores(give))
+    deal = jnp.concatenate(
+        [
+            jnp.concatenate([heads_low, heads_high]),
+            jnp.broadcast_to(small, (blocks,) + small.shape),
+        ],
+        axis=1,
+    )
+    here = lax.all_to_all(deal, "blk", 0, 0, tiled=True)
+    there = swap_cores(here)
+    w_triple, w_near = run_kernel(
+        lambda *refs: deal_kernel(cut, blocks, *refs),
+        [((width, 384), BF), ((128, width), BF)],
+        ins=[SMEM, VMEM, VMEM],
+        moved=5e6,
+    )(ids, here, there)
+    w_peer = from_peer(w_near, 1)
+
+    expand_deal = w_in.reshape(depth, blocks, units).transpose(1, 0, 2)
+    expand_mine = lax.all_to_all(expand_deal, "blk", 0, 0, tiled=True).reshape(width, units)
+    w_expand = jnp.concatenate([expand_mine, swap_cores(expand_mine)], axis=1)
+    shrink_mine = lax.all_to_all(w_out2.reshape(blocks, units, depth), "blk", 0, 0, tiled=True)
+    w_shrink = run_kernel(
+        lambda *refs: shrink_kernel(blocks, units, *refs),
+        [((2 * units, width), BF)],
+        ins=[VMEM, VMEM],
+        moved=4e6,
+    )(shrink_mine, swap_cores(shrink_mine))
+
+    tail = jnp.stack([here[:, 4 * cut :], there[:, 4 * cut :]])
+    places = tail[0, :, small_lines : small_lines + 3].astype(F32)
+    lines = sum(sizes)
+    tail = tail[:, :, :small_lines].reshape(2, blocks, -1)[:, :, : lines * lanes]
+    tail = tail.reshape(2, blocks, lines, lanes).transpose(0, 2, 1, 3).reshape(2, lines, 128).astype(F32)
+    ends = [sum(sizes[: k + 1]) for k in range(len(sizes))]
+    norms = tail[0, : ends[1]].reshape(4, width)
+    residual_shift = (tail[0, ends[1] : ends[2]] + tail[0, ends[2] : ends[3]]).reshape(1, width)
+    triple_lines = tail[:, ends[3] : ends[4]].reshape(2, 3, own_heads, 128)
+    triple_lines = jnp.where(me // own_heads == core, triple_lines[0], triple_lines[1])
+    triple_shift = lax.dynamic_index_in_dim(triple_lines, me % own_heads, 1, keepdims=False).reshape(1, 384)
+    expand_lines = lax.dynamic_slice_in_dim(tail[:, ends[4] :], me * (units // 128), units // 128, 1)
+    expand_shift = expand_lines.reshape(1, 2 * units)
+
+    start = (places[:, 0] * 256.0 + places[:, 1]).reshape(-1, 1)
+    is_live = places[:, 2].reshape(-1, 1)
+    index = lax.broadcasted_iota(F32, start.shape, 0)
+    steps = jnp.arange(ROT // 2, dtype=F32)
+    angle = (index - start) * (10000.0 ** (-2.0 * steps / ROT))[None, :]
+    marks = jnp.concatenate(
+        [
+            index,
+            jnp.where(is_live == 1.0, index, -1.0),
+            start,
+            jnp.zeros((start.shape[0], MARK_COS - 3), F32),
+            jnp.cos(angle),
+            jnp.sin(angle),
+            jnp.zeros((start.shape[0], 128 - MARK_SIN - ROT // 2), F32),
+        ],
+        axis=1,
+    )
+
+    def tiled(columns):
+        return pl.BlockSpec((quarter, columns), lambda i: (i, 0))
+
+    def fixed(value):
+        return pl.BlockSpec(value.shape, lambda i: (0,) * value.ndim)
+
+    def fixed_shape(*shape):
+        return pl.BlockSpec(shape, lambda i: (0,) * len(shape))
+
+    normed_attend, normed_feed, normal, mine = run_kernel(
+        lambda *refs: norm_kernel(r, *refs),
+        [((count, width), BF)] * 3 + [((count, 384), BF)],
+        grid=(4,),
+        ins=[SMEM] + [fixed(t) for t in all_tokens] + [fixed(norms), fixed(w_triple), fixed(triple_shift), fixed(marks)],
+        out_specs=[tiled(width)] * 3 + [tiled(384)],
+        scratch=[pltpu.VMEM((quarter, width), BF), pltpu.VMEM((quarter, 128), F32)],
+        flops=2 * count * width * 384,
+        moved=22e6,
+    )(ids, *all_tokens, norms, w_triple, triple_shift, marks)
+    peer = from_peer(mine, 1)
+    mine_there = swap_cores(mine)
+    peer_there = swap_cores(peer)
+
+    whole_cotangent, grads, cotangent_sums = run_kernel(
+        cotangent_kernel,
+        [((count, width), BF), ((count, 256), BF), ((8, width), F32)],
+        grid=(4,),
+        ins=[fixed(t) for t in all_cotangent] + [fixed(w_near), fixed(w_peer)],
+        out_specs=[tiled(width), tiled(256), fixed_shape(8, width)],
+        flops=2 * count * width * 256,
+        moved=11e6,
+    )(*all_cotangent, w_near, w_peer)
+    grads_there = swap_cores(grads)
+
+    act0, act1, grad0, grad1, unit_sums = run_kernel(
+        lambda *refs: feed_kernel(units, *refs),
+        [((count, units), BF)] * 4 + [((8, 2 * units), F32)],
+        grid=(4,),
+        ins=[tiled(width), tiled(width), fixed(w_expand), fixed(w_shrink), fixed(expand_shift)],
+        out_specs=[tiled(units)] * 4 + [fixed_shape(8, 2 * units)],
+        flops=8 * count * width * units,
+        moved=14e6,
+    )(normed_feed, whole_cotangent, w_expand, w_shrink, expand_shift)
+
+    tokens_first = ((0,), (0,))
+    shrink_there = swap_cores(dot(act1, whole_cotangent, tokens_first).astype(BF))
+    expand_there = swap_cores(dot(normed_feed, grad1, tokens_first).astype(BF))
+    grad_shrink = (dot(act0, whole_cotangent, tokens_first) + shrink_there.astype(F32)).astype(BF)
+    grad_expand = (dot(normed_feed, grad0, tokens_first) + expand_there.astype(F32)).astype(BF)
+    shrink_deal = grad_shrink.reshape(units, blocks, depth).transpose(1, 0, 2)
+    expand_deal = grad_expand.reshape(blocks, depth, units)
+    shrink_grad = lax.all_to_all(shrink_deal, "blk", 0, 0, tiled=True)
+    shrink_grad = shrink_grad.reshape(-1, depth).astype(F32)
+    expand_grad = lax.all_to_all(expand_deal, "blk", 0, 0, tiled=True)
+    expand_grad = expand_grad.transpose(1, 0, 2).reshape(depth, -1).astype(F32)
+
+    tile = share // 2
+    half_tile = lambda columns: pl.BlockSpec((tile, columns), lambda i: (i, 0))
+    line_tile = pl.BlockSpec((8, tile), lambda i: (0, i))
+    four = [mine, peer, mine_there, peer_there]
+    attended, keep1, send1, lines = run_kernel(
+        lambda *refs: query_kernel(r, scale, *refs),
+        [((share, 256), BF)] * 3 + [((8, share), F32)],
+        grid=(2,),
+        ins=[SMEM] + [fixed(mine)] * 4 + [fixed(grads), fixed(marks)],
+        out_specs=[half_tile(256)] * 3 + [line_tile],
+        scratch=[
+            pltpu.VMEM((2 * count, 256), BF),
+            pltpu.VMEM((2 * count, 256), BF),
+            pltpu.VMEM((share, 256), BF),
+            pltpu.VMEM((share, 256), BF),
+            pltpu.VMEM((2 * count, 128), F32),
+            pltpu.VMEM((8, 2 * count), F32),
+            pltpu.VMEM((share, 128), F32),
+        ],
+        flops=8 * share * 2 * count * 256,
+        moved=6e6,
+    )(ids, *four, grads, marks)
+    got1 = from_peer(send1, 1)
+    lines_peer = from_peer(lines, 1)
+    lines_there, lines_peer_there = swap_cores(lines), swap_cores(lines_peer)
+    keep2, send2 = run_kernel(
+        lambda *refs: key_kernel(r, scale, *refs),
+        [((share, 256), BF)] * 2,
+        grid=(2,),
+        ins=[SMEM] + [fixed(mine)] * 4 + [fixed(grads)] * 2 + [fixed(lines)] * 4 + [fixed(marks)],
+        out_specs=[half_tile(256)] * 2,
+        scratch=[
+            pltpu.VMEM((2 * count, 256), BF),
+            pltpu.VMEM((2 * count, 256), BF),
+            pltpu.VMEM((share, 256), BF),
+            pltpu.VMEM((share, 256), BF),
+            pltpu.VMEM((2 * count, 128), F32),
+            pltpu.VMEM((8, 2 * count), F32),
+            pltpu.VMEM((share, 128), F32),
+            pltpu.VMEM((8, 2 * count), F32),
+        ],
+        flops=8 * share * 2 * count * 256,
+        moved=6e6,
+    )(ids, *four, grads, grads_there, lines, lines_peer, lines_there, lines_peer_there, marks)
+    got2 = from_peer(send2, 1)
+
+    branches = run_kernel(
+        lambda *refs: branch_kernel(r, *refs),
+        [((quarter, width), BF)] * 4,
+        grid=(4,),
+        ins=[tiled(units)] * 2 + [fixed(attended), fixed(w_shrink), fixed(w_near), fixed(w_peer)],
+        out_specs=[fixed_shape(quarter, width)] * 4,
+        scratch=[pltpu.VMEM((count, 256), BF)],
+        flops=2 * count * width * (2 * units + 256),
+        moved=9e6,
+    )(act0, act1, attended, w_shrink, w_near, w_peer)
+    my_inputs = my_tokens.astype(F32)
+    my_mixed = (my_inputs + scatter(branches) + residual_shift).astype(BF)
+
+    def whole_block(value):
+        return jnp.concatenate(by_core(core, value, swap_cores(value)))
+
+    mixed = whole_block(my_mixed)
+
+    *combined, grad_linear, attended_near, sums, line_sums = run_kernel(
+        lambda *refs: inputs_kernel(r, *refs),
+        [((quarter, width), BF)] * 4 + [((count, 384), BF), ((count, 128), BF), ((8, width), F32), ((8, 384), F32)],
+        grid=(4,),
+        ins=[fixed(keep1)] * 4 + [tiled(units)] * 2 + [tiled(width), fixed(w_triple), fixed(w_expand), fixed(norms)],
+        out_specs=[fixed_shape(quarter, width)] * 4
+        + [tiled(384), fixed_shape(count, 128), fixed_shape(8, width), fixed_shape(8, 384)],
+        scratch=[pltpu.VMEM((count, 384), BF)],
+        flops=2 * count * width * (384 + 2 * units),
+        moved=16e6,
+    )(keep1, keep2, got1, got2, grad0, grad1, normal, w_triple, w_expand, norms)
+    combined = scatter(combined)
+    my_center = my_inputs - jnp.mean(my_inputs, axis=-1, keepdims=True)
+    my_inverse = lax.rsqrt(jnp.mean(my_center * my_center, axis=-1, keepdims=True) + EPSILON)
+    my_normal = my_center * my_inverse
+    my_grad = my_inverse * (
+        combined
+        - jnp.mean(combined, axis=-1, keepdims=True)
+        - my_normal * jnp.mean(combined * my_normal, axis=-1, keepdims=True)
+    )
+    tokens_grad = whole_block((my_cotangent.astype(F32) + my_grad).astype(BF))
+
+    grad_triple = dot(normed_attend, grad_linear, tokens_first)
+    grad_out = dot(attended_near, whole_cotangent, tokens_first)
+    keep, give = run_kernel(
+        lambda *refs: pack_kernel(cut, blocks, *refs),
+        [((blocks, 4 * cut, 128), F32), ((blocks, 4 * cut, 128), BF)],
+        ins=[SMEM, VMEM, VMEM],
+        moved=7e6,
+    )(ids, grad_triple, grad_out)
+    dealt = (keep + swap_cores(give).astype(F32)).astype(BF)
+    dealt = lax.all_to_all(dealt, "blk", 0, 0, tiled=True)
+    keep = lax.dynamic_slice_in_dim(dealt, core * own_heads, own_heads, 0)
+    give = lax.dynamic_slice_in_dim(dealt, (1 - core) * own_heads, own_heads, 0)
+    triple_grad, output_grad = run_kernel(
+        lambda *refs: unpack_kernel(cut, own_heads, *refs),
+        [((3, depth, own_heads * 128), F32), ((own_heads * 128, depth), F32)],
+        ins=[SMEM, VMEM, VMEM],
+        moved=4e6,
+    )(ids, keep, swap_cores(give))
+
+    packed = jnp.concatenate(
+        [sums[:4].reshape(-1), cotangent_sums[0], line_sums[0], unit_sums[0]]
+    )
+    other = swap_cores(packed)
+    added = packed + other
+    first, second = 4 * width, 5 * width
+    norm_sums = added[:first].reshape(4, width // 128, blocks, lanes).transpose(2, 0, 1, 3)
+    residual_sum = added[first:second].reshape(width // 128, 128)
+    residual_grad = lax.dynamic_slice_in_dim(residual_sum, me * lanes, lanes, 1)
+    line_sum = added[second : second + 384].reshape(3, 1, 128)
+    third = second + 384
+    unit_sum = (packed[third : third + units] + other[third + units :]).reshape(-1, 128)
+    unit_sum = lax.dynamic_update_slice_in_dim(
+        jnp.zeros((w_in.shape[1] // 128, 128), F32), unit_sum, me * (units // 128), 0
+    )
+    unit_sum = unit_sum.reshape(-1, blocks, lanes).transpose(1, 0, 2)
+    ours = (me // own_heads == core).astype(F32)
+    line_sum = lax.dynamic_update_slice_in_dim(
+        jnp.zeros((3, own_heads, 128), F32), line_sum * ours, me % own_heads, 1
+    )
+    line_sum = line_sum.reshape(3, own_heads, blocks, lanes).transpose(2, 0, 1, 3)
+    tiny = jnp.concatenate([value.reshape(blocks, -1) for value in (norm_sums, unit_sum, line_sum)], axis=1)
+    tiny = jnp.sum(lax.all_to_all(tiny, "blk", 0, 0, tiled=True), axis=0)
+    first = norm_gain.size
+    gain_grad = tiny[:first].reshape(norm_gain.shape)
+    shift_grad = tiny[first : 2 * first].reshape(norm_shift.shape)
+    expand_bias_grad = tiny[2 * first : 2 * first + b_in.size].reshape(b_in.shape)
+    triple_bias_grad = tiny[2 * first + b_in.size :].reshape(b_qkv.shape)
+    return (
+        mixed,
+        tokens_grad,
+        triple_grad,
+        triple_bias_grad,
+        output_grad,
+        residual_grad,
+        expand_grad,
+        expand_bias_grad,
+        shrink_grad,
+        residual_grad,
+        gain_grad,
+        shift_grad,
+    )
+
+
 def solution(mesh):
     placed = (
         P("blk", None),
@@ -472,8 +1188,9 @@
         P("blk"),
         P("blk", None),
     )
+    two_to_a_head = mesh.shape["blk"] == 2 * HEADS
     return jax.shard_map(
-        body,
+        body if two_to_a_head else general_body,
         mesh=mesh,
         in_specs=placed,
         out_specs=(

time: 582 us -> 497 us (0.85)
  local copies, waits for them, and re-layouts: 146 us -> 42.6 us
  Pallas kernels: 0 us -> 92.7 us
  matrix products: 78.2 us -> 21.2 us
  other arithmetic: 90.5 us -> 58.2 us
  waiting for transfers between devices: 157 us -> 171 us
  starting transfers between devices: 97.6 us -> 104 us
    pallas_call x0 -> x11, Pallas kernels: none -> 92.7 us  [the longest x1 23.3 us: body(): run_kernel(lambda *refs: norm_kernel(r, *refs), [((count, width), BF)] *...]
    ppermute x32 -> x33, waiting for transfers between devices: 155 us -> 84.1 us  [from_peer(): return lax.ppermute(value, 'blk', [(i, i ^ mask) for i in range(count)])]
    dot_general x18 -> x6, matrix products: 78.2 us -> 21.2 us  [dot(): lax.dot_general(left, right, (dims, ((), ())), preferred_element_type=F32)]
    all_to_all x1, waiting for transfers between devices: 0.01 us -> 30.2 us  [body(): lax.all_to_all(w_out2.reshape(blocks, units, depth), 'blk', 0, 0, tiled=T...]
    gather x4 -> x0, local copies, waits for them, and re-layouts: 29.4 us -> none  [the longest x1 11.8 us: body(): token_start = starts.reshape(-1)[index]]
    all_to_all x1, waiting for transfers between devices: 0.01 us -> 22.8 us  [body(): lax.all_to_all(expand_deal, 'blk', 0, 0, tiled=True).reshape(width, units)]
    reshape x32 -> x17, local copies, waits for them, and re-layouts: 26.7 us -> 5.22 us  [the longest x1 1.6 us: body(): tail = tail[:, :, :small_lines].reshape(2, blocks, -1)[:, :, :lines * lanes]]
    all_to_all x1, waiting for transfers between devices: 0.01 us -> 17.6 us  [body(): shrink_grad = lax.all_to_all(shrink_deal, 'blk', 0, 0, tiled=True)]
  transfers between devices with their start and end apart: 53 -> 56, of which waited for: 14 -> 15; matrix products, arithmetic and copies ran while one was open for 51% -> 24% of each run, Pallas kernels for 0% -> 18%
where the time goes in v2:
time: 497 us; the launch traced here: 492 us
  waiting for transfers between devices  171 us (34%)
  starting transfers between devices  104 us (21%)
  Pallas kernels  92.7 us (19%)
  other arithmetic  58.2 us (12%)
  local copies, waits for them, and re-layouts  42.6 us (9%)
  matrix products  21.2 us (4%)
    ppermute x33, waiting for transfers between devices, from_peer(): return lax.ppermute(value, 'blk', [(i, i ^ mask) for i in range(count)])  84.1 us
    ppermute x33, starting transfers between devices, from_peer(): return lax.ppermute(value, 'blk', [(i, i ^ mask) for i in range(count)])  33.5 us
    all_to_all x1, waiting for transfers between devices, body(): lax.all_to_all(w_out2.reshape(blocks, units, depth), 'blk', 0, 0, tiled=T...  30.2 us
    pallas_call x1, Pallas kernels, body(): run_kernel(lambda *refs: norm_kernel(r, *refs), [((count, width), BF)] *...  23.3 us
    all_to_all x1, waiting for transfers between devices, body(): lax.all_to_all(expand_deal, 'blk', 0, 0, tiled=True).reshape(width, units)  22.8 us
    dot_general x6, matrix products, dot(): lax.dot_general(left, right, (dims, ((), ())), preferred_element_type=F32)  21.2 us
    ppermute x16, starting transfers between devices, swap_cores(): return lax.ppermute(value, 'tp', [(0, 1), (1, 0)])  20.1 us
    all_to_all x1, waiting for transfers between devices, body(): shrink_grad = lax.all_to_all(shrink_deal, 'blk', 0, 0, tiled=True)  17.6 us
  transfers between devices with their start and end apart: 56, of which 15 were waited for; matrix products, arithmetic and copies ran while one was open for 24% of the time, Pallas kernels for 18%

profile of v2, /device:TPU:11, one launch (start us, length us, event | category | flops | bytes accessed | tf_op | source)
XLA Modules:
  0.0 491.9 jit_solution(10450644804343574047)
XLA Ops:
  0.7 6.8 %all-to-all-start.2 = ((bf16[16,256,128]{2,1,0:T(8,128)(2,1)}), bf16[16,256,128]{2,1,0:T(8,128)(2,1)}, u32[]{:S(2)}, u32[]{:S(2)}) async-start(bf16[16,256,128]{2,1,0:T(8,128)(2,1)} %bitcast.157), calls=%async_computation.2 | async-start | bytes 2097152 | tf_op jit(solution)/shard_map/all_to_all | solution.py:929
  12.0 30.2 %all-to-all-done.2.refs_0_ = bf16[16,256,128]{2,1,0:T(8,128)(2,1)} async-done(((bf16[16,256,128]{2,1,0:T(8,128)(2,1)}), bf16[16,256,128]{2,1,0:T(8,128)(2,1)}, u32[]{:S(2)}, u32[]{:S(2)}) %all-to-all-start.2) | async-done | bytes 1048608 | tf_op jit(solution)/shard_map/all_to_all | solution.py:929
  42.2 5.4 %all-to-all-start.1 = ((bf16[16,128,256]{2,1,0:T(8,128)(2,1)}), bf16[16,128,256]{2,1,0:T(8,128)(2,1)}, u32[]{:S(2)}, u32[]{:S(2)}) async-start(bf16[16,128,256]{2,1,0:T(8,128)(2,1)} %bitcast.136), calls=%async_computation.1 | async-start | bytes 2097152 | tf_op jit(solution)/shard_map/all_to_all | solution.py:927
  48.4 2.1 collective-permute-start.10
  51.0 4.5 collective-permute-start.7
  58.5 3.3 collective-permute-start.11
  64.5 22.8 %all-to-all-done.1 = bf16[16,128,256]{2,1,0:T(8,128)(2,1)} async-done(((bf16[16,128,256]{2,1,0:T(8,128)(2,1)}), bf16[16,128,256]{2,1,0:T(8,128)(2,1)}, u32[]{:S(2)}, u32[]{:S(2)}) %all-to-all-start.1) | async-done | bytes 1048608 | tf_op jit(solution)/shard_map/all_to_all | solution.py:927
  87.3 5.6 %all-to-all-start = ((bf16[16,272,128]{2,1,0:T(8,128)(2,1)}), bf16[16,272,128]{2,1,0:T(8,128)(2,1)S(1)}, u32[]{:S(2)}, u32[]{:S(2)}) async-start(bf16[16,272,128]{2,1,0:T(8,128)(2,1)} %pad_maximum_fusion.1), calls=%async_computation | async-start | bytes 2228224 | tf_op jit(solution)/shard_map/all_to_all | solution.py:916
  95.6 12.6 %collective-permute-done.11 = bf16[64,2048]{1,0:T(8,128)(2,1)} collective-permute-done((bf16[64,2048]{1,0:T(8,128)(2,1)}, bf16[64,2048]{1,0:T(8,128)(2,1)}, u32[]{:S(2)}, u32[]{:S(2)}) %collective-permute-start.11) | collective-permute-done | bytes 262176 | tf_op jit(solution)/shard_map/ppermute | solution.py:30
  114.7 2.6 collective-permute-start.4
  117.2 2.2 pad_maximum_fusion.4
  120.8 5.2 %collective-permute-done.14 = bf16[4,32,2048]{2,1,0:T(8,128)(2,1)} collective-permute-done((bf16[4,32,2048]{2,1,0:T(8,128)(2,1)}, bf16[4,32,2048]{2,1,0:T(8,128)(2,1)}, u32[]{:S(2)}, u32[]{:S(2)}) %collective-permute-start.14) | collective-permute-done | bytes 524320 | tf_op jit(solution)/shard_map/ppermute | solution.py:30
  126.1 2.1 pad_maximum_fusion.7
  128.3 8.5 %collective-permute-start.17 = (bf16[2048,256]{1,0:T(8,128)(2,1)}, bf16[2048,256]{1,0:T(8,128)(2,1)}, u32[]{:S(2)}, u32[]{:S(2)}) collective-permute-start(bf16[2048,256]{1,0:T(8,128)(2,1)} %bitcast.49), channel_id=1, source_target_pairs={{0,1},{1,0},{2,3},{3,2},{4,5},{5,4},{6,7},{7,6},{8,9},{9,8},{10,11... | collective-permute-start | bytes 3145736 | tf_op jit(solution)/shard_map/ppermute | solution.py:25
  138.7 2.3 iota_select_fusion
  145.8 6.2 %multiply_sine_fusion = (f32[2048,32]{1,0:T(8,128)}, f32[2048,32]{1,0:T(8,128)}) fusion(f32[2048]{0:T(1024)S(1)} %iota_subtract_fusion, f32[32]{0:T(128)} %multiply_power_fusion), kind=kLoop, calls=%fused_computation.9 | loop fusion | flops 65536 | bytes 532608 | tf_op jit(solution)/shard_map/sin | solution.py:963
  155.3 5.4 %concatenate.71.refs_8_.refs_6_.refs_11_ = f32[2048,128]{1,0:T(8,128)} concatenate(f32[2048,1]{1,0:T(8,128)} %iota.15, f32[2048,1]{1,0:T(8,128)} %iota_select_fusion, f32[2048,1]{1,0:T(8,128)} %copy.131, f32[2048,29]{1,0:T(8,128)} %broadcast_in_dim.26, f32[2048,32]{1,0:T(8,128)} %get-tuple-element.171, f32[2048,32]{1,0:T(8,128)} %get-tuple-element.170, f32[2048,32]{1,0:T(8,128)} %broadcast_in_dim.27), dimensions={1} | concatenate | bytes 2097152 | tf_op jit(solution)/shard_map/concatenate | solution.py:956
  161.0 3.5 shard_map.232.refs_3_
  165.0 3.0 pad_maximum_fusion.refs_2_.refs_8_
  169.6 1.6 reshape.358
  171.1 1.6 slice_convert_fusion
  172.7 2.3 copy.125
  175.1 2.6 copy.126
  178.5 1.7 slice.290
  180.3 3.0 shard_map.229
  184.7 23.3 %shard_map.230 = (bf16[1024,2048]{1,0:T(8,128)(2,1)}, bf16[1024,2048]{1,0:T(8,128)(2,1)}, bf16[1024,2048]{1,0:T(8,128)(2,1)}, bf16[1024,384]{1,0:T(8,128)(2,1)}) custom-call(s32[2]{0:T(128)S(1)} %pad_add_fusion.refs_0_, bf16[256,2048]{1,0:T(8,128)(2,1)S(1)} %bitcast.138, bf16[256,2048]{1,0:T(8,128)(2,1)} %bitcast.9.refs_2_, ...), custom_call_target="tpu_custom_call" | custom-call | flops 1610612736 | bytes 22000000 | tf_op jit(solution)/shard_map/pallas_call | solution.py:978
  209.5 6.9 %shard_map.231 = (bf16[1024,2048]{1,0:T(8,128)(2,1)}, bf16[1024,256]{1,0:T(8,128)(2,1)S(1)}, f32[8,2048]{1,0:T(8,128)S(1)}) custom-call(bf16[256,2048]{1,0:T(8,128)(2,1)S(1)} %bitcast.139, bf16[256,2048]{1,0:T(8,128)(2,1)} %bitcast.43.t1, bf16[256,2048]{1,0:T(8,128)(2,1)} %bitcast.46.t2, bf16[256,2048]{1,0:T(8,128)(2,1)} %bitcast.47.t3, ...), custom_call_target="tpu_custom_call" | custom-call | flops 1073741824 | bytes 11000000 | tf_op jit(solution)/shard_map/pallas_call | solution.py:992
  216.4 8.8 %shard_map.233 = (bf16[1024,256]{1,0:T(8,128)(2,1)S(1)}, bf16[1024,256]{1,0:T(8,128)(2,1)S(1)}, bf16[1024,256]{1,0:T(8,128)(2,1)S(1)}, bf16[1024,256]{1,0:T(8,128)(2,1)S(1)}, f32[8,512]{1,0:T(8,128)S(1)}) custom-call(bf16[1024,2048]{1,0:T(8,128)(2,1)} %get-tuple-element.49.refs_0_, bf16[1024,2048]{1,0:T(8,128)(2,1)} %get-tuple-element.51.refs_1_, ...), custom_call_target="tpu_custom_call" | custom-call | flops 4294967296 | bytes 14000000 | tf_op jit(solution)/shard_map/pallas_call | solution.py:1003
  225.3 2.3 convolution_convert_fusion
  230.1 4.5 convolution_convert_fusion.1
  235.1 9.3 %shard_map.234 = (bf16[512,256]{1,0:T(8,128)(2,1)S(1)}, bf16[512,256]{1,0:T(8,128)(2,1)S(1)}, bf16[512,256]{1,0:T(8,128)(2,1)S(1)}, f32[8,512]{1,0:T(8,128)S(1)}) custom-call(s32[2]{0:T(128)S(1)} %pad_add_fusion.refs_0_, bf16[1024,384]{1,0:T(8,128)(2,1)} %get-tuple-element.54.refs_1_, bf16[1024,384]{1,0:T(8,128)(2,1)} %collective-permute-done.19.refs_2_, ...), custom_call_target="tpu_custom_call" | custom-call | flops 2147483648 | bytes 6000000 | tf_op jit(solution)/shard_map/pallas_call | solution.py:1029
  246.0 2.6 fusion.2
  249.7 8.9 %shard_map.235 = (bf16[256,2048]{1,0:T(8,128)(2,1)S(1)}, bf16[256,2048]{1,0:T(8,128)(2,1)}, bf16[256,2048]{1,0:T(8,128)(2,1)}, bf16[256,2048]{1,0:T(8,128)(2,1)}) custom-call(bf16[1024,256]{1,0:T(8,128)(2,1)S(1)} %copy-done.1, bf16[1024,256]{1,0:T(8,128)(2,1)S(1)} %copy-done.3, bf16[512,256]{1,0:T(8,128)(2,1)S(1)} %get-tuple-element.56.refs_2_, ...), custom_call_target="tpu_custom_call" | custom-call | flops 3221225472 | bytes 9000000 | tf_op jit(solution)/shard_map/pallas_call | solution.py:1071
  258.5 1.6 convert_element_type.188
  261.4 1.6 convert_element_type.194
  264.2 6.4 %shard_map.236 = (bf16[512,256]{1,0:T(8,128)(2,1)S(1)}, bf16[512,256]{1,0:T(8,128)(2,1)S(1)}) custom-call(s32[2]{0:T(128)S(1)} %pad_add_fusion.refs_0_, bf16[1024,384]{1,0:T(8,128)(2,1)} %get-tuple-element.54.refs_1_, bf16[1024,384]{1,0:T(8,128)(2,1)} %collective-permute-done.19.refs_2_, bf16[1024,384]{1,0:T(8,128)(2,1)S(1)} %collective-permute-done.20.refs_3_, ...), custom_call_target="tpu_custom_call" | custom-call | flops 2147483648 | bytes 6000000 | tf_op jit(solution)/shard_map/pallas_call | solution.py:1050
  271.8 4.9 fusion
  276.7 16.8 %collective-permute-done.35.refs_3_ = bf16[512,256]{1,0:T(8,128)(2,1)S(1)} collective-permute-done((bf16[512,256]{1,0:T(8,128)(2,1)S(1)}, bf16[512,256]{1,0:T(8,128)(2,1)S(1)}, u32[]{:S(2)}, u32[]{:S(2)}) %collective-permute-start.35) | collective-permute-done | bytes 262176 | tf_op jit(solution)/shard_map/ppermute | solution.py:30
  293.5 17.1 %shard_map.237 = (bf16[256,2048]{1,0:T(8,128)(2,1)}, bf16[256,2048]{1,0:T(8,128)(2,1)}, bf16[256,2048]{1,0:T(8,128)(2,1)}, bf16[256,2048]{1,0:T(8,128)(2,1)}, bf...) custom-call(bf16[512,256]{1,0:T(8,128)(2,1)S(1)} %get-tuple-element.6, ...), custom_call_target="tpu_custom_call" | custom-call | flops 3758096384 | bytes 16000000 | tf_op jit(solution)/shard_map/pallas_call | solution.py:1089
  311.6 6.3 %fusion.46.refs_1_ = f32[2048,384]{1,0:T(8,128)} fusion(bf16[1024,2048]{1,0:T(8,128)(2,1)} %get-tuple-element.73, bf16[1024,384]{1,0:T(8,128)(2,1)S(1)} %get-tuple-element.74), kind=kOutput, calls=%fused_computation.145 | convolution fusion | flops 1610612736 | bytes 8126464 | tf_op jit(solution)/shard_map/dot_general | solution.py:21
  319.0 1.6 convert_element_type.206
  320.6 3.5 shard_map.238
  324.4 1.6 convert_element_type.212
  329.6 5.2 %all-to-all-start.4 = ((f32[16,1,960]{2,1,0:T(1,128)}), f32[16,1,960]{2,1,0:T(1,128)S(1)}, u32[]{:S(2)}, u32[]{:S(2)}) async-start(f32[16,1,960]{2,1,0:T(1,128)} %all_to_all.28), calls=%async_computation.4 | async-start | bytes 131072 | tf_op jit(solution)/shard_map/all_to_all | solution.py:1152
  334.9 15.9 %all-to-all-done.4 = f32[16,1,960]{2,1,0:T(1,128)S(1)} async-done(((f32[16,1,960]{2,1,0:T(1,128)}), f32[16,1,960]{2,1,0:T(1,128)S(1)}, u32[]{:S(2)}, u32[]{:S(2)}) %all-to-all-start.4) | async-done | bytes 61472 | tf_op jit(solution)/shard_map/all_to_all | solution.py:1152
  350.9 5.0 %all-to-all-start.5 = ((bf16[16,128,256]{2,1,0:T(8,128)(2,1)}), bf16[16,128,256]{2,1,0:T(8,128)(2,1)}, u32[]{:S(2)}, u32[]{:S(2)}) async-start(bf16[16,128,256]{2,1,0:T(8,128)(2,1)} %bitcast.65), calls=%async_computation.5 | async-start | bytes 2097152 | tf_op jit(solution)/shard_map/all_to_all | solution.py:1022
  363.8 1.6 convert_element_type.207
  370.2 2.6 add_convert_fusion
  372.8 7.7 %collective-permute-done.23 = bf16[128,2048]{1,0:T(8,128)(2,1)S(1)} collective-permute-done((bf16[128,2048]{1,0:T(8,128)(2,1)S(1)}, bf16[128,2048]{1,0:T(8,128)(2,1)S(1)}, u32[]{:S(2)}, u32[]{:S(2)}) %collective-permute-start.23) | collective-permute-done | bytes 524320 | tf_op jit(solution)/shard_map/ppermute | solution.py:30
  380.7 1.8 collective-permute-done.25
  384.8 2.3 collective-permute-start.26
  387.8 1.9 collective-permute-start.27
  390.5 2.0 collective-permute-done.37
  393.5 5.7 %all-to-all-start.6 = ((bf16[16,256,128]{2,1,0:T(8,128)(2,1)}), bf16[16,256,128]{2,1,0:T(8,128)(2,1)S(1)}, u32[]{:S(2)}, u32[]{:S(2)}) async-start(bf16[16,256,128]{2,1,0:T(8,128)(2,1)} %bitcast.145), calls=%async_computation.6 | async-start | bytes 2097152 | tf_op jit(solution)/shard_map/all_to_all | solution.py:1020
  400.3 1.6 add_convert_fusion.1
  403.7 2.1 collective-permute-start.41
  406.8 17.6 %all-to-all-done.6 = bf16[16,256,128]{2,1,0:T(8,128)(2,1)S(1)} async-done(((bf16[16,256,128]{2,1,0:T(8,128)(2,1)}), bf16[16,256,128]{2,1,0:T(8,128)(2,1)S(1)}, u32[]{:S(2)}, u32[]{:S(2)}) %all-to-all-start.6) | async-done | bytes 1048608 | tf_op jit(solution)/shard_map/all_to_all | solution.py:1020
  424.4 16.5 %all-to-all-start.3 = ((bf16[16,256,128]{2,1,0:T(8,128)(2,1)}), bf16[16,256,128]{2,1,0:T(8,128)(2,1)S(1)}, u32[]{:S(2)}, u32[]{:S(2)}) async-start(bf16[16,256,128]{2,1,0:T(8,128)(2,1)} %add_convert_fusion), calls=%async_computation.3 | async-start | bytes 2097152 | tf_op jit(solution)/shard_map/all_to_all | solution.py:1120
  441.0 1.5 bitcast_convert_fusion
  443.7 11.1 %collective-permute-done.42 = bf16[64,2048]{1,0:T(8,128)(2,1)S(1)} collective-permute-done((bf16[64,2048]{1,0:T(8,128)(2,1)}, bf16[64,2048]{1,0:T(8,128)(2,1)S(1)}, u32[]{:S(2)}, u32[]{:S(2)}) %collective-permute-start.42) | collective-permute-done | bytes 262176 | tf_op jit(solution)/shard_map/ppermute | solution.py:30
  455.1 24.9 %collective-permute-done.28 = bf16[64,2048]{1,0:T(8,128)(2,1)S(1)} collective-permute-done((bf16[64,2048]{1,0:T(8,128)(2,1)S(1)}, bf16[64,2048]{1,0:T(8,128)(2,1)S(1)}, u32[]{:S(2)}, u32[]{:S(2)}) %collective-permute-start.28) | collective-permute-done | bytes 262176 | tf_op jit(solution)/shard_map/ppermute | solution.py:30
  480.0 1.6 fusion.19
  484.2 1.5 copy.151
  489.0 2.1 shard_map.239
  (319 shorter events, 82.9 us)
Async XLA Ops:
  0.7 41.5 %all-to-all-start.2 = ((bf16[16,256,128]{2,1,0:T(8,128)(2,1)}), bf16[16,256,128]{2,1,0:T(8,128)(2,1)}, u32[]{:S(2)}, u32[]{:S(2)}) async-start(bf16[16,256,128]{2,1,0:T(8,128)(2,1)} %bitcast.157), calls=%async_computation.2 | async-start | bytes 2097152 | tf_op jit(solution)/shard_map/all_to_all | solution.py:929
  7.6 50.6 %collective-permute-start.2 = (bf16[64,2048]{1,0:T(8,128)(2,1)S(1)}, bf16[64,2048]{1,0:T(8,128)(2,1)S(1)}, u32[]{:S(2)}, u32[]{:S(2)}) collective-permute-start(bf16[64,2048]{1,0:T(8,128)(2,1)S(1)} %get-tuple-element.135), channel_id=1, source_target_pairs={{0,24},{2,26},{4,28},{6,30},{8,16},{10,18},{12,20},{14,22},{16,8},... | collective-permute-start | bytes 786440 | tf_op jit(solution)/shard_map/ppermute | solution.py:30
  8.8 49.7 %collective-permute-start.1 = (bf16[64,2048]{1,0:T(8,128)(2,1)S(1)}, bf16[64,2048]{1,0:T(8,128)(2,1)}, u32[]{:S(2)}, u32[]{:S(2)}) collective-permute-start(bf16[64,2048]{1,0:T(8,128)(2,1)S(1)} %get-tuple-element.135), channel_id=1, source_target_pairs={{0,16},{2,18},{4,20},{6,22},{8,24},{10,26},{12,28},{14,30},{16,0},... | collective-permute-start | bytes 786440 | tf_op jit(solution)/shard_map/ppermute | solution.py:30
  10.0 51.8 %collective-permute-start = (bf16[64,2048]{1,0:T(8,128)(2,1)S(1)}, bf16[64,2048]{1,0:T(8,128)(2,1)}, u32[]{:S(2)}, u32[]{:S(2)}) collective-permute-start(bf16[64,2048]{1,0:T(8,128)(2,1)S(1)} %get-tuple-element.135), channel_id=1, source_target_pairs={{0,8},{2,10},{4,12},{6,14},{8,0},{10,2},{12,4},{14,6},{16,24},{18,... | collective-permute-start | bytes 786440 | tf_op jit(solution)/shard_map/ppermute | solution.py:30
  10.9 36.7 %copy-start.22 = (bf16[128,2048]{1,0:T(8,128)(2,1)S(1)}, bf16[128,2048]{1,0:T(8,128)(2,1)}, u32[]{:S(2)}) copy-start(bf16[128,2048]{1,0:T(8,128)(2,1)} %param.27) | copy-start | bytes 1572868
  10.9 39.5 %copy-start.34 = (bf16[1024,128]{1,0:T(8,128)(2,1)S(1)}, bf16[1024,128]{1,0:T(8,128)(2,1)}, u32[]{:S(2)}) copy-start(bf16[1024,128]{1,0:T(8,128)(2,1)} %param.17) | copy-start | bytes 786436
  12.0 38.5 %copy-start.29 = (bf16[3,128,1024]{2,1,0:T(8,128)(2,1)S(1)}, bf16[3,128,1024]{2,1,0:T(8,128)(2,1)}, u32[]{:S(2)}) copy-start(bf16[3,128,1024]{2,1,0:T(8,128)(2,1)} %param.15) | copy-start | bytes 2359300
  42.2 45.1 %all-to-all-start.1 = ((bf16[16,128,256]{2,1,0:T(8,128)(2,1)}), bf16[16,128,256]{2,1,0:T(8,128)(2,1)}, u32[]{:S(2)}, u32[]{:S(2)}) async-start(bf16[16,128,256]{2,1,0:T(8,128)(2,1)} %bitcast.136), calls=%async_computation.1 | async-start | bytes 2097152 | tf_op jit(solution)/shard_map/all_to_all | solution.py:927
  48.4 47.3 %collective-permute-start.10 = (bf16[64,2048]{1,0:T(8,128)(2,1)}, bf16[64,2048]{1,0:T(8,128)(2,1)}, u32[]{:S(2)}, u32[]{:S(2)}) collective-permute-start(bf16[64,2048]{1,0:T(8,128)(2,1)} %constant_dynamic-slice_fusion.4), channel_id=1, source_target_pairs={{0,16},{2,18},{4,20},{6,22},{8,24},{10,26},{12,28},{14,30},{16,0},... | collective-permute-start | bytes 786440 | tf_op jit(solution)/shard_map/ppermute | solution.py:30
  51.0 12.1 %collective-permute-start.7 = (bf16[8,256,128]{2,1,0:T(8,128)(2,1)S(1)}, bf16[8,256,128]{2,1,0:T(8,128)(2,1)S(1)}, u32[]{:S(2)}, u32[]{:S(2)}) collective-permute-start(bf16[8,256,128]{2,1,0:T(8,128)(2,1)S(1)} %fusion.24), channel_id=1, source_target_pairs={{0,1},{1,0},{2,3},{3,2},{4,5},{5,4},{6,7},{7,6},{8,9},{9,8},{10,11... | collective-permute-start | bytes 1572872 | tf_op jit(solution)/shard_map/ppermute | solution.py:25
  58.2 37.4 %collective-permute-start.9 = (bf16[64,2048]{1,0:T(8,128)(2,1)}, bf16[64,2048]{1,0:T(8,128)(2,1)}, u32[]{:S(2)}, u32[]{:S(2)}) collective-permute-start(bf16[64,2048]{1,0:T(8,128)(2,1)} %constant_dynamic-slice_fusion.4), channel_id=1, source_target_pairs={{0,8},{2,10},{4,12},{6,14},{8,0},{10,2},{12,4},{14,6},{16,24},{18,... | collective-permute-start | bytes 786440 | tf_op jit(solution)/shard_map/ppermute | solution.py:30
  58.5 49.6 %collective-permute-start.11 = (bf16[64,2048]{1,0:T(8,128)(2,1)}, bf16[64,2048]{1,0:T(8,128)(2,1)}, u32[]{:S(2)}, u32[]{:S(2)}) collective-permute-start(bf16[64,2048]{1,0:T(8,128)(2,1)} %constant_dynamic-slice_fusion.4), channel_id=1, source_target_pairs={{0,24},{2,26},{4,28},{6,30},{8,16},{10,18},{12,20},{14,22},{16,8},... | collective-permute-start | bytes 786440 | tf_op jit(solution)/shard_map/ppermute | solution.py:30
  87.3 49.6 %all-to-all-start = ((bf16[16,272,128]{2,1,0:T(8,128)(2,1)}), bf16[16,272,128]{2,1,0:T(8,128)(2,1)S(1)}, u32[]{:S(2)}, u32[]{:S(2)}) async-start(bf16[16,272,128]{2,1,0:T(8,128)(2,1)} %pad_maximum_fusion.1), calls=%async_computation | async-start | bytes 2228224 | tf_op jit(solution)/shard_map/all_to_all | solution.py:916
  94.2 23.1 %collective-permute-start.5 = (bf16[4,32,2048]{2,1,0:T(8,128)(2,1)}, bf16[4,32,2048]{2,1,0:T(8,128)(2,1)}, u32[]{:S(2)}, u32[]{:S(2)}) collective-permute-start(bf16[4,32,2048]{2,1,0:T(8,128)(2,1)} %get-tuple-element.146), channel_id=1, source_target_pairs={{0,2},{2,0},{4,6},{6,4},{8,10},{10,8},{12,14},{14,12},{16,18},{18,... | collective-permute-start | bytes 1572872 | tf_op jit(solution)/shard_map/ppermute | solution.py:30
  94.4 18.3 %collective-permute-start.3 = (bf16[4,32,2048]{2,1,0:T(8,128)(2,1)}, bf16[4,32,2048]{2,1,0:T(8,128)(2,1)S(1)}, u32[]{:S(2)}, u32[]{:S(2)}) collective-permute-start(bf16[4,32,2048]{2,1,0:T(8,128)(2,1)} %get-tuple-element.147), channel_id=1, source_target_pairs={{0,4},{2,6},{4,0},{6,2},{8,12},{10,14},{12,8},{14,10},{16,20},{18,... | collective-permute-start | bytes 1572872 | tf_op jit(solution)/shard_map/ppermute | solution.py:30
  110.9 15.2 %collective-permute-start.14 = (bf16[4,32,2048]{2,1,0:T(8,128)(2,1)}, bf16[4,32,2048]{2,1,0:T(8,128)(2,1)}, u32[]{:S(2)}, u32[]{:S(2)}) collective-permute-start(bf16[4,32,2048]{2,1,0:T(8,128)(2,1)} %get-tuple-element.142), channel_id=1, source_target_pairs={{0,2},{2,0},{4,6},{6,4},{8,10},{10,8},{12,14},{14,12},{16,18},{18,... | collective-permute-start | bytes 1572872 | tf_op jit(solution)/shard_map/ppermute | solution.py:30
  111.2 16.9 %collective-permute-start.12 = (bf16[4,32,2048]{2,1,0:T(8,128)(2,1)}, bf16[4,32,2048]{2,1,0:T(8,128)(2,1)S(1)}, u32[]{:S(2)}, u32[]{:S(2)}) collective-permute-start(bf16[4,32,2048]{2,1,0:T(8,128)(2,1)} %get-tuple-element.143), channel_id=1, source_target_pairs={{0,4},{2,6},{4,0},{6,2},{8,12},{10,14},{12,8},{14,10},{16,20},{18,... | collective-permute-start | bytes 1572872 | tf_op jit(solution)/shard_map/ppermute | solution.py:30
  114.7 70.0 %collective-permute-start.4 = (bf16[2,4,32,2048]{3,2,1,0:T(8,128)(2,1)S(1)}, bf16[2,4,32,2048]{3,2,1,0:T(8,128)(2,1)}, u32[]{:S(2)}, u32[]{:S(2)}) collective-permute-start(bf16[2,4,32,2048]{3,2,1,0:T(8,128)(2,1)S(1)} %pad_maximum_fusion.3), channel_id=1, source_target_pairs={{0,2},{2,0},{4,6},{6,4},{8,10},{10,8},{12,14},{14,12},{16,18},{18,... | collective-permute-start | bytes 3145736 | tf_op jit(solution)/shard_map/ppermute | solution.py:30
  119.5 65.3 %collective-permute-start.6 = (bf16[2,4,32,2048]{3,2,1,0:T(8,128)(2,1)}, bf16[2,4,32,2048]{3,2,1,0:T(8,128)(2,1)}, u32[]{:S(2)}, u32[]{:S(2)}) collective-permute-start(bf16[2,4,32,2048]{3,2,1,0:T(8,128)(2,1)} %pad_maximum_fusion.4), channel_id=1, source_target_pairs={{0,4},{2,6},{4,0},{6,2},{8,12},{10,14},{12,8},{14,10},{16,20},{18,... | collective-permute-start | bytes 3145736 | tf_op jit(solution)/shard_map/ppermute | solution.py:30
  128.3 36.2 %collective-permute-start.17 = (bf16[2048,256]{1,0:T(8,128)(2,1)}, bf16[2048,256]{1,0:T(8,128)(2,1)}, u32[]{:S(2)}, u32[]{:S(2)}) collective-permute-start(bf16[2048,256]{1,0:T(8,128)(2,1)} %bitcast.49), channel_id=1, source_target_pairs={{0,1},{1,0},{2,3},{3,2},{4,5},{5,4},{6,7},{7,6},{8,9},{9,8},{10,11... | collective-permute-start | bytes 3145736 | tf_op jit(solution)/shard_map/ppermute | solution.py:25
  136.8 23.9 %collective-permute-start.18 = (bf16[16,256,128]{2,1,0:T(8,128)(2,1)}, bf16[16,256,128]{2,1,0:T(8,128)(2,1)}, u32[]{:S(2)}, u32[]{:S(2)}) collective-permute-start(bf16[16,256,128]{2,1,0:T(8,128)(2,1)} %all-to-all-done.2.refs_0_), channel_id=1, source_target_pairs={{0,1},{1,0},{2,3},{3,2},{4,5},{5,4},{6,7},{7,6},{8,9},{9,8},{10,11... | collective-permute-start | bytes 3145736 | tf_op jit(solution)/shard_map/ppermute | solution.py:25
  141.8 26.3 %collective-permute-start.8 = (bf16[16,272,128]{2,1,0:T(8,128)(2,1)S(1)}, bf16[16,272,128]{2,1,0:T(8,128)(2,1)}, u32[]{:S(2)}, u32[]{:S(2)}) collective-permute-start(bf16[16,272,128]{2,1,0:T(8,128)(2,1)S(1)} %all-to-all-done.refs_1_), channel_id=1, source_target_pairs={{0,1},{1,0},{2,3},{3,2},{4,5},{5,4},{6,7},{7,6},{8,9},{9,8},{10,11... | collective-permute-start | bytes 3342344 | tf_op jit(solution)/shard_map/ppermute | solution.py:25
  160.7 48.8 %collective-permute-start.13 = (bf16[2,4,32,2048]{3,2,1,0:T(8,128)(2,1)S(1)}, bf16[2,4,32,2048]{3,2,1,0:T(8,128)(2,1)}, u32[]{:S(2)}, u32[]{:S(2)}) collective-permute-start(bf16[2,4,32,2048]{3,2,1,0:T(8,128)(2,1)S(1)} %pad_maximum_fusion.6), channel_id=1, source_target_pairs={{0,2},{2,0},{4,6},{6,4},{8,10},{10,8},{12,14},{14,12},{16,18},{18,... | collective-permute-start | bytes 3145736 | tf_op jit(solution)/shard_map/ppermute | solution.py:30
  164.5 44.9 %collective-permute-start.15 = (bf16[2,4,32,2048]{3,2,1,0:T(8,128)(2,1)}, bf16[2,4,32,2048]{3,2,1,0:T(8,128)(2,1)}, u32[]{:S(2)}, u32[]{:S(2)}) collective-permute-start(bf16[2,4,32,2048]{3,2,1,0:T(8,128)(2,1)} %pad_maximum_fusion.7), channel_id=1, source_target_pairs={{0,4},{2,6},{4,0},{6,2},{8,12},{10,14},{12,8},{14,10},{16,20},{18,... | collective-permute-start | bytes 3145736 | tf_op jit(solution)/shard_map/ppermute | solution.py:30
  183.2 26.3 %collective-permute-start.16 = (bf16[128,2048]{1,0:T(8,128)(2,1)}, bf16[128,2048]{1,0:T(8,128)(2,1)S(1)}, u32[]{:S(2)}, u32[]{:S(2)}) collective-permute-start(bf16[128,2048]{1,0:T(8,128)(2,1)} %get-tuple-element.50.near.refs_4_), channel_id=1, source_target_pairs={{0,2},{2,0},{4,6},{6,4},{8,10},{10,8},{12,14},{14,12},{16,18},{18,... | collective-permute-start | bytes 1572872 | tf_op jit(solution)/shard_map/ppermute | solution.py:30
  184.7 24.5 %copy-start.30 = (f32[2,32,128]{1,2,0:T(8,128)S(1)}, f32[2,32,128]{1,2,0:T(8,128)}, u32[]{:S(2)}) copy-start(f32[2,32,128]{1,2,0:T(8,128)} %slice.290) | copy-start | bytes 98308
  208.1 27.0 %collective-permute-start.20 = (bf16[1024,384]{1,0:T(8,128)(2,1)}, bf16[1024,384]{1,0:T(8,128)(2,1)S(1)}, u32[]{:S(2)}, u32[]{:S(2)}) collective-permute-start(bf16[1024,384]{1,0:T(8,128)(2,1)} %get-tuple-element.54.refs_1_), channel_id=1, source_target_pairs={{0,1},{1,0},{2,3},{3,2},{4,5},{5,4},{6,7},{7,6},{8,9},{9,8},{10,11... | collective-permute-start | bytes 2359304 | tf_op jit(solution)/shard_map/ppermute | solution.py:25
  209.0 19.4 %collective-permute-start.19 = (bf16[1024,384]{1,0:T(8,128)(2,1)}, bf16[1024,384]{1,0:T(8,128)(2,1)}, u32[]{:S(2)}, u32[]{:S(2)}) collective-permute-start(bf16[1024,384]{1,0:T(8,128)(2,1)} %get-tuple-element.54.refs_1_), channel_id=1, source_target_pairs={{0,2},{2,0},{4,6},{6,4},{8,10},{10,8},{12,14},{14,12},{16,18},{18,... | collective-permute-start | bytes 2359304 | tf_op jit(solution)/shard_map/ppermute | solution.py:30
  227.5 17.3 %collective-permute-start.48 = (bf16[256,2048]{1,0:T(8,128)(2,1)}, bf16[256,2048]{1,0:T(8,128)(2,1)}, u32[]{:S(2)}, u32[]{:S(2)}) collective-permute-start(bf16[256,2048]{1,0:T(8,128)(2,1)} %convolution_convert_fusion), channel_id=1, source_target_pairs={{0,1},{1,0},{2,3},{3,2},{4,5},{5,4},{6,7},{7,6},{8,9},{9,8},{10,11... | collective-permute-start | bytes 3145736 | tf_op jit(solution)/shard_map/ppermute | solution.py:25
  228.4 6.7 %collective-permute-start.21 = (bf16[1024,384]{1,0:T(8,128)(2,1)}, bf16[1024,384]{1,0:T(8,128)(2,1)}, u32[]{:S(2)}, u32[]{:S(2)}) collective-permute-start(bf16[1024,384]{1,0:T(8,128)(2,1)} %collective-permute-done.19.refs_2_), channel_id=1, source_target_pairs={{0,1},{1,0},{2,3},{3,2},{4,5},{5,4},{6,7},{7,6},{8,9},{9,8},{10,11... | collective-permute-start | bytes 2359304 | tf_op jit(solution)/shard_map/ppermute | solution.py:25
  230.0 33.0 %collective-permute-start.30 = (bf16[1024,256]{1,0:T(8,128)(2,1)S(1)}, bf16[1024,256]{1,0:T(8,128)(2,1)S(1)}, u32[]{:S(2)}, u32[]{:S(2)}) collective-permute-start(bf16[1024,256]{1,0:T(8,128)(2,1)S(1)} %get-tuple-element.55.refs_5_), channel_id=1, source_target_pairs={{0,1},{1,0},{2,3},{3,2},{4,5},{5,4},{6,7},{7,6},{8,9},{9,8},{10,11... | collective-permute-start | bytes 1572872 | tf_op jit(solution)/shard_map/ppermute | solution.py:25
  234.6 37.2 %collective-permute-start.47 = (bf16[2048,256]{1,0:T(8,128)(2,1)}, bf16[2048,256]{1,0:T(8,128)(2,1)}, u32[]{:S(2)}, u32[]{:S(2)}) collective-permute-start(bf16[2048,256]{1,0:T(8,128)(2,1)} %convolution_convert_fusion.1), channel_id=1, source_target_pairs={{0,1},{1,0},{2,3},{3,2},{4,5},{5,4},{6,7},{7,6},{8,9},{9,8},{10,11... | collective-permute-start | bytes 3145736 | tf_op jit(solution)/shard_map/ppermute | solution.py:25
  244.4 18.8 %collective-permute-start.32 = (f32[8,512]{1,0:T(8,128)S(1)}, f32[8,512]{1,0:T(8,128)S(1)}, u32[]{:S(2)}, u32[]{:S(2)}) collective-permute-start(f32[8,512]{1,0:T(8,128)S(1)} %get-tuple-element.62.refs_7_), channel_id=1, source_target_pairs={{0,1},{1,0},{2,3},{3,2},{4,5},{5,4},{6,7},{7,6},{8,9},{9,8},{10,11... | collective-permute-start | bytes 49160 | tf_op jit(solution)/shard_map/ppermute | solution.py:25
  244.5 4.1 collective-permute-start.31
  244.8 31.9 %collective-permute-start.34 = (bf16[512,256]{1,0:T(8,128)(2,1)S(1)}, bf16[512,256]{1,0:T(8,128)(2,1)S(1)}, u32[]{:S(2)}, u32[]{:S(2)}) collective-permute-start(bf16[512,256]{1,0:T(8,128)(2,1)S(1)} %get-tuple-element.64), channel_id=1, source_target_pairs={{0,2},{2,0},{4,6},{6,4},{8,10},{10,8},{12,14},{14,12},{16,18},{18,... | collective-permute-start | bytes 786440 | tf_op jit(solution)/shard_map/ppermute | solution.py:30
  248.6 15.6 %collective-permute-start.33 = (f32[8,512]{1,0:T(8,128)S(1)}, f32[8,512]{1,0:T(8,128)S(1)}, u32[]{:S(2)}, u32[]{:S(2)}) collective-permute-start(f32[8,512]{1,0:T(8,128)S(1)} %collective-permute-done.31.refs_8_), channel_id=1, source_target_pairs={{0,1},{1,0},{2,3},{3,2},{4,5},{5,4},{6,7},{7,6},{8,9},{9,8},{10,11... | collective-permute-start | bytes 49160 | tf_op jit(solution)/shard_map/ppermute | solution.py:25
  262.9 96.0 %collective-permute-start.22 = (bf16[256,2048]{1,0:T(8,128)(2,1)}, bf16[256,2048]{1,0:T(8,128)(2,1)}, u32[]{:S(2)}, u32[]{:S(2)}) collective-permute-start(bf16[256,2048]{1,0:T(8,128)(2,1)} %get-tuple-element.58), channel_id=1, source_target_pairs={{0,2},{2,0},{4,6},{6,4},{8,10},{10,8},{12,14},{14,12},{16,18},{18,... | collective-permute-start | bytes 3145736 | tf_op jit(solution)/shard_map/ppermute | solution.py:30
  263.2 98.6 %collective-permute-start.24 = (bf16[256,2048]{1,0:T(8,128)(2,1)}, bf16[256,2048]{1,0:T(8,128)(2,1)}, u32[]{:S(2)}, u32[]{:S(2)}) collective-permute-start(bf16[256,2048]{1,0:T(8,128)(2,1)} %get-tuple-element.60), channel_id=1, source_target_pairs={{0,4},{2,6},{4,0},{6,2},{8,12},{10,14},{12,8},{14,10},{16,20},{18,... | collective-permute-start | bytes 3145736 | tf_op jit(solution)/shard_map/ppermute | solution.py:30
  270.5 23.0 %collective-permute-start.35 = (bf16[512,256]{1,0:T(8,128)(2,1)S(1)}, bf16[512,256]{1,0:T(8,128)(2,1)S(1)}, u32[]{:S(2)}, u32[]{:S(2)}) collective-permute-start(bf16[512,256]{1,0:T(8,128)(2,1)S(1)} %get-tuple-element.65), channel_id=1, source_target_pairs={{0,2},{2,0},{4,6},{6,4},{8,10},{10,8},{12,14},{14,12},{16,18},{18,... | collective-permute-start | bytes 786440 | tf_op jit(solution)/shard_map/ppermute | solution.py:30
  310.7 15.3 %collective-permute-start.46 = (f32[11136]{0:T(1024)S(1)}, f32[11136]{0:T(1024)S(1)}, u32[]{:S(2)}, u32[]{:S(2)}) collective-permute-start(f32[11136]{0:T(1024)S(1)} %pad_maximum_fusion.18), channel_id=1, source_target_pairs={{0,1},{1,0},{2,3},{3,2},{4,5},{5,4},{6,7},{7,6},{8,9},{9,8},{10,11... | collective-permute-start | bytes 133640 | tf_op jit(solution)/shard_map/ppermute | solution.py:25
  324.1 45.5 %collective-permute-start.44 = (bf16[16,256,128]{2,1,0:T(8,128)(2,1)S(1)}, bf16[16,256,128]{2,1,0:T(8,128)(2,1)}, u32[]{:S(2)}, u32[]{:S(2)}) collective-permute-start(bf16[16,256,128]{2,1,0:T(8,128)(2,1)S(1)} %get-tuple-element.77), channel_id=1, source_target_pairs={{0,1},{1,0},{2,3},{3,2},{4,5},{5,4},{6,7},{7,6},{8,9},{9,8},{10,11... | collective-permute-start | bytes 3145736 | tf_op jit(solution)/shard_map/ppermute | solution.py:25
  324.2 39.6 %collective-permute-start.36 = (bf16[256,2048]{1,0:T(8,128)(2,1)}, bf16[256,2048]{1,0:T(8,128)(2,1)}, u32[]{:S(2)}, u32[]{:S(2)}) collective-permute-start(bf16[256,2048]{1,0:T(8,128)(2,1)} %get-tuple-element.70), channel_id=1, source_target_pairs={{0,2},{2,0},{4,6},{6,4},{8,10},{10,8},{12,14},{14,12},{16,18},{18,... | collective-permute-start | bytes 3145736 | tf_op jit(solution)/shard_map/ppermute | solution.py:30
  326.0 40.2 %collective-permute-start.38 = (bf16[256,2048]{1,0:T(8,128)(2,1)}, bf16[256,2048]{1,0:T(8,128)(2,1)}, u32[]{:S(2)}, u32[]{:S(2)}) collective-permute-start(bf16[256,2048]{1,0:T(8,128)(2,1)} %get-tuple-element.72), channel_id=1, source_target_pairs={{0,4},{2,6},{4,0},{6,2},{8,12},{10,14},{12,8},{14,10},{16,20},{18,... | collective-permute-start | bytes 3145736 | tf_op jit(solution)/shard_map/ppermute | solution.py:30
  329.6 21.3 %all-to-all-start.4 = ((f32[16,1,960]{2,1,0:T(1,128)}), f32[16,1,960]{2,1,0:T(1,128)S(1)}, u32[]{:S(2)}, u32[]{:S(2)}) async-start(f32[16,1,960]{2,1,0:T(1,128)} %all_to_all.28), calls=%async_computation.4 | async-start | bytes 131072 | tf_op jit(solution)/shard_map/all_to_all | solution.py:1152
  334.9 156.2 %copy-start.39 = (f32[16,8]{0,1:T(8,128)}, f32[16,8]{0,1:T(8,128)S(1)}, u32[]{:S(2)}) copy-start(f32[16,8]{0,1:T(8,128)S(1)} %copy.144) | copy-start | bytes 1540
  350.9 42.6 %all-to-all-start.5 = ((bf16[16,128,256]{2,1,0:T(8,128)(2,1)}), bf16[16,128,256]{2,1,0:T(8,128)(2,1)}, u32[]{:S(2)}, u32[]{:S(2)}) async-start(bf16[16,128,256]{2,1,0:T(8,128)(2,1)} %bitcast.65), calls=%async_computation.5 | async-start | bytes 2097152 | tf_op jit(solution)/shard_map/all_to_all | solution.py:1022
  360.6 20.0 %collective-permute-start.23 = (bf16[128,2048]{1,0:T(8,128)(2,1)S(1)}, bf16[128,2048]{1,0:T(8,128)(2,1)S(1)}, u32[]{:S(2)}, u32[]{:S(2)}) collective-permute-start(bf16[128,2048]{1,0:T(8,128)(2,1)S(1)} %fusion.9), channel_id=1, source_target_pairs={{0,4},{2,6},{4,0},{6,2},{8,12},{10,14},{12,8},{14,10},{16,20},{18,... | collective-permute-start | bytes 1572872 | tf_op jit(solution)/shard_map/ppermute | solution.py:30
  363.4 19.1 %collective-permute-start.25 = (bf16[128,2048]{1,0:T(8,128)(2,1)S(1)}, bf16[128,2048]{1,0:T(8,128)(2,1)S(1)}, u32[]{:S(2)}, u32[]{:S(2)}) collective-permute-start(bf16[128,2048]{1,0:T(8,128)(2,1)S(1)} %fusion.7), channel_id=1, source_target_pairs={{0,2},{2,0},{4,6},{6,4},{8,10},{10,8},{12,14},{14,12},{16,18},{18,... | collective-permute-start | bytes 1572872 | tf_op jit(solution)/shard_map/ppermute | solution.py:30
  365.6 26.9 %collective-permute-start.37 = (bf16[128,2048]{1,0:T(8,128)(2,1)S(1)}, bf16[128,2048]{1,0:T(8,128)(2,1)S(1)}, u32[]{:S(2)}, u32[]{:S(2)}) collective-permute-start(bf16[128,2048]{1,0:T(8,128)(2,1)S(1)} %fusion.5), channel_id=1, source_target_pairs={{0,4},{2,6},{4,0},{6,2},{8,12},{10,14},{12,8},{14,10},{16,20},{18,... | collective-permute-start | bytes 1572872 | tf_op jit(solution)/shard_map/ppermute | solution.py:30
  368.6 31.7 %collective-permute-start.39 = (bf16[128,2048]{1,0:T(8,128)(2,1)}, bf16[128,2048]{1,0:T(8,128)(2,1)}, u32[]{:S(2)}, u32[]{:S(2)}) collective-permute-start(bf16[128,2048]{1,0:T(8,128)(2,1)} %fusion.3), channel_id=1, source_target_pairs={{0,2},{2,0},{4,6},{6,4},{8,10},{10,8},{12,14},{14,12},{16,18},{18,... | collective-permute-start | bytes 1572872 | tf_op jit(solution)/shard_map/ppermute | solution.py:30
  384.8 70.2 %collective-permute-start.26 = (bf16[64,2048]{1,0:T(8,128)(2,1)}, bf16[64,2048]{1,0:T(8,128)(2,1)}, u32[]{:S(2)}, u32[]{:S(2)}) collective-permute-start(bf16[64,2048]{1,0:T(8,128)(2,1)} %pad_maximum_fusion.10), channel_id=1, source_target_pairs={{0,8},{2,10},{4,12},{6,14},{8,0},{10,2},{12,4},{14,6},{16,24},{18,... | collective-permute-start | bytes 786440 | tf_op jit(solution)/shard_map/ppermute | solution.py:30
  387.8 67.3 %collective-permute-start.27 = (bf16[64,2048]{1,0:T(8,128)(2,1)}, bf16[64,2048]{1,0:T(8,128)(2,1)}, u32[]{:S(2)}, u32[]{:S(2)}) collective-permute-start(bf16[64,2048]{1,0:T(8,128)(2,1)} %pad_maximum_fusion.11), channel_id=1, source_target_pairs={{0,16},{2,18},{4,20},{6,22},{8,24},{10,26},{12,28},{14,30},{16,0},... | collective-permute-start | bytes 786440 | tf_op jit(solution)/shard_map/ppermute | solution.py:30
  393.5 30.9 %all-to-all-start.6 = ((bf16[16,256,128]{2,1,0:T(8,128)(2,1)}), bf16[16,256,128]{2,1,0:T(8,128)(2,1)S(1)}, u32[]{:S(2)}, u32[]{:S(2)}) async-start(bf16[16,256,128]{2,1,0:T(8,128)(2,1)} %bitcast.145), calls=%async_computation.6 | async-start | bytes 2097152 | tf_op jit(solution)/shard_map/all_to_all | solution.py:1020
  402.7 39.8 %collective-permute-start.40 = (bf16[64,2048]{1,0:T(8,128)(2,1)}, bf16[64,2048]{1,0:T(8,128)(2,1)S(1)}, u32[]{:S(2)}, u32[]{:S(2)}) collective-permute-start(bf16[64,2048]{1,0:T(8,128)(2,1)} %pad_maximum_fusion.13), channel_id=1, source_target_pairs={{0,8},{2,10},{4,12},{6,14},{8,0},{10,2},{12,4},{14,6},{16,24},{18,... | collective-permute-start | bytes 786440 | tf_op jit(solution)/shard_map/ppermute | solution.py:30
  403.7 40.0 %collective-permute-start.41 = (bf16[64,2048]{1,0:T(8,128)(2,1)}, bf16[64,2048]{1,0:T(8,128)(2,1)S(1)}, u32[]{:S(2)}, u32[]{:S(2)}) collective-permute-start(bf16[64,2048]{1,0:T(8,128)(2,1)} %pad_maximum_fusion.14), channel_id=1, source_target_pairs={{0,16},{2,18},{4,20},{6,22},{8,24},{10,26},{12,28},{14,30},{16,0},... | collective-permute-start | bytes 786440 | tf_op jit(solution)/shard_map/ppermute | solution.py:30
  406.5 48.2 %collective-permute-start.42 = (bf16[64,2048]{1,0:T(8,128)(2,1)}, bf16[64,2048]{1,0:T(8,128)(2,1)S(1)}, u32[]{:S(2)}, u32[]{:S(2)}) collective-permute-start(bf16[64,2048]{1,0:T(8,128)(2,1)} %pad_maximum_fusion.15), channel_id=1, source_target_pairs={{0,24},{2,26},{4,28},{6,30},{8,16},{10,18},{12,20},{14,22},{16,8},... | collective-permute-start | bytes 786440 | tf_op jit(solution)/shard_map/ppermute | solution.py:30
  424.4 61.4 %all-to-all-start.3 = ((bf16[16,256,128]{2,1,0:T(8,128)(2,1)}), bf16[16,256,128]{2,1,0:T(8,128)(2,1)S(1)}, u32[]{:S(2)}, u32[]{:S(2)}) async-start(bf16[16,256,128]{2,1,0:T(8,128)(2,1)} %add_convert_fusion), calls=%async_computation.3 | async-start | bytes 2097152 | tf_op jit(solution)/shard_map/all_to_all | solution.py:1120
  440.9 39.1 %copy-start.23 = (bf16[128,2048]{1,0:T(8,128)(2,1)S(1)}, bf16[128,2048]{1,0:T(8,128)(2,1)}, u32[]{:S(2)}) copy-start(bf16[128,2048]{1,0:T(8,128)(2,1)} %param.27) | copy-start | bytes 1572868
  440.9 39.1 %copy-start.32 = (bf16[32,2048]{1,0:T(8,128)(2,1)S(1)}, bf16[32,2048]{1,0:T(8,128)(2,1)}, u32[]{:S(2)}) copy-start(bf16[32,2048]{1,0:T(8,128)(2,1)} %get-tuple-element.160) | copy-start | bytes 393220
  441.0 39.1 %copy-start.33 = (bf16[32,2048]{1,0:T(8,128)(2,1)S(1)}, bf16[32,2048]{1,0:T(8,128)(2,1)}, u32[]{:S(2)}) copy-start(bf16[32,2048]{1,0:T(8,128)(2,1)} %get-tuple-element.164) | copy-start | bytes 393220
  442.5 37.5 %collective-permute-start.28 = (bf16[64,2048]{1,0:T(8,128)(2,1)S(1)}, bf16[64,2048]{1,0:T(8,128)(2,1)S(1)}, u32[]{:S(2)}, u32[]{:S(2)}) collective-permute-start(bf16[64,2048]{1,0:T(8,128)(2,1)S(1)} %copy-done.35), channel_id=1, source_target_pairs={{0,24},{2,26},{4,28},{6,30},{8,16},{10,18},{12,20},{14,22},{16,8},... | collective-permute-start | bytes 786440 | tf_op jit(solution)/shard_map/ppermute | solution.py:30
  481.6 4.2 collective-permute-start.43
  485.8 1.5 collective-permute-start.29
  485.9 3.1 collective-permute-start.45
  (43 other events, 269.5 us)

commit v3 on v1

--- a/solution.py
+++ b/solution.py
@@ -3,6 +3,8 @@
 import jax
 import jax.numpy as jnp
 from jax import lax
+from jax.experimental import pallas as pl
+from jax.experimental.pallas import tpu as pltpu
 from jax.sharding import PartitionSpec as P
 
 HEADS = 8
@@ -59,7 +61,7 @@
     )
 
 
-def body(
+def general_body(
     tokens,
     w_qkv,
     b_qkv,
@@ -271,7 +273,8 @@
     mine = jnp.concatenate([queries, keys, linear[:, 2]], axis=1).astype(BF)
 
     def align(value, r):
-        return value.reshape((size_x, -1) + value.shape[1:])[jnp.arange(size_x) ^ r].reshape(value.shape)
+        slabs = value.reshape((size_x, -1) + value.shape[1:])
+        return jnp.stack([slabs[x ^ r] for x in range(size_x)]).reshape(value.shape)
 
     pieces = [mine] + [align(from_peer(mine, r), r) for r in masks_x]
     pieces = jnp.stack(pieces).reshape(group, count, 3, columns)
@@ -455,6 +458,940 @@
     )
 
 
+VMEM = pl.BlockSpec(memory_space=pltpu.VMEM)
+SMEM = pl.BlockSpec(memory_space=pltpu.SMEM)
+GRANT = 28 * 1024 * 1024
+MARK_COS, MARK_SIN = 32, 64
+COST = 1.0
+WIDE = 256
+
+
+def run_kernel(kernel, outs, grid=None, ins=None, out_specs=None, scratch=(), flops=0, moved=0, name=None):
+    outs = [jax.ShapeDtypeStruct(shape, kind) for shape, kind in outs]
+    single = len(outs) == 1
+    out_specs = out_specs or [VMEM] * len(outs)
+    extra = {} if grid is None else {"grid": grid}
+    return pl.pallas_call(
+        kernel,
+        out_shape=outs[0] if single else outs,
+        in_specs=ins,
+        out_specs=out_specs[0] if single else out_specs,
+        scratch_shapes=list(scratch),
+        compiler_params=pltpu.CompilerParams(vmem_limit_bytes=GRANT),
+        cost_estimate=pl.CostEstimate(flops=int(flops * COST), bytes_accessed=int(moved * COST), transcendentals=0),
+        name=name,
+        **extra,
+    )
+
+
+def chunk_bits(half, at, lanes):
+    z = at % lanes
+    low, high = (at // lanes) % 2, at // (2 * lanes)
+    x, y = (high, low) if half == 0 else (low, high)
+    return x + 2 * y + 4 * z
+
+
+class Rows:
+    def __init__(self, blocks, cores, rows):
+        self.blocks, self.rows = blocks, rows
+        self.part = rows // cores
+        self.chunk = self.part // 2
+        self.half = blocks * self.chunk
+        self.count = 2 * self.half
+        self.share = self.half
+        self.sizes_z = blocks // 4
+
+    def natural(self, me, core, half, at):
+        block = me ^ chunk_bits(half, at, self.sizes_z)
+        return block * self.rows + core * self.part + half * self.chunk
+
+    def x_rows(self, x):
+        h, q = self.half // 2, self.half // 4
+        return [
+            (x * h, 0, h),
+            (self.half + x * q, h, q),
+            (self.half + 2 * q + x * q, h + q, q),
+        ]
+
+    def pairs(self):
+        mine, peer = self.x_rows(0), self.x_rows(1)
+        both = [(a[0], b[0], a[2]) for a, b in zip(mine, peer)]
+        return both + [(b, a, n) for a, b, n in both]
+
+
+def nn(left, right):
+    return lax.dot_general(left, right, (((1,), (0,)), ((), ())), preferred_element_type=F32)
+
+
+def nt(left, right):
+    return lax.dot_general(left, right, (((1,), (1,)), ((), ())), preferred_element_type=F32)
+
+
+def lane_of(shape):
+    return lax.broadcasted_iota(jnp.int32, shape, len(shape) - 1)
+
+
+def turn_lanes(values, table, active, sign):
+    lane = lane_of(values.shape)
+    first, second = lane < ROT // 2, lane < ROT
+    cosine = jnp.where(first, pltpu.roll(table, 128 - MARK_COS, 1), table)
+    sine_first = pltpu.roll(table, 128 - MARK_SIN, 1)
+    sine_second = pltpu.roll(table, 128 - MARK_SIN + ROT // 2, 1)
+    sine = jnp.where(first, -sine_first, sine_second) * sign
+    cosine = jnp.where(second & active, cosine, 1.0)
+    sine = jnp.where(second & active, sine, 0.0)
+    partner = jnp.where(first, pltpu.roll(values, 128 - ROT // 2, 1), pltpu.roll(values, ROT // 2, 1))
+    return values * cosine + partner * sine
+
+
+def deal_kernel(cut, blocks, ids, speed, here, there, triple, near, marks, norms, shifts, lines, flip):
+    me, core = ids[0], ids[1]
+    width = lines.shape[2]
+    for source in range(blocks):
+        for who, ref in ((core, here), (1 - core, there)):
+            at = pl.multiple_of(source * 2 * cut + who * cut, cut)
+            for s in range(3):
+                triple[pl.ds(at, cut), s * 128 : (s + 1) * 128] = ref[source, s * cut : (s + 1) * cut, :]
+            at = pl.multiple_of(who * cut, cut)
+            near[pl.ds(at, cut), source * 128 : (source + 1) * 128] = ref[source, 3 * cut : 4 * cut, :]
+
+    lanes = 128 // blocks
+    row = lax.broadcasted_iota(jnp.int32, (128, width), 0)
+    lane = lane_of((128, width))
+    deal = ((row // lanes == lane // 128) & (row % lanes == lane % lanes)).astype(BF)
+    lane = lane_of((16, width)) % 128 // lanes
+    flip[...] = jnp.zeros_like(flip)
+    for which, ref in enumerate((here, there)):
+        total = jnp.zeros((16, width), F32)
+        for source in range(blocks):
+            small = ref[source, 4 * cut : 4 * cut + 16, :]
+            total = total + jnp.where(lane == source, nn(small, deal), 0.0)
+            if which == 0:
+                small = small.astype(F32)
+                flip[source : source + 1, :] = small[10:11] * 256.0 + small[11:12]
+                flip[blocks + source : blocks + source + 1, :] = small[12:13]
+        lines[which] = total
+    norms[:4, :] = lines[0, :4, :]
+    norms[4:5, :] = lines[0, 4:5, :] + lines[0, 5:6, :]
+    norms[5:, :] = jnp.zeros((3, width), F32)
+    shifts[...] = jnp.zeros_like(shifts)
+    heads = blocks // 2
+    ours = me // heads == core
+    for s in range(3):
+        at = pl.multiple_of((me % heads + s % 2 * heads) * 128, 128)
+        both = [lines[k, 6 + s // 2 : 7 + s // 2, pl.ds(at, 128)] for k in (0, 1)]
+        shifts[0:1, s * 128 : (s + 1) * 128] = jnp.where(ours, both[0], both[1])
+    units = 2 * width // blocks
+    at = pl.multiple_of(me % heads * units, units)
+    for k in (0, 1):
+        shifts[1:2, k * units : (k + 1) * units] = lines[k, pl.ds(8 + me // heads, 1), pl.ds(at, units)]
+
+    turned = flip[...].T
+    lane = lane_of((128, 128))
+    row = lax.broadcasted_iota(jnp.int32, (128, 128), 0).astype(F32)
+    for q in range(blocks // 4):
+        place = jnp.zeros((128, 128), F32)
+        for g in range(4):
+            b = 4 * q + g
+            place = jnp.where(lane // 32 == g, row + b * 128.0 - turned[:, b : b + 1], place)
+        angle = place * speed[0:1, :]
+        cosine, sine = jnp.cos(angle), jnp.sin(angle)
+        for g in range(4):
+            b = 4 * q + g
+            index = row + b * 128.0
+            table = jnp.where(lane == 0, index, 0.0)
+            table = jnp.where(lane == 1, jnp.where(turned[:, blocks + b : blocks + b + 1] == 1.0, index, -1.0), table)
+            table = jnp.where(lane == 2, turned[:, b : b + 1], table)
+            table = jnp.where(lane // 32 == 1, pltpu.roll(cosine, (MARK_COS - g * 32) % 128, 1), table)
+            table = jnp.where(lane // 32 == 2, pltpu.roll(sine, (MARK_SIN - g * 32) % 128, 1), table)
+            marks[b * 128 : (b + 1) * 128, :] = table
+
+
+def feed_deal_kernel(blocks, units, expand, shrink, out):
+    for k in range(blocks):
+        out[k, :units, :] = expand[:, k * units : (k + 1) * units].T
+        out[k, units:, :] = shrink[k * units : (k + 1) * units, :]
+
+
+def pick(i, refs, tile):
+    for k, ref in enumerate(refs):
+
+        @pl.when(i == k)
+        def _(ref=ref):
+            tile[...] = ref[...]
+
+
+def norm_kernel(r, ids, t0, t1, t2, t3, norms, weight, shifts, marks, feed, stats, mine, tile, table, attend):
+    i = pl.program_id(0)
+    me, core = ids[0], ids[1]
+    pick(i, (t0, t1, t2, t3), tile)
+    for half in (0, 1):
+
+        @pl.when(i // 2 == half)
+        def _(half=half):
+            for q in range(8):
+                at = r.natural(me, core, half, (i % 2) * 8 + q)
+                table[q * r.chunk : (q + 1) * r.chunk, :] = marks[pl.ds(pl.multiple_of(at, r.chunk), r.chunk), :]
+
+    step = 16
+    lane = lane_of((step, 128))
+
+    @pl.loop(0, tile.shape[0] // step, unroll=4)
+    def _(j):
+        rows = pl.ds(pl.multiple_of(j * step, step), step)
+        values = tile[rows, :].astype(F32)
+        mean = jnp.mean(values, axis=-1, keepdims=True)
+        center = values - mean
+        inverse = lax.rsqrt(jnp.mean(center * center, axis=-1, keepdims=True) + EPSILON)
+        value = center * inverse
+        attend[rows, :] = (value * norms[0:1, :] + norms[2:3, :]).astype(BF)
+        feed[rows, :] = (value * norms[1:2, :] + norms[3:4, :]).astype(BF)
+        stats[rows, :] = jnp.where(lane == 0, mean, inverse)
+
+    linear = nn(attend[...], weight[...]) + shifts[0:1, :384]
+    active = me % 2 == 0
+    for s in (0, 1):
+        cols = slice(s * 128, (s + 1) * 128)
+        mine[:, cols] = turn_lanes(linear[:, cols], table[...], active, 1.0).astype(BF)
+    mine[:, 256:] = linear[:, 256:].astype(BF)
+
+
+def normal_of(tile, stats):
+    return (tile.astype(F32) - stats[:, 0:1]) * stats[:, 1:2]
+
+
+def gather_columns(r, out, low, high, column):
+    cols = slice(column * 128, (column + 1) * 128)
+    out[:, :128] = low[:, cols]
+    for here, there, size in r.pairs():
+        out[here : here + size, 128:] = high[there : there + size, cols]
+
+
+def gather_marks(r, ids, marks, table, line):
+    me, core = ids[0], ids[1]
+    for w in (0, 1):
+        who = core if w == 0 else 1 - core
+        for half in (0, 1):
+            for q in range(16):
+                at = r.natural(me, who, half, q)
+                to = w * r.count + half * r.half + q * r.chunk
+                table[to : to + r.chunk, :] = marks[pl.ds(pl.multiple_of(at, r.chunk), r.chunk), :]
+    for b in range(2 * r.count // 128):
+        line[:, b * 128 : (b + 1) * 128] = table[b * 128 : (b + 1) * 128, :].T[:8, :]
+
+
+def own_rows(r, out, ref, columns=slice(None)):
+    for row, place, size in r.x_rows(0):
+        out[place : place + size, :] = ref[row : row + size, columns]
+
+
+def query_kernel(r, scale, ids, a00, a01, a10, a11, grads, marks, attended, keep, send, lines,
+                 keys, values, queries, pushes, table, line, mine):
+    i = pl.program_id(0)
+    me = ids[0]
+    count, tile = r.count, r.share // 2
+
+    @pl.when(i == 0)
+    def _():
+        gather_columns(r, keys.at[:count], a00, a01, 1)
+        gather_columns(r, keys.at[count:], a10, a11, 1)
+        gather_columns(r, values.at[:count], a00, a01, 2)
+        gather_columns(r, values.at[count:], a10, a11, 2)
+        for row, place, size in r.x_rows(0):
+            queries[place : place + size, :128] = a00[row : row + size, :128]
+        for (row, place, size), (there, _, _) in zip(r.x_rows(0), r.x_rows(1)):
+            queries[place : place + size, 128:] = a01[there : there + size, :128]
+        own_rows(r, pushes, grads)
+        gather_marks(r, ids, marks, table, line)
+        own_rows(r, mine, table.at[:count])
+
+    rows = pl.ds(pl.multiple_of(i * tile, tile), tile)
+    mark = mine[rows, :]
+    q_at, q_start = mark[:, 0:1], mark[:, 2:3]
+    k_at, k_live = line[0:1, :], line[1:2, :]
+    mask = ((k_live >= q_start) & (k_at <= q_at)) | (k_at == q_at)
+    scores = jnp.where(mask, nt(queries[rows, :], keys[...]) * scale, NEGATIVE)
+    top = jnp.max(scores, axis=-1, keepdims=True)
+    weight = jnp.where(mask, jnp.exp(scores - top), 0.0)
+    total = jnp.sum(weight, axis=-1, keepdims=True)
+    prob = weight * (1.0 / total)
+    result = nn(prob.astype(BF), values[...])
+    grad = pushes[rows, :]
+    delta = jnp.sum(grad.astype(F32) * result, axis=-1, keepdims=True)
+    slope = (prob * (nt(grad, values[...]) - delta)).astype(BF)
+    back = nn(slope, keys[...]) * scale
+    result = result.astype(BF)
+    attended[...] = result
+    for k, ref in enumerate((keep, send)):
+        cols = slice(k * 128, (k + 1) * 128)
+        ref[:, :128] = turn_lanes(back[:, cols], mark, me % 2 == k, -1.0).astype(BF)
+        ref[:, 128:] = result[:, cols]
+    lane = lane_of((tile, 128))
+    both = jnp.where(lane == 0, top + jnp.log(total), jnp.where(lane == 1, delta, 0.0))
+    for b in range(tile // 128):
+        lines[:, b * 128 : (b + 1) * 128] = both[b * 128 : (b + 1) * 128, :].T[:8, :]
+
+
+def key_kernel(r, scale, ids, a00, a01, a10, a11, grads, other_grads, l00, l01, l10, l11, marks, keep, send,
+               queries, pushes, keys, values, table, line, mine, tops):
+    i = pl.program_id(0)
+    me = ids[0]
+    count, tile = r.count, r.share // 2
+
+    @pl.when(i == 0)
+    def _():
+        gather_columns(r, queries.at[:count], a00, a01, 0)
+        gather_columns(r, queries.at[count:], a10, a11, 0)
+        pushes[:count, :] = grads[...]
+        pushes[count:, :] = other_grads[...]
+        for k, out in ((1, keys), (2, values)):
+            cols = slice(k * 128, (k + 1) * 128)
+            for row, place, size in r.x_rows(0):
+                out[place : place + size, :128] = a00[row : row + size, cols]
+            for (row, place, size), (there, _, _) in zip(r.x_rows(0), r.x_rows(1)):
+                out[place : place + size, 128:] = a01[there : there + size, cols]
+        gather_marks(r, ids, marks, table, line)
+        own_rows(r, mine, table.at[:count])
+        for base, low, high in ((0, l00, l01), (count, l10, l11)):
+            for x, ref in ((0, low), (1, high)):
+                for row, place, size in r.x_rows(x):
+                    tops[:, base + row : base + row + size] = ref[:, place : place + size]
+
+    rows = pl.ds(pl.multiple_of(i * tile, tile), tile)
+    mark = mine[rows, :]
+    k_at, k_live = mark[:, 0:1], mark[:, 1:2]
+    q_at, q_start = line[0:1, :], line[2:3, :]
+    mask = ((k_live >= q_start) & (k_at <= q_at)) | (k_at == q_at)
+    scores = nt(keys[rows, :], queries[...]) * scale
+    prob = jnp.where(mask, jnp.exp(scores - tops[0:1, :]), 0.0)
+    grad_values = nn(prob.astype(BF), pushes[...])
+    slope = (prob * (nt(values[rows, :], pushes[...]) - tops[1:2, :])).astype(BF)
+    back = nn(slope, queries[...]) * scale
+    for k, ref in enumerate((keep, send)):
+        cols = slice(k * 128, (k + 1) * 128)
+        ref[:, :128] = turn_lanes(back[:, cols], mark, me % 2 == k, -1.0).astype(BF)
+        ref[:, 128:] = grad_values[:, cols].astype(BF)
+
+
+def feed_kernel(units, blocks, normed, c0, c1, c2, c3, mine, other, shifts, near, peer,
+                act, grad, act_turned, grad_turned, expand, shrink, sums, pushes, push_sums, tile, turned):
+    i = pl.program_id(0)
+
+    @pl.when(i == 0)
+    def _():
+        sums[...] = jnp.zeros_like(sums)
+        push_sums[...] = jnp.zeros_like(push_sums)
+        turned[:, :128] = near[...].T
+        turned[:, 128:] = peer[...].T
+        for source in range(blocks):
+            cols = slice(source * 128, (source + 1) * 128)
+            for at, ref in ((0, mine), (units, other)):
+                expand[at : at + units, cols] = ref[source, :units, :]
+                shrink[at : at + units, cols] = ref[source, units:, :]
+
+    pick(i, (c0, c1, c2, c3), tile)
+    pushes[...] = nn(tile[...], turned[...]).astype(BF)
+    expanded = nt(normed[...], expand[...]) + shifts[1:2, : 2 * units]
+    activated, bend = gelu_and_slope(expanded)
+    activated = activated.astype(BF)
+    act[...] = activated
+    act_turned[...] = activated.T
+    slope = (bend * nt(tile[...], shrink[...])).astype(BF)
+    grad[...] = slope
+    grad_turned[...] = slope.T
+    sums[0:1, :] += jnp.sum(slope.astype(F32), axis=0, keepdims=True)
+    push_sums[0:1, :] += jnp.sum(tile[...].astype(F32), axis=0, keepdims=True)
+
+
+def by_quarter(left, quarters):
+    size = quarters[0].shape[0]
+    total = nn(left[:, :size], quarters[0][...])
+    for k in range(1, len(quarters)):
+        total = total + nn(left[:, k * size : (k + 1) * size], quarters[k][...])
+    return total
+
+
+def outer_kernel(units, grad_turned, act_turned, normed, c0, c1, c2, c3, *rest):
+    out = rest[-1]
+    for k in (0, 1):
+        result = by_quarter(act_turned, (c0, c1, c2, c3)) if k else nn(grad_turned[...], normed[...])
+        for b in range(WIDE // 128):
+            lanes = slice(b * 128, (b + 1) * 128)
+            rows = slice(k * units, (k + 1) * units)
+            part = result[:, lanes]
+            if len(rest) > 1:
+                part = part + rest[0][b, rows, :].astype(F32)
+            out[b, rows, :] = part.astype(BF)
+
+
+def branch_kernel(r, act, attended, shrink, near, peer, o0, o1, o2, o3):
+    outs = (o0, o1, o2, o3)
+    size = r.count // 4
+    extra = nn(attended[:, :128], near[...]) + nn(attended[:, 128:], peer[...])
+    for k in range(4):
+        result = nn(act[k * size : (k + 1) * size, :], shrink[...])
+        covered = False
+        for row, place, length in r.x_rows(0):
+            if row == k * size:
+                outs[k][:length, :] = (result[:length] + extra[place : place + length]).astype(BF)
+                if length < size:
+                    outs[k][length:, :] = result[length:].astype(BF)
+                covered = True
+        if not covered:
+            outs[k][...] = result.astype(BF)
+
+
+def inputs_kernel(r, keep1, keep2, got1, got2, grad, t0, t1, t2, t3, stats, triple, expand, gains, cotangent_sums, unit_sums,
+                  o0, o1, o2, o3, linear, near, sums, line_sums):
+    j = pl.program_id(0)
+    size = r.count // 4
+
+    @pl.when(j == 0)
+    def _():
+        for x, one, two in ((0, keep1, keep2), (1, got1, got2)):
+            for row, place, length in r.x_rows(x):
+                linear[row : row + length, :128] = one[place : place + length, :128]
+                linear[row : row + length, 128:] = two[place : place + length, :]
+                near[row : row + length, :] = one[place : place + length, 128:]
+        line_sums[...] = jnp.zeros_like(line_sums)
+        line_sums[0:1, :384] = jnp.sum(linear[...].astype(F32), axis=0, keepdims=True)
+
+    sums[...] = jnp.zeros_like(sums)
+    for k, (ref, tokens) in enumerate(((o0, t0), (o1, t1), (o2, t2), (o3, t3))):
+        rows = slice(k * size, (k + 1) * size)
+        attend = nt(linear[rows, :], triple[...])
+        feed = nn(grad[rows, :], expand[...])
+        value = normal_of(tokens[...], stats[rows, :])
+        sums[0:1, :] += jnp.sum(value * attend, axis=0, keepdims=True)
+        sums[1:2, :] += jnp.sum(value * feed, axis=0, keepdims=True)
+        sums[2:3, :] += jnp.sum(attend, axis=0, keepdims=True)
+        sums[3:4, :] += jnp.sum(feed, axis=0, keepdims=True)
+        ref[...] = (gains[0:1, :] * attend + gains[1:2, :] * feed).astype(BF)
+    sums[4:5, :] = cotangent_sums[0:1, :]
+    for k in (0, 1):
+
+        @pl.when(j == k)
+        def _(k=k):
+            sums[5:6, :] = line_sums[0:1, k * WIDE : (k + 1) * WIDE]
+            sums[6:7, :] = unit_sums[0:1, k * WIDE : (k + 1) * WIDE]
+
+
+def small_kernel(blocks, units, ids, mine, other, out, lines):
+    me, core = ids[0], ids[1]
+    width = lines.shape[1]
+    heads, lanes = blocks // 2, 128 // blocks
+    lines[...] = jnp.zeros_like(lines)
+    lines[0:5, :] = mine[0:5, :] + other[0:5, :]
+    ours = jnp.where(me // heads == core, 1.0, 0.0)
+    for s in range(3):
+        at = pl.multiple_of((me % heads + s % 2 * heads) * 128, 128)
+        cols = slice(s * 128, (s + 1) * 128)
+        lines[6 + s // 2 : 7 + s // 2, pl.ds(at, 128)] = (mine[5:6, cols] + other[5:6, cols]) * ours
+    at = pl.multiple_of(me % heads * units, units)
+    total = mine[6:7, :units] + other[6:7, units : 2 * units]
+    for k in (0, 1):
+
+        @pl.when(me // heads == k)
+        def _(k=k):
+            lines[8 + k : 9 + k, pl.ds(at, units)] = total
+
+    row = lax.broadcasted_iota(jnp.int32, (width, 128), 0)
+    lane = lane_of((width, 128))
+    deal = ((lane // lanes == row // 128) & (lane % lanes == row % lanes)).astype(BF)
+    value = lines[...]
+    high = value.astype(BF)
+    low = (value - high.astype(F32)).astype(BF)
+    lane = lane_of((16, width)) % 128 // lanes
+    line = lax.broadcasted_iota(jnp.int32, (16, width), 0)
+    for b in range(blocks):
+        sent = (lane == b) & ((line != 4) | (me == b))
+        for k, part in enumerate((high, low)):
+            part = jnp.where(sent, part.astype(F32), 0.0).astype(BF)
+            out[b, k * 16 : (k + 1) * 16, :] = nn(part, deal).astype(BF)
+
+
+def fold_kernel(keep1, got1, keep2, got2, one, one_send, two, two_send):
+    for keep, got, outs in ((keep1, got1, (one, one_send)), (keep2, got2, (two, two_send))):
+        half = outs[0].shape[0]
+        for k, out in enumerate(outs):
+            rows = slice(k * half, (k + 1) * half)
+            out[...] = (keep[rows, :].astype(F32) + got[rows, :].astype(F32)).astype(BF)
+
+
+def by_z_kernel(chunk, one, one_got, two, two_got, *outs):
+    for half, (mine, got) in enumerate(((one, one_got), (two, two_got))):
+        for z, out in enumerate(outs):
+            rows = slice(z * chunk, (z + 1) * chunk)
+            value = mine[rows, :].astype(F32) + got[rows, :].astype(F32)
+            out[half * chunk : (half + 1) * chunk, :] = value.astype(BF)
+
+
+def line_outer_kernel(cut, ids, linear, near, t0, t1, t2, t3, stats, norms, c0, c1, c2, c3,
+                      keep, give, turned, near_turned, normed, result):
+    core = ids[1]
+
+    @pl.when(pl.program_id(0) == 0)
+    def _():
+        turned[...] = linear[...].T
+        near_turned[...] = near[...].T
+
+    size = t0.shape[0]
+    for k, tokens in enumerate((t0, t1, t2, t3)):
+        rows = slice(k * size, (k + 1) * size)
+        value = normal_of(tokens[...], stats[rows, :])
+        normed[rows, :] = (value * norms[0:1, :] + norms[2:3, :]).astype(BF)
+    result[:384, :] = nn(turned[...], normed[...])
+    result[384:, :] = by_quarter(near_turned, (c0, c1, c2, c3))
+    for who, out in ((core, keep), (1 - core, give)):
+        for s in range(4):
+            at = pl.multiple_of(s * 2 * cut + who * cut, cut)
+            for b in range(WIDE // 128):
+                part = result[pl.ds(at, cut), b * 128 : (b + 1) * 128]
+                out[b, s * cut : (s + 1) * cut, :] = part.astype(out.dtype)
+
+
+def unpack_kernel(cut, heads, ids, mine, other, whole, triple, outward, small, pair):
+    core = ids[1]
+    for k in range(heads):
+        for s in range(4):
+            for who, ref in ((core, mine), (1 - core, other)):
+                pair[pl.ds(pl.multiple_of(who * cut, cut), cut), :] = ref[k, s * cut : (s + 1) * cut, :].astype(F32)
+            if s < 3:
+                triple[s, :, k * 128 : (k + 1) * 128] = pair[...].T
+            else:
+                outward[k * 128 : (k + 1) * 128, :] = pair[...]
+    total = jnp.zeros(small.shape, F32)
+    for b in range(2 * heads):
+        for k in (0, 1):
+            at = 4 * cut + 16 * k
+            total = total + whole[b, at : at + 16, :].astype(F32)
+    small[...] = total
+
+
+def feed_unpack_kernel(units, got, expand, shrink):
+    k = pl.program_id(0)
+    expand[...] = got[0, :units, :].astype(F32).T
+    shrink[...] = got[0, units:, :].astype(F32)
+
+
+def join(*values):
+    return lax.optimization_barrier(values)
+
+
+def body(
+    tokens,
+    w_qkv,
+    b_qkv,
+    w_out,
+    b_out,
+    w_in,
+    b_in,
+    w_out2,
+    b_out2,
+    norm_gain,
+    norm_shift,
+    doc_start,
+    live,
+    cotangent,
+):
+    blocks = lax.axis_size("blk")
+    cores = lax.axis_size("tp")
+    me, core = lax.axis_index("blk"), lax.axis_index("tp")
+    ids = jnp.stack([me, core]).astype(jnp.int32)
+    rows, width = tokens.shape
+    depth = w_in.shape[0]
+    r = Rows(blocks, cores, rows)
+    part, count, share = r.part, r.count, r.share
+    quarter = count // 4
+    units = w_in.shape[1] // blocks
+    cut = depth // cores
+    own_heads = HEADS // cores * 2
+    scale = 1.0 / math.sqrt(HEAD)
+    masks_z = [4 * i for i in range(1, blocks // 4)]
+    grid = (width // WIDE,)
+
+    once = pl.Buffered(1)
+
+    def tiled(columns):
+        return pl.BlockSpec((quarter, columns), lambda i: (i, 0))
+
+    def across(lines):
+        return pl.BlockSpec((lines, WIDE), lambda j: (0, j))
+
+    def fixed(value):
+        return pl.BlockSpec(value.shape, lambda i: (0,) * value.ndim, pipeline_mode=once)
+
+    def fixed_shape(*shape):
+        return pl.BlockSpec(shape, lambda i: (0,) * len(shape))
+
+    def packed_rows(value, lines):
+        flat = value.reshape(-1)
+        return jnp.pad(flat, (0, lines * 128 - flat.size)).reshape(lines, 128)
+
+    small = jnp.concatenate(
+        [
+            packed_rows(norm_gain, 2),
+            packed_rows(norm_shift, 2),
+            packed_rows(b_out, 1),
+            packed_rows(b_out2, 1),
+            packed_rows(b_qkv, 2),
+            packed_rows(b_in, 2),
+            jnp.stack([doc_start // 256, doc_start % 256, live]).astype(BF),
+            jnp.zeros((3, 128), BF),
+        ]
+    )
+
+    def over_z(value):
+        return [from_peer(value, mask) for mask in masks_z]
+
+    def halves(pieces):
+        one = jnp.concatenate([value[: r.chunk] for value in pieces])
+        two = jnp.concatenate([value[r.chunk :] for value in pieces])
+        return one, two
+
+    my_tokens = lax.dynamic_slice_in_dim(tokens, core * part, part, 0)
+    my_cotangent = lax.dynamic_slice_in_dim(cotangent, core * part, part, 0)
+    triple = w_qkv.reshape(3, cores, cut, own_heads, 128).transpose(1, 3, 0, 2, 4)
+    triple = triple.reshape(cores, own_heads, 3 * cut, 128)
+    outward = w_out.reshape(own_heads, cores, cut, 128).transpose(1, 0, 2, 3)
+    dealt = jnp.concatenate([triple, outward], axis=2)
+    keep = lax.dynamic_index_in_dim(dealt, core, 0, keepdims=False)
+    give = lax.dynamic_index_in_dim(dealt, 1 - core, 0, keepdims=False)
+    feed_deal = run_kernel(
+        lambda *refs: feed_deal_kernel(blocks, units, *refs),
+        [((blocks, 2 * units, depth), BF)],
+        ins=[VMEM, VMEM],
+        name="feed_deal",
+        moved=4e6,
+    )(w_in, w_out2)
+    tokens_z = join(my_tokens, *over_z(my_tokens))
+    keep, got, feed_deal, my_cotangent, *tokens_z = join(keep, swap_cores(give), feed_deal, my_cotangent, *tokens_z)
+
+    heads_low, heads_high = by_core(core, keep, got)
+    deal = jnp.concatenate(
+        [
+            jnp.concatenate([heads_low, heads_high]),
+            jnp.broadcast_to(small, (blocks,) + small.shape),
+        ],
+        axis=1,
+    )
+    here = lax.all_to_all(deal, "blk", 0, 0, tiled=True)
+    one, two = halves(tokens_z)
+    cotangent_z = over_z(my_cotangent)
+    one, one_y, two, two_x = join(one, from_peer(one, 2), two, from_peer(two, 1))
+
+    one, two = jnp.concatenate([one, one_y]), jnp.concatenate([two, two_x])
+    mine_one, mine_two = halves(join(my_cotangent, *cotangent_z))
+    here, feed_deal, one, one_x, two, two_y, mine_one, mine_y, mine_two, mine_x = join(
+        here,
+        feed_deal,
+        one,
+        from_peer(one, 1),
+        two,
+        from_peer(two, 2),
+        mine_one,
+        from_peer(mine_one, 2),
+        mine_two,
+        from_peer(mine_two, 1),
+    )
+    all_tokens = [one, one_x, two, two_y]
+
+    one, two = jnp.concatenate([mine_one, mine_y]), jnp.concatenate([mine_two, mine_x])
+    here, there = join(here, swap_cores(here))
+    steps = jnp.arange(ROT // 2, dtype=F32)
+    speed = jnp.tile(10000.0 ** (-2.0 * steps / ROT), 4).reshape(1, 128)
+    w_triple, w_near, marks, norms, shifts = run_kernel(
+        lambda *refs: deal_kernel(cut, blocks, *refs),
+        [
+            ((width, 384), BF),
+            ((128, width), BF),
+            ((blocks * rows, 128), F32),
+            ((8, width), F32),
+            ((8, 512), F32),
+        ],
+        ins=[SMEM, VMEM, VMEM, VMEM],
+        scratch=[pltpu.VMEM((2, 16, width), F32), pltpu.VMEM((128, 128), F32)],
+        name="deal",
+        moved=8e6,
+    )(ids, speed, here, there)
+    norms, feed_deal = join(norms, feed_deal)
+    feed_mine = lax.all_to_all(feed_deal, "blk", 0, 0, tiled=True)
+    normed_feed, stats, mine = run_kernel(
+        lambda *refs: norm_kernel(r, *refs),
+        [((count, width), BF), ((count, 128), F32), ((count, 384), BF)],
+        grid=(4,),
+        ins=[SMEM] + [fixed(t) for t in all_tokens] + [fixed(norms), fixed(w_triple), fixed(shifts), fixed(marks)],
+        out_specs=[tiled(width), tiled(128), tiled(384)],
+        scratch=[pltpu.VMEM((quarter, width), BF), pltpu.VMEM((quarter, 128), F32), pltpu.VMEM((quarter, width), BF)],
+        flops=2 * count * width * 384,
+        name="norm",
+        moved=22e6,
+    )(ids, *all_tokens, norms, w_triple, shifts, marks)
+    w_peer = from_peer(w_near, 1)
+    mine, one, one_x, two, two_y = join(mine, one, from_peer(one, 1), two, from_peer(two, 2))
+
+    peer, mine_there = from_peer(mine, 1), swap_cores(mine)
+    all_cotangent = [one, one_x, two, two_y]
+    feed_mine, w_peer, *all_cotangent = join(feed_mine, w_peer, *all_cotangent)
+
+    feed_mine, feed_other = join(feed_mine, swap_cores(feed_mine))
+
+    turned = pl.BlockSpec((2 * units, quarter), lambda i: (0, i))
+    act, grad, act_turned, grad_turned, w_expand, w_shrink, unit_sums, grads, cotangent_sums = run_kernel(
+        lambda *refs: feed_kernel(units, blocks, *refs),
+        [((count, 2 * units), BF)] * 2
+        + [((2 * units, count), BF)] * 2
+        + [((2 * units, width), BF)] * 2
+        + [((8, 2 * units), F32), ((count, 256), BF), ((8, width), F32)],
+        grid=(4,),
+        ins=[tiled(width)]
+        + [fixed(t) for t in all_cotangent]
+        + [fixed(feed_mine), fixed(feed_mine), fixed(shifts), fixed(w_near), fixed(w_peer)],
+        out_specs=[tiled(2 * units)] * 2
+        + [turned] * 2
+        + [fixed_shape(2 * units, width)] * 2
+        + [fixed_shape(8, 2 * units), tiled(256), fixed_shape(8, width)],
+        scratch=[pltpu.VMEM((quarter, width), BF), pltpu.VMEM((width, 256), BF)],
+        flops=8 * count * width * units,
+        name="feed",
+        moved=20e6,
+    )(normed_feed, *all_cotangent, feed_mine, feed_other, shifts, w_near, w_peer)
+    mine, peer, mine_there, act_turned, grad_turned = join(mine, peer, mine_there, act_turned, grad_turned)
+
+    dealt_spec = pl.BlockSpec((WIDE // 128, 2 * units, 128), lambda j: (j, 0, 0))
+
+    def outer(half, *extra):
+        some = pl.BlockSpec((units, count), lambda j: (half, 0))
+        return run_kernel(
+            lambda *refs: outer_kernel(units, *refs),
+            [((blocks, 2 * units, 128), BF)],
+            grid=grid,
+            ins=[some, some, across(count)] + [across(quarter)] * 4 + [dealt_spec] * len(extra),
+            out_specs=[dealt_spec],
+            flops=4 * count * width * units,
+            name="outer",
+            moved=12e6,
+        )(grad_turned, act_turned, normed_feed, *all_cotangent, *extra)
+
+    peer_there, feed_sent, grads = join(swap_cores(peer), outer(1), grads)
+
+    tile = share // 2
+    half_tile = lambda columns: pl.BlockSpec((tile, columns), lambda i: (i, 0))
+    line_tile = pl.BlockSpec((8, tile), lambda i: (0, i))
+    four = [mine, peer, mine_there, peer_there]
+    common = [
+        pltpu.VMEM((2 * count, 256), BF),
+        pltpu.VMEM((2 * count, 256), BF),
+        pltpu.VMEM((share, 256), BF),
+        pltpu.VMEM((share, 256), BF),
+        pltpu.VMEM((2 * count, 128), F32),
+        pltpu.VMEM((8, 2 * count), F32),
+        pltpu.VMEM((share, 128), F32),
+    ]
+    attended, keep1, send1, lines = run_kernel(
+        lambda *refs: query_kernel(r, scale, *refs),
+        [((share, 256), BF)] * 3 + [((8, share), F32)],
+        grid=(2,),
+        ins=[SMEM] + [fixed(mine)] * 4 + [fixed(grads), fixed(marks)],
+        out_specs=[half_tile(256)] * 3 + [line_tile],
+        scratch=common,
+        flops=8 * share * 2 * count * 256,
+        name="query",
+        moved=6e6,
+    )(ids, *four, grads, marks)
+    feed_got, grads_there, attended, send1, lines = join(
+        swap_cores(feed_sent), swap_cores(grads), attended, send1, lines
+    )
+
+    diagonal = [(2 * b + c, 2 * (b ^ 1) + 1 - c) for b in range(blocks) for c in (0, 1)]
+    lines_peer, lines_there = from_peer(lines, 1), swap_cores(lines)
+    lines_far = lax.ppermute(lines, ("blk", "tp"), diagonal)
+    feed_grads = outer(0, feed_got)
+    feed_grads, lines, lines_peer, lines_there, lines_far = join(feed_grads, lines, lines_peer, lines_there, lines_far)
+
+    keep2, send2 = run_kernel(
+        lambda *refs: key_kernel(r, scale, *refs),
+        [((share, 256), BF)] * 2,
+        grid=(2,),
+        ins=[SMEM] + [fixed(mine)] * 4 + [fixed(grads)] * 2 + [fixed(lines)] * 4 + [fixed(marks)],
+        out_specs=[half_tile(256)] * 2,
+        scratch=common + [pltpu.VMEM((8, 2 * count), F32)],
+        flops=8 * share * 2 * count * 256,
+        name="key",
+        moved=6e6,
+    )(ids, *four, grads, grads_there, lines, lines_peer, lines_there, lines_far, marks)
+    send2, feed_grads, attended = join(send2, feed_grads, attended)
+    feed_dealt = lax.all_to_all(feed_grads, "blk", 0, 0, tiled=True)
+    branches = run_kernel(
+        lambda *refs: branch_kernel(r, *refs),
+        [((quarter, width), BF)] * 4,
+        grid=grid,
+        ins=[fixed(act), fixed(attended), across(2 * units), across(128), across(128)],
+        out_specs=[across(quarter)] * 4,
+        flops=2 * count * width * (2 * units + 128),
+        name="branch",
+        moved=9e6,
+    )(act, attended, w_shrink, w_near, w_peer)
+    got1, got2, *branches = join(from_peer(send1, 1), from_peer(send2, 1), *branches)
+    mixed_one, mixed_two = from_peer(branches[1], 1), from_peer(branches[3], 2)
+
+    def fold(*refs):
+        return run_kernel(
+            fold_kernel,
+            [((quarter // 2, width), BF)] * 4,
+            grid=grid,
+            ins=[across(quarter)] * 4,
+            out_specs=[across(quarter // 2)] * 4,
+            name="fold",
+            moved=6e6,
+        )(*refs)
+
+    def by_z(*refs):
+        return run_kernel(
+            lambda *refs: by_z_kernel(r.chunk, *refs),
+            [((part, width), BF)] * (1 + len(masks_z)),
+            grid=grid,
+            ins=[across(quarter // 2)] * 4,
+            out_specs=[across(part)] * (1 + len(masks_z)),
+            name="by_z",
+            moved=3e6,
+        )(*refs)
+
+    def total(pieces, got):
+        value = pieces[0].astype(F32)
+        for piece in got:
+            value = value + piece.astype(F32)
+        return value
+
+    def pieces_over_z(pieces):
+        return [from_peer(piece, mask) for piece, mask in zip(pieces[1:], masks_z)]
+
+    *combined, grad_linear, attended_near, sums, _ = run_kernel(
+        lambda *refs: inputs_kernel(r, *refs),
+        [((quarter, width), BF)] * 4 + [((count, 384), BF), ((count, 128), BF), ((8, width), F32), ((8, 512), F32)],
+        grid=grid,
+        ins=[fixed(keep1)] * 4
+        + [fixed(grad)]
+        + [across(quarter)] * 4
+        + [fixed(stats), pl.BlockSpec((WIDE, 384), lambda j: (j, 0)), across(2 * units)]
+        + [across(8), across(8), fixed(unit_sums)],
+        out_specs=[across(quarter)] * 4
+        + [fixed_shape(count, 384), fixed_shape(count, 128), across(8), fixed_shape(8, 512)],
+        flops=2 * count * width * (384 + 2 * units),
+        name="inputs",
+        moved=16e6,
+    )(keep1, keep2, got1, got2, grad, *all_tokens, stats, w_triple, w_expand, norms, cotangent_sums, unit_sums)
+    grad_linear, sums, *combined = join(grad_linear, sums, *combined)
+
+    got_one, got_two = from_peer(combined[1], 1), from_peer(combined[3], 2)
+    line_spec = pl.BlockSpec((WIDE // 128, 4 * cut, 128), lambda j: (j, 0, 0))
+    keep, give = run_kernel(
+        lambda *refs: line_outer_kernel(cut, *refs),
+        [((blocks, 4 * cut, 128), F32), ((blocks, 4 * cut, 128), BF)],
+        grid=grid,
+        ins=[SMEM, fixed(grad_linear), fixed(attended_near)]
+        + [across(quarter)] * 4
+        + [fixed(stats), across(8)]
+        + [across(quarter)] * 4,
+        out_specs=[line_spec] * 2,
+        scratch=[
+            pltpu.VMEM((384, count), BF),
+            pltpu.VMEM((128, count), BF),
+            pltpu.VMEM((count, WIDE), BF),
+            pltpu.VMEM((512, WIDE), F32),
+        ],
+        flops=2 * count * width * 512,
+        name="line_outer",
+        moved=12e6,
+    )(ids, grad_linear, attended_near, *all_tokens, stats, norms, *all_cotangent)
+    mixed_one, mixed_two, keep, give, sums, sums_other = join(
+        mixed_one, mixed_two, keep, give, sums, swap_cores(sums)
+    )
+
+    one, one_send, two, two_send = fold(branches[0], mixed_one, branches[2], mixed_two)
+    small = run_kernel(
+        lambda *refs: small_kernel(blocks, units, *refs),
+        [((blocks, 32, 128), BF)],
+        ins=[SMEM, VMEM, VMEM],
+        scratch=[pltpu.VMEM((16, width), F32)],
+        name="small",
+        moved=1e6,
+    )(ids, sums, sums_other)
+    got, small, one, one_send, two, two_send = join(swap_cores(give), small, one, one_send, two, two_send)
+    mixed_one, mixed_two = from_peer(one_send, 2), from_peer(two_send, 1)
+    dealt = jnp.concatenate([(keep + got.astype(F32)).astype(BF), small], axis=1)
+    dealt, feed_dealt = join(dealt, feed_dealt)
+    dealt = lax.all_to_all(dealt, "blk", 0, 0, tiled=True)
+    expand_grad, shrink_grad = run_kernel(
+        lambda *refs: feed_unpack_kernel(units, *refs),
+        [(w_in.shape, F32), (w_out2.shape, F32)],
+        grid=(blocks,),
+        ins=[pl.BlockSpec((1, 2 * units, 128), lambda k: (k, 0, 0))],
+        out_specs=[pl.BlockSpec((depth, units), lambda k: (0, k)), pl.BlockSpec((units, depth), lambda k: (k, 0))],
+        name="feed_unpack",
+        moved=6e6,
+    )(feed_dealt)
+    got_one, got_two, mixed_one, mixed_two, expand_grad, shrink_grad = join(
+        got_one, got_two, mixed_one, mixed_two, expand_grad, shrink_grad
+    )
+    mixed_pieces = by_z(one, mixed_one, two, mixed_two)
+    one, one_send, two, two_send, *mixed_pieces = join(
+        *fold(combined[0], got_one, combined[2], got_two), *mixed_pieces
+    )
+    got_one, got_two, *mixed_got = join(
+        from_peer(one_send, 2), from_peer(two_send, 1), *pieces_over_z(mixed_pieces)
+    )
+
+    joined = join(*by_z(one, got_one, two, got_two), *mixed_got)
+    pieces, mixed_got = joined[: 1 + len(masks_z)], joined[1 + len(masks_z) :]
+    combined_got = pieces_over_z(pieces)
+
+    def whole_block(value):
+        return jnp.concatenate(by_core(core, value, swap_cores(value)))
+
+    my_inputs = my_tokens.astype(F32)
+    mixed = whole_block((my_inputs + total(mixed_pieces, mixed_got) + norms[4:5, :]).astype(BF))
+    dealt, mixed = join(dealt, mixed)
+    keep = lax.dynamic_slice_in_dim(dealt, core * own_heads, own_heads, 0)
+    give = lax.dynamic_slice_in_dim(dealt, (1 - core) * own_heads, own_heads, 0)
+    triple_grad, output_grad, small = run_kernel(
+        lambda *refs: unpack_kernel(cut, own_heads, *refs),
+        [((3, depth, own_heads * 128), F32), ((own_heads * 128, depth), F32), ((16, 128), F32)],
+        ins=[SMEM, VMEM, VMEM, VMEM],
+        scratch=[pltpu.VMEM((128, 128), F32)],
+        name="unpack",
+        moved=4e6,
+    )(ids, keep, swap_cores(give), dealt)
+    small = small.reshape(16, 16, -1)
+    residual_grad = small[4]
+    small, triple_grad, output_grad, *combined_got = join(small, triple_grad, output_grad, *combined_got)
+
+    combined_sum = total(pieces, combined_got)
+    my_center = my_inputs - jnp.mean(my_inputs, axis=-1, keepdims=True)
+    my_inverse = lax.rsqrt(jnp.mean(my_center * my_center, axis=-1, keepdims=True) + EPSILON)
+    my_normal = my_center * my_inverse
+    my_grad = my_inverse * (
+        combined_sum
+        - jnp.mean(combined_sum, axis=-1, keepdims=True)
+        - my_normal * jnp.mean(combined_sum * my_normal, axis=-1, keepdims=True)
+    )
+    tokens_grad = whole_block((my_cotangent.astype(F32) + my_grad).astype(BF))
+    return (
+        mixed,
+        tokens_grad,
+        triple_grad,
+        small[6:8].reshape(32, -1)[:24].reshape(b_qkv.shape),
+        output_grad,
+        residual_grad,
+        expand_grad,
+        small[8:10].reshape(b_in.shape),
+        shrink_grad,
+        residual_grad,
+        small[0:2],
+        small[2:4],
+    )
+
+
 def solution(mesh):
     placed = (
         P("blk", None),
@@ -472,8 +1409,9 @@
         P("blk"),
         P("blk", None),
     )
+    two_to_a_head = mesh.shape["blk"] == 2 * HEADS
     return jax.shard_map(
-        body,
+        body if two_to_a_head else general_body,
         mesh=mesh,
         in_specs=placed,
         out_specs=(

time: 582 us -> 418 us (0.72)
  Pallas kernels: 0 us -> 96.9 us
  local copies, waits for them, and re-layouts: 146 us -> 53.1 us
  matrix products: 78.2 us -> 0 us
  other arithmetic: 90.5 us -> 12.8 us
  starting transfers between devices: 97.6 us -> 89.9 us
    pallas_call x0 -> x18, Pallas kernels: none -> 96.9 us  [the longest x1 11.1 us: body(): run_kernel(lambda *refs: feed_kernel(units, blocks, *refs), [((count, 2 *...]
    dot_general x18 -> x0, matrix products: 78.2 us -> none  [dot(): lax.dot_general(left, right, (dims, ((), ())), preferred_element_type=F32)]
    gather x4 -> x0, local copies, waits for them, and re-layouts: 29.4 us -> none  [the longest x1 11.8 us: body(): token_start = starts.reshape(-1)[index]]
    another operation x29 -> x2, other arithmetic: 29.1 us -> 0.09 us  [the longest x1 0.07 us: body(): ids = jnp.stack([me, core]).astype(jnp.int32)]
    reshape x36 -> x10, local copies, waits for them, and re-layouts: 27.6 us -> 2.06 us  [the longest x1 0.72 us: body(): outward = w_out.reshape(own_heads, cores, cut, 128).transpose(1, 0, 2, 3)]
    unnamed x238 -> x179, local copies, waits for them, and re-layouts: 16.1 us -> 41.6 us
    convert_element_type x17 -> x1, other arithmetic: 25.3 us -> 0.29 us  [body(): (keep + got.astype(F32)).astype(BF)]
    concatenate x17 -> x5, local copies, waits for them, and re-layouts: 20.2 us -> 3.34 us  [the longest x2 2.16 us: body(): one, two = (jnp.concatenate([one, one_y]), jnp.concatenate([two, two_x]))]
  transfers between devices with their start and end apart: 53 -> 51, of which waited for: 14 -> 19; matrix products, arithmetic and copies ran while one was open for 51% -> 6% of each run, Pallas kernels for 0% -> 21%
where the time goes in v3:
time: 418 us; the launch traced here: 415 us
  waiting for transfers between devices  161 us (39%)
  Pallas kernels  96.9 us (23%)
  starting transfers between devices  89.9 us (22%)
  local copies, waits for them, and re-layouts  53.1 us (13%)
  other arithmetic  12.8 us (3%)
    ppermute x33, waiting for transfers between devices, from_peer(): return lax.ppermute(value, 'blk', [(i, i ^ mask) for i in range(count)])  154 us
    unnamed x179, local copies, waits for them, and re-layouts  41.6 us
    ppermute x33, starting transfers between devices, from_peer(): return lax.ppermute(value, 'blk', [(i, i ^ mask) for i in range(count)])  37.8 us
    ppermute x13, starting transfers between devices, swap_cores(): return lax.ppermute(value, 'tp', [(0, 1), (1, 0)])  27.3 us
    pallas_call x1, Pallas kernels, body(): run_kernel(lambda *refs: feed_kernel(units, blocks, *refs), [((count, 2 *...  11.1 us
    pallas_call x1, Pallas kernels, body(): run_kernel(lambda *refs: norm_kernel(r, *refs), [((count, width), BF), ((...  10.3 us
    pallas_call x1, Pallas kernels, body(): run_kernel(lambda *refs: feed_unpack_kernel(units, *refs), [(w_in.shape,...  10.2 us
    pallas_call x2, Pallas kernels, outer(): run_kernel(lambda *refs: outer_kernel(units, *refs), [((blocks, 2 * units...  9.7 us
  transfers between devices with their start and end apart: 51, of which 19 were waited for; matrix products, arithmetic and copies ran while one was open for 6% of the time, Pallas kernels for 21%

profile of v3, /device:TPU:11, one launch (start us, length us, event | category | flops | bytes accessed | tf_op | source)
XLA Modules:
  0.0 415.0 jit_solution(2373671788458707917)
XLA Ops:
  2.1 2.3 collective-permute-start.2
  4.6 1.3 copy.78
  7.8 2.1 fusion.13
  9.8 1.5 collective-permute-start
  12.5 1.7 feed_deal.1
  14.3 1.6 collective-permute-done.2
  15.9 14.0 %collective-permute-done.3 = bf16[64,2048]{1,0:T(8,128)(2,1)} collective-permute-done((bf16[64,2048]{1,0:T(8,128)(2,1)S(1)}, bf16[64,2048]{1,0:T(8,128)(2,1)}, u32[]{:S(2)}, u32[]{:S(2)}) %collective-permute-start.3) | collective-permute-done | bytes 262176 | tf_op jit(solution)/shard_map/ppermute | solution.py:30
  29.8 1.3 collective-permute-start.10
  31.1 1.4 collective-permute-start.9
  35.0 1.3 collective-permute-start.4
  38.5 4.7 %all-to-all-start = ((bf16[16,272,128]{2,1,0:T(8,128)(2,1)}), bf16[16,272,128]{2,1,0:T(8,128)(2,1)S(1)}, u32[]{:S(2)}, u32[]{:S(2)}) async-start(bf16[16,272,128]{2,1,0:T(8,128)(2,1)} %pad_maximum_fusion.1), calls=%async_computation | async-start | bytes 2228224 | tf_op jit(solution)/shard_map/all_to_all | solution.py:1078
  43.3 6.7 %collective-permute-done.9 = bf16[64,2048]{1,0:T(8,128)(2,1)} collective-permute-done((bf16[64,2048]{1,0:T(8,128)(2,1)S(1)}, bf16[64,2048]{1,0:T(8,128)(2,1)}, u32[]{:S(2)}, u32[]{:S(2)}) %collective-permute-start.9) | collective-permute-done | bytes 262176 | tf_op jit(solution)/shard_map/ppermute | solution.py:30
  52.1 1.4 collective-permute-start.7
  57.9 28.1 %collective-permute-done.12 = bf16[128,2048]{1,0:T(8,128)(2,1)S(1)} collective-permute-done((bf16[128,2048]{1,0:T(8,128)(2,1)S(1)}, bf16[128,2048]{1,0:T(8,128)(2,1)S(1)}, u32[]{:S(2)}, u32[]{:S(2)}) %collective-permute-start.12) | collective-permute-done | bytes 524320 | tf_op jit(solution)/shard_map/ppermute | solution.py:30
  86.0 1.5 collective-permute-done.11
  90.3 10.1 %collective-permute-start.13 = (bf16[16,272,128]{2,1,0:T(8,128)(2,1)S(1)}, bf16[16,272,128]{2,1,0:T(8,128)(2,1)S(1)}, u32[]{:S(2)}, u32[]{:S(2)}) collective-permute-start(bf16[16,272,128]{2,1,0:T(8,128)(2,1)S(1)} %all-to-all-done.refs_2_), channel_id=1, source_target_pairs={{0,1},{1,0},{2,3},{3,2},{4,5},{5,4},{6,7},{7,6},{8,9},{9,8},{10,11... | collective-permute-start | bytes 3342344 | tf_op jit(solution)/shard_map/ppermute | solution.py:25
  100.6 2.2 collective-permute-done.13.refs_3_
  102.8 3.5 deal.1
  109.3 5.7 %all-to-all-start.1 = ((bf16[16,512,128]{2,1,0:T(8,128)(2,1)}), bf16[16,512,128]{2,1,0:T(8,128)(2,1)}, u32[]{:S(2)}, u32[]{:S(2)}) async-start(bf16[16,512,128]{2,1,0:T(8,128)(2,1)} %feed_deal.1), calls=%async_computation.1 | async-start | bytes 4194304 | tf_op jit(solution)/shard_map/all_to_all | solution.py:1118
  120.2 1.4 copy-done.23
  122.8 10.3 %norm.1 = (bf16[1024,2048]{1,0:T(8,128)(2,1)S(1)}, f32[1024,128]{1,0:T(8,128)S(1)}, bf16[1024,384]{1,0:T(8,128)(2,1)S(1)}) custom-call(s32[2]{0:T(128)S(1)} %pad_add_fusion.refs_0_, bf16[256,2048]{1,0:T(8,128)(2,1)S(1)} %copy-done.14, bf16[256,2048]{1,0:T(8,128)(2,1)S(1)} %copy-done.20, bf16[256,2048]{1,0:T(8,128)(2,1)S(1)} %copy-done.11, ...), custom_call_target="tpu_custom_call" | custom-call | flops 1610612736 | bytes 22000000 | tf_op jit(solution)/shard_map/norm/pallas_call | solution.py:1119
  133.1 2.0 copy-done.2
  136.0 23.8 %collective-permute-done.15.refs_4_.refs_6_.refs_12_ = bf16[256,2048]{1,0:T(8,128)(2,1)S(1)} collective-permute-done((bf16[256,2048]{1,0:T(8,128)(2,1)S(1)}, bf16[256,2048]{1,0:T(8,128)(2,1)S(1)}, u32[]{:S(2)}, u32[]{:S(2)}) %collective-permute-start.15) | collective-permute-done | bytes 1048608 | tf_op jit(solution)/shard_map/ppermute | solution.py:30
  160.8 11.6 %collective-permute-done.18.refs_9_.refs_4_ = bf16[128,2048]{1,0:T(8,128)(2,1)S(1)} collective-permute-done((bf16[128,2048]{1,0:T(8,128)(2,1)}, bf16[128,2048]{1,0:T(8,128)(2,1)S(1)}, u32[]{:S(2)}, u32[]{:S(2)}) %collective-permute-start.18) | collective-permute-done | bytes 524320 | tf_op jit(solution)/shard_map/ppermute | solution.py:30
  175.7 2.8 collective-permute-done.19.refs_6_
  178.4 2.2 copy-done.3
  183.9 11.1 %feed.1 = (bf16[1024,512]{1,0:T(8,128)(2,1)S(1)}, bf16[1024,512]{1,0:T(8,128)(2,1)S(1)}, bf16[512,1024]{1,0:T(8,128)(2,1)S(1)}, bf16[512,1024]{1,0:T(8,128)(2,1)...) custom-call(bf16[1024,2048]{1,0:T(8,128)(2,1)S(1)} %copy-done.3, ...), custom_call_target="tpu_custom_call" | custom-call | flops 4294967296 | bytes 20000000 | tf_op jit(solution)/shard_map/feed/pallas_call | solution.py:1140
  195.1 1.3 copy-done.50
  196.4 1.3 copy-done.52
  199.2 4.9 %outer.2 = bf16[16,512,128]{2,1,0:T(8,128)(2,1)S(1)} custom-call(bf16[512,1024]{1,0:T(8,128)(2,1)S(1)} %get-tuple-element.254.refs_0_, bf16[512,1024]{1,0:T(8,128)(2,1)S(1)} %get-tuple-element.255.refs_1_, bf16[1024,2048]{1,0:T(8,128)(2,1)S(1)} %copy-done.4, bf16[256,2048]{1,0:T(8,128)(2,1)S(1)} %constant_dynamic-update-slice_fusion.4.refs_1_.refs_3_.refs_9_, ...), custom_call_target="tpu_custom_call" | custom-call | flops 2147483648 | bytes 12000000 | tf_op jit(solution)/shard_map/outer/pallas_call | solution.py:1165
  204.7 7.6 %query.1 = (bf16[512,256]{1,0:T(8,128)(2,1)S(1)}, bf16[512,256]{1,0:T(8,128)(2,1)S(1)}, bf16[512,256]{1,0:T(8,128)(2,1)S(1)}, f32[8,512]{1,0:T(8,128)S(1)}) custom-call(s32[2]{0:T(128)S(1)} %pad_add_fusion.refs_0_, bf16[1024,384]{1,0:T(8,128)(2,1)S(1)} %copy-done.41, bf16[1024,384]{1,0:T(8,128)(2,1)S(1)} %collective-permute-done.16.refs_2_, ...), custom_call_target="tpu_custom_call" | custom-call | flops 2147483648 | bytes 6000000 | tf_op jit(solution)/shard_map/query/pallas_call | solution.py:1191
  214.2 4.8 %outer.3 = bf16[16,512,128]{2,1,0:T(8,128)(2,1)S(1)} custom-call(bf16[512,1024]{1,0:T(8,128)(2,1)S(1)} %get-tuple-element.254.refs_0_, bf16[512,1024]{1,0:T(8,128)(2,1)S(1)} %get-tuple-element.255.refs_1_, bf16[1024,2048]{1,0:T(8,128)(2,1)S(1)} %copy-done.4, bf16[256,2048]{1,0:T(8,128)(2,1)S(1)} %constant_dynamic-update-slice_fusion.4.refs_1_.refs_3_.refs_9_, ...), custom_call_target="tpu_custom_call" | custom-call | flops 2147483648 | bytes 12000000 | tf_op jit(solution)/shard_map/outer/pallas_call | solution.py:1165
  219.1 1.3 copy-done.9
  220.4 4.7 %key.1 = (bf16[512,256]{1,0:T(8,128)(2,1)S(1)}, bf16[512,256]{1,0:T(8,128)(2,1)S(1)}) custom-call(s32[2]{0:T(128)S(1)} %pad_add_fusion.refs_0_, bf16[1024,384]{1,0:T(8,128)(2,1)S(1)} %copy-done.41, bf16[1024,384]{1,0:T(8,128)(2,1)S(1)} %collective-permute-done.16.refs_2_, bf16[1024,384]{1,0:T(8,128)(2,1)S(1)} %collective-permute-done.17.refs_3_, ...), custom_call_target="tpu_custom_call" | custom-call | flops 2147483648 | bytes 6000000 | tf_op jit(solution)/shard_map/key/pallas_call | solution.py:1212
  226.6 6.2 %all-to-all-start.2 = ((bf16[16,512,128]{2,1,0:T(8,128)(2,1)}), bf16[16,512,128]{2,1,0:T(8,128)(2,1)}, u32[]{:S(2)}, u32[]{:S(2)}) async-start(bf16[16,512,128]{2,1,0:T(8,128)(2,1)} %copy-done.9), calls=%async_computation.2 | async-start | bytes 4194304 | tf_op jit(solution)/shard_map/all_to_all | solution.py:1224
  236.3 1.6 copy-done.53
  240.2 5.5 %branch.1 = (bf16[256,2048]{1,0:T(8,128)(2,1)S(1)}, bf16[256,2048]{1,0:T(8,128)(2,1)S(1)}, bf16[256,2048]{1,0:T(8,128)(2,1)S(1)}, bf16[256,2048]{1,0:T(8,128)(2,1)S(1)}) custom-call(bf16[1024,512]{1,0:T(8,128)(2,1)S(1)} %copy-done.57, bf16[512,256]{1,0:T(8,128)(2,1)S(1)} %copy-done.63, bf16[512,2048]{1,0:T(8,128)(2,1)S(1)} %copy-done.53, ...), custom_call_target="tpu_custom_call" | custom-call | flops 2684354560 | bytes 9000000 | tf_op jit(solution)/shard_map/branch/pallas_call | solution.py:1225
  245.7 4.5 %collective-permute-done.27.refs_3_ = bf16[512,256]{1,0:T(8,128)(2,1)S(1)} collective-permute-done((bf16[512,256]{1,0:T(8,128)(2,1)}, bf16[512,256]{1,0:T(8,128)(2,1)S(1)}, u32[]{:S(2)}, u32[]{:S(2)}) %collective-permute-start.27) | collective-permute-done | bytes 262176 | tf_op jit(solution)/shard_map/ppermute | solution.py:30
  251.4 7.5 %collective-permute-start.29 = (bf16[256,2048]{1,0:T(8,128)(2,1)S(1)}, bf16[256,2048]{1,0:T(8,128)(2,1)S(1)}, u32[]{:S(2)}, u32[]{:S(2)}) collective-permute-start(bf16[256,2048]{1,0:T(8,128)(2,1)S(1)} %get-tuple-element.285), channel_id=1, source_target_pairs={{0,4},{2,6},{4,0},{6,2},{8,12},{10,14},{12,8},{14,10},{16,20},{18,... | collective-permute-start | bytes 3145736 | tf_op jit(solution)/shard_map/ppermute | solution.py:30
  259.9 9.3 %inputs.1 = (bf16[256,2048]{1,0:T(8,128)(2,1)S(1)}, bf16[256,2048]{1,0:T(8,128)(2,1)}, bf16[256,2048]{1,0:T(8,128)(2,1)S(1)}, bf16[256,2048]{1,0:T(8,128)(2,1)},...) custom-call(bf16[512,256]{1,0:T(8,128)(2,1)S(1)} %copy-done.61, ...), custom_call_target="tpu_custom_call" | custom-call | flops 3758096384 | bytes 16000000 | tf_op jit(solution)/shard_map/inputs/pallas_call | solution.py:1269
  271.3 7.6 %collective-permute-start.30 = (f32[8,2048]{1,0:T(8,128)S(1)}, f32[8,2048]{1,0:T(8,128)S(1)}, u32[]{:S(2)}, u32[]{:S(2)}) collective-permute-start(f32[8,2048]{1,0:T(8,128)S(1)} %get-tuple-element.308.refs_1_), channel_id=1, source_target_pairs={{0,1},{1,0},{2,3},{3,2},{4,5},{5,4},{6,7},{7,6},{8,9},{9,8},{10,11... | collective-permute-start | bytes 196616 | tf_op jit(solution)/shard_map/ppermute | solution.py:25
  278.9 8.3 %line_outer.1 = (f32[16,256,128]{2,1,0:T(8,128)S(1)}, bf16[16,256,128]{2,1,0:T(8,128)(2,1)S(1)}) custom-call(s32[2]{0:T(128)S(1)} %pad_add_fusion.refs_0_, bf16[1024,384]{1,0:T(8,128)(2,1)S(1)} %get-tuple-element.301.refs_1_, bf16[1024,128]{1,0:T(8,128)(2,1)S(1)} %get-tuple-element.302.refs_2_, bf16[256,2048]{1,0:T(8,128)(2,1)S(1)} %copy-done.15, ...), custom_call_target="tpu_custom_call" | custom-call | flops 2147483648 | bytes 12000000 | tf_op jit(solution)/shard_map/line_outer/pallas_call | solution.py:1288
  287.2 3.7 collective-permute-done.28.got1
  293.5 3.1 small.1
  296.6 3.4 fold.2
  302.4 7.7 %all-to-all-start.3 = ((bf16[16,288,128]{2,1,0:T(8,128)(2,1)}), bf16[16,288,128]{2,1,0:T(8,128)(2,1)S(1)}, u32[]{:S(2)}, u32[]{:S(2)}) async-start(bf16[16,288,128]{2,1,0:T(8,128)(2,1)} %pad_maximum_fusion), calls=%async_computation.3 | async-start | bytes 2359296 | tf_op jit(solution)/shard_map/all_to_all | solution.py:1324
  310.0 10.2 %feed_unpack.1 = (f32[128,4096]{1,0:T(8,128)}, f32[4096,128]{1,0:T(8,128)}) custom-call(bf16[16,512,128]{2,1,0:T(8,128)(2,1)} %all-to-all-done.2.refs_0_), custom_call_target="tpu_custom_call" | custom-call | bytes 6000000 | tf_op jit(solution)/shard_map/feed_unpack/pallas_call | solution.py:1325
  320.2 16.9 %collective-permute-done.34.refs_1_ = bf16[128,2048]{1,0:T(8,128)(2,1)} collective-permute-done((bf16[128,2048]{1,0:T(8,128)(2,1)}, bf16[128,2048]{1,0:T(8,128)(2,1)}, u32[]{:S(2)}, u32[]{:S(2)}) %collective-permute-start.34) | collective-permute-done | bytes 524320 | tf_op jit(solution)/shard_map/ppermute | solution.py:30
  339.2 3.9 by_z.2
  343.1 1.4 fold.3
  345.6 3.1 collective-permute-start.37
  351.3 5.8 %collective-permute-done.38 = bf16[64,2048]{1,0:T(8,128)(2,1)S(1)} collective-permute-done((bf16[64,2048]{1,0:T(8,128)(2,1)S(1)}, bf16[64,2048]{1,0:T(8,128)(2,1)S(1)}, u32[]{:S(2)}, u32[]{:S(2)}) %collective-permute-start.38) | collective-permute-done | bytes 262176 | tf_op jit(solution)/shard_map/ppermute | solution.py:30
  357.1 1.5 collective-permute-done.39
  358.7 14.0 %collective-permute-done.40 = bf16[64,2048]{1,0:T(8,128)(2,1)S(1)} collective-permute-done((bf16[64,2048]{1,0:T(8,128)(2,1)S(1)}, bf16[64,2048]{1,0:T(8,128)(2,1)S(1)}, u32[]{:S(2)}, u32[]{:S(2)}) %collective-permute-start.40) | collective-permute-done | bytes 262176 | tf_op jit(solution)/shard_map/ppermute | solution.py:30
  373.8 2.9 collective-permute-start.41
  376.7 1.3 collective-permute-done.41
  380.3 2.1 collective-permute-start.44
  383.0 2.4 unpack.1
  385.5 5.6 %collective-permute-done.43 = bf16[64,2048]{1,0:T(8,128)(2,1)S(1)} collective-permute-done((bf16[64,2048]{1,0:T(8,128)(2,1)S(1)}, bf16[64,2048]{1,0:T(8,128)(2,1)S(1)}, u32[]{:S(2)}, u32[]{:S(2)}) %collective-permute-start.43) | collective-permute-done | bytes 262176 | tf_op jit(solution)/shard_map/ppermute | solution.py:30
  391.1 3.3 collective-permute-done.44
  394.4 11.5 %collective-permute-done.45 = bf16[64,2048]{1,0:T(8,128)(2,1)} collective-permute-done((bf16[64,2048]{1,0:T(8,128)(2,1)S(1)}, bf16[64,2048]{1,0:T(8,128)(2,1)}, u32[]{:S(2)}, u32[]{:S(2)}) %collective-permute-start.45) | collective-permute-done | bytes 262176 | tf_op jit(solution)/shard_map/ppermute | solution.py:30
  406.0 1.3 fusion.18
  407.3 1.4 fusion.8
  408.7 1.3 collective-permute-start.46
  (292 shorter events, 71.4 us)
Async XLA Ops:
  1.8 30.6 %copy-start.64 = (bf16[64,2048]{1,0:T(8,128)(2,1)}, bf16[64,2048]{1,0:T(8,128)(2,1)S(1)}, u32[]{:S(2)}) copy-start(bf16[64,2048]{1,0:T(8,128)(2,1)S(1)} %get-tuple-element.204) | copy-start | bytes 786436
  1.8 12.4 %collective-permute-start.1 = (bf16[64,2048]{1,0:T(8,128)(2,1)S(1)}, bf16[64,2048]{1,0:T(8,128)(2,1)}, u32[]{:S(2)}, u32[]{:S(2)}) collective-permute-start(bf16[64,2048]{1,0:T(8,128)(2,1)S(1)} %get-tuple-element.204), channel_id=1, source_target_pairs={{0,8},{2,10},{4,12},{6,14},{8,0},{10,2},{12,4},{14,6},{16,24},{18,... | collective-permute-start | bytes 786440 | tf_op jit(solution)/shard_map/ppermute | solution.py:30
  2.1 13.8 %collective-permute-start.2 = (bf16[64,2048]{1,0:T(8,128)(2,1)S(1)}, bf16[64,2048]{1,0:T(8,128)(2,1)}, u32[]{:S(2)}, u32[]{:S(2)}) collective-permute-start(bf16[64,2048]{1,0:T(8,128)(2,1)S(1)} %get-tuple-element.204), channel_id=1, source_target_pairs={{0,16},{2,18},{4,20},{6,22},{8,24},{10,26},{12,28},{14,30},{16,0},... | collective-permute-start | bytes 786440 | tf_op jit(solution)/shard_map/ppermute | solution.py:30
  4.4 25.4 %collective-permute-start.3 = (bf16[64,2048]{1,0:T(8,128)(2,1)S(1)}, bf16[64,2048]{1,0:T(8,128)(2,1)}, u32[]{:S(2)}, u32[]{:S(2)}) collective-permute-start(bf16[64,2048]{1,0:T(8,128)(2,1)S(1)} %get-tuple-element.204), channel_id=1, source_target_pairs={{0,24},{2,26},{4,28},{6,30},{8,16},{10,18},{12,20},{14,22},{16,8},... | collective-permute-start | bytes 786440 | tf_op jit(solution)/shard_map/ppermute | solution.py:30
  9.8 20.0 %collective-permute-start = (bf16[8,256,128]{2,1,0:T(8,128)(2,1)}, bf16[8,256,128]{2,1,0:T(8,128)(2,1)}, u32[]{:S(2)}, u32[]{:S(2)}) collective-permute-start(bf16[8,256,128]{2,1,0:T(8,128)(2,1)} %get-tuple-element.438), channel_id=1, source_target_pairs={{0,1},{1,0},{2,3},{3,2},{4,5},{5,4},{6,7},{7,6},{8,9},{9,8},{10,11... | collective-permute-start | bytes 1572872 | tf_op jit(solution)/shard_map/ppermute | solution.py:25
  14.3 35.7 %copy-start.66 = (bf16[64,2048]{1,0:T(8,128)(2,1)}, bf16[64,2048]{1,0:T(8,128)(2,1)S(1)}, u32[]{:S(2)}) copy-start(bf16[64,2048]{1,0:T(8,128)(2,1)S(1)} %constant_dynamic-slice_fusion.3) | copy-start | bytes 786436
  29.8 13.4 %collective-permute-start.10 = (bf16[64,2048]{1,0:T(8,128)(2,1)S(1)}, bf16[64,2048]{1,0:T(8,128)(2,1)}, u32[]{:S(2)}, u32[]{:S(2)}) collective-permute-start(bf16[64,2048]{1,0:T(8,128)(2,1)S(1)} %constant_dynamic-slice_fusion.3), channel_id=1, source_target_pairs={{0,24},{2,26},{4,28},{6,30},{8,16},{10,18},{12,20},{14,22},{16,8},... | collective-permute-start | bytes 786440 | tf_op jit(solution)/shard_map/ppermute | solution.py:30
  31.1 12.1 %collective-permute-start.8 = (bf16[64,2048]{1,0:T(8,128)(2,1)S(1)}, bf16[64,2048]{1,0:T(8,128)(2,1)}, u32[]{:S(2)}, u32[]{:S(2)}) collective-permute-start(bf16[64,2048]{1,0:T(8,128)(2,1)S(1)} %constant_dynamic-slice_fusion.3), channel_id=1, source_target_pairs={{0,8},{2,10},{4,12},{6,14},{8,0},{10,2},{12,4},{14,6},{16,24},{18,... | collective-permute-start | bytes 786440 | tf_op jit(solution)/shard_map/ppermute | solution.py:30
  31.1 18.9 %collective-permute-start.9 = (bf16[64,2048]{1,0:T(8,128)(2,1)S(1)}, bf16[64,2048]{1,0:T(8,128)(2,1)}, u32[]{:S(2)}, u32[]{:S(2)}) collective-permute-start(bf16[64,2048]{1,0:T(8,128)(2,1)S(1)} %constant_dynamic-slice_fusion.3), channel_id=1, source_target_pairs={{0,16},{2,18},{4,20},{6,22},{8,24},{10,26},{12,28},{14,30},{16,0},... | collective-permute-start | bytes 786440 | tf_op jit(solution)/shard_map/ppermute | solution.py:30
  34.7 16.3 %collective-permute-start.5 = (bf16[128,2048]{1,0:T(8,128)(2,1)S(1)}, bf16[128,2048]{1,0:T(8,128)(2,1)}, u32[]{:S(2)}, u32[]{:S(2)}) collective-permute-start(bf16[128,2048]{1,0:T(8,128)(2,1)S(1)} %pad_maximum_fusion.3), channel_id=1, source_target_pairs={{0,2},{2,0},{4,6},{6,4},{8,10},{10,8},{12,14},{14,12},{16,18},{18,... | collective-permute-start | bytes 1572872 | tf_op jit(solution)/shard_map/ppermute | solution.py:30
  35.0 16.0 %collective-permute-start.4 = (bf16[128,2048]{1,0:T(8,128)(2,1)S(1)}, bf16[128,2048]{1,0:T(8,128)(2,1)}, u32[]{:S(2)}, u32[]{:S(2)}) collective-permute-start(bf16[128,2048]{1,0:T(8,128)(2,1)S(1)} %pad_maximum_fusion.2), channel_id=1, source_target_pairs={{0,4},{2,6},{4,0},{6,2},{8,12},{10,14},{12,8},{14,10},{16,20},{18,... | collective-permute-start | bytes 1572872 | tf_op jit(solution)/shard_map/ppermute | solution.py:30
  38.5 51.8 %all-to-all-start = ((bf16[16,272,128]{2,1,0:T(8,128)(2,1)}), bf16[16,272,128]{2,1,0:T(8,128)(2,1)S(1)}, u32[]{:S(2)}, u32[]{:S(2)}) async-start(bf16[16,272,128]{2,1,0:T(8,128)(2,1)} %pad_maximum_fusion.1), calls=%async_computation | async-start | bytes 2228224 | tf_op jit(solution)/shard_map/all_to_all | solution.py:1078
  52.1 35.3 %collective-permute-start.7 = (bf16[256,2048]{1,0:T(8,128)(2,1)S(1)}, bf16[256,2048]{1,0:T(8,128)(2,1)S(1)}, u32[]{:S(2)}, u32[]{:S(2)}) collective-permute-start(bf16[256,2048]{1,0:T(8,128)(2,1)S(1)} %constant_dynamic-update-slice_fusion.2.refs_3_.refs_7_.refs_5_), channel_id=1, source_target_pairs={{0,4},{2,6},{4,0},{6,2},{8,12},{10,14},{12,8},{14,10},{16,20},{18,... | collective-permute-start | bytes 3145736 | tf_op jit(solution)/shard_map/ppermute | solution.py:30
  54.7 32.8 %copy-start.13 = (bf16[256,2048]{1,0:T(8,128)(2,1)}, bf16[256,2048]{1,0:T(8,128)(2,1)S(1)}, u32[]{:S(2)}) copy-start(bf16[256,2048]{1,0:T(8,128)(2,1)S(1)} %constant_dynamic-update-slice_fusion.refs_1_.refs_5_.refs_3_) | copy-start | bytes 3145732
  54.7 34.6 %collective-permute-start.6 = (bf16[256,2048]{1,0:T(8,128)(2,1)S(1)}, bf16[256,2048]{1,0:T(8,128)(2,1)S(1)}, u32[]{:S(2)}, u32[]{:S(2)}) collective-permute-start(bf16[256,2048]{1,0:T(8,128)(2,1)S(1)} %constant_dynamic-update-slice_fusion.refs_1_.refs_5_.refs_3_), channel_id=1, source_target_pairs={{0,2},{2,0},{4,6},{6,4},{8,10},{10,8},{12,14},{14,12},{16,18},{18,... | collective-permute-start | bytes 3145736 | tf_op jit(solution)/shard_map/ppermute | solution.py:30
  56.3 29.7 %collective-permute-start.12 = (bf16[128,2048]{1,0:T(8,128)(2,1)S(1)}, bf16[128,2048]{1,0:T(8,128)(2,1)S(1)}, u32[]{:S(2)}, u32[]{:S(2)}) collective-permute-start(bf16[128,2048]{1,0:T(8,128)(2,1)S(1)} %pad_maximum_fusion.5), channel_id=1, source_target_pairs={{0,2},{2,0},{4,6},{6,4},{8,10},{10,8},{12,14},{14,12},{16,18},{18,... | collective-permute-start | bytes 1572872 | tf_op jit(solution)/shard_map/ppermute | solution.py:30
  57.6 31.7 %copy-start.68 = (bf16[128,2048]{1,0:T(8,128)(2,1)}, bf16[128,2048]{1,0:T(8,128)(2,1)S(1)}, u32[]{:S(2)}) copy-start(bf16[128,2048]{1,0:T(8,128)(2,1)S(1)} %pad_maximum_fusion.4) | copy-start | bytes 1572868
  57.6 29.9 %collective-permute-start.11 = (bf16[128,2048]{1,0:T(8,128)(2,1)S(1)}, bf16[128,2048]{1,0:T(8,128)(2,1)S(1)}, u32[]{:S(2)}, u32[]{:S(2)}) collective-permute-start(bf16[128,2048]{1,0:T(8,128)(2,1)S(1)} %pad_maximum_fusion.4), channel_id=1, source_target_pairs={{0,4},{2,6},{4,0},{6,2},{8,12},{10,14},{12,8},{14,10},{16,20},{18,... | collective-permute-start | bytes 1572872 | tf_op jit(solution)/shard_map/ppermute | solution.py:30
  90.3 12.5 %collective-permute-start.13 = (bf16[16,272,128]{2,1,0:T(8,128)(2,1)S(1)}, bf16[16,272,128]{2,1,0:T(8,128)(2,1)S(1)}, u32[]{:S(2)}, u32[]{:S(2)}) collective-permute-start(bf16[16,272,128]{2,1,0:T(8,128)(2,1)S(1)} %all-to-all-done.refs_2_), channel_id=1, source_target_pairs={{0,1},{1,0},{2,3},{3,2},{4,5},{5,4},{6,7},{7,6},{8,9},{9,8},{10,11... | collective-permute-start | bytes 3342344 | tf_op jit(solution)/shard_map/ppermute | solution.py:25
  109.3 63.9 %all-to-all-start.1 = ((bf16[16,512,128]{2,1,0:T(8,128)(2,1)}), bf16[16,512,128]{2,1,0:T(8,128)(2,1)}, u32[]{:S(2)}, u32[]{:S(2)}) async-start(bf16[16,512,128]{2,1,0:T(8,128)(2,1)} %feed_deal.1), calls=%async_computation.1 | async-start | bytes 4194304 | tf_op jit(solution)/shard_map/all_to_all | solution.py:1118
  115.2 44.6 %collective-permute-start.15 = (bf16[256,2048]{1,0:T(8,128)(2,1)S(1)}, bf16[256,2048]{1,0:T(8,128)(2,1)S(1)}, u32[]{:S(2)}, u32[]{:S(2)}) collective-permute-start(bf16[256,2048]{1,0:T(8,128)(2,1)S(1)} %constant_dynamic-update-slice_fusion.6.refs_3_.refs_5_.refs_11_), channel_id=1, source_target_pairs={{0,4},{2,6},{4,0},{6,2},{8,12},{10,14},{12,8},{14,10},{16,20},{18,... | collective-permute-start | bytes 3145736 | tf_op jit(solution)/shard_map/ppermute | solution.py:30
  118.6 41.2 %collective-permute-start.14 = (bf16[256,2048]{1,0:T(8,128)(2,1)S(1)}, bf16[256,2048]{1,0:T(8,128)(2,1)S(1)}, u32[]{:S(2)}, u32[]{:S(2)}) collective-permute-start(bf16[256,2048]{1,0:T(8,128)(2,1)S(1)} %constant_dynamic-update-slice_fusion.4.refs_1_.refs_3_.refs_9_), channel_id=1, source_target_pairs={{0,2},{2,0},{4,6},{6,4},{8,10},{10,8},{12,14},{14,12},{16,18},{18,... | collective-permute-start | bytes 3145736 | tf_op jit(solution)/shard_map/ppermute | solution.py:30
  119.0 53.5 %collective-permute-start.18 = (bf16[128,2048]{1,0:T(8,128)(2,1)}, bf16[128,2048]{1,0:T(8,128)(2,1)S(1)}, u32[]{:S(2)}, u32[]{:S(2)}) collective-permute-start(bf16[128,2048]{1,0:T(8,128)(2,1)} %copy-done.42), channel_id=1, source_target_pairs={{0,2},{2,0},{4,6},{6,4},{8,10},{10,8},{12,14},{14,12},{16,18},{18,... | collective-permute-start | bytes 1572872 | tf_op jit(solution)/shard_map/ppermute | solution.py:30
  136.0 23.9 %copy-start.40 = (bf16[1024,384]{1,0:T(8,128)(2,1)}, bf16[1024,384]{1,0:T(8,128)(2,1)S(1)}, u32[]{:S(2)}) copy-start(bf16[1024,384]{1,0:T(8,128)(2,1)S(1)} %get-tuple-element.259.refs_1_) | copy-start | bytes 2359300
  173.2 5.2 %collective-permute-start.19 = (bf16[16,512,128]{2,1,0:T(8,128)(2,1)}, bf16[16,512,128]{2,1,0:T(8,128)(2,1)S(1)}, u32[]{:S(2)}, u32[]{:S(2)}) collective-permute-start(bf16[16,512,128]{2,1,0:T(8,128)(2,1)} %all-to-all-done.1.refs_5_), channel_id=1, source_target_pairs={{0,1},{1,0},{2,3},{3,2},{4,5},{5,4},{6,7},{7,6},{8,9},{9,8},{10,11... | collective-permute-start | bytes 6291464 | tf_op jit(solution)/shard_map/ppermute | solution.py:25
  174.4 24.3 %collective-permute-start.16 = (bf16[1024,384]{1,0:T(8,128)(2,1)}, bf16[1024,384]{1,0:T(8,128)(2,1)S(1)}, u32[]{:S(2)}, u32[]{:S(2)}) collective-permute-start(bf16[1024,384]{1,0:T(8,128)(2,1)} %copy-done.40), channel_id=1, source_target_pairs={{0,2},{2,0},{4,6},{6,4},{8,10},{10,8},{12,14},{14,12},{16,18},{18,... | collective-permute-start | bytes 2359304 | tf_op jit(solution)/shard_map/ppermute | solution.py:30
  175.4 23.3 %collective-permute-start.17 = (bf16[1024,384]{1,0:T(8,128)(2,1)}, bf16[1024,384]{1,0:T(8,128)(2,1)S(1)}, u32[]{:S(2)}, u32[]{:S(2)}) collective-permute-start(bf16[1024,384]{1,0:T(8,128)(2,1)} %copy-done.40), channel_id=1, source_target_pairs={{0,1},{1,0},{2,3},{3,2},{4,5},{5,4},{6,7},{7,6},{8,9},{9,8},{10,11... | collective-permute-start | bytes 2359304 | tf_op jit(solution)/shard_map/ppermute | solution.py:25
  198.7 5.3 %collective-permute-start.20 = (bf16[1024,384]{1,0:T(8,128)(2,1)S(1)}, bf16[1024,384]{1,0:T(8,128)(2,1)S(1)}, u32[]{:S(2)}, u32[]{:S(2)}) collective-permute-start(bf16[1024,384]{1,0:T(8,128)(2,1)S(1)} %collective-permute-done.16.refs_2_), channel_id=1, source_target_pairs={{0,1},{1,0},{2,3},{3,2},{4,5},{5,4},{6,7},{7,6},{8,9},{9,8},{10,11... | collective-permute-start | bytes 2359304 | tf_op jit(solution)/shard_map/ppermute | solution.py:25
  204.1 8.2 %collective-permute-start.21 = (bf16[16,512,128]{2,1,0:T(8,128)(2,1)S(1)}, bf16[16,512,128]{2,1,0:T(8,128)(2,1)S(1)}, u32[]{:S(2)}, u32[]{:S(2)}) collective-permute-start(bf16[16,512,128]{2,1,0:T(8,128)(2,1)S(1)} %outer.2), channel_id=1, source_target_pairs={{0,1},{1,0},{2,3},{3,2},{4,5},{5,4},{6,7},{7,6},{8,9},{9,8},{10,11... | collective-permute-start | bytes 6291464 | tf_op jit(solution)/shard_map/ppermute | solution.py:25
  204.3 8.0 %collective-permute-start.22 = (bf16[1024,256]{1,0:T(8,128)(2,1)S(1)}, bf16[1024,256]{1,0:T(8,128)(2,1)S(1)}, u32[]{:S(2)}, u32[]{:S(2)}) collective-permute-start(bf16[1024,256]{1,0:T(8,128)(2,1)S(1)} %get-tuple-element.258.refs_5_), channel_id=1, source_target_pairs={{0,1},{1,0},{2,3},{3,2},{4,5},{5,4},{6,7},{7,6},{8,9},{9,8},{10,11... | collective-permute-start | bytes 1572872 | tf_op jit(solution)/shard_map/ppermute | solution.py:25
  212.3 8.1 %collective-permute-start.24 = (f32[8,512]{1,0:T(8,128)S(1)}, f32[8,512]{1,0:T(8,128)S(1)}, u32[]{:S(2)}, u32[]{:S(2)}) collective-permute-start(f32[8,512]{1,0:T(8,128)S(1)} %get-tuple-element.269.refs_7_), channel_id=1, source_target_pairs={{0,2},{2,0},{4,6},{6,4},{8,10},{10,8},{12,14},{14,12},{16,18},{18,... | collective-permute-start | bytes 49160 | tf_op jit(solution)/shard_map/ppermute | solution.py:30
  213.3 7.1 %collective-permute-start.25 = (f32[8,512]{1,0:T(8,128)S(1)}, f32[8,512]{1,0:T(8,128)S(1)}, u32[]{:S(2)}, u32[]{:S(2)}) collective-permute-start(f32[8,512]{1,0:T(8,128)S(1)} %get-tuple-element.269.refs_7_), channel_id=1, source_target_pairs={{0,1},{1,0},{2,3},{3,2},{4,5},{5,4},{6,7},{7,6},{8,9},{9,8},{10,11... | collective-permute-start | bytes 49160 | tf_op jit(solution)/shard_map/ppermute | solution.py:25
  213.7 6.7 %collective-permute-start.26 = (f32[8,512]{1,0:T(8,128)S(1)}, f32[8,512]{1,0:T(8,128)S(1)}, u32[]{:S(2)}, u32[]{:S(2)}) collective-permute-start(f32[8,512]{1,0:T(8,128)S(1)} %get-tuple-element.269.refs_7_), channel_id=1, source_target_pairs={{0,3},{1,2},{2,1},{3,0},{4,7},{5,6},{6,5},{7,4},{8,11},{9,10},{10,... | collective-permute-start | bytes 49160 | tf_op jit(solution)/shard_map/ppermute | solution.py:1208
  226.6 75.8 %all-to-all-start.2 = ((bf16[16,512,128]{2,1,0:T(8,128)(2,1)}), bf16[16,512,128]{2,1,0:T(8,128)(2,1)}, u32[]{:S(2)}, u32[]{:S(2)}) async-start(bf16[16,512,128]{2,1,0:T(8,128)(2,1)} %copy-done.9), calls=%async_computation.2 | async-start | bytes 4194304 | tf_op jit(solution)/shard_map/all_to_all | solution.py:1224
  232.8 12.9 %collective-permute-start.23 = (bf16[512,256]{1,0:T(8,128)(2,1)}, bf16[512,256]{1,0:T(8,128)(2,1)S(1)}, u32[]{:S(2)}, u32[]{:S(2)}) collective-permute-start(bf16[512,256]{1,0:T(8,128)(2,1)} %copy-done.48), channel_id=1, source_target_pairs={{0,2},{2,0},{4,6},{6,4},{8,10},{10,8},{12,14},{14,12},{16,18},{18,... | collective-permute-start | bytes 786440 | tf_op jit(solution)/shard_map/ppermute | solution.py:30
  233.0 17.1 %collective-permute-start.27 = (bf16[512,256]{1,0:T(8,128)(2,1)}, bf16[512,256]{1,0:T(8,128)(2,1)S(1)}, u32[]{:S(2)}, u32[]{:S(2)}) collective-permute-start(bf16[512,256]{1,0:T(8,128)(2,1)} %copy-done.49), channel_id=1, source_target_pairs={{0,2},{2,0},{4,6},{6,4},{8,10},{10,8},{12,14},{14,12},{16,18},{18,... | collective-permute-start | bytes 786440 | tf_op jit(solution)/shard_map/ppermute | solution.py:30
  240.1 18.8 %copy-start.18 = (bf16[256,2048]{1,0:T(8,128)(2,1)S(1)}, bf16[256,2048]{1,0:T(8,128)(2,1)}, u32[]{:S(2)}) copy-start(bf16[256,2048]{1,0:T(8,128)(2,1)} %copy-done.16) | copy-start | bytes 3145732
  240.1 18.8 %copy-start.21 = (bf16[256,2048]{1,0:T(8,128)(2,1)S(1)}, bf16[256,2048]{1,0:T(8,128)(2,1)}, u32[]{:S(2)}) copy-start(bf16[256,2048]{1,0:T(8,128)(2,1)} %copy-done.19) | copy-start | bytes 3145732
  240.1 18.8 %copy-start.24 = (bf16[2048,384]{1,0:T(8,128)(2,1)S(1)}, bf16[2048,384]{1,0:T(8,128)(2,1)}, u32[]{:S(2)}) copy-start(bf16[2048,384]{1,0:T(8,128)(2,1)} %copy-done.22) | copy-start | bytes 4718596
  250.2 40.8 %collective-permute-start.28 = (bf16[256,2048]{1,0:T(8,128)(2,1)S(1)}, bf16[256,2048]{1,0:T(8,128)(2,1)S(1)}, u32[]{:S(2)}, u32[]{:S(2)}) collective-permute-start(bf16[256,2048]{1,0:T(8,128)(2,1)S(1)} %get-tuple-element.284), channel_id=1, source_target_pairs={{0,2},{2,0},{4,6},{6,4},{8,10},{10,8},{12,14},{14,12},{16,18},{18,... | collective-permute-start | bytes 3145736 | tf_op jit(solution)/shard_map/ppermute | solution.py:30
  251.4 39.5 %collective-permute-start.29 = (bf16[256,2048]{1,0:T(8,128)(2,1)S(1)}, bf16[256,2048]{1,0:T(8,128)(2,1)S(1)}, u32[]{:S(2)}, u32[]{:S(2)}) collective-permute-start(bf16[256,2048]{1,0:T(8,128)(2,1)S(1)} %get-tuple-element.285), channel_id=1, source_target_pairs={{0,4},{2,6},{4,0},{6,2},{8,12},{10,14},{12,8},{14,10},{16,20},{18,... | collective-permute-start | bytes 3145736 | tf_op jit(solution)/shard_map/ppermute | solution.py:30
  259.9 19.0 %copy-start.8 = (bf16[256,2048]{1,0:T(8,128)(2,1)S(1)}, bf16[256,2048]{1,0:T(8,128)(2,1)}, u32[]{:S(2)}) copy-start(bf16[256,2048]{1,0:T(8,128)(2,1)} %copy-done.5) | copy-start | bytes 3145732
  271.3 16.0 %collective-permute-start.30 = (f32[8,2048]{1,0:T(8,128)S(1)}, f32[8,2048]{1,0:T(8,128)S(1)}, u32[]{:S(2)}, u32[]{:S(2)}) collective-permute-start(f32[8,2048]{1,0:T(8,128)S(1)} %get-tuple-element.308.refs_1_), channel_id=1, source_target_pairs={{0,1},{1,0},{2,3},{3,2},{4,5},{5,4},{6,7},{7,6},{8,9},{9,8},{10,11... | collective-permute-start | bytes 196616 | tf_op jit(solution)/shard_map/ppermute | solution.py:25
  290.9 9.0 %collective-permute-start.31 = (bf16[16,256,128]{2,1,0:T(8,128)(2,1)S(1)}, bf16[16,256,128]{2,1,0:T(8,128)(2,1)S(1)}, u32[]{:S(2)}, u32[]{:S(2)}) collective-permute-start(bf16[16,256,128]{2,1,0:T(8,128)(2,1)S(1)} %get-tuple-element.307), channel_id=1, source_target_pairs={{0,1},{1,0},{2,3},{3,2},{4,5},{5,4},{6,7},{7,6},{8,9},{9,8},{10,11... | collective-permute-start | bytes 3145736 | tf_op jit(solution)/shard_map/ppermute | solution.py:25
  291.4 28.8 %collective-permute-start.32 = (bf16[256,2048]{1,0:T(8,128)(2,1)}, bf16[256,2048]{1,0:T(8,128)(2,1)S(1)}, u32[]{:S(2)}, u32[]{:S(2)}) collective-permute-start(bf16[256,2048]{1,0:T(8,128)(2,1)} %get-tuple-element.323), channel_id=1, source_target_pairs={{0,2},{2,0},{4,6},{6,4},{8,10},{10,8},{12,14},{14,12},{16,18},{18,... | collective-permute-start | bytes 3145736 | tf_op jit(solution)/shard_map/ppermute | solution.py:30
  292.3 27.9 %collective-permute-start.33 = (bf16[256,2048]{1,0:T(8,128)(2,1)}, bf16[256,2048]{1,0:T(8,128)(2,1)S(1)}, u32[]{:S(2)}, u32[]{:S(2)}) collective-permute-start(bf16[256,2048]{1,0:T(8,128)(2,1)} %get-tuple-element.324), channel_id=1, source_target_pairs={{0,4},{2,6},{4,0},{6,2},{8,12},{10,14},{12,8},{14,10},{16,20},{18,... | collective-permute-start | bytes 3145736 | tf_op jit(solution)/shard_map/ppermute | solution.py:30
  299.9 37.2 %collective-permute-start.34 = (bf16[128,2048]{1,0:T(8,128)(2,1)}, bf16[128,2048]{1,0:T(8,128)(2,1)}, u32[]{:S(2)}, u32[]{:S(2)}) collective-permute-start(bf16[128,2048]{1,0:T(8,128)(2,1)} %get-tuple-element.325), channel_id=1, source_target_pairs={{0,4},{2,6},{4,0},{6,2},{8,12},{10,14},{12,8},{14,10},{16,20},{18,... | collective-permute-start | bytes 1572872 | tf_op jit(solution)/shard_map/ppermute | solution.py:30
  300.3 36.8 %collective-permute-start.35 = (bf16[128,2048]{1,0:T(8,128)(2,1)}, bf16[128,2048]{1,0:T(8,128)(2,1)}, u32[]{:S(2)}, u32[]{:S(2)}) collective-permute-start(bf16[128,2048]{1,0:T(8,128)(2,1)} %get-tuple-element.326), channel_id=1, source_target_pairs={{0,2},{2,0},{4,6},{6,4},{8,10},{10,8},{12,14},{14,12},{16,18},{18,... | collective-permute-start | bytes 1572872 | tf_op jit(solution)/shard_map/ppermute | solution.py:30
  302.4 77.4 %all-to-all-start.3 = ((bf16[16,288,128]{2,1,0:T(8,128)(2,1)}), bf16[16,288,128]{2,1,0:T(8,128)(2,1)S(1)}, u32[]{:S(2)}, u32[]{:S(2)}) async-start(bf16[16,288,128]{2,1,0:T(8,128)(2,1)} %pad_maximum_fusion), calls=%async_computation.3 | async-start | bytes 2359296 | tf_op jit(solution)/shard_map/all_to_all | solution.py:1324
  310.0 33.1 %copy-start.31 = (bf16[256,2048]{1,0:T(8,128)(2,1)S(1)}, bf16[256,2048]{1,0:T(8,128)(2,1)}, u32[]{:S(2)}) copy-start(bf16[256,2048]{1,0:T(8,128)(2,1)} %copy-done.30) | copy-start | bytes 3145732
  310.0 33.1 %copy-start.33 = (bf16[256,2048]{1,0:T(8,128)(2,1)S(1)}, bf16[256,2048]{1,0:T(8,128)(2,1)}, u32[]{:S(2)}) copy-start(bf16[256,2048]{1,0:T(8,128)(2,1)} %copy-done.32) | copy-start | bytes 3145732
  344.5 29.0 %copy-start.65 = (bf16[64,2048]{1,0:T(8,128)(2,1)S(1)}, bf16[64,2048]{1,0:T(8,128)(2,1)}, u32[]{:S(2)}) copy-start(bf16[64,2048]{1,0:T(8,128)(2,1)} %copy-done.64) | copy-start | bytes 786436
  344.5 28.1 %collective-permute-start.36 = (bf16[128,2048]{1,0:T(8,128)(2,1)S(1)}, bf16[128,2048]{1,0:T(8,128)(2,1)S(1)}, u32[]{:S(2)}, u32[]{:S(2)}) collective-permute-start(bf16[128,2048]{1,0:T(8,128)(2,1)S(1)} %get-tuple-element.347), channel_id=1, source_target_pairs={{0,4},{2,6},{4,0},{6,2},{8,12},{10,14},{12,8},{14,10},{16,20},{18,... | collective-permute-start | bytes 1572872 | tf_op jit(solution)/shard_map/ppermute | solution.py:30
  345.6 27.1 %collective-permute-start.37 = (bf16[128,2048]{1,0:T(8,128)(2,1)S(1)}, bf16[128,2048]{1,0:T(8,128)(2,1)S(1)}, u32[]{:S(2)}, u32[]{:S(2)}) collective-permute-start(bf16[128,2048]{1,0:T(8,128)(2,1)S(1)} %get-tuple-element.348), channel_id=1, source_target_pairs={{0,2},{2,0},{4,6},{6,4},{8,10},{10,8},{12,14},{14,12},{16,18},{18,... | collective-permute-start | bytes 1572872 | tf_op jit(solution)/shard_map/ppermute | solution.py:30
  348.6 8.5 %collective-permute-start.38 = (bf16[64,2048]{1,0:T(8,128)(2,1)S(1)}, bf16[64,2048]{1,0:T(8,128)(2,1)S(1)}, u32[]{:S(2)}, u32[]{:S(2)}) collective-permute-start(bf16[64,2048]{1,0:T(8,128)(2,1)S(1)} %get-tuple-element.349), channel_id=1, source_target_pairs={{0,8},{2,10},{4,12},{6,14},{8,0},{10,2},{12,4},{14,6},{16,24},{18,... | collective-permute-start | bytes 786440 | tf_op jit(solution)/shard_map/ppermute | solution.py:30
  349.9 8.8 %collective-permute-start.39 = (bf16[64,2048]{1,0:T(8,128)(2,1)S(1)}, bf16[64,2048]{1,0:T(8,128)(2,1)S(1)}, u32[]{:S(2)}, u32[]{:S(2)}) collective-permute-start(bf16[64,2048]{1,0:T(8,128)(2,1)S(1)} %get-tuple-element.350), channel_id=1, source_target_pairs={{0,16},{2,18},{4,20},{6,22},{8,24},{10,26},{12,28},{14,30},{16,0},... | collective-permute-start | bytes 786440 | tf_op jit(solution)/shard_map/ppermute | solution.py:30
  350.8 21.9 %collective-permute-start.40 = (bf16[64,2048]{1,0:T(8,128)(2,1)S(1)}, bf16[64,2048]{1,0:T(8,128)(2,1)S(1)}, u32[]{:S(2)}, u32[]{:S(2)}) collective-permute-start(bf16[64,2048]{1,0:T(8,128)(2,1)S(1)} %get-tuple-element.351), channel_id=1, source_target_pairs={{0,24},{2,26},{4,28},{6,30},{8,16},{10,18},{12,20},{14,22},{16,8},... | collective-permute-start | bytes 786440 | tf_op jit(solution)/shard_map/ppermute | solution.py:30
  373.8 4.2 %collective-permute-start.41 = (bf16[64,2048]{1,0:T(8,128)(2,1)S(1)}, bf16[64,2048]{1,0:T(8,128)(2,1)}, u32[]{:S(2)}, u32[]{:S(2)}) collective-permute-start(bf16[64,2048]{1,0:T(8,128)(2,1)S(1)} %get-tuple-element.445), channel_id=1, source_target_pairs={{0,1},{1,0},{2,3},{3,2},{4,5},{5,4},{6,7},{7,6},{8,9},{9,8},{10,11... | collective-permute-start | bytes 786440 | tf_op jit(solution)/shard_map/ppermute | solution.py:25
  379.9 27.4 %copy-start.67 = (bf16[64,2048]{1,0:T(8,128)(2,1)S(1)}, bf16[64,2048]{1,0:T(8,128)(2,1)}, u32[]{:S(2)}) copy-start(bf16[64,2048]{1,0:T(8,128)(2,1)} %copy-done.66) | copy-start | bytes 786436
  379.9 3.1 collective-permute-start.42
  380.3 10.8 %collective-permute-start.43 = (bf16[64,2048]{1,0:T(8,128)(2,1)S(1)}, bf16[64,2048]{1,0:T(8,128)(2,1)S(1)}, u32[]{:S(2)}, u32[]{:S(2)}) collective-permute-start(bf16[64,2048]{1,0:T(8,128)(2,1)S(1)} %get-tuple-element.371), channel_id=1, source_target_pairs={{0,8},{2,10},{4,12},{6,14},{8,0},{10,2},{12,4},{14,6},{16,24},{18,... | collective-permute-start | bytes 786440 | tf_op jit(solution)/shard_map/ppermute | solution.py:30
  380.3 14.1 %collective-permute-start.44 = (bf16[64,2048]{1,0:T(8,128)(2,1)S(1)}, bf16[64,2048]{1,0:T(8,128)(2,1)S(1)}, u32[]{:S(2)}, u32[]{:S(2)}) collective-permute-start(bf16[64,2048]{1,0:T(8,128)(2,1)S(1)} %get-tuple-element.372), channel_id=1, source_target_pairs={{0,16},{2,18},{4,20},{6,22},{8,24},{10,26},{12,28},{14,30},{16,0},... | collective-permute-start | bytes 786440 | tf_op jit(solution)/shard_map/ppermute | solution.py:30
  382.5 23.5 %collective-permute-start.45 = (bf16[64,2048]{1,0:T(8,128)(2,1)S(1)}, bf16[64,2048]{1,0:T(8,128)(2,1)}, u32[]{:S(2)}, u32[]{:S(2)}) collective-permute-start(bf16[64,2048]{1,0:T(8,128)(2,1)S(1)} %get-tuple-element.373), channel_id=1, source_target_pairs={{0,24},{2,26},{4,28},{6,30},{8,16},{10,18},{12,20},{14,22},{16,8},... | collective-permute-start | bytes 786440 | tf_op jit(solution)/shard_map/ppermute | solution.py:30
  408.7 4.8 %collective-permute-start.46 = (bf16[64,2048]{1,0:T(8,128)(2,1)S(1)}, bf16[64,2048]{1,0:T(8,128)(2,1)S(1)}, u32[]{:S(2)}, u32[]{:S(2)}) collective-permute-start(bf16[64,2048]{1,0:T(8,128)(2,1)S(1)} %fusion.8), channel_id=1, source_target_pairs={{0,1},{1,0},{2,3},{3,2},{4,5},{5,4},{6,7},{7,6},{8,9},{9,8},{10,11... | collective-permute-start | bytes 786440 | tf_op jit(solution)/shard_map/ppermute | solution.py:25
  (69 other events, 336.7 us)

commit v4 on v3

--- a/solution.py
+++ b/solution.py
@@ -1097,7 +1097,8 @@
     all_tokens = [one, one_x, two, two_y]
 
     one, two = jnp.concatenate([mine_one, mine_y]), jnp.concatenate([mine_two, mine_x])
-    here, there = join(here, swap_cores(here))
+    here, there, feed_deal = join(here, swap_cores(here), feed_deal)
+    feed_mine = lax.all_to_all(feed_deal, "blk", 0, 0, tiled=True)
     steps = jnp.arange(ROT // 2, dtype=F32)
     speed = jnp.tile(10000.0 ** (-2.0 * steps / ROT), 4).reshape(1, 128)
     w_triple, w_near, marks, norms, shifts = run_kernel(
@@ -1114,8 +1115,6 @@
         name="deal",
         moved=8e6,
     )(ids, speed, here, there)
-    norms, feed_deal = join(norms, feed_deal)
-    feed_mine = lax.all_to_all(feed_deal, "blk", 0, 0, tiled=True)
     normed_feed, stats, mine = run_kernel(
         lambda *refs: norm_kernel(r, *refs),
         [((count, width), BF), ((count, 128), F32), ((count, 384), BF)],
@@ -1132,7 +1131,7 @@
 
     peer, mine_there = from_peer(mine, 1), swap_cores(mine)
     all_cotangent = [one, one_x, two, two_y]
-    feed_mine, w_peer, *all_cotangent = join(feed_mine, w_peer, *all_cotangent)
+    feed_mine, *all_cotangent = join(feed_mine, *all_cotangent)
 
     feed_mine, feed_other = join(feed_mine, swap_cores(feed_mine))
 
@@ -1220,7 +1219,7 @@
         name="key",
         moved=6e6,
     )(ids, *four, grads, grads_there, lines, lines_peer, lines_there, lines_far, marks)
-    send2, feed_grads, attended = join(send2, feed_grads, attended)
+    feed_grads, attended = join(feed_grads, attended)
     feed_dealt = lax.all_to_all(feed_grads, "blk", 0, 0, tiled=True)
     branches = run_kernel(
         lambda *refs: branch_kernel(r, *refs),

time: 418 us -> 409 us (0.978)
  starting transfers between devices: 89.9 us -> 81.3 us
  local copies, waits for them, and re-layouts: 53.1 us -> 45.7 us
  Pallas kernels: 96.9 us -> 102 us
    unnamed x179 -> x191, local copies, waits for them, and re-layouts: 41.6 us -> 35.2 us
    pallas_call x2, Pallas kernels: 9.7 us -> 13.9 us  [outer(): run_kernel(lambda *refs: outer_kernel(units, *refs), [((blocks, 2 * units...]
  transfers between devices with their start and end apart: 51 -> 51, of which waited for: 19 -> 23; matrix products, arithmetic and copies ran while one was open for 6% -> 6% of each run, Pallas kernels for 21% -> 25%
where the time goes in v4:
time: 409 us; the launch traced here: 407 us
  waiting for transfers between devices  164 us (40%)
  Pallas kernels  102 us (25%)
  starting transfers between devices  81.3 us (20%)
  local copies, waits for them, and re-layouts  45.7 us (11%)
  other arithmetic  12.8 us (3%)
    ppermute x33, waiting for transfers between devices, from_peer(): return lax.ppermute(value, 'blk', [(i, i ^ mask) for i in range(count)])  157 us
    ppermute x33, starting transfers between devices, from_peer(): return lax.ppermute(value, 'blk', [(i, i ^ mask) for i in range(count)])  35.9 us
    unnamed x191, local copies, waits for them, and re-layouts  35.2 us
    ppermute x13, starting transfers between devices, swap_cores(): return lax.ppermute(value, 'tp', [(0, 1), (1, 0)])  23.6 us
    pallas_call x2, Pallas kernels, outer(): run_kernel(lambda *refs: outer_kernel(units, *refs), [((blocks, 2 * units...  13.9 us
    pallas_call x1, Pallas kernels, body(): run_kernel(lambda *refs: feed_kernel(units, blocks, *refs), [((count, 2 *...  11.5 us
    pallas_call x1, Pallas kernels, body(): run_kernel(lambda *refs: norm_kernel(r, *refs), [((count, width), BF), ((...  10.3 us
    pallas_call x1, Pallas kernels, body(): run_kernel(lambda *refs: feed_unpack_kernel(units, *refs), [(w_in.shape,...  10.2 us
  transfers between devices with their start and end apart: 51, of which 23 were waited for; matrix products, arithmetic and copies ran while one was open for 6% of the time, Pallas kernels for 25%

profile of v4, /device:TPU:11, one launch (start us, length us, event | category | flops | bytes accessed | tf_op | source)
XLA Modules:
  0.0 407.3 jit_solution(16134983545556447336)
XLA Ops:
  2.1 2.3 collective-permute-start.2
  7.8 2.1 fusion.13
  9.8 1.5 collective-permute-start
  12.5 1.7 feed_deal.1
  14.3 1.6 collective-permute-done.2
  15.9 14.0 %collective-permute-done.3 = bf16[64,2048]{1,0:T(8,128)(2,1)} collective-permute-done((bf16[64,2048]{1,0:T(8,128)(2,1)S(1)}, bf16[64,2048]{1,0:T(8,128)(2,1)}, u32[]{:S(2)}, u32[]{:S(2)}) %collective-permute-start.3) | collective-permute-done | bytes 262176 | tf_op jit(solution)/shard_map/ppermute | solution.py:30
  31.1 1.4 collective-permute-start.9
  38.5 4.7 %all-to-all-start = ((bf16[16,272,128]{2,1,0:T(8,128)(2,1)}), bf16[16,272,128]{2,1,0:T(8,128)(2,1)S(1)}, u32[]{:S(2)}, u32[]{:S(2)}) async-start(bf16[16,272,128]{2,1,0:T(8,128)(2,1)} %pad_maximum_fusion.1), calls=%async_computation | async-start | bytes 2228224 | tf_op jit(solution)/shard_map/all_to_all | solution.py:1078
  43.3 6.7 %collective-permute-done.9 = bf16[64,2048]{1,0:T(8,128)(2,1)} collective-permute-done((bf16[64,2048]{1,0:T(8,128)(2,1)S(1)}, bf16[64,2048]{1,0:T(8,128)(2,1)}, u32[]{:S(2)}, u32[]{:S(2)}) %collective-permute-start.9) | collective-permute-done | bytes 262176 | tf_op jit(solution)/shard_map/ppermute | solution.py:30
  52.1 1.4 collective-permute-start.7
  57.9 28.1 %collective-permute-done.12 = bf16[128,2048]{1,0:T(8,128)(2,1)S(1)} collective-permute-done((bf16[128,2048]{1,0:T(8,128)(2,1)S(1)}, bf16[128,2048]{1,0:T(8,128)(2,1)S(1)}, u32[]{:S(2)}, u32[]{:S(2)}) %collective-permute-start.12) | collective-permute-done | bytes 524320 | tf_op jit(solution)/shard_map/ppermute | solution.py:30
  86.0 1.5 collective-permute-done.11
  90.3 10.1 %collective-permute-start.13 = (bf16[16,272,128]{2,1,0:T(8,128)(2,1)S(1)}, bf16[16,272,128]{2,1,0:T(8,128)(2,1)S(1)}, u32[]{:S(2)}, u32[]{:S(2)}) collective-permute-start(bf16[16,272,128]{2,1,0:T(8,128)(2,1)S(1)} %all-to-all-done.refs_2_), channel_id=1, source_target_pairs={{0,1},{1,0},{2,3},{3,2},{4,5},{5,4},{6,7},{7,6},{8,9},{9,8},{10,11... | collective-permute-start | bytes 3342344 | tf_op jit(solution)/shard_map/ppermute | solution.py:25
  100.4 2.4 collective-permute-done.13.refs_3_
  103.8 5.6 %all-to-all-start.1 = ((bf16[16,512,128]{2,1,0:T(8,128)(2,1)}), bf16[16,512,128]{2,1,0:T(8,128)(2,1)}, u32[]{:S(2)}, u32[]{:S(2)}) async-start(bf16[16,512,128]{2,1,0:T(8,128)(2,1)} %feed_deal.1), calls=%async_computation.1 | async-start | bytes 4194304 | tf_op jit(solution)/shard_map/all_to_all | solution.py:1101
  111.4 1.4 copy-done.13
  114.0 3.5 deal.1
  118.4 1.5 copy-done.15
  121.1 10.3 %norm.1 = (bf16[1024,2048]{1,0:T(8,128)(2,1)S(1)}, f32[1024,128]{1,0:T(8,128)S(1)}, bf16[1024,384]{1,0:T(8,128)(2,1)S(1)}) custom-call(s32[2]{0:T(128)S(1)} %pad_add_fusion.refs_0_, bf16[256,2048]{1,0:T(8,128)(2,1)S(1)} %copy-done.10, bf16[256,2048]{1,0:T(8,128)(2,1)S(1)} %copy-done.18, bf16[256,2048]{1,0:T(8,128)(2,1)S(1)} %copy-done.7, ...), custom_call_target="tpu_custom_call" | custom-call | flops 1610612736 | bytes 22000000 | tf_op jit(solution)/shard_map/norm/pallas_call | solution.py:1118
  131.5 2.0 copy-done.2
  134.3 19.9 %collective-permute-done.15.refs_4_.refs_6_.refs_12_ = bf16[256,2048]{1,0:T(8,128)(2,1)S(1)} collective-permute-done((bf16[256,2048]{1,0:T(8,128)(2,1)S(1)}, bf16[256,2048]{1,0:T(8,128)(2,1)S(1)}, u32[]{:S(2)}, u32[]{:S(2)}) %collective-permute-start.15) | collective-permute-done | bytes 1048608 | tf_op jit(solution)/shard_map/ppermute | solution.py:30
  154.2 1.4 all-to-all-done.1.refs_5_
  155.6 2.0 collective-permute-start.18
  159.7 2.0 collective-permute-done.18.refs_6_
  161.6 9.8 %collective-permute-done.19.refs_9_.refs_4_ = bf16[128,2048]{1,0:T(8,128)(2,1)S(1)} collective-permute-done((bf16[128,2048]{1,0:T(8,128)(2,1)}, bf16[128,2048]{1,0:T(8,128)(2,1)S(1)}, u32[]{:S(2)}, u32[]{:S(2)}) %collective-permute-start.19) | collective-permute-done | bytes 524320 | tf_op jit(solution)/shard_map/ppermute | solution.py:30
  171.4 2.4 copy-done.3
  174.8 11.5 %feed.1 = (bf16[1024,512]{1,0:T(8,128)(2,1)S(1)}, bf16[1024,512]{1,0:T(8,128)(2,1)S(1)}, bf16[512,1024]{1,0:T(8,128)(2,1)S(1)}, bf16[512,1024]{1,0:T(8,128)(2,1)...) custom-call(bf16[1024,2048]{1,0:T(8,128)(2,1)S(1)} %copy-done.3, ...), custom_call_target="tpu_custom_call" | custom-call | flops 4294967296 | bytes 20000000 | tf_op jit(solution)/shard_map/feed/pallas_call | solution.py:1139
  189.1 7.5 %outer.2 = bf16[16,512,128]{2,1,0:T(8,128)(2,1)S(1)} custom-call(bf16[512,1024]{1,0:T(8,128)(2,1)S(1)} %get-tuple-element.249.refs_0_, bf16[512,1024]{1,0:T(8,128)(2,1)S(1)} %get-tuple-element.250.refs_1_, bf16[1024,2048]{1,0:T(8,128)(2,1)S(1)} %copy-done.4, bf16[256,2048]{1,0:T(8,128)(2,1)S(1)} %constant_dynamic-update-slice_fusion.4.refs_1_.refs_3_.refs_9_, ...), custom_call_target="tpu_custom_call" | custom-call | flops 2147483648 | bytes 12000000 | tf_op jit(solution)/shard_map/outer/pallas_call | solution.py:1164
  197.3 7.8 %query.1 = (bf16[512,256]{1,0:T(8,128)(2,1)S(1)}, bf16[512,256]{1,0:T(8,128)(2,1)S(1)}, bf16[512,256]{1,0:T(8,128)(2,1)S(1)}, f32[8,512]{1,0:T(8,128)S(1)}) custom-call(s32[2]{0:T(128)S(1)} %pad_add_fusion.refs_0_, bf16[1024,384]{1,0:T(8,128)(2,1)S(1)} %copy-done.40, bf16[1024,384]{1,0:T(8,128)(2,1)S(1)} %collective-permute-done.16.refs_2_, ...), custom_call_target="tpu_custom_call" | custom-call | flops 2147483648 | bytes 6000000 | tf_op jit(solution)/shard_map/query/pallas_call | solution.py:1190
  207.8 6.4 %outer.3 = bf16[16,512,128]{2,1,0:T(8,128)(2,1)S(1)} custom-call(bf16[512,1024]{1,0:T(8,128)(2,1)S(1)} %get-tuple-element.249.refs_0_, bf16[512,1024]{1,0:T(8,128)(2,1)S(1)} %get-tuple-element.250.refs_1_, bf16[1024,2048]{1,0:T(8,128)(2,1)S(1)} %copy-done.4, bf16[256,2048]{1,0:T(8,128)(2,1)S(1)} %constant_dynamic-update-slice_fusion.4.refs_1_.refs_3_.refs_9_, ...), custom_call_target="tpu_custom_call" | custom-call | flops 2147483648 | bytes 12000000 | tf_op jit(solution)/shard_map/outer/pallas_call | solution.py:1164
  214.3 1.3 copy-done.5
  215.6 6.0 %all-to-all-start.2 = ((bf16[16,512,128]{2,1,0:T(8,128)(2,1)}), bf16[16,512,128]{2,1,0:T(8,128)(2,1)}, u32[]{:S(2)}, u32[]{:S(2)}) async-start(bf16[16,512,128]{2,1,0:T(8,128)(2,1)} %copy-done.5), calls=%async_computation.2 | async-start | bytes 4194304 | tf_op jit(solution)/shard_map/all_to_all | solution.py:1223
  229.8 4.5 %key.1 = (bf16[512,256]{1,0:T(8,128)(2,1)S(1)}, bf16[512,256]{1,0:T(8,128)(2,1)S(1)}) custom-call(s32[2]{0:T(128)S(1)} %pad_add_fusion.refs_0_, bf16[1024,384]{1,0:T(8,128)(2,1)S(1)} %copy-done.41, bf16[1024,384]{1,0:T(8,128)(2,1)S(1)} %copy-done.43, bf16[1024,384]{1,0:T(8,128)(2,1)S(1)} %copy-done.45, bf16[1024,384]{1,0:T(8,128)(2,1)S(1)} %copy-done.47, ...), custom_call_target="tpu_custom_call" | custom-call | flops 2147483648 | bytes 6000000 | tf_op jit(solution)/shard_map/key/pallas_call | solution.py:1211
  235.7 5.5 %branch.1 = (bf16[256,2048]{1,0:T(8,128)(2,1)S(1)}, bf16[256,2048]{1,0:T(8,128)(2,1)S(1)}, bf16[256,2048]{1,0:T(8,128)(2,1)S(1)}, bf16[256,2048]{1,0:T(8,128)(2,1)S(1)}) custom-call(bf16[1024,512]{1,0:T(8,128)(2,1)S(1)} %copy-done.65, bf16[512,256]{1,0:T(8,128)(2,1)S(1)} %copy-done.69, bf16[512,2048]{1,0:T(8,128)(2,1)S(1)} %copy-done.61, ...), custom_call_target="tpu_custom_call" | custom-call | flops 2684354560 | bytes 9000000 | tf_op jit(solution)/shard_map/branch/pallas_call | solution.py:1224
  241.2 4.6 %collective-permute-done.27.refs_3_ = bf16[512,256]{1,0:T(8,128)(2,1)S(1)} collective-permute-done((bf16[512,256]{1,0:T(8,128)(2,1)S(1)}, bf16[512,256]{1,0:T(8,128)(2,1)S(1)}, u32[]{:S(2)}, u32[]{:S(2)}) %collective-permute-start.27) | collective-permute-done | bytes 262176 | tf_op jit(solution)/shard_map/ppermute | solution.py:30
  246.8 8.2 %collective-permute-start.29 = (bf16[256,2048]{1,0:T(8,128)(2,1)S(1)}, bf16[256,2048]{1,0:T(8,128)(2,1)S(1)}, u32[]{:S(2)}, u32[]{:S(2)}) collective-permute-start(bf16[256,2048]{1,0:T(8,128)(2,1)S(1)} %get-tuple-element.279), channel_id=1, source_target_pairs={{0,4},{2,6},{4,0},{6,2},{8,12},{10,14},{12,8},{14,10},{16,20},{18,... | collective-permute-start | bytes 3145736 | tf_op jit(solution)/shard_map/ppermute | solution.py:30
  255.0 9.1 %inputs.1 = (bf16[256,2048]{1,0:T(8,128)(2,1)S(1)}, bf16[256,2048]{1,0:T(8,128)(2,1)}, bf16[256,2048]{1,0:T(8,128)(2,1)S(1)}, bf16[256,2048]{1,0:T(8,128)(2,1)},...) custom-call(bf16[512,256]{1,0:T(8,128)(2,1)S(1)} %copy-done.67, ...), custom_call_target="tpu_custom_call" | custom-call | flops 3758096384 | bytes 16000000 | tf_op jit(solution)/shard_map/inputs/pallas_call | solution.py:1268
  265.1 1.9 collective-permute-start.30
  267.0 8.6 %line_outer.1 = (f32[16,256,128]{2,1,0:T(8,128)S(1)}, bf16[16,256,128]{2,1,0:T(8,128)(2,1)S(1)}) custom-call(s32[2]{0:T(128)S(1)} %pad_add_fusion.refs_0_, bf16[1024,384]{1,0:T(8,128)(2,1)S(1)} %get-tuple-element.295.refs_1_, bf16[1024,128]{1,0:T(8,128)(2,1)S(1)} %get-tuple-element.296.refs_2_, bf16[256,2048]{1,0:T(8,128)(2,1)S(1)} %copy-done.11, ...), custom_call_target="tpu_custom_call" | custom-call | flops 2147483648 | bytes 12000000 | tf_op jit(solution)/shard_map/line_outer/pallas_call | solution.py:1287
  275.6 2.1 collective-permute-done.28.got1
  277.7 3.8 collective-permute-done.29.got2
  281.5 2.1 collective-permute-start.31
  283.8 2.4 collective-permute-start.33
  286.2 3.3 small.1
  289.5 3.4 fold.2
  294.9 4.6 %all-to-all-start.3 = ((bf16[16,288,128]{2,1,0:T(8,128)(2,1)}), bf16[16,288,128]{2,1,0:T(8,128)(2,1)S(1)}, u32[]{:S(2)}, u32[]{:S(2)}) async-start(bf16[16,288,128]{2,1,0:T(8,128)(2,1)} %pad_maximum_fusion), calls=%async_computation.3 | async-start | bytes 2359296 | tf_op jit(solution)/shard_map/all_to_all | solution.py:1323
  299.5 10.2 %feed_unpack.1 = (f32[128,4096]{1,0:T(8,128)}, f32[4096,128]{1,0:T(8,128)}) custom-call(bf16[16,512,128]{2,1,0:T(8,128)(2,1)} %all-to-all-done.2.refs_0_), custom_call_target="tpu_custom_call" | custom-call | bytes 6000000 | tf_op jit(solution)/shard_map/feed_unpack/pallas_call | solution.py:1324
  309.7 4.3 %collective-permute-done.33.got2 = bf16[256,2048]{1,0:T(8,128)(2,1)S(1)} collective-permute-done((bf16[256,2048]{1,0:T(8,128)(2,1)}, bf16[256,2048]{1,0:T(8,128)(2,1)S(1)}, u32[]{:S(2)}, u32[]{:S(2)}) %collective-permute-start.33) | collective-permute-done | bytes 1048608 | tf_op jit(solution)/shard_map/ppermute | solution.py:30
  314.0 16.5 %collective-permute-done.34.refs_1_ = bf16[128,2048]{1,0:T(8,128)(2,1)} collective-permute-done((bf16[128,2048]{1,0:T(8,128)(2,1)}, bf16[128,2048]{1,0:T(8,128)(2,1)}, u32[]{:S(2)}, u32[]{:S(2)}) %collective-permute-start.34) | collective-permute-done | bytes 524320 | tf_op jit(solution)/shard_map/ppermute | solution.py:30
  332.6 3.9 by_z.2
  336.5 1.4 fold.3
  339.1 1.8 collective-permute-start.37
  340.9 2.6 collective-permute-start.40
  343.6 2.9 collective-permute-done.38
  346.5 2.8 collective-permute-done.39
  349.3 16.9 %collective-permute-done.40 = bf16[64,2048]{1,0:T(8,128)(2,1)S(1)} collective-permute-done((bf16[64,2048]{1,0:T(8,128)(2,1)S(1)}, bf16[64,2048]{1,0:T(8,128)(2,1)S(1)}, u32[]{:S(2)}, u32[]{:S(2)}) %collective-permute-start.40) | collective-permute-done | bytes 262176 | tf_op jit(solution)/shard_map/ppermute | solution.py:30
  367.3 1.6 collective-permute-start.41
  373.1 2.2 collective-permute-start.45
  375.3 2.4 unpack.1
  377.8 4.1 %collective-permute-done.43 = bf16[64,2048]{1,0:T(8,128)(2,1)S(1)} collective-permute-done((bf16[64,2048]{1,0:T(8,128)(2,1)S(1)}, bf16[64,2048]{1,0:T(8,128)(2,1)S(1)}, u32[]{:S(2)}, u32[]{:S(2)}) %collective-permute-start.43) | collective-permute-done | bytes 262176 | tf_op jit(solution)/shard_map/ppermute | solution.py:30
  381.9 3.1 collective-permute-done.44
  385.0 13.2 %collective-permute-done.45 = bf16[64,2048]{1,0:T(8,128)(2,1)} collective-permute-done((bf16[64,2048]{1,0:T(8,128)(2,1)S(1)}, bf16[64,2048]{1,0:T(8,128)(2,1)}, u32[]{:S(2)}, u32[]{:S(2)}) %collective-permute-start.45) | collective-permute-done | bytes 262176 | tf_op jit(solution)/shard_map/ppermute | solution.py:30
  399.6 1.4 fusion.8
  401.0 1.3 collective-permute-start.46
  (304 shorter events, 67.1 us)
Async XLA Ops:
  1.8 30.6 %copy-start.70 = (bf16[64,2048]{1,0:T(8,128)(2,1)}, bf16[64,2048]{1,0:T(8,128)(2,1)S(1)}, u32[]{:S(2)}) copy-start(bf16[64,2048]{1,0:T(8,128)(2,1)S(1)} %get-tuple-element.201) | copy-start | bytes 786436
  1.8 12.4 %collective-permute-start.1 = (bf16[64,2048]{1,0:T(8,128)(2,1)S(1)}, bf16[64,2048]{1,0:T(8,128)(2,1)}, u32[]{:S(2)}, u32[]{:S(2)}) collective-permute-start(bf16[64,2048]{1,0:T(8,128)(2,1)S(1)} %get-tuple-element.201), channel_id=1, source_target_pairs={{0,8},{2,10},{4,12},{6,14},{8,0},{10,2},{12,4},{14,6},{16,24},{18,... | collective-permute-start | bytes 786440 | tf_op jit(solution)/shard_map/ppermute | solution.py:30
  2.1 13.8 %collective-permute-start.2 = (bf16[64,2048]{1,0:T(8,128)(2,1)S(1)}, bf16[64,2048]{1,0:T(8,128)(2,1)}, u32[]{:S(2)}, u32[]{:S(2)}) collective-permute-start(bf16[64,2048]{1,0:T(8,128)(2,1)S(1)} %get-tuple-element.201), channel_id=1, source_target_pairs={{0,16},{2,18},{4,20},{6,22},{8,24},{10,26},{12,28},{14,30},{16,0},... | collective-permute-start | bytes 786440 | tf_op jit(solution)/shard_map/ppermute | solution.py:30
  4.4 25.4 %collective-permute-start.3 = (bf16[64,2048]{1,0:T(8,128)(2,1)S(1)}, bf16[64,2048]{1,0:T(8,128)(2,1)}, u32[]{:S(2)}, u32[]{:S(2)}) collective-permute-start(bf16[64,2048]{1,0:T(8,128)(2,1)S(1)} %get-tuple-element.201), channel_id=1, source_target_pairs={{0,24},{2,26},{4,28},{6,30},{8,16},{10,18},{12,20},{14,22},{16,8},... | collective-permute-start | bytes 786440 | tf_op jit(solution)/shard_map/ppermute | solution.py:30
  9.8 20.0 %collective-permute-start = (bf16[8,256,128]{2,1,0:T(8,128)(2,1)}, bf16[8,256,128]{2,1,0:T(8,128)(2,1)}, u32[]{:S(2)}, u32[]{:S(2)}) collective-permute-start(bf16[8,256,128]{2,1,0:T(8,128)(2,1)} %get-tuple-element.432), channel_id=1, source_target_pairs={{0,1},{1,0},{2,3},{3,2},{4,5},{5,4},{6,7},{7,6},{8,9},{9,8},{10,11... | collective-permute-start | bytes 1572872 | tf_op jit(solution)/shard_map/ppermute | solution.py:25
  14.3 35.7 %copy-start.72 = (bf16[64,2048]{1,0:T(8,128)(2,1)}, bf16[64,2048]{1,0:T(8,128)(2,1)S(1)}, u32[]{:S(2)}) copy-start(bf16[64,2048]{1,0:T(8,128)(2,1)S(1)} %constant_dynamic-slice_fusion.3) | copy-start | bytes 786436
  29.8 13.4 %collective-permute-start.10 = (bf16[64,2048]{1,0:T(8,128)(2,1)S(1)}, bf16[64,2048]{1,0:T(8,128)(2,1)}, u32[]{:S(2)}, u32[]{:S(2)}) collective-permute-start(bf16[64,2048]{1,0:T(8,128)(2,1)S(1)} %constant_dynamic-slice_fusion.3), channel_id=1, source_target_pairs={{0,24},{2,26},{4,28},{6,30},{8,16},{10,18},{12,20},{14,22},{16,8},... | collective-permute-start | bytes 786440 | tf_op jit(solution)/shard_map/ppermute | solution.py:30
  31.1 12.1 %collective-permute-start.8 = (bf16[64,2048]{1,0:T(8,128)(2,1)S(1)}, bf16[64,2048]{1,0:T(8,128)(2,1)}, u32[]{:S(2)}, u32[]{:S(2)}) collective-permute-start(bf16[64,2048]{1,0:T(8,128)(2,1)S(1)} %constant_dynamic-slice_fusion.3), channel_id=1, source_target_pairs={{0,8},{2,10},{4,12},{6,14},{8,0},{10,2},{12,4},{14,6},{16,24},{18,... | collective-permute-start | bytes 786440 | tf_op jit(solution)/shard_map/ppermute | solution.py:30
  31.1 18.9 %collective-permute-start.9 = (bf16[64,2048]{1,0:T(8,128)(2,1)S(1)}, bf16[64,2048]{1,0:T(8,128)(2,1)}, u32[]{:S(2)}, u32[]{:S(2)}) collective-permute-start(bf16[64,2048]{1,0:T(8,128)(2,1)S(1)} %constant_dynamic-slice_fusion.3), channel_id=1, source_target_pairs={{0,16},{2,18},{4,20},{6,22},{8,24},{10,26},{12,28},{14,30},{16,0},... | collective-permute-start | bytes 786440 | tf_op jit(solution)/shard_map/ppermute | solution.py:30
  34.7 16.3 %collective-permute-start.5 = (bf16[128,2048]{1,0:T(8,128)(2,1)S(1)}, bf16[128,2048]{1,0:T(8,128)(2,1)}, u32[]{:S(2)}, u32[]{:S(2)}) collective-permute-start(bf16[128,2048]{1,0:T(8,128)(2,1)S(1)} %pad_maximum_fusion.3), channel_id=1, source_target_pairs={{0,2},{2,0},{4,6},{6,4},{8,10},{10,8},{12,14},{14,12},{16,18},{18,... | collective-permute-start | bytes 1572872 | tf_op jit(solution)/shard_map/ppermute | solution.py:30
  35.0 16.0 %collective-permute-start.4 = (bf16[128,2048]{1,0:T(8,128)(2,1)S(1)}, bf16[128,2048]{1,0:T(8,128)(2,1)}, u32[]{:S(2)}, u32[]{:S(2)}) collective-permute-start(bf16[128,2048]{1,0:T(8,128)(2,1)S(1)} %pad_maximum_fusion.2), channel_id=1, source_target_pairs={{0,4},{2,6},{4,0},{6,2},{8,12},{10,14},{12,8},{14,10},{16,20},{18,... | collective-permute-start | bytes 1572872 | tf_op jit(solution)/shard_map/ppermute | solution.py:30
  38.5 51.7 %all-to-all-start = ((bf16[16,272,128]{2,1,0:T(8,128)(2,1)}), bf16[16,272,128]{2,1,0:T(8,128)(2,1)S(1)}, u32[]{:S(2)}, u32[]{:S(2)}) async-start(bf16[16,272,128]{2,1,0:T(8,128)(2,1)} %pad_maximum_fusion.1), calls=%async_computation | async-start | bytes 2228224 | tf_op jit(solution)/shard_map/all_to_all | solution.py:1078
  52.1 35.3 %collective-permute-start.7 = (bf16[256,2048]{1,0:T(8,128)(2,1)S(1)}, bf16[256,2048]{1,0:T(8,128)(2,1)S(1)}, u32[]{:S(2)}, u32[]{:S(2)}) collective-permute-start(bf16[256,2048]{1,0:T(8,128)(2,1)S(1)} %constant_dynamic-update-slice_fusion.2.refs_3_.refs_7_.refs_5_), channel_id=1, source_target_pairs={{0,4},{2,6},{4,0},{6,2},{8,12},{10,14},{12,8},{14,10},{16,20},{18,... | collective-permute-start | bytes 3145736 | tf_op jit(solution)/shard_map/ppermute | solution.py:30
  54.7 32.8 %copy-start.9 = (bf16[256,2048]{1,0:T(8,128)(2,1)}, bf16[256,2048]{1,0:T(8,128)(2,1)S(1)}, u32[]{:S(2)}) copy-start(bf16[256,2048]{1,0:T(8,128)(2,1)S(1)} %constant_dynamic-update-slice_fusion.refs_1_.refs_5_.refs_3_) | copy-start | bytes 3145732
  54.7 34.5 %collective-permute-start.6 = (bf16[256,2048]{1,0:T(8,128)(2,1)S(1)}, bf16[256,2048]{1,0:T(8,128)(2,1)S(1)}, u32[]{:S(2)}, u32[]{:S(2)}) collective-permute-start(bf16[256,2048]{1,0:T(8,128)(2,1)S(1)} %constant_dynamic-update-slice_fusion.refs_1_.refs_5_.refs_3_), channel_id=1, source_target_pairs={{0,2},{2,0},{4,6},{6,4},{8,10},{10,8},{12,14},{14,12},{16,18},{18,... | collective-permute-start | bytes 3145736 | tf_op jit(solution)/shard_map/ppermute | solution.py:30
  56.3 29.7 %collective-permute-start.12 = (bf16[128,2048]{1,0:T(8,128)(2,1)S(1)}, bf16[128,2048]{1,0:T(8,128)(2,1)S(1)}, u32[]{:S(2)}, u32[]{:S(2)}) collective-permute-start(bf16[128,2048]{1,0:T(8,128)(2,1)S(1)} %pad_maximum_fusion.5), channel_id=1, source_target_pairs={{0,2},{2,0},{4,6},{6,4},{8,10},{10,8},{12,14},{14,12},{16,18},{18,... | collective-permute-start | bytes 1572872 | tf_op jit(solution)/shard_map/ppermute | solution.py:30
  57.6 29.9 %copy-start.74 = (bf16[128,2048]{1,0:T(8,128)(2,1)}, bf16[128,2048]{1,0:T(8,128)(2,1)S(1)}, u32[]{:S(2)}) copy-start(bf16[128,2048]{1,0:T(8,128)(2,1)S(1)} %pad_maximum_fusion.4) | copy-start | bytes 1572868
  57.6 29.9 %collective-permute-start.11 = (bf16[128,2048]{1,0:T(8,128)(2,1)S(1)}, bf16[128,2048]{1,0:T(8,128)(2,1)S(1)}, u32[]{:S(2)}, u32[]{:S(2)}) collective-permute-start(bf16[128,2048]{1,0:T(8,128)(2,1)S(1)} %pad_maximum_fusion.4), channel_id=1, source_target_pairs={{0,4},{2,6},{4,0},{6,2},{8,12},{10,14},{12,8},{14,10},{16,20},{18,... | collective-permute-start | bytes 1572872 | tf_op jit(solution)/shard_map/ppermute | solution.py:30
  90.3 12.5 %collective-permute-start.13 = (bf16[16,272,128]{2,1,0:T(8,128)(2,1)S(1)}, bf16[16,272,128]{2,1,0:T(8,128)(2,1)S(1)}, u32[]{:S(2)}, u32[]{:S(2)}) collective-permute-start(bf16[16,272,128]{2,1,0:T(8,128)(2,1)S(1)} %all-to-all-done.refs_2_), channel_id=1, source_target_pairs={{0,1},{1,0},{2,3},{3,2},{4,5},{5,4},{6,7},{7,6},{8,9},{9,8},{10,11... | collective-permute-start | bytes 3342344 | tf_op jit(solution)/shard_map/ppermute | solution.py:25
  103.8 51.8 %all-to-all-start.1 = ((bf16[16,512,128]{2,1,0:T(8,128)(2,1)}), bf16[16,512,128]{2,1,0:T(8,128)(2,1)}, u32[]{:S(2)}, u32[]{:S(2)}) async-start(bf16[16,512,128]{2,1,0:T(8,128)(2,1)} %feed_deal.1), calls=%async_computation.1 | async-start | bytes 4194304 | tf_op jit(solution)/shard_map/all_to_all | solution.py:1101
  109.5 44.6 %collective-permute-start.15 = (bf16[256,2048]{1,0:T(8,128)(2,1)S(1)}, bf16[256,2048]{1,0:T(8,128)(2,1)S(1)}, u32[]{:S(2)}, u32[]{:S(2)}) collective-permute-start(bf16[256,2048]{1,0:T(8,128)(2,1)S(1)} %constant_dynamic-update-slice_fusion.6.refs_3_.refs_5_.refs_11_), channel_id=1, source_target_pairs={{0,4},{2,6},{4,0},{6,2},{8,12},{10,14},{12,8},{14,10},{16,20},{18,... | collective-permute-start | bytes 3145736 | tf_op jit(solution)/shard_map/ppermute | solution.py:30
  110.9 43.3 %collective-permute-start.14 = (bf16[256,2048]{1,0:T(8,128)(2,1)S(1)}, bf16[256,2048]{1,0:T(8,128)(2,1)}, u32[]{:S(2)}, u32[]{:S(2)}) collective-permute-start(bf16[256,2048]{1,0:T(8,128)(2,1)S(1)} %constant_dynamic-update-slice_fusion.4.refs_1_.refs_3_.refs_9_), channel_id=1, source_target_pairs={{0,2},{2,0},{4,6},{6,4},{8,10},{10,8},{12,14},{14,12},{16,18},{18,... | collective-permute-start | bytes 3145736 | tf_op jit(solution)/shard_map/ppermute | solution.py:30
  134.3 19.9 %copy-start.39 = (bf16[1024,384]{1,0:T(8,128)(2,1)}, bf16[1024,384]{1,0:T(8,128)(2,1)S(1)}, u32[]{:S(2)}) copy-start(bf16[1024,384]{1,0:T(8,128)(2,1)S(1)} %get-tuple-element.254.refs_1_) | copy-start | bytes 2359300
  155.6 6.0 %collective-permute-start.18 = (bf16[16,512,128]{2,1,0:T(8,128)(2,1)}, bf16[16,512,128]{2,1,0:T(8,128)(2,1)S(1)}, u32[]{:S(2)}, u32[]{:S(2)}) collective-permute-start(bf16[16,512,128]{2,1,0:T(8,128)(2,1)} %all-to-all-done.1.refs_5_), channel_id=1, source_target_pairs={{0,1},{1,0},{2,3},{3,2},{4,5},{5,4},{6,7},{7,6},{8,9},{9,8},{10,11... | collective-permute-start | bytes 6291464 | tf_op jit(solution)/shard_map/ppermute | solution.py:25
  157.6 13.8 %collective-permute-start.19 = (bf16[128,2048]{1,0:T(8,128)(2,1)}, bf16[128,2048]{1,0:T(8,128)(2,1)S(1)}, u32[]{:S(2)}, u32[]{:S(2)}) collective-permute-start(bf16[128,2048]{1,0:T(8,128)(2,1)} %copy-done.48), channel_id=1, source_target_pairs={{0,2},{2,0},{4,6},{6,4},{8,10},{10,8},{12,14},{14,12},{16,18},{18,... | collective-permute-start | bytes 1572872 | tf_op jit(solution)/shard_map/ppermute | solution.py:30
  158.2 30.1 %collective-permute-start.16 = (bf16[1024,384]{1,0:T(8,128)(2,1)}, bf16[1024,384]{1,0:T(8,128)(2,1)S(1)}, u32[]{:S(2)}, u32[]{:S(2)}) collective-permute-start(bf16[1024,384]{1,0:T(8,128)(2,1)} %copy-done.39), channel_id=1, source_target_pairs={{0,2},{2,0},{4,6},{6,4},{8,10},{10,8},{12,14},{14,12},{16,18},{18,... | collective-permute-start | bytes 2359304 | tf_op jit(solution)/shard_map/ppermute | solution.py:30
  159.1 29.2 %collective-permute-start.17 = (bf16[1024,384]{1,0:T(8,128)(2,1)}, bf16[1024,384]{1,0:T(8,128)(2,1)S(1)}, u32[]{:S(2)}, u32[]{:S(2)}) collective-permute-start(bf16[1024,384]{1,0:T(8,128)(2,1)} %copy-done.39), channel_id=1, source_target_pairs={{0,1},{1,0},{2,3},{3,2},{4,5},{5,4},{6,7},{7,6},{8,9},{9,8},{10,11... | collective-permute-start | bytes 2359304 | tf_op jit(solution)/shard_map/ppermute | solution.py:25
  188.3 8.4 %collective-permute-start.20 = (bf16[1024,384]{1,0:T(8,128)(2,1)S(1)}, bf16[1024,384]{1,0:T(8,128)(2,1)S(1)}, u32[]{:S(2)}, u32[]{:S(2)}) collective-permute-start(bf16[1024,384]{1,0:T(8,128)(2,1)S(1)} %collective-permute-done.16.refs_2_), channel_id=1, source_target_pairs={{0,1},{1,0},{2,3},{3,2},{4,5},{5,4},{6,7},{7,6},{8,9},{9,8},{10,11... | collective-permute-start | bytes 2359304 | tf_op jit(solution)/shard_map/ppermute | solution.py:25
  196.7 9.2 %collective-permute-start.21 = (bf16[16,512,128]{2,1,0:T(8,128)(2,1)S(1)}, bf16[16,512,128]{2,1,0:T(8,128)(2,1)S(1)}, u32[]{:S(2)}, u32[]{:S(2)}) collective-permute-start(bf16[16,512,128]{2,1,0:T(8,128)(2,1)S(1)} %outer.2), channel_id=1, source_target_pairs={{0,1},{1,0},{2,3},{3,2},{4,5},{5,4},{6,7},{7,6},{8,9},{9,8},{10,11... | collective-permute-start | bytes 6291464 | tf_op jit(solution)/shard_map/ppermute | solution.py:25
  197.0 8.8 %collective-permute-start.22 = (bf16[1024,256]{1,0:T(8,128)(2,1)S(1)}, bf16[1024,256]{1,0:T(8,128)(2,1)S(1)}, u32[]{:S(2)}, u32[]{:S(2)}) collective-permute-start(bf16[1024,256]{1,0:T(8,128)(2,1)S(1)} %get-tuple-element.253.refs_5_), channel_id=1, source_target_pairs={{0,1},{1,0},{2,3},{3,2},{4,5},{5,4},{6,7},{7,6},{8,9},{9,8},{10,11... | collective-permute-start | bytes 1572872 | tf_op jit(solution)/shard_map/ppermute | solution.py:25
  205.9 8.4 %collective-permute-start.24 = (f32[8,512]{1,0:T(8,128)S(1)}, f32[8,512]{1,0:T(8,128)S(1)}, u32[]{:S(2)}, u32[]{:S(2)}) collective-permute-start(f32[8,512]{1,0:T(8,128)S(1)} %get-tuple-element.264.refs_7_), channel_id=1, source_target_pairs={{0,2},{2,0},{4,6},{6,4},{8,10},{10,8},{12,14},{14,12},{16,18},{18,... | collective-permute-start | bytes 49160 | tf_op jit(solution)/shard_map/ppermute | solution.py:30
  206.4 7.9 %collective-permute-start.25 = (f32[8,512]{1,0:T(8,128)S(1)}, f32[8,512]{1,0:T(8,128)S(1)}, u32[]{:S(2)}, u32[]{:S(2)}) collective-permute-start(f32[8,512]{1,0:T(8,128)S(1)} %get-tuple-element.264.refs_7_), channel_id=1, source_target_pairs={{0,1},{1,0},{2,3},{3,2},{4,5},{5,4},{6,7},{7,6},{8,9},{9,8},{10,11... | collective-permute-start | bytes 49160 | tf_op jit(solution)/shard_map/ppermute | solution.py:25
  207.0 8.6 %collective-permute-start.26 = (f32[8,512]{1,0:T(8,128)S(1)}, f32[8,512]{1,0:T(8,128)S(1)}, u32[]{:S(2)}, u32[]{:S(2)}) collective-permute-start(f32[8,512]{1,0:T(8,128)S(1)} %get-tuple-element.264.refs_7_), channel_id=1, source_target_pairs={{0,3},{1,2},{2,1},{3,0},{4,7},{5,6},{6,5},{7,4},{8,11},{9,10},{10,... | collective-permute-start | bytes 49160 | tf_op jit(solution)/shard_map/ppermute | solution.py:1207
  215.6 79.3 %all-to-all-start.2 = ((bf16[16,512,128]{2,1,0:T(8,128)(2,1)}), bf16[16,512,128]{2,1,0:T(8,128)(2,1)}, u32[]{:S(2)}, u32[]{:S(2)}) async-start(bf16[16,512,128]{2,1,0:T(8,128)(2,1)} %copy-done.5), calls=%async_computation.2 | async-start | bytes 4194304 | tf_op jit(solution)/shard_map/all_to_all | solution.py:1223
  221.6 19.5 %collective-permute-start.23 = (bf16[512,256]{1,0:T(8,128)(2,1)}, bf16[512,256]{1,0:T(8,128)(2,1)S(1)}, u32[]{:S(2)}, u32[]{:S(2)}) collective-permute-start(bf16[512,256]{1,0:T(8,128)(2,1)} %copy-done.57), channel_id=1, source_target_pairs={{0,2},{2,0},{4,6},{6,4},{8,10},{10,8},{12,14},{14,12},{16,18},{18,... | collective-permute-start | bytes 786440 | tf_op jit(solution)/shard_map/ppermute | solution.py:30
  234.3 11.5 %collective-permute-start.27 = (bf16[512,256]{1,0:T(8,128)(2,1)S(1)}, bf16[512,256]{1,0:T(8,128)(2,1)S(1)}, u32[]{:S(2)}, u32[]{:S(2)}) collective-permute-start(bf16[512,256]{1,0:T(8,128)(2,1)S(1)} %get-tuple-element.268), channel_id=1, source_target_pairs={{0,2},{2,0},{4,6},{6,4},{8,10},{10,8},{12,14},{14,12},{16,18},{18,... | collective-permute-start | bytes 786440 | tf_op jit(solution)/shard_map/ppermute | solution.py:30
  235.6 19.4 %copy-start.8 = (bf16[256,2048]{1,0:T(8,128)(2,1)S(1)}, bf16[256,2048]{1,0:T(8,128)(2,1)}, u32[]{:S(2)}) copy-start(bf16[256,2048]{1,0:T(8,128)(2,1)} %copy-done.6) | copy-start | bytes 3145732
  235.6 19.4 %copy-start.11 = (bf16[256,2048]{1,0:T(8,128)(2,1)S(1)}, bf16[256,2048]{1,0:T(8,128)(2,1)}, u32[]{:S(2)}) copy-start(bf16[256,2048]{1,0:T(8,128)(2,1)} %copy-done.9) | copy-start | bytes 3145732
  235.6 19.4 %copy-start.16 = (bf16[256,2048]{1,0:T(8,128)(2,1)S(1)}, bf16[256,2048]{1,0:T(8,128)(2,1)}, u32[]{:S(2)}) copy-start(bf16[256,2048]{1,0:T(8,128)(2,1)} %copy-done.14) | copy-start | bytes 3145732
  235.6 19.4 %copy-start.19 = (bf16[256,2048]{1,0:T(8,128)(2,1)S(1)}, bf16[256,2048]{1,0:T(8,128)(2,1)}, u32[]{:S(2)}) copy-start(bf16[256,2048]{1,0:T(8,128)(2,1)} %copy-done.17) | copy-start | bytes 3145732
  245.8 31.9 %collective-permute-start.28 = (bf16[256,2048]{1,0:T(8,128)(2,1)S(1)}, bf16[256,2048]{1,0:T(8,128)(2,1)S(1)}, u32[]{:S(2)}, u32[]{:S(2)}) collective-permute-start(bf16[256,2048]{1,0:T(8,128)(2,1)S(1)} %get-tuple-element.278), channel_id=1, source_target_pairs={{0,2},{2,0},{4,6},{6,4},{8,10},{10,8},{12,14},{14,12},{16,18},{18,... | collective-permute-start | bytes 3145736 | tf_op jit(solution)/shard_map/ppermute | solution.py:30
  246.8 34.7 %collective-permute-start.29 = (bf16[256,2048]{1,0:T(8,128)(2,1)S(1)}, bf16[256,2048]{1,0:T(8,128)(2,1)S(1)}, u32[]{:S(2)}, u32[]{:S(2)}) collective-permute-start(bf16[256,2048]{1,0:T(8,128)(2,1)S(1)} %get-tuple-element.279), channel_id=1, source_target_pairs={{0,4},{2,6},{4,0},{6,2},{8,12},{10,14},{12,8},{14,10},{16,20},{18,... | collective-permute-start | bytes 3145736 | tf_op jit(solution)/shard_map/ppermute | solution.py:30
  265.1 10.5 %collective-permute-start.30 = (f32[8,2048]{1,0:T(8,128)S(1)}, f32[8,2048]{1,0:T(8,128)S(1)}, u32[]{:S(2)}, u32[]{:S(2)}) collective-permute-start(f32[8,2048]{1,0:T(8,128)S(1)} %get-tuple-element.302.refs_1_), channel_id=1, source_target_pairs={{0,1},{1,0},{2,3},{3,2},{4,5},{5,4},{6,7},{7,6},{8,9},{9,8},{10,11... | collective-permute-start | bytes 196616 | tf_op jit(solution)/shard_map/ppermute | solution.py:25
  281.5 11.4 %collective-permute-start.31 = (bf16[16,256,128]{2,1,0:T(8,128)(2,1)S(1)}, bf16[16,256,128]{2,1,0:T(8,128)(2,1)S(1)}, u32[]{:S(2)}, u32[]{:S(2)}) collective-permute-start(bf16[16,256,128]{2,1,0:T(8,128)(2,1)S(1)} %get-tuple-element.301), channel_id=1, source_target_pairs={{0,1},{1,0},{2,3},{3,2},{4,5},{5,4},{6,7},{7,6},{8,9},{9,8},{10,11... | collective-permute-start | bytes 3145736 | tf_op jit(solution)/shard_map/ppermute | solution.py:25
  283.6 26.1 %collective-permute-start.32 = (bf16[256,2048]{1,0:T(8,128)(2,1)}, bf16[256,2048]{1,0:T(8,128)(2,1)S(1)}, u32[]{:S(2)}, u32[]{:S(2)}) collective-permute-start(bf16[256,2048]{1,0:T(8,128)(2,1)} %get-tuple-element.317), channel_id=1, source_target_pairs={{0,2},{2,0},{4,6},{6,4},{8,10},{10,8},{12,14},{14,12},{16,18},{18,... | collective-permute-start | bytes 3145736 | tf_op jit(solution)/shard_map/ppermute | solution.py:30
  283.8 30.2 %collective-permute-start.33 = (bf16[256,2048]{1,0:T(8,128)(2,1)}, bf16[256,2048]{1,0:T(8,128)(2,1)S(1)}, u32[]{:S(2)}, u32[]{:S(2)}) collective-permute-start(bf16[256,2048]{1,0:T(8,128)(2,1)} %get-tuple-element.318), channel_id=1, source_target_pairs={{0,4},{2,6},{4,0},{6,2},{8,12},{10,14},{12,8},{14,10},{16,20},{18,... | collective-permute-start | bytes 3145736 | tf_op jit(solution)/shard_map/ppermute | solution.py:30
  292.9 37.6 %collective-permute-start.34 = (bf16[128,2048]{1,0:T(8,128)(2,1)}, bf16[128,2048]{1,0:T(8,128)(2,1)}, u32[]{:S(2)}, u32[]{:S(2)}) collective-permute-start(bf16[128,2048]{1,0:T(8,128)(2,1)} %get-tuple-element.319), channel_id=1, source_target_pairs={{0,4},{2,6},{4,0},{6,2},{8,12},{10,14},{12,8},{14,10},{16,20},{18,... | collective-permute-start | bytes 1572872 | tf_op jit(solution)/shard_map/ppermute | solution.py:30
  292.9 37.6 %collective-permute-start.35 = (bf16[128,2048]{1,0:T(8,128)(2,1)}, bf16[128,2048]{1,0:T(8,128)(2,1)}, u32[]{:S(2)}, u32[]{:S(2)}) collective-permute-start(bf16[128,2048]{1,0:T(8,128)(2,1)} %get-tuple-element.320), channel_id=1, source_target_pairs={{0,2},{2,0},{4,6},{6,4},{8,10},{10,8},{12,14},{14,12},{16,18},{18,... | collective-permute-start | bytes 1572872 | tf_op jit(solution)/shard_map/ppermute | solution.py:30
  294.9 77.2 %all-to-all-start.3 = ((bf16[16,288,128]{2,1,0:T(8,128)(2,1)}), bf16[16,288,128]{2,1,0:T(8,128)(2,1)S(1)}, u32[]{:S(2)}, u32[]{:S(2)}) async-start(bf16[16,288,128]{2,1,0:T(8,128)(2,1)} %pad_maximum_fusion), calls=%async_computation.3 | async-start | bytes 2359296 | tf_op jit(solution)/shard_map/all_to_all | solution.py:1323
  299.5 37.0 %copy-start.27 = (bf16[256,2048]{1,0:T(8,128)(2,1)S(1)}, bf16[256,2048]{1,0:T(8,128)(2,1)}, u32[]{:S(2)}) copy-start(bf16[256,2048]{1,0:T(8,128)(2,1)} %copy-done.26) | copy-start | bytes 3145732
  299.5 37.0 %copy-start.29 = (bf16[256,2048]{1,0:T(8,128)(2,1)S(1)}, bf16[256,2048]{1,0:T(8,128)(2,1)}, u32[]{:S(2)}) copy-start(bf16[256,2048]{1,0:T(8,128)(2,1)} %copy-done.28) | copy-start | bytes 3145732
  337.9 29.1 %copy-start.71 = (bf16[64,2048]{1,0:T(8,128)(2,1)S(1)}, bf16[64,2048]{1,0:T(8,128)(2,1)}, u32[]{:S(2)}) copy-start(bf16[64,2048]{1,0:T(8,128)(2,1)} %copy-done.70) | copy-start | bytes 786436
  337.9 28.2 %collective-permute-start.36 = (bf16[128,2048]{1,0:T(8,128)(2,1)S(1)}, bf16[128,2048]{1,0:T(8,128)(2,1)S(1)}, u32[]{:S(2)}, u32[]{:S(2)}) collective-permute-start(bf16[128,2048]{1,0:T(8,128)(2,1)S(1)} %get-tuple-element.341), channel_id=1, source_target_pairs={{0,4},{2,6},{4,0},{6,2},{8,12},{10,14},{12,8},{14,10},{16,20},{18,... | collective-permute-start | bytes 1572872 | tf_op jit(solution)/shard_map/ppermute | solution.py:30
  339.1 27.0 %collective-permute-start.37 = (bf16[128,2048]{1,0:T(8,128)(2,1)S(1)}, bf16[128,2048]{1,0:T(8,128)(2,1)S(1)}, u32[]{:S(2)}, u32[]{:S(2)}) collective-permute-start(bf16[128,2048]{1,0:T(8,128)(2,1)S(1)} %get-tuple-element.342), channel_id=1, source_target_pairs={{0,2},{2,0},{4,6},{6,4},{8,10},{10,8},{12,14},{14,12},{16,18},{18,... | collective-permute-start | bytes 1572872 | tf_op jit(solution)/shard_map/ppermute | solution.py:30
  340.9 5.5 %collective-permute-start.38 = (bf16[64,2048]{1,0:T(8,128)(2,1)S(1)}, bf16[64,2048]{1,0:T(8,128)(2,1)S(1)}, u32[]{:S(2)}, u32[]{:S(2)}) collective-permute-start(bf16[64,2048]{1,0:T(8,128)(2,1)S(1)} %get-tuple-element.343), channel_id=1, source_target_pairs={{0,8},{2,10},{4,12},{6,14},{8,0},{10,2},{12,4},{14,6},{16,24},{18,... | collective-permute-start | bytes 786440 | tf_op jit(solution)/shard_map/ppermute | solution.py:30
  340.9 8.4 %collective-permute-start.39 = (bf16[64,2048]{1,0:T(8,128)(2,1)S(1)}, bf16[64,2048]{1,0:T(8,128)(2,1)S(1)}, u32[]{:S(2)}, u32[]{:S(2)}) collective-permute-start(bf16[64,2048]{1,0:T(8,128)(2,1)S(1)} %get-tuple-element.344), channel_id=1, source_target_pairs={{0,16},{2,18},{4,20},{6,22},{8,24},{10,26},{12,28},{14,30},{16,0},... | collective-permute-start | bytes 786440 | tf_op jit(solution)/shard_map/ppermute | solution.py:30
  340.9 25.2 %collective-permute-start.40 = (bf16[64,2048]{1,0:T(8,128)(2,1)S(1)}, bf16[64,2048]{1,0:T(8,128)(2,1)S(1)}, u32[]{:S(2)}, u32[]{:S(2)}) collective-permute-start(bf16[64,2048]{1,0:T(8,128)(2,1)S(1)} %get-tuple-element.345), channel_id=1, source_target_pairs={{0,24},{2,26},{4,28},{6,30},{8,16},{10,18},{12,20},{14,22},{16,8},... | collective-permute-start | bytes 786440 | tf_op jit(solution)/shard_map/ppermute | solution.py:30
  367.3 2.9 collective-permute-start.41
  372.2 27.4 %copy-start.73 = (bf16[64,2048]{1,0:T(8,128)(2,1)S(1)}, bf16[64,2048]{1,0:T(8,128)(2,1)}, u32[]{:S(2)}) copy-start(bf16[64,2048]{1,0:T(8,128)(2,1)} %copy-done.72) | copy-start | bytes 786436
  372.2 3.1 collective-permute-start.42
  372.6 9.3 %collective-permute-start.43 = (bf16[64,2048]{1,0:T(8,128)(2,1)S(1)}, bf16[64,2048]{1,0:T(8,128)(2,1)S(1)}, u32[]{:S(2)}, u32[]{:S(2)}) collective-permute-start(bf16[64,2048]{1,0:T(8,128)(2,1)S(1)} %get-tuple-element.365), channel_id=1, source_target_pairs={{0,8},{2,10},{4,12},{6,14},{8,0},{10,2},{12,4},{14,6},{16,24},{18,... | collective-permute-start | bytes 786440 | tf_op jit(solution)/shard_map/ppermute | solution.py:30
  372.6 12.4 %collective-permute-start.44 = (bf16[64,2048]{1,0:T(8,128)(2,1)S(1)}, bf16[64,2048]{1,0:T(8,128)(2,1)S(1)}, u32[]{:S(2)}, u32[]{:S(2)}) collective-permute-start(bf16[64,2048]{1,0:T(8,128)(2,1)S(1)} %get-tuple-element.366), channel_id=1, source_target_pairs={{0,16},{2,18},{4,20},{6,22},{8,24},{10,26},{12,28},{14,30},{16,0},... | collective-permute-start | bytes 786440 | tf_op jit(solution)/shard_map/ppermute | solution.py:30
  373.1 25.2 %collective-permute-start.45 = (bf16[64,2048]{1,0:T(8,128)(2,1)S(1)}, bf16[64,2048]{1,0:T(8,128)(2,1)}, u32[]{:S(2)}, u32[]{:S(2)}) collective-permute-start(bf16[64,2048]{1,0:T(8,128)(2,1)S(1)} %get-tuple-element.367), channel_id=1, source_target_pairs={{0,24},{2,26},{4,28},{6,30},{8,16},{10,18},{12,20},{14,22},{16,8},... | collective-permute-start | bytes 786440 | tf_op jit(solution)/shard_map/ppermute | solution.py:30
  401.0 4.8 %collective-permute-start.46 = (bf16[64,2048]{1,0:T(8,128)(2,1)S(1)}, bf16[64,2048]{1,0:T(8,128)(2,1)S(1)}, u32[]{:S(2)}, u32[]{:S(2)}) collective-permute-start(bf16[64,2048]{1,0:T(8,128)(2,1)S(1)} %fusion.8), channel_id=1, source_target_pairs={{0,1},{1,0},{2,3},{3,2},{4,5},{5,4},{6,7},{7,6},{8,9},{9,8},{10,11... | collective-permute-start | bytes 786440 | tf_op jit(solution)/shard_map/ppermute | solution.py:25
  (75 other events, 448.8 us)

commit v5 on v4

--- a/solution.py
+++ b/solution.py
@@ -462,11 +462,12 @@
 SMEM = pl.BlockSpec(memory_space=pltpu.SMEM)
 GRANT = 28 * 1024 * 1024
 MARK_COS, MARK_SIN = 32, 64
-COST = 1.0
+WEIGHTS = {"deal": 10, "norm": 10, "feed": 10, "query": 10, "key": 3, "by_z": 3, "fold": 100}
 WIDE = 256
 
 
 def run_kernel(kernel, outs, grid=None, ins=None, out_specs=None, scratch=(), flops=0, moved=0, name=None):
+    weight = WEIGHTS.get(name, 1)
     outs = [jax.ShapeDtypeStruct(shape, kind) for shape, kind in outs]
     single = len(outs) == 1
     out_specs = out_specs or [VMEM] * len(outs)
@@ -478,7 +479,7 @@
         out_specs=out_specs[0] if single else out_specs,
         scratch_shapes=list(scratch),
         compiler_params=pltpu.CompilerParams(vmem_limit_bytes=GRANT),
-        cost_estimate=pl.CostEstimate(flops=int(flops * COST), bytes_accessed=int(moved * COST), transcendentals=0),
+        cost_estimate=pl.CostEstimate(flops=int(flops * weight), bytes_accessed=int(moved * weight), transcendentals=0),
         name=name,
         **extra,
     )
@@ -969,9 +970,10 @@
 
 
 def feed_unpack_kernel(units, got, expand, shrink):
-    k = pl.program_id(0)
-    expand[...] = got[0, :units, :].astype(F32).T
-    shrink[...] = got[0, units:, :].astype(F32)
+    for k in range(got.shape[0]):
+        rows = slice(k * units, (k + 1) * units)
+        expand[:, rows] = got[k, :units, :].astype(F32).T
+        shrink[rows, :] = got[k, units:, :].astype(F32)
 
 
 def join(*values):
@@ -1198,9 +1200,8 @@
         name="query",
         moved=6e6,
     )(ids, *four, grads, marks)
-    feed_got, grads_there, attended, send1, lines = join(
-        swap_cores(feed_sent), swap_cores(grads), attended, send1, lines
-    )
+    grads_there, attended, send1, lines = join(swap_cores(grads), attended, send1, lines)
+    feed_got = swap_cores(feed_sent)
 
     diagonal = [(2 * b + c, 2 * (b ^ 1) + 1 - c) for b in range(blocks) for c in (0, 1)]
     lines_peer, lines_there = from_peer(lines, 1), swap_cores(lines)
@@ -1324,9 +1325,12 @@
     expand_grad, shrink_grad = run_kernel(
         lambda *refs: feed_unpack_kernel(units, *refs),
         [(w_in.shape, F32), (w_out2.shape, F32)],
-        grid=(blocks,),
-        ins=[pl.BlockSpec((1, 2 * units, 128), lambda k: (k, 0, 0))],
-        out_specs=[pl.BlockSpec((depth, units), lambda k: (0, k)), pl.BlockSpec((units, depth), lambda k: (k, 0))],
+        grid=(4,),
+        ins=[pl.BlockSpec((blocks // 4, 2 * units, 128), lambda k: (k, 0, 0))],
+        out_specs=[
+            pl.BlockSpec((depth, units * blocks // 4), lambda k: (0, k)),
+            pl.BlockSpec((units * blocks // 4, depth), lambda k: (k, 0)),
+        ],
         name="feed_unpack",
         moved=6e6,
     )(feed_dealt)
@@ -1337,9 +1341,8 @@
     one, one_send, two, two_send, *mixed_pieces = join(
         *fold(combined[0], got_one, combined[2], got_two), *mixed_pieces
     )
-    got_one, got_two, *mixed_got = join(
-        from_peer(one_send, 2), from_peer(two_send, 1), *pieces_over_z(mixed_pieces)
-    )
+    mixed_got = pieces_over_z(mixed_pieces)
+    got_one, got_two = join(from_peer(one_send, 2), from_peer(two_send, 1))
 
     joined = join(*by_z(one, got_one, two, got_two), *mixed_got)
     pieces, mixed_got = joined[: 1 + len(masks_z)], joined[1 + len(masks_z) :]

time: 409 us -> 405 us (level)
  Pallas kernels: 102 us -> 91.3 us
  waiting for transfers between devices: 164 us -> 171 us
    ppermute x33, waiting for transfers between devices: 157 us -> 164 us  [from_peer(): return lax.ppermute(value, 'blk', [(i, i ^ mask) for i in range(count)])]
    pallas_call x1, Pallas kernels: 10.2 us -> 4.43 us  [body(): run_kernel(lambda *refs: feed_unpack_kernel(units, *refs), [(w_in.shape,...]
    pallas_call x2, Pallas kernels: 13.9 us -> 9.71 us  [outer(): run_kernel(lambda *refs: outer_kernel(units, *refs), [((blocks, 2 * units...]
    unnamed x191 -> x195, local copies, waits for them, and re-layouts: 35.2 us -> 34.5 us
  transfers between devices with their start and end apart: 51 -> 51, of which waited for: 23 -> 23; matrix products, arithmetic and copies ran while one was open for 6% -> 6% of each run, Pallas kernels for 25% -> 23%
where the time goes in v5:
time: 405 us; the launch traced here: 404 us
  waiting for transfers between devices  171 us (42%)
  Pallas kernels  91.3 us (23%)
  starting transfers between devices  81.1 us (20%)
  local copies, waits for them, and re-layouts  46 us (11%)
  other arithmetic  12.7 us (3%)
    ppermute x33, waiting for transfers between devices, from_peer(): return lax.ppermute(value, 'blk', [(i, i ^ mask) for i in range(count)])  164 us
    ppermute x33, starting transfers between devices, from_peer(): return lax.ppermute(value, 'blk', [(i, i ^ mask) for i in range(count)])  35.4 us
    unnamed x195, local copies, waits for them, and re-layouts  34.5 us
    ppermute x13, starting transfers between devices, swap_cores(): return lax.ppermute(value, 'tp', [(0, 1), (1, 0)])  23.6 us
    pallas_call x1, Pallas kernels, body(): run_kernel(lambda *refs: feed_kernel(units, blocks, *refs), [((count, 2 *...  11.1 us
    pallas_call x1, Pallas kernels, body(): run_kernel(lambda *refs: norm_kernel(r, *refs), [((count, width), BF), ((...  10.4 us
    pallas_call x2, Pallas kernels, outer(): run_kernel(lambda *refs: outer_kernel(units, *refs), [((blocks, 2 * units...  9.71 us
    pallas_call x1, Pallas kernels, body(): run_kernel(lambda *refs: inputs_kernel(r, *refs), [((quarter, width), BF)...  9.13 us
  transfers between devices with their start and end apart: 51, of which 23 were waited for; matrix products, arithmetic and copies ran while one was open for 6% of the time, Pallas kernels for 23%

profile of v5, /device:TPU:11, one launch (start us, length us, event | category | flops | bytes accessed | tf_op | source)
XLA Modules:
  0.0 403.7 jit_solution(15833064018253612917)
XLA Ops:
  2.1 2.3 collective-permute-start.2
  7.8 2.1 fusion.13
  9.8 1.5 collective-permute-start
  12.5 1.7 feed_deal.1
  14.3 1.6 collective-permute-done.2
  15.9 14.0 %collective-permute-done.3 = bf16[64,2048]{1,0:T(8,128)(2,1)} collective-permute-done((bf16[64,2048]{1,0:T(8,128)(2,1)S(1)}, bf16[64,2048]{1,0:T(8,128)(2,1)}, u32[]{:S(2)}, u32[]{:S(2)}) %collective-permute-start.3) | collective-permute-done | bytes 262176 | tf_op jit(solution)/shard_map/ppermute | solution.py:30
  31.1 1.4 collective-permute-start.9
  38.5 4.7 %all-to-all-start = ((bf16[16,272,128]{2,1,0:T(8,128)(2,1)}), bf16[16,272,128]{2,1,0:T(8,128)(2,1)S(1)}, u32[]{:S(2)}, u32[]{:S(2)}) async-start(bf16[16,272,128]{2,1,0:T(8,128)(2,1)} %pad_maximum_fusion.1), calls=%async_computation | async-start | bytes 2228224 | tf_op jit(solution)/shard_map/all_to_all | solution.py:1080
  43.3 6.7 %collective-permute-done.9 = bf16[64,2048]{1,0:T(8,128)(2,1)} collective-permute-done((bf16[64,2048]{1,0:T(8,128)(2,1)S(1)}, bf16[64,2048]{1,0:T(8,128)(2,1)}, u32[]{:S(2)}, u32[]{:S(2)}) %collective-permute-start.9) | collective-permute-done | bytes 262176 | tf_op jit(solution)/shard_map/ppermute | solution.py:30
  52.1 1.4 collective-permute-start.7
  57.9 28.1 %collective-permute-done.12 = bf16[128,2048]{1,0:T(8,128)(2,1)S(1)} collective-permute-done((bf16[128,2048]{1,0:T(8,128)(2,1)S(1)}, bf16[128,2048]{1,0:T(8,128)(2,1)S(1)}, u32[]{:S(2)}, u32[]{:S(2)}) %collective-permute-start.12) | collective-permute-done | bytes 524320 | tf_op jit(solution)/shard_map/ppermute | solution.py:30
  86.0 1.5 collective-permute-done.11
  90.3 10.1 %collective-permute-start.13 = (bf16[16,272,128]{2,1,0:T(8,128)(2,1)S(1)}, bf16[16,272,128]{2,1,0:T(8,128)(2,1)S(1)}, u32[]{:S(2)}, u32[]{:S(2)}) collective-permute-start(bf16[16,272,128]{2,1,0:T(8,128)(2,1)S(1)} %all-to-all-done.refs_2_), channel_id=1, source_target_pairs={{0,1},{1,0},{2,3},{3,2},{4,5},{5,4},{6,7},{7,6},{8,9},{9,8},{10,11... | collective-permute-start | bytes 3342344 | tf_op jit(solution)/shard_map/ppermute | solution.py:25
  100.4 2.4 collective-permute-done.13.refs_3_
  103.8 5.6 %all-to-all-start.1 = ((bf16[16,512,128]{2,1,0:T(8,128)(2,1)}), bf16[16,512,128]{2,1,0:T(8,128)(2,1)}, u32[]{:S(2)}, u32[]{:S(2)}) async-start(bf16[16,512,128]{2,1,0:T(8,128)(2,1)} %feed_deal.1), calls=%async_computation.1 | async-start | bytes 4194304 | tf_op jit(solution)/shard_map/all_to_all | solution.py:1103
  111.0 1.6 constant_dynamic-update-slice_fusion.5
  114.0 3.5 deal.1
  117.6 10.4 %norm.1 = (bf16[1024,2048]{1,0:T(8,128)(2,1)S(1)}, f32[1024,128]{1,0:T(8,128)S(1)}, bf16[1024,384]{1,0:T(8,128)(2,1)S(1)}) custom-call(s32[2]{0:T(128)S(1)} %pad_add_fusion.refs_0_, bf16[256,2048]{1,0:T(8,128)(2,1)S(1)} %copy-done.16, bf16[256,2048]{1,0:T(8,128)(2,1)S(1)} %copy-done.24, bf16[256,2048]{1,0:T(8,128)(2,1)S(1)} %copy-done.13, ...), custom_call_target="tpu_custom_call" | custom-call | flops 16106127360 | bytes 220000000 | tf_op jit(solution)/shard_map/norm/pallas_call | solution.py:1120
  128.0 2.0 copy-done.2
  130.9 23.3 %collective-permute-done.15.refs_4_.refs_6_.refs_12_ = bf16[256,2048]{1,0:T(8,128)(2,1)S(1)} collective-permute-done((bf16[256,2048]{1,0:T(8,128)(2,1)S(1)}, bf16[256,2048]{1,0:T(8,128)(2,1)S(1)}, u32[]{:S(2)}, u32[]{:S(2)}) %collective-permute-start.15) | collective-permute-done | bytes 1048608 | tf_op jit(solution)/shard_map/ppermute | solution.py:30
  155.6 2.6 collective-permute-start.18
  158.3 1.4 collective-permute-start.16
  160.2 2.0 collective-permute-done.18.refs_6_
  162.2 9.8 %collective-permute-done.19.refs_9_.refs_4_ = bf16[128,2048]{1,0:T(8,128)(2,1)S(1)} collective-permute-done((bf16[128,2048]{1,0:T(8,128)(2,1)}, bf16[128,2048]{1,0:T(8,128)(2,1)S(1)}, u32[]{:S(2)}, u32[]{:S(2)}) %collective-permute-start.19) | collective-permute-done | bytes 524320 | tf_op jit(solution)/shard_map/ppermute | solution.py:30
  172.0 2.4 copy-done.3
  176.6 11.1 %feed.1 = (bf16[1024,512]{1,0:T(8,128)(2,1)S(1)}, bf16[1024,512]{1,0:T(8,128)(2,1)S(1)}, bf16[512,1024]{1,0:T(8,128)(2,1)S(1)}, bf16[512,1024]{1,0:T(8,128)(2,1)...) custom-call(bf16[1024,2048]{1,0:T(8,128)(2,1)S(1)} %copy-done.3, ...), custom_call_target="tpu_custom_call" | custom-call | flops 42949672960 | bytes 200000000 | tf_op jit(solution)/shard_map/feed/pallas_call | solution.py:1141
  191.4 4.9 %outer.2 = bf16[16,512,128]{2,1,0:T(8,128)(2,1)S(1)} custom-call(bf16[512,1024]{1,0:T(8,128)(2,1)S(1)} %get-tuple-element.245.refs_0_, bf16[512,1024]{1,0:T(8,128)(2,1)S(1)} %get-tuple-element.246.refs_1_, bf16[1024,2048]{1,0:T(8,128)(2,1)S(1)} %copy-done.4, bf16[256,2048]{1,0:T(8,128)(2,1)S(1)} %constant_dynamic-update-slice_fusion.4.refs_1_.refs_3_.refs_9_, ...), custom_call_target="tpu_custom_call" | custom-call | flops 2147483648 | bytes 12000000 | tf_op jit(solution)/shard_map/outer/pallas_call | solution.py:1166
  196.9 7.8 %query.1 = (bf16[512,256]{1,0:T(8,128)(2,1)S(1)}, bf16[512,256]{1,0:T(8,128)(2,1)S(1)}, bf16[512,256]{1,0:T(8,128)(2,1)S(1)}, f32[8,512]{1,0:T(8,128)S(1)}) custom-call(s32[2]{0:T(128)S(1)} %pad_add_fusion.refs_0_, bf16[1024,384]{1,0:T(8,128)(2,1)S(1)} %copy-done.44, bf16[1024,384]{1,0:T(8,128)(2,1)S(1)} %collective-permute-done.16.refs_2_, ...), custom_call_target="tpu_custom_call" | custom-call | flops 21474836480 | bytes 60000000 | tf_op jit(solution)/shard_map/query/pallas_call | solution.py:1192
  205.3 1.5 collective-permute-start.26
  206.7 4.8 %outer.3 = bf16[16,512,128]{2,1,0:T(8,128)(2,1)S(1)} custom-call(bf16[512,1024]{1,0:T(8,128)(2,1)S(1)} %get-tuple-element.245.refs_0_, bf16[512,1024]{1,0:T(8,128)(2,1)S(1)} %get-tuple-element.246.refs_1_, bf16[1024,2048]{1,0:T(8,128)(2,1)S(1)} %copy-done.4, bf16[256,2048]{1,0:T(8,128)(2,1)S(1)} %constant_dynamic-update-slice_fusion.4.refs_1_.refs_3_.refs_9_, ...), custom_call_target="tpu_custom_call" | custom-call | flops 2147483648 | bytes 12000000 | tf_op jit(solution)/shard_map/outer/pallas_call | solution.py:1166
  213.0 5.8 %all-to-all-start.2 = ((bf16[16,512,128]{2,1,0:T(8,128)(2,1)}), bf16[16,512,128]{2,1,0:T(8,128)(2,1)}, u32[]{:S(2)}, u32[]{:S(2)}) async-start(bf16[16,512,128]{2,1,0:T(8,128)(2,1)} %copy-done.9), calls=%async_computation.2 | async-start | bytes 4194304 | tf_op jit(solution)/shard_map/all_to_all | solution.py:1224
  226.9 4.5 %key.1 = (bf16[512,256]{1,0:T(8,128)(2,1)S(1)}, bf16[512,256]{1,0:T(8,128)(2,1)S(1)}) custom-call(s32[2]{0:T(128)S(1)} %pad_add_fusion.refs_0_, bf16[1024,384]{1,0:T(8,128)(2,1)S(1)} %copy-done.45, bf16[1024,384]{1,0:T(8,128)(2,1)S(1)} %copy-done.47, bf16[1024,384]{1,0:T(8,128)(2,1)S(1)} %copy-done.49, bf16[1024,384]{1,0:T(8,128)(2,1)S(1)} %copy-done.51, ...), custom_call_target="tpu_custom_call" | custom-call | flops 6442450944 | bytes 18000000 | tf_op jit(solution)/shard_map/key/pallas_call | solution.py:1212
  232.8 5.5 %branch.1 = (bf16[256,2048]{1,0:T(8,128)(2,1)S(1)}, bf16[256,2048]{1,0:T(8,128)(2,1)S(1)}, bf16[256,2048]{1,0:T(8,128)(2,1)S(1)}, bf16[256,2048]{1,0:T(8,128)(2,1)S(1)}) custom-call(bf16[1024,512]{1,0:T(8,128)(2,1)S(1)} %copy-done.69, bf16[512,256]{1,0:T(8,128)(2,1)S(1)} %copy-done.73, bf16[512,2048]{1,0:T(8,128)(2,1)S(1)} %copy-done.67, ...), custom_call_target="tpu_custom_call" | custom-call | flops 2684354560 | bytes 9000000 | tf_op jit(solution)/shard_map/branch/pallas_call | solution.py:1225
  238.3 5.0 %collective-permute-done.27.refs_3_ = bf16[512,256]{1,0:T(8,128)(2,1)S(1)} collective-permute-done((bf16[512,256]{1,0:T(8,128)(2,1)S(1)}, bf16[512,256]{1,0:T(8,128)(2,1)S(1)}, u32[]{:S(2)}, u32[]{:S(2)}) %collective-permute-start.27) | collective-permute-done | bytes 262176 | tf_op jit(solution)/shard_map/ppermute | solution.py:30
  244.6 7.8 %collective-permute-start.29 = (bf16[256,2048]{1,0:T(8,128)(2,1)S(1)}, bf16[256,2048]{1,0:T(8,128)(2,1)S(1)}, u32[]{:S(2)}, u32[]{:S(2)}) collective-permute-start(bf16[256,2048]{1,0:T(8,128)(2,1)S(1)} %get-tuple-element.274), channel_id=1, source_target_pairs={{0,4},{2,6},{4,0},{6,2},{8,12},{10,14},{12,8},{14,10},{16,20},{18,... | collective-permute-start | bytes 3145736 | tf_op jit(solution)/shard_map/ppermute | solution.py:30
  252.5 9.1 %inputs.1 = (bf16[256,2048]{1,0:T(8,128)(2,1)S(1)}, bf16[256,2048]{1,0:T(8,128)(2,1)}, bf16[256,2048]{1,0:T(8,128)(2,1)S(1)}, bf16[256,2048]{1,0:T(8,128)(2,1)},...) custom-call(bf16[512,256]{1,0:T(8,128)(2,1)S(1)} %copy-done.71, ...), custom_call_target="tpu_custom_call" | custom-call | flops 3758096384 | bytes 16000000 | tf_op jit(solution)/shard_map/inputs/pallas_call | solution.py:1269
  263.6 1.8 collective-permute-start.30
  265.4 8.3 %line_outer.1 = (f32[16,256,128]{2,1,0:T(8,128)S(1)}, bf16[16,256,128]{2,1,0:T(8,128)(2,1)S(1)}) custom-call(s32[2]{0:T(128)S(1)} %pad_add_fusion.refs_0_, bf16[1024,384]{1,0:T(8,128)(2,1)S(1)} %get-tuple-element.290.refs_1_, bf16[1024,128]{1,0:T(8,128)(2,1)S(1)} %get-tuple-element.291.refs_2_, bf16[256,2048]{1,0:T(8,128)(2,1)S(1)} %copy-done.17, ...), custom_call_target="tpu_custom_call" | custom-call | flops 2147483648 | bytes 12000000 | tf_op jit(solution)/shard_map/line_outer/pallas_call | solution.py:1288
  273.8 1.4 collective-permute-done.28.got1
  275.1 4.4 %collective-permute-done.29.got2 = bf16[256,2048]{1,0:T(8,128)(2,1)S(1)} collective-permute-done((bf16[256,2048]{1,0:T(8,128)(2,1)S(1)}, bf16[256,2048]{1,0:T(8,128)(2,1)S(1)}, u32[]{:S(2)}, u32[]{:S(2)}) %collective-permute-start.29) | collective-permute-done | bytes 1048608 | tf_op jit(solution)/shard_map/ppermute | solution.py:30
  279.6 1.5 collective-permute-start.31
  281.3 2.3 collective-permute-start.33
  283.6 3.3 small.1
  286.9 3.4 fold.2
  292.4 4.5 %all-to-all-start.3 = ((bf16[16,288,128]{2,1,0:T(8,128)(2,1)}), bf16[16,288,128]{2,1,0:T(8,128)(2,1)S(1)}, u32[]{:S(2)}, u32[]{:S(2)}) async-start(bf16[16,288,128]{2,1,0:T(8,128)(2,1)} %pad_maximum_fusion), calls=%async_computation.3 | async-start | bytes 2359296 | tf_op jit(solution)/shard_map/all_to_all | solution.py:1324
  296.9 4.4 %feed_unpack.1 = (f32[128,4096]{1,0:T(8,128)}, f32[4096,128]{1,0:T(8,128)}) custom-call(bf16[16,512,128]{2,1,0:T(8,128)(2,1)} %all-to-all-done.2.refs_0_), custom_call_target="tpu_custom_call" | custom-call | bytes 6000000 | tf_op jit(solution)/shard_map/feed_unpack/pallas_call | solution.py:1325
  301.3 4.7 %collective-permute-done.32.got1 = bf16[256,2048]{1,0:T(8,128)(2,1)S(1)} collective-permute-done((bf16[256,2048]{1,0:T(8,128)(2,1)}, bf16[256,2048]{1,0:T(8,128)(2,1)S(1)}, u32[]{:S(2)}, u32[]{:S(2)}) %collective-permute-start.32) | collective-permute-done | bytes 1048608 | tf_op jit(solution)/shard_map/ppermute | solution.py:30
  306.1 5.4 %collective-permute-done.33.got2 = bf16[256,2048]{1,0:T(8,128)(2,1)S(1)} collective-permute-done((bf16[256,2048]{1,0:T(8,128)(2,1)}, bf16[256,2048]{1,0:T(8,128)(2,1)S(1)}, u32[]{:S(2)}, u32[]{:S(2)}) %collective-permute-start.33) | collective-permute-done | bytes 1048608 | tf_op jit(solution)/shard_map/ppermute | solution.py:30
  311.5 16.5 %collective-permute-done.34.refs_1_ = bf16[128,2048]{1,0:T(8,128)(2,1)} collective-permute-done((bf16[128,2048]{1,0:T(8,128)(2,1)}, bf16[128,2048]{1,0:T(8,128)(2,1)}, u32[]{:S(2)}, u32[]{:S(2)}) %collective-permute-start.34) | collective-permute-done | bytes 524320 | tf_op jit(solution)/shard_map/ppermute | solution.py:30
  330.0 3.9 by_z.2
  333.9 1.4 fold.3
  336.6 1.8 collective-permute-start.37
  338.4 2.6 collective-permute-start.40
  341.0 5.0 %collective-permute-done.36.refs_1_ = bf16[128,2048]{1,0:T(8,128)(2,1)S(1)} collective-permute-done((bf16[128,2048]{1,0:T(8,128)(2,1)S(1)}, bf16[128,2048]{1,0:T(8,128)(2,1)S(1)}, u32[]{:S(2)}, u32[]{:S(2)}) %collective-permute-start.36) | collective-permute-done | bytes 524320 | tf_op jit(solution)/shard_map/ppermute | solution.py:30
  346.0 1.4 collective-permute-done.37.refs_3_
  348.3 15.1 %collective-permute-done.40 = bf16[64,2048]{1,0:T(8,128)(2,1)S(1)} collective-permute-done((bf16[64,2048]{1,0:T(8,128)(2,1)S(1)}, bf16[64,2048]{1,0:T(8,128)(2,1)S(1)}, u32[]{:S(2)}, u32[]{:S(2)}) %collective-permute-start.40) | collective-permute-done | bytes 262176 | tf_op jit(solution)/shard_map/ppermute | solution.py:30
  363.8 1.6 collective-permute-start.41
  369.5 2.2 collective-permute-start.45
  371.7 2.4 unpack.1
  374.2 4.1 %collective-permute-done.43 = bf16[64,2048]{1,0:T(8,128)(2,1)S(1)} collective-permute-done((bf16[64,2048]{1,0:T(8,128)(2,1)S(1)}, bf16[64,2048]{1,0:T(8,128)(2,1)S(1)}, u32[]{:S(2)}, u32[]{:S(2)}) %collective-permute-start.43) | collective-permute-done | bytes 262176 | tf_op jit(solution)/shard_map/ppermute | solution.py:30
  378.3 3.1 collective-permute-done.44
  381.5 13.2 %collective-permute-done.45 = bf16[64,2048]{1,0:T(8,128)(2,1)} collective-permute-done((bf16[64,2048]{1,0:T(8,128)(2,1)S(1)}, bf16[64,2048]{1,0:T(8,128)(2,1)}, u32[]{:S(2)}, u32[]{:S(2)}) %collective-permute-start.45) | collective-permute-done | bytes 262176 | tf_op jit(solution)/shard_map/ppermute | solution.py:30
  396.0 1.4 fusion.8
  397.4 1.3 collective-permute-start.46
  (308 shorter events, 67.3 us)
Async XLA Ops:
  1.8 30.6 %copy-start.74 = (bf16[64,2048]{1,0:T(8,128)(2,1)}, bf16[64,2048]{1,0:T(8,128)(2,1)S(1)}, u32[]{:S(2)}) copy-start(bf16[64,2048]{1,0:T(8,128)(2,1)S(1)} %get-tuple-element.197) | copy-start | bytes 786436
  1.8 12.4 %collective-permute-start.1 = (bf16[64,2048]{1,0:T(8,128)(2,1)S(1)}, bf16[64,2048]{1,0:T(8,128)(2,1)}, u32[]{:S(2)}, u32[]{:S(2)}) collective-permute-start(bf16[64,2048]{1,0:T(8,128)(2,1)S(1)} %get-tuple-element.197), channel_id=1, source_target_pairs={{0,8},{2,10},{4,12},{6,14},{8,0},{10,2},{12,4},{14,6},{16,24},{18,... | collective-permute-start | bytes 786440 | tf_op jit(solution)/shard_map/ppermute | solution.py:30
  2.1 13.8 %collective-permute-start.2 = (bf16[64,2048]{1,0:T(8,128)(2,1)S(1)}, bf16[64,2048]{1,0:T(8,128)(2,1)}, u32[]{:S(2)}, u32[]{:S(2)}) collective-permute-start(bf16[64,2048]{1,0:T(8,128)(2,1)S(1)} %get-tuple-element.197), channel_id=1, source_target_pairs={{0,16},{2,18},{4,20},{6,22},{8,24},{10,26},{12,28},{14,30},{16,0},... | collective-permute-start | bytes 786440 | tf_op jit(solution)/shard_map/ppermute | solution.py:30
  4.4 25.4 %collective-permute-start.3 = (bf16[64,2048]{1,0:T(8,128)(2,1)S(1)}, bf16[64,2048]{1,0:T(8,128)(2,1)}, u32[]{:S(2)}, u32[]{:S(2)}) collective-permute-start(bf16[64,2048]{1,0:T(8,128)(2,1)S(1)} %get-tuple-element.197), channel_id=1, source_target_pairs={{0,24},{2,26},{4,28},{6,30},{8,16},{10,18},{12,20},{14,22},{16,8},... | collective-permute-start | bytes 786440 | tf_op jit(solution)/shard_map/ppermute | solution.py:30
  9.8 20.0 %collective-permute-start = (bf16[8,256,128]{2,1,0:T(8,128)(2,1)}, bf16[8,256,128]{2,1,0:T(8,128)(2,1)}, u32[]{:S(2)}, u32[]{:S(2)}) collective-permute-start(bf16[8,256,128]{2,1,0:T(8,128)(2,1)} %get-tuple-element.424), channel_id=1, source_target_pairs={{0,1},{1,0},{2,3},{3,2},{4,5},{5,4},{6,7},{7,6},{8,9},{9,8},{10,11... | collective-permute-start | bytes 1572872 | tf_op jit(solution)/shard_map/ppermute | solution.py:25
  14.3 35.7 %copy-start.76 = (bf16[64,2048]{1,0:T(8,128)(2,1)}, bf16[64,2048]{1,0:T(8,128)(2,1)S(1)}, u32[]{:S(2)}) copy-start(bf16[64,2048]{1,0:T(8,128)(2,1)S(1)} %constant_dynamic-slice_fusion.3) | copy-start | bytes 786436
  29.8 13.4 %collective-permute-start.10 = (bf16[64,2048]{1,0:T(8,128)(2,1)S(1)}, bf16[64,2048]{1,0:T(8,128)(2,1)}, u32[]{:S(2)}, u32[]{:S(2)}) collective-permute-start(bf16[64,2048]{1,0:T(8,128)(2,1)S(1)} %constant_dynamic-slice_fusion.3), channel_id=1, source_target_pairs={{0,24},{2,26},{4,28},{6,30},{8,16},{10,18},{12,20},{14,22},{16,8},... | collective-permute-start | bytes 786440 | tf_op jit(solution)/shard_map/ppermute | solution.py:30
  31.1 12.1 %collective-permute-start.8 = (bf16[64,2048]{1,0:T(8,128)(2,1)S(1)}, bf16[64,2048]{1,0:T(8,128)(2,1)}, u32[]{:S(2)}, u32[]{:S(2)}) collective-permute-start(bf16[64,2048]{1,0:T(8,128)(2,1)S(1)} %constant_dynamic-slice_fusion.3), channel_id=1, source_target_pairs={{0,8},{2,10},{4,12},{6,14},{8,0},{10,2},{12,4},{14,6},{16,24},{18,... | collective-permute-start | bytes 786440 | tf_op jit(solution)/shard_map/ppermute | solution.py:30
  31.1 18.9 %collective-permute-start.9 = (bf16[64,2048]{1,0:T(8,128)(2,1)S(1)}, bf16[64,2048]{1,0:T(8,128)(2,1)}, u32[]{:S(2)}, u32[]{:S(2)}) collective-permute-start(bf16[64,2048]{1,0:T(8,128)(2,1)S(1)} %constant_dynamic-slice_fusion.3), channel_id=1, source_target_pairs={{0,16},{2,18},{4,20},{6,22},{8,24},{10,26},{12,28},{14,30},{16,0},... | collective-permute-start | bytes 786440 | tf_op jit(solution)/shard_map/ppermute | solution.py:30
  34.7 16.3 %collective-permute-start.5 = (bf16[128,2048]{1,0:T(8,128)(2,1)S(1)}, bf16[128,2048]{1,0:T(8,128)(2,1)}, u32[]{:S(2)}, u32[]{:S(2)}) collective-permute-start(bf16[128,2048]{1,0:T(8,128)(2,1)S(1)} %pad_maximum_fusion.3), channel_id=1, source_target_pairs={{0,2},{2,0},{4,6},{6,4},{8,10},{10,8},{12,14},{14,12},{16,18},{18,... | collective-permute-start | bytes 1572872 | tf_op jit(solution)/shard_map/ppermute | solution.py:30
  35.0 16.0 %collective-permute-start.4 = (bf16[128,2048]{1,0:T(8,128)(2,1)S(1)}, bf16[128,2048]{1,0:T(8,128)(2,1)}, u32[]{:S(2)}, u32[]{:S(2)}) collective-permute-start(bf16[128,2048]{1,0:T(8,128)(2,1)S(1)} %pad_maximum_fusion.2), channel_id=1, source_target_pairs={{0,4},{2,6},{4,0},{6,2},{8,12},{10,14},{12,8},{14,10},{16,20},{18,... | collective-permute-start | bytes 1572872 | tf_op jit(solution)/shard_map/ppermute | solution.py:30
  38.5 51.7 %all-to-all-start = ((bf16[16,272,128]{2,1,0:T(8,128)(2,1)}), bf16[16,272,128]{2,1,0:T(8,128)(2,1)S(1)}, u32[]{:S(2)}, u32[]{:S(2)}) async-start(bf16[16,272,128]{2,1,0:T(8,128)(2,1)} %pad_maximum_fusion.1), calls=%async_computation | async-start | bytes 2228224 | tf_op jit(solution)/shard_map/all_to_all | solution.py:1080
  52.1 35.3 %collective-permute-start.7 = (bf16[256,2048]{1,0:T(8,128)(2,1)S(1)}, bf16[256,2048]{1,0:T(8,128)(2,1)S(1)}, u32[]{:S(2)}, u32[]{:S(2)}) collective-permute-start(bf16[256,2048]{1,0:T(8,128)(2,1)S(1)} %constant_dynamic-update-slice_fusion.2.refs_3_.refs_7_.refs_5_), channel_id=1, source_target_pairs={{0,4},{2,6},{4,0},{6,2},{8,12},{10,14},{12,8},{14,10},{16,20},{18,... | collective-permute-start | bytes 3145736 | tf_op jit(solution)/shard_map/ppermute | solution.py:30
  54.7 32.8 %copy-start.15 = (bf16[256,2048]{1,0:T(8,128)(2,1)}, bf16[256,2048]{1,0:T(8,128)(2,1)S(1)}, u32[]{:S(2)}) copy-start(bf16[256,2048]{1,0:T(8,128)(2,1)S(1)} %constant_dynamic-update-slice_fusion.refs_1_.refs_5_.refs_3_) | copy-start | bytes 3145732
  54.7 34.5 %collective-permute-start.6 = (bf16[256,2048]{1,0:T(8,128)(2,1)S(1)}, bf16[256,2048]{1,0:T(8,128)(2,1)S(1)}, u32[]{:S(2)}, u32[]{:S(2)}) collective-permute-start(bf16[256,2048]{1,0:T(8,128)(2,1)S(1)} %constant_dynamic-update-slice_fusion.refs_1_.refs_5_.refs_3_), channel_id=1, source_target_pairs={{0,2},{2,0},{4,6},{6,4},{8,10},{10,8},{12,14},{14,12},{16,18},{18,... | collective-permute-start | bytes 3145736 | tf_op jit(solution)/shard_map/ppermute | solution.py:30
  56.3 29.7 %collective-permute-start.12 = (bf16[128,2048]{1,0:T(8,128)(2,1)S(1)}, bf16[128,2048]{1,0:T(8,128)(2,1)S(1)}, u32[]{:S(2)}, u32[]{:S(2)}) collective-permute-start(bf16[128,2048]{1,0:T(8,128)(2,1)S(1)} %pad_maximum_fusion.5), channel_id=1, source_target_pairs={{0,2},{2,0},{4,6},{6,4},{8,10},{10,8},{12,14},{14,12},{16,18},{18,... | collective-permute-start | bytes 1572872 | tf_op jit(solution)/shard_map/ppermute | solution.py:30
  57.6 29.9 %copy-start.78 = (bf16[128,2048]{1,0:T(8,128)(2,1)}, bf16[128,2048]{1,0:T(8,128)(2,1)S(1)}, u32[]{:S(2)}) copy-start(bf16[128,2048]{1,0:T(8,128)(2,1)S(1)} %pad_maximum_fusion.4) | copy-start | bytes 1572868
  57.6 29.9 %collective-permute-start.11 = (bf16[128,2048]{1,0:T(8,128)(2,1)S(1)}, bf16[128,2048]{1,0:T(8,128)(2,1)S(1)}, u32[]{:S(2)}, u32[]{:S(2)}) collective-permute-start(bf16[128,2048]{1,0:T(8,128)(2,1)S(1)} %pad_maximum_fusion.4), channel_id=1, source_target_pairs={{0,4},{2,6},{4,0},{6,2},{8,12},{10,14},{12,8},{14,10},{16,20},{18,... | collective-permute-start | bytes 1572872 | tf_op jit(solution)/shard_map/ppermute | solution.py:30
  90.3 12.5 %collective-permute-start.13 = (bf16[16,272,128]{2,1,0:T(8,128)(2,1)S(1)}, bf16[16,272,128]{2,1,0:T(8,128)(2,1)S(1)}, u32[]{:S(2)}, u32[]{:S(2)}) collective-permute-start(bf16[16,272,128]{2,1,0:T(8,128)(2,1)S(1)} %all-to-all-done.refs_2_), channel_id=1, source_target_pairs={{0,1},{1,0},{2,3},{3,2},{4,5},{5,4},{6,7},{7,6},{8,9},{9,8},{10,11... | collective-permute-start | bytes 3342344 | tf_op jit(solution)/shard_map/ppermute | solution.py:25
  103.8 51.8 %all-to-all-start.1 = ((bf16[16,512,128]{2,1,0:T(8,128)(2,1)}), bf16[16,512,128]{2,1,0:T(8,128)(2,1)}, u32[]{:S(2)}, u32[]{:S(2)}) async-start(bf16[16,512,128]{2,1,0:T(8,128)(2,1)} %feed_deal.1), calls=%async_computation.1 | async-start | bytes 4194304 | tf_op jit(solution)/shard_map/all_to_all | solution.py:1103
  109.7 44.4 %collective-permute-start.15 = (bf16[256,2048]{1,0:T(8,128)(2,1)S(1)}, bf16[256,2048]{1,0:T(8,128)(2,1)S(1)}, u32[]{:S(2)}, u32[]{:S(2)}) collective-permute-start(bf16[256,2048]{1,0:T(8,128)(2,1)S(1)} %constant_dynamic-update-slice_fusion.6.refs_3_.refs_5_.refs_11_), channel_id=1, source_target_pairs={{0,4},{2,6},{4,0},{6,2},{8,12},{10,14},{12,8},{14,10},{16,20},{18,... | collective-permute-start | bytes 3145736 | tf_op jit(solution)/shard_map/ppermute | solution.py:30
  113.7 40.5 %collective-permute-start.14 = (bf16[256,2048]{1,0:T(8,128)(2,1)S(1)}, bf16[256,2048]{1,0:T(8,128)(2,1)S(1)}, u32[]{:S(2)}, u32[]{:S(2)}) collective-permute-start(bf16[256,2048]{1,0:T(8,128)(2,1)S(1)} %constant_dynamic-update-slice_fusion.4.refs_1_.refs_3_.refs_9_), channel_id=1, source_target_pairs={{0,2},{2,0},{4,6},{6,4},{8,10},{10,8},{12,14},{14,12},{16,18},{18,... | collective-permute-start | bytes 3145736 | tf_op jit(solution)/shard_map/ppermute | solution.py:30
  130.9 23.3 %copy-start.43 = (bf16[1024,384]{1,0:T(8,128)(2,1)}, bf16[1024,384]{1,0:T(8,128)(2,1)S(1)}, u32[]{:S(2)}) copy-start(bf16[1024,384]{1,0:T(8,128)(2,1)S(1)} %get-tuple-element.249.refs_1_) | copy-start | bytes 2359300
  155.6 6.6 %collective-permute-start.18 = (bf16[16,512,128]{2,1,0:T(8,128)(2,1)}, bf16[16,512,128]{2,1,0:T(8,128)(2,1)S(1)}, u32[]{:S(2)}, u32[]{:S(2)}) collective-permute-start(bf16[16,512,128]{2,1,0:T(8,128)(2,1)} %all-to-all-done.1.refs_5_), channel_id=1, source_target_pairs={{0,1},{1,0},{2,3},{3,2},{4,5},{5,4},{6,7},{7,6},{8,9},{9,8},{10,11... | collective-permute-start | bytes 6291464 | tf_op jit(solution)/shard_map/ppermute | solution.py:25
  158.2 13.8 %collective-permute-start.19 = (bf16[128,2048]{1,0:T(8,128)(2,1)}, bf16[128,2048]{1,0:T(8,128)(2,1)S(1)}, u32[]{:S(2)}, u32[]{:S(2)}) collective-permute-start(bf16[128,2048]{1,0:T(8,128)(2,1)} %copy-done.52), channel_id=1, source_target_pairs={{0,2},{2,0},{4,6},{6,4},{8,10},{10,8},{12,14},{14,12},{16,18},{18,... | collective-permute-start | bytes 1572872 | tf_op jit(solution)/shard_map/ppermute | solution.py:30
  158.3 31.8 %collective-permute-start.16 = (bf16[1024,384]{1,0:T(8,128)(2,1)}, bf16[1024,384]{1,0:T(8,128)(2,1)S(1)}, u32[]{:S(2)}, u32[]{:S(2)}) collective-permute-start(bf16[1024,384]{1,0:T(8,128)(2,1)} %copy-done.43), channel_id=1, source_target_pairs={{0,2},{2,0},{4,6},{6,4},{8,10},{10,8},{12,14},{14,12},{16,18},{18,... | collective-permute-start | bytes 2359304 | tf_op jit(solution)/shard_map/ppermute | solution.py:30
  159.7 30.4 %collective-permute-start.17 = (bf16[1024,384]{1,0:T(8,128)(2,1)}, bf16[1024,384]{1,0:T(8,128)(2,1)S(1)}, u32[]{:S(2)}, u32[]{:S(2)}) collective-permute-start(bf16[1024,384]{1,0:T(8,128)(2,1)} %copy-done.43), channel_id=1, source_target_pairs={{0,1},{1,0},{2,3},{3,2},{4,5},{5,4},{6,7},{7,6},{8,9},{9,8},{10,11... | collective-permute-start | bytes 2359304 | tf_op jit(solution)/shard_map/ppermute | solution.py:25
  190.1 6.1 %collective-permute-start.20 = (bf16[1024,384]{1,0:T(8,128)(2,1)S(1)}, bf16[1024,384]{1,0:T(8,128)(2,1)S(1)}, u32[]{:S(2)}, u32[]{:S(2)}) collective-permute-start(bf16[1024,384]{1,0:T(8,128)(2,1)S(1)} %collective-permute-done.16.refs_2_), channel_id=1, source_target_pairs={{0,1},{1,0},{2,3},{3,2},{4,5},{5,4},{6,7},{7,6},{8,9},{9,8},{10,11... | collective-permute-start | bytes 2359304 | tf_op jit(solution)/shard_map/ppermute | solution.py:25
  196.3 10.4 %collective-permute-start.23 = (bf16[16,512,128]{2,1,0:T(8,128)(2,1)S(1)}, bf16[16,512,128]{2,1,0:T(8,128)(2,1)S(1)}, u32[]{:S(2)}, u32[]{:S(2)}) collective-permute-start(bf16[16,512,128]{2,1,0:T(8,128)(2,1)S(1)} %outer.2), channel_id=1, source_target_pairs={{0,1},{1,0},{2,3},{3,2},{4,5},{5,4},{6,7},{7,6},{8,9},{9,8},{10,11... | collective-permute-start | bytes 6291464 | tf_op jit(solution)/shard_map/ppermute | solution.py:25
  196.4 8.4 %collective-permute-start.21 = (bf16[1024,256]{1,0:T(8,128)(2,1)S(1)}, bf16[1024,256]{1,0:T(8,128)(2,1)S(1)}, u32[]{:S(2)}, u32[]{:S(2)}) collective-permute-start(bf16[1024,256]{1,0:T(8,128)(2,1)S(1)} %get-tuple-element.248.refs_5_), channel_id=1, source_target_pairs={{0,1},{1,0},{2,3},{3,2},{4,5},{5,4},{6,7},{7,6},{8,9},{9,8},{10,11... | collective-permute-start | bytes 1572872 | tf_op jit(solution)/shard_map/ppermute | solution.py:25
  204.8 6.8 %collective-permute-start.24 = (f32[8,512]{1,0:T(8,128)S(1)}, f32[8,512]{1,0:T(8,128)S(1)}, u32[]{:S(2)}, u32[]{:S(2)}) collective-permute-start(f32[8,512]{1,0:T(8,128)S(1)} %get-tuple-element.259.refs_7_), channel_id=1, source_target_pairs={{0,2},{2,0},{4,6},{6,4},{8,10},{10,8},{12,14},{14,12},{16,18},{18,... | collective-permute-start | bytes 49160 | tf_op jit(solution)/shard_map/ppermute | solution.py:30
  204.9 6.7 %collective-permute-start.25 = (f32[8,512]{1,0:T(8,128)S(1)}, f32[8,512]{1,0:T(8,128)S(1)}, u32[]{:S(2)}, u32[]{:S(2)}) collective-permute-start(f32[8,512]{1,0:T(8,128)S(1)} %get-tuple-element.259.refs_7_), channel_id=1, source_target_pairs={{0,1},{1,0},{2,3},{3,2},{4,5},{5,4},{6,7},{7,6},{8,9},{9,8},{10,11... | collective-permute-start | bytes 49160 | tf_op jit(solution)/shard_map/ppermute | solution.py:25
  205.3 7.7 %collective-permute-start.26 = (f32[8,512]{1,0:T(8,128)S(1)}, f32[8,512]{1,0:T(8,128)S(1)}, u32[]{:S(2)}, u32[]{:S(2)}) collective-permute-start(f32[8,512]{1,0:T(8,128)S(1)} %get-tuple-element.259.refs_7_), channel_id=1, source_target_pairs={{0,3},{1,2},{2,1},{3,0},{4,7},{5,6},{6,5},{7,4},{8,11},{9,10},{10,... | collective-permute-start | bytes 49160 | tf_op jit(solution)/shard_map/ppermute | solution.py:1208
  213.0 79.4 %all-to-all-start.2 = ((bf16[16,512,128]{2,1,0:T(8,128)(2,1)}), bf16[16,512,128]{2,1,0:T(8,128)(2,1)}, u32[]{:S(2)}, u32[]{:S(2)}) async-start(bf16[16,512,128]{2,1,0:T(8,128)(2,1)} %copy-done.9), calls=%async_computation.2 | async-start | bytes 4194304 | tf_op jit(solution)/shard_map/all_to_all | solution.py:1224
  218.7 19.6 %collective-permute-start.22 = (bf16[512,256]{1,0:T(8,128)(2,1)}, bf16[512,256]{1,0:T(8,128)(2,1)S(1)}, u32[]{:S(2)}, u32[]{:S(2)}) collective-permute-start(bf16[512,256]{1,0:T(8,128)(2,1)} %copy-done.61), channel_id=1, source_target_pairs={{0,2},{2,0},{4,6},{6,4},{8,10},{10,8},{12,14},{14,12},{16,18},{18,... | collective-permute-start | bytes 786440 | tf_op jit(solution)/shard_map/ppermute | solution.py:30
  231.4 11.9 %collective-permute-start.27 = (bf16[512,256]{1,0:T(8,128)(2,1)S(1)}, bf16[512,256]{1,0:T(8,128)(2,1)S(1)}, u32[]{:S(2)}, u32[]{:S(2)}) collective-permute-start(bf16[512,256]{1,0:T(8,128)(2,1)S(1)} %get-tuple-element.263), channel_id=1, source_target_pairs={{0,2},{2,0},{4,6},{6,4},{8,10},{10,8},{12,14},{14,12},{16,18},{18,... | collective-permute-start | bytes 786440 | tf_op jit(solution)/shard_map/ppermute | solution.py:30
  232.7 19.7 %copy-start.14 = (bf16[256,2048]{1,0:T(8,128)(2,1)S(1)}, bf16[256,2048]{1,0:T(8,128)(2,1)}, u32[]{:S(2)}) copy-start(bf16[256,2048]{1,0:T(8,128)(2,1)} %copy-done.12) | copy-start | bytes 3145732
  232.7 19.7 %copy-start.17 = (bf16[256,2048]{1,0:T(8,128)(2,1)S(1)}, bf16[256,2048]{1,0:T(8,128)(2,1)}, u32[]{:S(2)}) copy-start(bf16[256,2048]{1,0:T(8,128)(2,1)} %copy-done.15) | copy-start | bytes 3145732
  232.7 19.7 %copy-start.22 = (bf16[256,2048]{1,0:T(8,128)(2,1)S(1)}, bf16[256,2048]{1,0:T(8,128)(2,1)}, u32[]{:S(2)}) copy-start(bf16[256,2048]{1,0:T(8,128)(2,1)} %copy-done.20) | copy-start | bytes 3145732
  232.7 19.7 %copy-start.25 = (bf16[256,2048]{1,0:T(8,128)(2,1)S(1)}, bf16[256,2048]{1,0:T(8,128)(2,1)}, u32[]{:S(2)}) copy-start(bf16[256,2048]{1,0:T(8,128)(2,1)} %copy-done.23) | copy-start | bytes 3145732
  243.3 31.8 %collective-permute-start.28 = (bf16[256,2048]{1,0:T(8,128)(2,1)S(1)}, bf16[256,2048]{1,0:T(8,128)(2,1)S(1)}, u32[]{:S(2)}, u32[]{:S(2)}) collective-permute-start(bf16[256,2048]{1,0:T(8,128)(2,1)S(1)} %get-tuple-element.273), channel_id=1, source_target_pairs={{0,2},{2,0},{4,6},{6,4},{8,10},{10,8},{12,14},{14,12},{16,18},{18,... | collective-permute-start | bytes 3145736 | tf_op jit(solution)/shard_map/ppermute | solution.py:30
  244.6 35.0 %collective-permute-start.29 = (bf16[256,2048]{1,0:T(8,128)(2,1)S(1)}, bf16[256,2048]{1,0:T(8,128)(2,1)S(1)}, u32[]{:S(2)}, u32[]{:S(2)}) collective-permute-start(bf16[256,2048]{1,0:T(8,128)(2,1)S(1)} %get-tuple-element.274), channel_id=1, source_target_pairs={{0,4},{2,6},{4,0},{6,2},{8,12},{10,14},{12,8},{14,10},{16,20},{18,... | collective-permute-start | bytes 3145736 | tf_op jit(solution)/shard_map/ppermute | solution.py:30
  263.6 10.1 %collective-permute-start.30 = (f32[8,2048]{1,0:T(8,128)S(1)}, f32[8,2048]{1,0:T(8,128)S(1)}, u32[]{:S(2)}, u32[]{:S(2)}) collective-permute-start(f32[8,2048]{1,0:T(8,128)S(1)} %get-tuple-element.297.refs_1_), channel_id=1, source_target_pairs={{0,1},{1,0},{2,3},{3,2},{4,5},{5,4},{6,7},{7,6},{8,9},{9,8},{10,11... | collective-permute-start | bytes 196616 | tf_op jit(solution)/shard_map/ppermute | solution.py:25
  279.6 10.7 %collective-permute-start.31 = (bf16[16,256,128]{2,1,0:T(8,128)(2,1)S(1)}, bf16[16,256,128]{2,1,0:T(8,128)(2,1)S(1)}, u32[]{:S(2)}, u32[]{:S(2)}) collective-permute-start(bf16[16,256,128]{2,1,0:T(8,128)(2,1)S(1)} %get-tuple-element.296), channel_id=1, source_target_pairs={{0,1},{1,0},{2,3},{3,2},{4,5},{5,4},{6,7},{7,6},{8,9},{9,8},{10,11... | collective-permute-start | bytes 3145736 | tf_op jit(solution)/shard_map/ppermute | solution.py:25
  281.1 25.0 %collective-permute-start.32 = (bf16[256,2048]{1,0:T(8,128)(2,1)}, bf16[256,2048]{1,0:T(8,128)(2,1)S(1)}, u32[]{:S(2)}, u32[]{:S(2)}) collective-permute-start(bf16[256,2048]{1,0:T(8,128)(2,1)} %get-tuple-element.312), channel_id=1, source_target_pairs={{0,2},{2,0},{4,6},{6,4},{8,10},{10,8},{12,14},{14,12},{16,18},{18,... | collective-permute-start | bytes 3145736 | tf_op jit(solution)/shard_map/ppermute | solution.py:30
  281.3 30.2 %collective-permute-start.33 = (bf16[256,2048]{1,0:T(8,128)(2,1)}, bf16[256,2048]{1,0:T(8,128)(2,1)S(1)}, u32[]{:S(2)}, u32[]{:S(2)}) collective-permute-start(bf16[256,2048]{1,0:T(8,128)(2,1)} %get-tuple-element.313), channel_id=1, source_target_pairs={{0,4},{2,6},{4,0},{6,2},{8,12},{10,14},{12,8},{14,10},{16,20},{18,... | collective-permute-start | bytes 3145736 | tf_op jit(solution)/shard_map/ppermute | solution.py:30
  290.3 37.6 %collective-permute-start.34 = (bf16[128,2048]{1,0:T(8,128)(2,1)}, bf16[128,2048]{1,0:T(8,128)(2,1)}, u32[]{:S(2)}, u32[]{:S(2)}) collective-permute-start(bf16[128,2048]{1,0:T(8,128)(2,1)} %get-tuple-element.314), channel_id=1, source_target_pairs={{0,4},{2,6},{4,0},{6,2},{8,12},{10,14},{12,8},{14,10},{16,20},{18,... | collective-permute-start | bytes 1572872 | tf_op jit(solution)/shard_map/ppermute | solution.py:30
  290.4 37.6 %collective-permute-start.35 = (bf16[128,2048]{1,0:T(8,128)(2,1)}, bf16[128,2048]{1,0:T(8,128)(2,1)}, u32[]{:S(2)}, u32[]{:S(2)}) collective-permute-start(bf16[128,2048]{1,0:T(8,128)(2,1)} %get-tuple-element.315), channel_id=1, source_target_pairs={{0,2},{2,0},{4,6},{6,4},{8,10},{10,8},{12,14},{14,12},{16,18},{18,... | collective-permute-start | bytes 1572872 | tf_op jit(solution)/shard_map/ppermute | solution.py:30
  292.4 76.2 %all-to-all-start.3 = ((bf16[16,288,128]{2,1,0:T(8,128)(2,1)}), bf16[16,288,128]{2,1,0:T(8,128)(2,1)S(1)}, u32[]{:S(2)}, u32[]{:S(2)}) async-start(bf16[16,288,128]{2,1,0:T(8,128)(2,1)} %pad_maximum_fusion), calls=%async_computation.3 | async-start | bytes 2359296 | tf_op jit(solution)/shard_map/all_to_all | solution.py:1324
  296.9 37.0 %copy-start.29 = (bf16[256,2048]{1,0:T(8,128)(2,1)S(1)}, bf16[256,2048]{1,0:T(8,128)(2,1)}, u32[]{:S(2)}) copy-start(bf16[256,2048]{1,0:T(8,128)(2,1)} %copy-done.28) | copy-start | bytes 3145732
  296.9 37.0 %copy-start.31 = (bf16[256,2048]{1,0:T(8,128)(2,1)S(1)}, bf16[256,2048]{1,0:T(8,128)(2,1)}, u32[]{:S(2)}) copy-start(bf16[256,2048]{1,0:T(8,128)(2,1)} %copy-done.30) | copy-start | bytes 3145732
  335.3 28.1 %copy-start.75 = (bf16[64,2048]{1,0:T(8,128)(2,1)S(1)}, bf16[64,2048]{1,0:T(8,128)(2,1)}, u32[]{:S(2)}) copy-start(bf16[64,2048]{1,0:T(8,128)(2,1)} %copy-done.74) | copy-start | bytes 786436
  335.4 10.7 %collective-permute-start.36 = (bf16[128,2048]{1,0:T(8,128)(2,1)S(1)}, bf16[128,2048]{1,0:T(8,128)(2,1)S(1)}, u32[]{:S(2)}, u32[]{:S(2)}) collective-permute-start(bf16[128,2048]{1,0:T(8,128)(2,1)S(1)} %get-tuple-element.336), channel_id=1, source_target_pairs={{0,4},{2,6},{4,0},{6,2},{8,12},{10,14},{12,8},{14,10},{16,20},{18,... | collective-permute-start | bytes 1572872 | tf_op jit(solution)/shard_map/ppermute | solution.py:30
  336.6 10.9 %collective-permute-start.37 = (bf16[128,2048]{1,0:T(8,128)(2,1)S(1)}, bf16[128,2048]{1,0:T(8,128)(2,1)S(1)}, u32[]{:S(2)}, u32[]{:S(2)}) collective-permute-start(bf16[128,2048]{1,0:T(8,128)(2,1)S(1)} %get-tuple-element.337), channel_id=1, source_target_pairs={{0,2},{2,0},{4,6},{6,4},{8,10},{10,8},{12,14},{14,12},{16,18},{18,... | collective-permute-start | bytes 1572872 | tf_op jit(solution)/shard_map/ppermute | solution.py:30
  338.4 10.0 %collective-permute-start.38 = (bf16[64,2048]{1,0:T(8,128)(2,1)S(1)}, bf16[64,2048]{1,0:T(8,128)(2,1)S(1)}, u32[]{:S(2)}, u32[]{:S(2)}) collective-permute-start(bf16[64,2048]{1,0:T(8,128)(2,1)S(1)} %get-tuple-element.345), channel_id=1, source_target_pairs={{0,8},{2,10},{4,12},{6,14},{8,0},{10,2},{12,4},{14,6},{16,24},{18,... | collective-permute-start | bytes 786440 | tf_op jit(solution)/shard_map/ppermute | solution.py:30
  338.4 10.0 %collective-permute-start.39 = (bf16[64,2048]{1,0:T(8,128)(2,1)S(1)}, bf16[64,2048]{1,0:T(8,128)(2,1)S(1)}, u32[]{:S(2)}, u32[]{:S(2)}) collective-permute-start(bf16[64,2048]{1,0:T(8,128)(2,1)S(1)} %get-tuple-element.346), channel_id=1, source_target_pairs={{0,16},{2,18},{4,20},{6,22},{8,24},{10,26},{12,28},{14,30},{16,0},... | collective-permute-start | bytes 786440 | tf_op jit(solution)/shard_map/ppermute | solution.py:30
  338.4 25.1 %collective-permute-start.40 = (bf16[64,2048]{1,0:T(8,128)(2,1)S(1)}, bf16[64,2048]{1,0:T(8,128)(2,1)S(1)}, u32[]{:S(2)}, u32[]{:S(2)}) collective-permute-start(bf16[64,2048]{1,0:T(8,128)(2,1)S(1)} %get-tuple-element.347), channel_id=1, source_target_pairs={{0,24},{2,26},{4,28},{6,30},{8,16},{10,18},{12,20},{14,22},{16,8},... | collective-permute-start | bytes 786440 | tf_op jit(solution)/shard_map/ppermute | solution.py:30
  363.8 2.9 collective-permute-start.41
  368.6 27.4 %copy-start.77 = (bf16[64,2048]{1,0:T(8,128)(2,1)S(1)}, bf16[64,2048]{1,0:T(8,128)(2,1)}, u32[]{:S(2)}) copy-start(bf16[64,2048]{1,0:T(8,128)(2,1)} %copy-done.76) | copy-start | bytes 786436
  368.6 3.1 collective-permute-start.42
  369.1 9.3 %collective-permute-start.43 = (bf16[64,2048]{1,0:T(8,128)(2,1)S(1)}, bf16[64,2048]{1,0:T(8,128)(2,1)S(1)}, u32[]{:S(2)}, u32[]{:S(2)}) collective-permute-start(bf16[64,2048]{1,0:T(8,128)(2,1)S(1)} %get-tuple-element.357), channel_id=1, source_target_pairs={{0,8},{2,10},{4,12},{6,14},{8,0},{10,2},{12,4},{14,6},{16,24},{18,... | collective-permute-start | bytes 786440 | tf_op jit(solution)/shard_map/ppermute | solution.py:30
  369.1 12.4 %collective-permute-start.44 = (bf16[64,2048]{1,0:T(8,128)(2,1)S(1)}, bf16[64,2048]{1,0:T(8,128)(2,1)S(1)}, u32[]{:S(2)}, u32[]{:S(2)}) collective-permute-start(bf16[64,2048]{1,0:T(8,128)(2,1)S(1)} %get-tuple-element.358), channel_id=1, source_target_pairs={{0,16},{2,18},{4,20},{6,22},{8,24},{10,26},{12,28},{14,30},{16,0},... | collective-permute-start | bytes 786440 | tf_op jit(solution)/shard_map/ppermute | solution.py:30
  369.5 25.2 %collective-permute-start.45 = (bf16[64,2048]{1,0:T(8,128)(2,1)S(1)}, bf16[64,2048]{1,0:T(8,128)(2,1)}, u32[]{:S(2)}, u32[]{:S(2)}) collective-permute-start(bf16[64,2048]{1,0:T(8,128)(2,1)S(1)} %get-tuple-element.359), channel_id=1, source_target_pairs={{0,24},{2,26},{4,28},{6,30},{8,16},{10,18},{12,20},{14,22},{16,8},... | collective-permute-start | bytes 786440 | tf_op jit(solution)/shard_map/ppermute | solution.py:30
  397.4 4.8 %collective-permute-start.46 = (bf16[64,2048]{1,0:T(8,128)(2,1)S(1)}, bf16[64,2048]{1,0:T(8,128)(2,1)S(1)}, u32[]{:S(2)}, u32[]{:S(2)}) collective-permute-start(bf16[64,2048]{1,0:T(8,128)(2,1)S(1)} %fusion.8), channel_id=1, source_target_pairs={{0,1},{1,0},{2,3},{3,2},{4,5},{5,4},{6,7},{7,6},{8,9},{9,8},{10,11... | collective-permute-start | bytes 786440 | tf_op jit(solution)/shard_map/ppermute | solution.py:25
  (77 other events, 471.1 us)

commit v6 on v5

--- a/solution.py
+++ b/solution.py
@@ -462,7 +462,9 @@
 SMEM = pl.BlockSpec(memory_space=pltpu.SMEM)
 GRANT = 28 * 1024 * 1024
 MARK_COS, MARK_SIN = 32, 64
-WEIGHTS = {"deal": 10, "norm": 10, "feed": 10, "query": 10, "key": 3, "by_z": 3, "fold": 100}
+WEIGHTS = {
+    "deal": 10, "norm": 10, "feed": 10, "query": 10, "key": 3, "by_z": 3, "fold": 100, "small": 100, "inputs": 0.3, "feed_unpack": 30
+}
 WIDE = 256
 
 

time: 405 us -> 404 us (level)
  no operation moved by 1% of the time
where the time goes in v6:
time: 404 us; the launch traced here: 403 us
  waiting for transfers between devices  171 us (42%)
  Pallas kernels  90.9 us (22%)
  starting transfers between devices  81.1 us (20%)
  local copies, waits for them, and re-layouts  45.1 us (11%)
  other arithmetic  12.7 us (3%)
    ppermute x33, waiting for transfers between devices, from_peer(): return lax.ppermute(value, 'blk', [(i, i ^ mask) for i in range(count)])  165 us
    ppermute x33, starting transfers between devices, from_peer(): return lax.ppermute(value, 'blk', [(i, i ^ mask) for i in range(count)])  35.4 us
    unnamed x195, local copies, waits for them, and re-layouts  33.6 us
    ppermute x13, starting transfers between devices, swap_cores(): return lax.ppermute(value, 'tp', [(0, 1), (1, 0)])  23.6 us
    pallas_call x1, Pallas kernels, body(): run_kernel(lambda *refs: feed_kernel(units, blocks, *refs), [((count, 2 *...  11.1 us
    pallas_call x1, Pallas kernels, body(): run_kernel(lambda *refs: norm_kernel(r, *refs), [((count, width), BF), ((...  10.4 us
    pallas_call x2, Pallas kernels, outer(): run_kernel(lambda *refs: outer_kernel(units, *refs), [((blocks, 2 * units...  9.67 us
    pallas_call x1, Pallas kernels, body(): run_kernel(lambda *refs: inputs_kernel(r, *refs), [((quarter, width), BF)...  8.81 us
  transfers between devices with their start and end apart: 51, of which 23 were waited for; matrix products, arithmetic and copies ran while one was open for 6% of the time, Pallas kernels for 23%

profile of v6, /device:TPU:11, one launch (start us, length us, event | category | flops | bytes accessed | tf_op | source)
XLA Modules:
  0.0 402.7 jit_solution(8637079568862505200)
XLA Ops:
  2.1 2.3 collective-permute-start.2
  7.8 2.1 fusion.13
  9.8 1.5 collective-permute-start
  12.5 1.7 feed_deal.1
  14.3 1.6 collective-permute-done.2
  15.9 14.0 %collective-permute-done.3 = bf16[64,2048]{1,0:T(8,128)(2,1)} collective-permute-done((bf16[64,2048]{1,0:T(8,128)(2,1)S(1)}, bf16[64,2048]{1,0:T(8,128)(2,1)}, u32[]{:S(2)}, u32[]{:S(2)}) %collective-permute-start.3) | collective-permute-done | bytes 262176 | tf_op jit(solution)/shard_map/ppermute | solution.py:30
  31.1 1.4 collective-permute-start.9
  38.5 4.7 %all-to-all-start = ((bf16[16,272,128]{2,1,0:T(8,128)(2,1)}), bf16[16,272,128]{2,1,0:T(8,128)(2,1)S(1)}, u32[]{:S(2)}, u32[]{:S(2)}) async-start(bf16[16,272,128]{2,1,0:T(8,128)(2,1)} %pad_maximum_fusion.1), calls=%async_computation | async-start | bytes 2228224 | tf_op jit(solution)/shard_map/all_to_all | solution.py:1082
  43.3 6.7 %collective-permute-done.9 = bf16[64,2048]{1,0:T(8,128)(2,1)} collective-permute-done((bf16[64,2048]{1,0:T(8,128)(2,1)S(1)}, bf16[64,2048]{1,0:T(8,128)(2,1)}, u32[]{:S(2)}, u32[]{:S(2)}) %collective-permute-start.9) | collective-permute-done | bytes 262176 | tf_op jit(solution)/shard_map/ppermute | solution.py:30
  52.1 1.4 collective-permute-start.7
  57.9 28.1 %collective-permute-done.12 = bf16[128,2048]{1,0:T(8,128)(2,1)S(1)} collective-permute-done((bf16[128,2048]{1,0:T(8,128)(2,1)S(1)}, bf16[128,2048]{1,0:T(8,128)(2,1)S(1)}, u32[]{:S(2)}, u32[]{:S(2)}) %collective-permute-start.12) | collective-permute-done | bytes 524320 | tf_op jit(solution)/shard_map/ppermute | solution.py:30
  86.0 1.5 collective-permute-done.11
  90.3 10.1 %collective-permute-start.13 = (bf16[16,272,128]{2,1,0:T(8,128)(2,1)S(1)}, bf16[16,272,128]{2,1,0:T(8,128)(2,1)S(1)}, u32[]{:S(2)}, u32[]{:S(2)}) collective-permute-start(bf16[16,272,128]{2,1,0:T(8,128)(2,1)S(1)} %all-to-all-done.refs_2_), channel_id=1, source_target_pairs={{0,1},{1,0},{2,3},{3,2},{4,5},{5,4},{6,7},{7,6},{8,9},{9,8},{10,11... | collective-permute-start | bytes 3342344 | tf_op jit(solution)/shard_map/ppermute | solution.py:25
  100.4 2.4 collective-permute-done.13.refs_3_
  103.8 5.6 %all-to-all-start.1 = ((bf16[16,512,128]{2,1,0:T(8,128)(2,1)}), bf16[16,512,128]{2,1,0:T(8,128)(2,1)}, u32[]{:S(2)}, u32[]{:S(2)}) async-start(bf16[16,512,128]{2,1,0:T(8,128)(2,1)} %feed_deal.1), calls=%async_computation.1 | async-start | bytes 4194304 | tf_op jit(solution)/shard_map/all_to_all | solution.py:1105
  111.0 1.6 constant_dynamic-update-slice_fusion.5
  114.0 3.5 deal.1
  117.6 10.4 %norm.1 = (bf16[1024,2048]{1,0:T(8,128)(2,1)S(1)}, f32[1024,128]{1,0:T(8,128)S(1)}, bf16[1024,384]{1,0:T(8,128)(2,1)S(1)}) custom-call(s32[2]{0:T(128)S(1)} %pad_add_fusion.refs_0_, bf16[256,2048]{1,0:T(8,128)(2,1)S(1)} %copy-done.14, bf16[256,2048]{1,0:T(8,128)(2,1)S(1)} %copy-done.22, bf16[256,2048]{1,0:T(8,128)(2,1)S(1)} %copy-done.11, ...), custom_call_target="tpu_custom_call" | custom-call | flops 16106127360 | bytes 220000000 | tf_op jit(solution)/shard_map/norm/pallas_call | solution.py:1122
  128.0 2.0 copy-done.2
  130.9 23.3 %collective-permute-done.15.refs_4_.refs_6_.refs_12_ = bf16[256,2048]{1,0:T(8,128)(2,1)S(1)} collective-permute-done((bf16[256,2048]{1,0:T(8,128)(2,1)S(1)}, bf16[256,2048]{1,0:T(8,128)(2,1)S(1)}, u32[]{:S(2)}, u32[]{:S(2)}) %collective-permute-start.15) | collective-permute-done | bytes 1048608 | tf_op jit(solution)/shard_map/ppermute | solution.py:30
  155.6 2.6 collective-permute-start.18
  158.3 1.4 collective-permute-start.16
  160.2 2.0 collective-permute-done.18.refs_6_
  162.2 9.8 %collective-permute-done.19.refs_9_.refs_4_ = bf16[128,2048]{1,0:T(8,128)(2,1)S(1)} collective-permute-done((bf16[128,2048]{1,0:T(8,128)(2,1)}, bf16[128,2048]{1,0:T(8,128)(2,1)S(1)}, u32[]{:S(2)}, u32[]{:S(2)}) %collective-permute-start.19) | collective-permute-done | bytes 524320 | tf_op jit(solution)/shard_map/ppermute | solution.py:30
  172.0 2.4 copy-done.3
  176.6 11.1 %feed.1 = (bf16[1024,512]{1,0:T(8,128)(2,1)S(1)}, bf16[1024,512]{1,0:T(8,128)(2,1)S(1)}, bf16[512,1024]{1,0:T(8,128)(2,1)S(1)}, bf16[512,1024]{1,0:T(8,128)(2,1)...) custom-call(bf16[1024,2048]{1,0:T(8,128)(2,1)S(1)} %copy-done.3, ...), custom_call_target="tpu_custom_call" | custom-call | flops 42949672960 | bytes 200000000 | tf_op jit(solution)/shard_map/feed/pallas_call | solution.py:1143
  190.4 4.9 %outer.2 = bf16[16,512,128]{2,1,0:T(8,128)(2,1)S(1)} custom-call(bf16[512,1024]{1,0:T(8,128)(2,1)S(1)} %get-tuple-element.245.refs_0_, bf16[512,1024]{1,0:T(8,128)(2,1)S(1)} %get-tuple-element.246.refs_1_, bf16[1024,2048]{1,0:T(8,128)(2,1)S(1)} %copy-done.4, bf16[256,2048]{1,0:T(8,128)(2,1)S(1)} %constant_dynamic-update-slice_fusion.4.refs_1_.refs_3_.refs_9_, ...), custom_call_target="tpu_custom_call" | custom-call | flops 2147483648 | bytes 12000000 | tf_op jit(solution)/shard_map/outer/pallas_call | solution.py:1168
  195.9 7.8 %query.1 = (bf16[512,256]{1,0:T(8,128)(2,1)S(1)}, bf16[512,256]{1,0:T(8,128)(2,1)S(1)}, bf16[512,256]{1,0:T(8,128)(2,1)S(1)}, f32[8,512]{1,0:T(8,128)S(1)}) custom-call(s32[2]{0:T(128)S(1)} %pad_add_fusion.refs_0_, bf16[1024,384]{1,0:T(8,128)(2,1)S(1)} %copy-done.50, bf16[1024,384]{1,0:T(8,128)(2,1)S(1)} %collective-permute-done.16.refs_2_, ...), custom_call_target="tpu_custom_call" | custom-call | flops 21474836480 | bytes 60000000 | tf_op jit(solution)/shard_map/query/pallas_call | solution.py:1194
  204.3 1.5 collective-permute-start.26
  205.8 4.8 %outer.3 = bf16[16,512,128]{2,1,0:T(8,128)(2,1)S(1)} custom-call(bf16[512,1024]{1,0:T(8,128)(2,1)S(1)} %get-tuple-element.245.refs_0_, bf16[512,1024]{1,0:T(8,128)(2,1)S(1)} %get-tuple-element.246.refs_1_, bf16[1024,2048]{1,0:T(8,128)(2,1)S(1)} %copy-done.4, bf16[256,2048]{1,0:T(8,128)(2,1)S(1)} %constant_dynamic-update-slice_fusion.4.refs_1_.refs_3_.refs_9_, ...), custom_call_target="tpu_custom_call" | custom-call | flops 2147483648 | bytes 12000000 | tf_op jit(solution)/shard_map/outer/pallas_call | solution.py:1168
  212.0 5.8 %all-to-all-start.2 = ((bf16[16,512,128]{2,1,0:T(8,128)(2,1)}), bf16[16,512,128]{2,1,0:T(8,128)(2,1)}, u32[]{:S(2)}, u32[]{:S(2)}) async-start(bf16[16,512,128]{2,1,0:T(8,128)(2,1)} %copy-done.9), calls=%async_computation.2 | async-start | bytes 4194304 | tf_op jit(solution)/shard_map/all_to_all | solution.py:1226
  225.9 4.5 %key.1 = (bf16[512,256]{1,0:T(8,128)(2,1)S(1)}, bf16[512,256]{1,0:T(8,128)(2,1)S(1)}) custom-call(s32[2]{0:T(128)S(1)} %pad_add_fusion.refs_0_, bf16[1024,384]{1,0:T(8,128)(2,1)S(1)} %copy-done.51, bf16[1024,384]{1,0:T(8,128)(2,1)S(1)} %copy-done.53, bf16[1024,384]{1,0:T(8,128)(2,1)S(1)} %copy-done.55, bf16[1024,384]{1,0:T(8,128)(2,1)S(1)} %copy-done.57, ...), custom_call_target="tpu_custom_call" | custom-call | flops 6442450944 | bytes 18000000 | tf_op jit(solution)/shard_map/key/pallas_call | solution.py:1214
  231.8 5.5 %branch.1 = (bf16[256,2048]{1,0:T(8,128)(2,1)S(1)}, bf16[256,2048]{1,0:T(8,128)(2,1)S(1)}, bf16[256,2048]{1,0:T(8,128)(2,1)S(1)}, bf16[256,2048]{1,0:T(8,128)(2,1)S(1)}) custom-call(bf16[1024,512]{1,0:T(8,128)(2,1)S(1)} %copy-done.71, bf16[512,256]{1,0:T(8,128)(2,1)S(1)} %copy-done.73, bf16[512,2048]{1,0:T(8,128)(2,1)S(1)} %copy-done.69, ...), custom_call_target="tpu_custom_call" | custom-call | flops 2684354560 | bytes 9000000 | tf_op jit(solution)/shard_map/branch/pallas_call | solution.py:1227
  237.3 5.0 %collective-permute-done.27.refs_3_ = bf16[512,256]{1,0:T(8,128)(2,1)S(1)} collective-permute-done((bf16[512,256]{1,0:T(8,128)(2,1)S(1)}, bf16[512,256]{1,0:T(8,128)(2,1)S(1)}, u32[]{:S(2)}, u32[]{:S(2)}) %collective-permute-start.27) | collective-permute-done | bytes 262176 | tf_op jit(solution)/shard_map/ppermute | solution.py:30
  243.6 7.8 %collective-permute-start.29 = (bf16[256,2048]{1,0:T(8,128)(2,1)S(1)}, bf16[256,2048]{1,0:T(8,128)(2,1)S(1)}, u32[]{:S(2)}, u32[]{:S(2)}) collective-permute-start(bf16[256,2048]{1,0:T(8,128)(2,1)S(1)} %get-tuple-element.274), channel_id=1, source_target_pairs={{0,4},{2,6},{4,0},{6,2},{8,12},{10,14},{12,8},{14,10},{16,20},{18,... | collective-permute-start | bytes 3145736 | tf_op jit(solution)/shard_map/ppermute | solution.py:30
  251.5 8.8 %inputs.1 = (bf16[256,2048]{1,0:T(8,128)(2,1)S(1)}, bf16[256,2048]{1,0:T(8,128)(2,1)}, bf16[256,2048]{1,0:T(8,128)(2,1)S(1)}, bf16[256,2048]{1,0:T(8,128)(2,1)},...) custom-call(bf16[512,256]{1,0:T(8,128)(2,1)S(1)} %copy-done.45, ...), custom_call_target="tpu_custom_call" | custom-call | flops 1127428864 | bytes 4800000 | tf_op jit(solution)/shard_map/inputs/pallas_call | solution.py:1271
  262.3 1.8 collective-permute-start.30
  264.1 8.3 %line_outer.1 = (f32[16,256,128]{2,1,0:T(8,128)S(1)}, bf16[16,256,128]{2,1,0:T(8,128)(2,1)S(1)}) custom-call(s32[2]{0:T(128)S(1)} %pad_add_fusion.refs_0_, bf16[1024,384]{1,0:T(8,128)(2,1)S(1)} %get-tuple-element.290.refs_1_, bf16[1024,128]{1,0:T(8,128)(2,1)S(1)} %get-tuple-element.291.refs_2_, bf16[256,2048]{1,0:T(8,128)(2,1)S(1)} %copy-done.15, ...), custom_call_target="tpu_custom_call" | custom-call | flops 2147483648 | bytes 12000000 | tf_op jit(solution)/shard_map/line_outer/pallas_call | solution.py:1290
  272.4 1.8 collective-permute-done.28.got1
  274.2 4.4 %collective-permute-done.29.got2 = bf16[256,2048]{1,0:T(8,128)(2,1)S(1)} collective-permute-done((bf16[256,2048]{1,0:T(8,128)(2,1)S(1)}, bf16[256,2048]{1,0:T(8,128)(2,1)S(1)}, u32[]{:S(2)}, u32[]{:S(2)}) %collective-permute-start.29) | collective-permute-done | bytes 1048608 | tf_op jit(solution)/shard_map/ppermute | solution.py:30
  278.6 1.5 collective-permute-start.31
  280.3 2.3 collective-permute-start.33
  282.6 3.3 small.1
  285.9 3.4 fold.2
  291.4 4.5 %all-to-all-start.3 = ((bf16[16,288,128]{2,1,0:T(8,128)(2,1)}), bf16[16,288,128]{2,1,0:T(8,128)(2,1)S(1)}, u32[]{:S(2)}, u32[]{:S(2)}) async-start(bf16[16,288,128]{2,1,0:T(8,128)(2,1)} %pad_maximum_fusion), calls=%async_computation.3 | async-start | bytes 2359296 | tf_op jit(solution)/shard_map/all_to_all | solution.py:1326
  295.9 4.4 %feed_unpack.1 = (f32[128,4096]{1,0:T(8,128)}, f32[4096,128]{1,0:T(8,128)}) custom-call(bf16[16,512,128]{2,1,0:T(8,128)(2,1)} %all-to-all-done.2.refs_0_), custom_call_target="tpu_custom_call" | custom-call | bytes 180000000 | tf_op jit(solution)/shard_map/feed_unpack/pallas_call | solution.py:1327
  300.3 4.8 %collective-permute-done.32.got1 = bf16[256,2048]{1,0:T(8,128)(2,1)S(1)} collective-permute-done((bf16[256,2048]{1,0:T(8,128)(2,1)}, bf16[256,2048]{1,0:T(8,128)(2,1)S(1)}, u32[]{:S(2)}, u32[]{:S(2)}) %collective-permute-start.32) | collective-permute-done | bytes 1048608 | tf_op jit(solution)/shard_map/ppermute | solution.py:30
  305.1 5.4 %collective-permute-done.33.got2 = bf16[256,2048]{1,0:T(8,128)(2,1)S(1)} collective-permute-done((bf16[256,2048]{1,0:T(8,128)(2,1)}, bf16[256,2048]{1,0:T(8,128)(2,1)S(1)}, u32[]{:S(2)}, u32[]{:S(2)}) %collective-permute-start.33) | collective-permute-done | bytes 1048608 | tf_op jit(solution)/shard_map/ppermute | solution.py:30
  310.6 16.4 %collective-permute-done.34.refs_1_ = bf16[128,2048]{1,0:T(8,128)(2,1)} collective-permute-done((bf16[128,2048]{1,0:T(8,128)(2,1)}, bf16[128,2048]{1,0:T(8,128)(2,1)}, u32[]{:S(2)}, u32[]{:S(2)}) %collective-permute-start.34) | collective-permute-done | bytes 524320 | tf_op jit(solution)/shard_map/ppermute | solution.py:30
  329.1 3.9 by_z.2
  333.0 1.4 fold.3
  335.6 1.8 collective-permute-start.37
  337.4 2.6 collective-permute-start.40
  340.0 5.0 %collective-permute-done.36.refs_1_ = bf16[128,2048]{1,0:T(8,128)(2,1)S(1)} collective-permute-done((bf16[128,2048]{1,0:T(8,128)(2,1)S(1)}, bf16[128,2048]{1,0:T(8,128)(2,1)S(1)}, u32[]{:S(2)}, u32[]{:S(2)}) %collective-permute-start.36) | collective-permute-done | bytes 524320 | tf_op jit(solution)/shard_map/ppermute | solution.py:30
  345.1 1.4 collective-permute-done.37.refs_3_
  347.3 15.1 %collective-permute-done.40 = bf16[64,2048]{1,0:T(8,128)(2,1)S(1)} collective-permute-done((bf16[64,2048]{1,0:T(8,128)(2,1)S(1)}, bf16[64,2048]{1,0:T(8,128)(2,1)S(1)}, u32[]{:S(2)}, u32[]{:S(2)}) %collective-permute-start.40) | collective-permute-done | bytes 262176 | tf_op jit(solution)/shard_map/ppermute | solution.py:30
  362.8 1.6 collective-permute-start.41
  368.5 2.2 collective-permute-start.45
  370.7 2.4 unpack.1
  373.2 4.1 %collective-permute-done.43 = bf16[64,2048]{1,0:T(8,128)(2,1)S(1)} collective-permute-done((bf16[64,2048]{1,0:T(8,128)(2,1)S(1)}, bf16[64,2048]{1,0:T(8,128)(2,1)S(1)}, u32[]{:S(2)}, u32[]{:S(2)}) %collective-permute-start.43) | collective-permute-done | bytes 262176 | tf_op jit(solution)/shard_map/ppermute | solution.py:30
  377.4 3.1 collective-permute-done.44
  380.5 13.2 %collective-permute-done.45 = bf16[64,2048]{1,0:T(8,128)(2,1)} collective-permute-done((bf16[64,2048]{1,0:T(8,128)(2,1)S(1)}, bf16[64,2048]{1,0:T(8,128)(2,1)}, u32[]{:S(2)}, u32[]{:S(2)}) %collective-permute-start.45) | collective-permute-done | bytes 262176 | tf_op jit(solution)/shard_map/ppermute | solution.py:30
  395.1 1.4 fusion.8
  396.4 1.3 collective-permute-start.46
  (308 shorter events, 66.3 us)
Async XLA Ops:
  1.8 30.6 %copy-start.74 = (bf16[64,2048]{1,0:T(8,128)(2,1)}, bf16[64,2048]{1,0:T(8,128)(2,1)S(1)}, u32[]{:S(2)}) copy-start(bf16[64,2048]{1,0:T(8,128)(2,1)S(1)} %get-tuple-element.197) | copy-start | bytes 786436
  1.8 12.4 %collective-permute-start.1 = (bf16[64,2048]{1,0:T(8,128)(2,1)S(1)}, bf16[64,2048]{1,0:T(8,128)(2,1)}, u32[]{:S(2)}, u32[]{:S(2)}) collective-permute-start(bf16[64,2048]{1,0:T(8,128)(2,1)S(1)} %get-tuple-element.197), channel_id=1, source_target_pairs={{0,8},{2,10},{4,12},{6,14},{8,0},{10,2},{12,4},{14,6},{16,24},{18,... | collective-permute-start | bytes 786440 | tf_op jit(solution)/shard_map/ppermute | solution.py:30
  2.1 13.8 %collective-permute-start.2 = (bf16[64,2048]{1,0:T(8,128)(2,1)S(1)}, bf16[64,2048]{1,0:T(8,128)(2,1)}, u32[]{:S(2)}, u32[]{:S(2)}) collective-permute-start(bf16[64,2048]{1,0:T(8,128)(2,1)S(1)} %get-tuple-element.197), channel_id=1, source_target_pairs={{0,16},{2,18},{4,20},{6,22},{8,24},{10,26},{12,28},{14,30},{16,0},... | collective-permute-start | bytes 786440 | tf_op jit(solution)/shard_map/ppermute | solution.py:30
  4.4 25.4 %collective-permute-start.3 = (bf16[64,2048]{1,0:T(8,128)(2,1)S(1)}, bf16[64,2048]{1,0:T(8,128)(2,1)}, u32[]{:S(2)}, u32[]{:S(2)}) collective-permute-start(bf16[64,2048]{1,0:T(8,128)(2,1)S(1)} %get-tuple-element.197), channel_id=1, source_target_pairs={{0,24},{2,26},{4,28},{6,30},{8,16},{10,18},{12,20},{14,22},{16,8},... | collective-permute-start | bytes 786440 | tf_op jit(solution)/shard_map/ppermute | solution.py:30
  9.8 20.0 %collective-permute-start = (bf16[8,256,128]{2,1,0:T(8,128)(2,1)}, bf16[8,256,128]{2,1,0:T(8,128)(2,1)}, u32[]{:S(2)}, u32[]{:S(2)}) collective-permute-start(bf16[8,256,128]{2,1,0:T(8,128)(2,1)} %get-tuple-element.424), channel_id=1, source_target_pairs={{0,1},{1,0},{2,3},{3,2},{4,5},{5,4},{6,7},{7,6},{8,9},{9,8},{10,11... | collective-permute-start | bytes 1572872 | tf_op jit(solution)/shard_map/ppermute | solution.py:25
  14.3 35.7 %copy-start.76 = (bf16[64,2048]{1,0:T(8,128)(2,1)}, bf16[64,2048]{1,0:T(8,128)(2,1)S(1)}, u32[]{:S(2)}) copy-start(bf16[64,2048]{1,0:T(8,128)(2,1)S(1)} %constant_dynamic-slice_fusion.3) | copy-start | bytes 786436
  29.8 13.4 %collective-permute-start.10 = (bf16[64,2048]{1,0:T(8,128)(2,1)S(1)}, bf16[64,2048]{1,0:T(8,128)(2,1)}, u32[]{:S(2)}, u32[]{:S(2)}) collective-permute-start(bf16[64,2048]{1,0:T(8,128)(2,1)S(1)} %constant_dynamic-slice_fusion.3), channel_id=1, source_target_pairs={{0,24},{2,26},{4,28},{6,30},{8,16},{10,18},{12,20},{14,22},{16,8},... | collective-permute-start | bytes 786440 | tf_op jit(solution)/shard_map/ppermute | solution.py:30
  31.1 12.1 %collective-permute-start.8 = (bf16[64,2048]{1,0:T(8,128)(2,1)S(1)}, bf16[64,2048]{1,0:T(8,128)(2,1)}, u32[]{:S(2)}, u32[]{:S(2)}) collective-permute-start(bf16[64,2048]{1,0:T(8,128)(2,1)S(1)} %constant_dynamic-slice_fusion.3), channel_id=1, source_target_pairs={{0,8},{2,10},{4,12},{6,14},{8,0},{10,2},{12,4},{14,6},{16,24},{18,... | collective-permute-start | bytes 786440 | tf_op jit(solution)/shard_map/ppermute | solution.py:30
  31.1 18.9 %collective-permute-start.9 = (bf16[64,2048]{1,0:T(8,128)(2,1)S(1)}, bf16[64,2048]{1,0:T(8,128)(2,1)}, u32[]{:S(2)}, u32[]{:S(2)}) collective-permute-start(bf16[64,2048]{1,0:T(8,128)(2,1)S(1)} %constant_dynamic-slice_fusion.3), channel_id=1, source_target_pairs={{0,16},{2,18},{4,20},{6,22},{8,24},{10,26},{12,28},{14,30},{16,0},... | collective-permute-start | bytes 786440 | tf_op jit(solution)/shard_map/ppermute | solution.py:30
  34.7 16.3 %collective-permute-start.5 = (bf16[128,2048]{1,0:T(8,128)(2,1)S(1)}, bf16[128,2048]{1,0:T(8,128)(2,1)}, u32[]{:S(2)}, u32[]{:S(2)}) collective-permute-start(bf16[128,2048]{1,0:T(8,128)(2,1)S(1)} %pad_maximum_fusion.3), channel_id=1, source_target_pairs={{0,2},{2,0},{4,6},{6,4},{8,10},{10,8},{12,14},{14,12},{16,18},{18,... | collective-permute-start | bytes 1572872 | tf_op jit(solution)/shard_map/ppermute | solution.py:30
  35.0 16.0 %collective-permute-start.4 = (bf16[128,2048]{1,0:T(8,128)(2,1)S(1)}, bf16[128,2048]{1,0:T(8,128)(2,1)}, u32[]{:S(2)}, u32[]{:S(2)}) collective-permute-start(bf16[128,2048]{1,0:T(8,128)(2,1)S(1)} %pad_maximum_fusion.2), channel_id=1, source_target_pairs={{0,4},{2,6},{4,0},{6,2},{8,12},{10,14},{12,8},{14,10},{16,20},{18,... | collective-permute-start | bytes 1572872 | tf_op jit(solution)/shard_map/ppermute | solution.py:30
  38.5 51.7 %all-to-all-start = ((bf16[16,272,128]{2,1,0:T(8,128)(2,1)}), bf16[16,272,128]{2,1,0:T(8,128)(2,1)S(1)}, u32[]{:S(2)}, u32[]{:S(2)}) async-start(bf16[16,272,128]{2,1,0:T(8,128)(2,1)} %pad_maximum_fusion.1), calls=%async_computation | async-start | bytes 2228224 | tf_op jit(solution)/shard_map/all_to_all | solution.py:1082
  52.1 35.3 %collective-permute-start.7 = (bf16[256,2048]{1,0:T(8,128)(2,1)S(1)}, bf16[256,2048]{1,0:T(8,128)(2,1)S(1)}, u32[]{:S(2)}, u32[]{:S(2)}) collective-permute-start(bf16[256,2048]{1,0:T(8,128)(2,1)S(1)} %constant_dynamic-update-slice_fusion.2.refs_3_.refs_7_.refs_5_), channel_id=1, source_target_pairs={{0,4},{2,6},{4,0},{6,2},{8,12},{10,14},{12,8},{14,10},{16,20},{18,... | collective-permute-start | bytes 3145736 | tf_op jit(solution)/shard_map/ppermute | solution.py:30
  54.7 32.8 %copy-start.13 = (bf16[256,2048]{1,0:T(8,128)(2,1)}, bf16[256,2048]{1,0:T(8,128)(2,1)S(1)}, u32[]{:S(2)}) copy-start(bf16[256,2048]{1,0:T(8,128)(2,1)S(1)} %constant_dynamic-update-slice_fusion.refs_1_.refs_5_.refs_3_) | copy-start | bytes 3145732
  54.7 34.5 %collective-permute-start.6 = (bf16[256,2048]{1,0:T(8,128)(2,1)S(1)}, bf16[256,2048]{1,0:T(8,128)(2,1)S(1)}, u32[]{:S(2)}, u32[]{:S(2)}) collective-permute-start(bf16[256,2048]{1,0:T(8,128)(2,1)S(1)} %constant_dynamic-update-slice_fusion.refs_1_.refs_5_.refs_3_), channel_id=1, source_target_pairs={{0,2},{2,0},{4,6},{6,4},{8,10},{10,8},{12,14},{14,12},{16,18},{18,... | collective-permute-start | bytes 3145736 | tf_op jit(solution)/shard_map/ppermute | solution.py:30
  56.3 29.7 %collective-permute-start.12 = (bf16[128,2048]{1,0:T(8,128)(2,1)S(1)}, bf16[128,2048]{1,0:T(8,128)(2,1)S(1)}, u32[]{:S(2)}, u32[]{:S(2)}) collective-permute-start(bf16[128,2048]{1,0:T(8,128)(2,1)S(1)} %pad_maximum_fusion.5), channel_id=1, source_target_pairs={{0,2},{2,0},{4,6},{6,4},{8,10},{10,8},{12,14},{14,12},{16,18},{18,... | collective-permute-start | bytes 1572872 | tf_op jit(solution)/shard_map/ppermute | solution.py:30
  57.6 29.9 %copy-start.78 = (bf16[128,2048]{1,0:T(8,128)(2,1)}, bf16[128,2048]{1,0:T(8,128)(2,1)S(1)}, u32[]{:S(2)}) copy-start(bf16[128,2048]{1,0:T(8,128)(2,1)S(1)} %pad_maximum_fusion.4) | copy-start | bytes 1572868
  57.6 29.9 %collective-permute-start.11 = (bf16[128,2048]{1,0:T(8,128)(2,1)S(1)}, bf16[128,2048]{1,0:T(8,128)(2,1)S(1)}, u32[]{:S(2)}, u32[]{:S(2)}) collective-permute-start(bf16[128,2048]{1,0:T(8,128)(2,1)S(1)} %pad_maximum_fusion.4), channel_id=1, source_target_pairs={{0,4},{2,6},{4,0},{6,2},{8,12},{10,14},{12,8},{14,10},{16,20},{18,... | collective-permute-start | bytes 1572872 | tf_op jit(solution)/shard_map/ppermute | solution.py:30
  90.3 12.5 %collective-permute-start.13 = (bf16[16,272,128]{2,1,0:T(8,128)(2,1)S(1)}, bf16[16,272,128]{2,1,0:T(8,128)(2,1)S(1)}, u32[]{:S(2)}, u32[]{:S(2)}) collective-permute-start(bf16[16,272,128]{2,1,0:T(8,128)(2,1)S(1)} %all-to-all-done.refs_2_), channel_id=1, source_target_pairs={{0,1},{1,0},{2,3},{3,2},{4,5},{5,4},{6,7},{7,6},{8,9},{9,8},{10,11... | collective-permute-start | bytes 3342344 | tf_op jit(solution)/shard_map/ppermute | solution.py:25
  103.8 51.8 %all-to-all-start.1 = ((bf16[16,512,128]{2,1,0:T(8,128)(2,1)}), bf16[16,512,128]{2,1,0:T(8,128)(2,1)}, u32[]{:S(2)}, u32[]{:S(2)}) async-start(bf16[16,512,128]{2,1,0:T(8,128)(2,1)} %feed_deal.1), calls=%async_computation.1 | async-start | bytes 4194304 | tf_op jit(solution)/shard_map/all_to_all | solution.py:1105
  109.7 44.4 %collective-permute-start.15 = (bf16[256,2048]{1,0:T(8,128)(2,1)S(1)}, bf16[256,2048]{1,0:T(8,128)(2,1)S(1)}, u32[]{:S(2)}, u32[]{:S(2)}) collective-permute-start(bf16[256,2048]{1,0:T(8,128)(2,1)S(1)} %constant_dynamic-update-slice_fusion.6.refs_3_.refs_5_.refs_11_), channel_id=1, source_target_pairs={{0,4},{2,6},{4,0},{6,2},{8,12},{10,14},{12,8},{14,10},{16,20},{18,... | collective-permute-start | bytes 3145736 | tf_op jit(solution)/shard_map/ppermute | solution.py:30
  113.7 40.5 %collective-permute-start.14 = (bf16[256,2048]{1,0:T(8,128)(2,1)S(1)}, bf16[256,2048]{1,0:T(8,128)(2,1)S(1)}, u32[]{:S(2)}, u32[]{:S(2)}) collective-permute-start(bf16[256,2048]{1,0:T(8,128)(2,1)S(1)} %constant_dynamic-update-slice_fusion.4.refs_1_.refs_3_.refs_9_), channel_id=1, source_target_pairs={{0,2},{2,0},{4,6},{6,4},{8,10},{10,8},{12,14},{14,12},{16,18},{18,... | collective-permute-start | bytes 3145736 | tf_op jit(solution)/shard_map/ppermute | solution.py:30
  130.9 23.3 %copy-start.49 = (bf16[1024,384]{1,0:T(8,128)(2,1)}, bf16[1024,384]{1,0:T(8,128)(2,1)S(1)}, u32[]{:S(2)}) copy-start(bf16[1024,384]{1,0:T(8,128)(2,1)S(1)} %get-tuple-element.249.refs_1_) | copy-start | bytes 2359300
  155.6 6.6 %collective-permute-start.18 = (bf16[16,512,128]{2,1,0:T(8,128)(2,1)}, bf16[16,512,128]{2,1,0:T(8,128)(2,1)S(1)}, u32[]{:S(2)}, u32[]{:S(2)}) collective-permute-start(bf16[16,512,128]{2,1,0:T(8,128)(2,1)} %all-to-all-done.1.refs_5_), channel_id=1, source_target_pairs={{0,1},{1,0},{2,3},{3,2},{4,5},{5,4},{6,7},{7,6},{8,9},{9,8},{10,11... | collective-permute-start | bytes 6291464 | tf_op jit(solution)/shard_map/ppermute | solution.py:25
  158.2 13.8 %collective-permute-start.19 = (bf16[128,2048]{1,0:T(8,128)(2,1)}, bf16[128,2048]{1,0:T(8,128)(2,1)S(1)}, u32[]{:S(2)}, u32[]{:S(2)}) collective-permute-start(bf16[128,2048]{1,0:T(8,128)(2,1)} %copy-done.58), channel_id=1, source_target_pairs={{0,2},{2,0},{4,6},{6,4},{8,10},{10,8},{12,14},{14,12},{16,18},{18,... | collective-permute-start | bytes 1572872 | tf_op jit(solution)/shard_map/ppermute | solution.py:30
  158.3 30.9 %collective-permute-start.16 = (bf16[1024,384]{1,0:T(8,128)(2,1)}, bf16[1024,384]{1,0:T(8,128)(2,1)S(1)}, u32[]{:S(2)}, u32[]{:S(2)}) collective-permute-start(bf16[1024,384]{1,0:T(8,128)(2,1)} %copy-done.49), channel_id=1, source_target_pairs={{0,2},{2,0},{4,6},{6,4},{8,10},{10,8},{12,14},{14,12},{16,18},{18,... | collective-permute-start | bytes 2359304 | tf_op jit(solution)/shard_map/ppermute | solution.py:30
  159.7 29.5 %collective-permute-start.17 = (bf16[1024,384]{1,0:T(8,128)(2,1)}, bf16[1024,384]{1,0:T(8,128)(2,1)S(1)}, u32[]{:S(2)}, u32[]{:S(2)}) collective-permute-start(bf16[1024,384]{1,0:T(8,128)(2,1)} %copy-done.49), channel_id=1, source_target_pairs={{0,1},{1,0},{2,3},{3,2},{4,5},{5,4},{6,7},{7,6},{8,9},{9,8},{10,11... | collective-permute-start | bytes 2359304 | tf_op jit(solution)/shard_map/ppermute | solution.py:25
  189.2 6.1 %collective-permute-start.20 = (bf16[1024,384]{1,0:T(8,128)(2,1)S(1)}, bf16[1024,384]{1,0:T(8,128)(2,1)S(1)}, u32[]{:S(2)}, u32[]{:S(2)}) collective-permute-start(bf16[1024,384]{1,0:T(8,128)(2,1)S(1)} %collective-permute-done.16.refs_2_), channel_id=1, source_target_pairs={{0,1},{1,0},{2,3},{3,2},{4,5},{5,4},{6,7},{7,6},{8,9},{9,8},{10,11... | collective-permute-start | bytes 2359304 | tf_op jit(solution)/shard_map/ppermute | solution.py:25
  195.3 10.4 %collective-permute-start.23 = (bf16[16,512,128]{2,1,0:T(8,128)(2,1)S(1)}, bf16[16,512,128]{2,1,0:T(8,128)(2,1)S(1)}, u32[]{:S(2)}, u32[]{:S(2)}) collective-permute-start(bf16[16,512,128]{2,1,0:T(8,128)(2,1)S(1)} %outer.2), channel_id=1, source_target_pairs={{0,1},{1,0},{2,3},{3,2},{4,5},{5,4},{6,7},{7,6},{8,9},{9,8},{10,11... | collective-permute-start | bytes 6291464 | tf_op jit(solution)/shard_map/ppermute | solution.py:25
  195.4 8.4 %collective-permute-start.21 = (bf16[1024,256]{1,0:T(8,128)(2,1)S(1)}, bf16[1024,256]{1,0:T(8,128)(2,1)S(1)}, u32[]{:S(2)}, u32[]{:S(2)}) collective-permute-start(bf16[1024,256]{1,0:T(8,128)(2,1)S(1)} %get-tuple-element.248.refs_5_), channel_id=1, source_target_pairs={{0,1},{1,0},{2,3},{3,2},{4,5},{5,4},{6,7},{7,6},{8,9},{9,8},{10,11... | collective-permute-start | bytes 1572872 | tf_op jit(solution)/shard_map/ppermute | solution.py:25
  203.8 6.8 %collective-permute-start.24 = (f32[8,512]{1,0:T(8,128)S(1)}, f32[8,512]{1,0:T(8,128)S(1)}, u32[]{:S(2)}, u32[]{:S(2)}) collective-permute-start(f32[8,512]{1,0:T(8,128)S(1)} %get-tuple-element.259.refs_7_), channel_id=1, source_target_pairs={{0,2},{2,0},{4,6},{6,4},{8,10},{10,8},{12,14},{14,12},{16,18},{18,... | collective-permute-start | bytes 49160 | tf_op jit(solution)/shard_map/ppermute | solution.py:30
  204.0 6.7 %collective-permute-start.25 = (f32[8,512]{1,0:T(8,128)S(1)}, f32[8,512]{1,0:T(8,128)S(1)}, u32[]{:S(2)}, u32[]{:S(2)}) collective-permute-start(f32[8,512]{1,0:T(8,128)S(1)} %get-tuple-element.259.refs_7_), channel_id=1, source_target_pairs={{0,1},{1,0},{2,3},{3,2},{4,5},{5,4},{6,7},{7,6},{8,9},{9,8},{10,11... | collective-permute-start | bytes 49160 | tf_op jit(solution)/shard_map/ppermute | solution.py:25
  204.3 7.7 %collective-permute-start.26 = (f32[8,512]{1,0:T(8,128)S(1)}, f32[8,512]{1,0:T(8,128)S(1)}, u32[]{:S(2)}, u32[]{:S(2)}) collective-permute-start(f32[8,512]{1,0:T(8,128)S(1)} %get-tuple-element.259.refs_7_), channel_id=1, source_target_pairs={{0,3},{1,2},{2,1},{3,0},{4,7},{5,6},{6,5},{7,4},{8,11},{9,10},{10,... | collective-permute-start | bytes 49160 | tf_op jit(solution)/shard_map/ppermute | solution.py:1210
  212.0 79.4 %all-to-all-start.2 = ((bf16[16,512,128]{2,1,0:T(8,128)(2,1)}), bf16[16,512,128]{2,1,0:T(8,128)(2,1)}, u32[]{:S(2)}, u32[]{:S(2)}) async-start(bf16[16,512,128]{2,1,0:T(8,128)(2,1)} %copy-done.9), calls=%async_computation.2 | async-start | bytes 4194304 | tf_op jit(solution)/shard_map/all_to_all | solution.py:1226
  217.8 19.6 %collective-permute-start.22 = (bf16[512,256]{1,0:T(8,128)(2,1)}, bf16[512,256]{1,0:T(8,128)(2,1)S(1)}, u32[]{:S(2)}, u32[]{:S(2)}) collective-permute-start(bf16[512,256]{1,0:T(8,128)(2,1)} %copy-done.67), channel_id=1, source_target_pairs={{0,2},{2,0},{4,6},{6,4},{8,10},{10,8},{12,14},{14,12},{16,18},{18,... | collective-permute-start | bytes 786440 | tf_op jit(solution)/shard_map/ppermute | solution.py:30
  230.5 11.9 %collective-permute-start.27 = (bf16[512,256]{1,0:T(8,128)(2,1)S(1)}, bf16[512,256]{1,0:T(8,128)(2,1)S(1)}, u32[]{:S(2)}, u32[]{:S(2)}) collective-permute-start(bf16[512,256]{1,0:T(8,128)(2,1)S(1)} %get-tuple-element.263), channel_id=1, source_target_pairs={{0,2},{2,0},{4,6},{6,4},{8,10},{10,8},{12,14},{14,12},{16,18},{18,... | collective-permute-start | bytes 786440 | tf_op jit(solution)/shard_map/ppermute | solution.py:30
  231.7 19.7 %copy-start.12 = (bf16[256,2048]{1,0:T(8,128)(2,1)S(1)}, bf16[256,2048]{1,0:T(8,128)(2,1)}, u32[]{:S(2)}) copy-start(bf16[256,2048]{1,0:T(8,128)(2,1)} %copy-done.10) | copy-start | bytes 3145732
  231.7 19.7 %copy-start.15 = (bf16[256,2048]{1,0:T(8,128)(2,1)S(1)}, bf16[256,2048]{1,0:T(8,128)(2,1)}, u32[]{:S(2)}) copy-start(bf16[256,2048]{1,0:T(8,128)(2,1)} %copy-done.13) | copy-start | bytes 3145732
  231.8 19.7 %copy-start.20 = (bf16[256,2048]{1,0:T(8,128)(2,1)S(1)}, bf16[256,2048]{1,0:T(8,128)(2,1)}, u32[]{:S(2)}) copy-start(bf16[256,2048]{1,0:T(8,128)(2,1)} %copy-done.18) | copy-start | bytes 3145732
  231.8 19.7 %copy-start.23 = (bf16[256,2048]{1,0:T(8,128)(2,1)S(1)}, bf16[256,2048]{1,0:T(8,128)(2,1)}, u32[]{:S(2)}) copy-start(bf16[256,2048]{1,0:T(8,128)(2,1)} %copy-done.21) | copy-start | bytes 3145732
  242.4 31.8 %collective-permute-start.28 = (bf16[256,2048]{1,0:T(8,128)(2,1)S(1)}, bf16[256,2048]{1,0:T(8,128)(2,1)S(1)}, u32[]{:S(2)}, u32[]{:S(2)}) collective-permute-start(bf16[256,2048]{1,0:T(8,128)(2,1)S(1)} %get-tuple-element.273), channel_id=1, source_target_pairs={{0,2},{2,0},{4,6},{6,4},{8,10},{10,8},{12,14},{14,12},{16,18},{18,... | collective-permute-start | bytes 3145736 | tf_op jit(solution)/shard_map/ppermute | solution.py:30
  243.6 35.0 %collective-permute-start.29 = (bf16[256,2048]{1,0:T(8,128)(2,1)S(1)}, bf16[256,2048]{1,0:T(8,128)(2,1)S(1)}, u32[]{:S(2)}, u32[]{:S(2)}) collective-permute-start(bf16[256,2048]{1,0:T(8,128)(2,1)S(1)} %get-tuple-element.274), channel_id=1, source_target_pairs={{0,4},{2,6},{4,0},{6,2},{8,12},{10,14},{12,8},{14,10},{16,20},{18,... | collective-permute-start | bytes 3145736 | tf_op jit(solution)/shard_map/ppermute | solution.py:30
  262.3 10.0 %collective-permute-start.30 = (f32[8,2048]{1,0:T(8,128)S(1)}, f32[8,2048]{1,0:T(8,128)S(1)}, u32[]{:S(2)}, u32[]{:S(2)}) collective-permute-start(f32[8,2048]{1,0:T(8,128)S(1)} %get-tuple-element.297.refs_1_), channel_id=1, source_target_pairs={{0,1},{1,0},{2,3},{3,2},{4,5},{5,4},{6,7},{7,6},{8,9},{9,8},{10,11... | collective-permute-start | bytes 196616 | tf_op jit(solution)/shard_map/ppermute | solution.py:25
  278.6 10.7 %collective-permute-start.31 = (bf16[16,256,128]{2,1,0:T(8,128)(2,1)S(1)}, bf16[16,256,128]{2,1,0:T(8,128)(2,1)S(1)}, u32[]{:S(2)}, u32[]{:S(2)}) collective-permute-start(bf16[16,256,128]{2,1,0:T(8,128)(2,1)S(1)} %get-tuple-element.296), channel_id=1, source_target_pairs={{0,1},{1,0},{2,3},{3,2},{4,5},{5,4},{6,7},{7,6},{8,9},{9,8},{10,11... | collective-permute-start | bytes 3145736 | tf_op jit(solution)/shard_map/ppermute | solution.py:25
  280.1 25.0 %collective-permute-start.32 = (bf16[256,2048]{1,0:T(8,128)(2,1)}, bf16[256,2048]{1,0:T(8,128)(2,1)S(1)}, u32[]{:S(2)}, u32[]{:S(2)}) collective-permute-start(bf16[256,2048]{1,0:T(8,128)(2,1)} %get-tuple-element.312), channel_id=1, source_target_pairs={{0,2},{2,0},{4,6},{6,4},{8,10},{10,8},{12,14},{14,12},{16,18},{18,... | collective-permute-start | bytes 3145736 | tf_op jit(solution)/shard_map/ppermute | solution.py:30
  280.3 30.3 %collective-permute-start.33 = (bf16[256,2048]{1,0:T(8,128)(2,1)}, bf16[256,2048]{1,0:T(8,128)(2,1)S(1)}, u32[]{:S(2)}, u32[]{:S(2)}) collective-permute-start(bf16[256,2048]{1,0:T(8,128)(2,1)} %get-tuple-element.313), channel_id=1, source_target_pairs={{0,4},{2,6},{4,0},{6,2},{8,12},{10,14},{12,8},{14,10},{16,20},{18,... | collective-permute-start | bytes 3145736 | tf_op jit(solution)/shard_map/ppermute | solution.py:30
  289.3 37.6 %collective-permute-start.34 = (bf16[128,2048]{1,0:T(8,128)(2,1)}, bf16[128,2048]{1,0:T(8,128)(2,1)}, u32[]{:S(2)}, u32[]{:S(2)}) collective-permute-start(bf16[128,2048]{1,0:T(8,128)(2,1)} %get-tuple-element.314), channel_id=1, source_target_pairs={{0,4},{2,6},{4,0},{6,2},{8,12},{10,14},{12,8},{14,10},{16,20},{18,... | collective-permute-start | bytes 1572872 | tf_op jit(solution)/shard_map/ppermute | solution.py:30
  289.4 37.6 %collective-permute-start.35 = (bf16[128,2048]{1,0:T(8,128)(2,1)}, bf16[128,2048]{1,0:T(8,128)(2,1)}, u32[]{:S(2)}, u32[]{:S(2)}) collective-permute-start(bf16[128,2048]{1,0:T(8,128)(2,1)} %get-tuple-element.315), channel_id=1, source_target_pairs={{0,2},{2,0},{4,6},{6,4},{8,10},{10,8},{12,14},{14,12},{16,18},{18,... | collective-permute-start | bytes 1572872 | tf_op jit(solution)/shard_map/ppermute | solution.py:30
  291.4 76.2 %all-to-all-start.3 = ((bf16[16,288,128]{2,1,0:T(8,128)(2,1)}), bf16[16,288,128]{2,1,0:T(8,128)(2,1)S(1)}, u32[]{:S(2)}, u32[]{:S(2)}) async-start(bf16[16,288,128]{2,1,0:T(8,128)(2,1)} %pad_maximum_fusion), calls=%async_computation.3 | async-start | bytes 2359296 | tf_op jit(solution)/shard_map/all_to_all | solution.py:1326
  295.9 37.1 %copy-start.35 = (bf16[256,2048]{1,0:T(8,128)(2,1)S(1)}, bf16[256,2048]{1,0:T(8,128)(2,1)}, u32[]{:S(2)}) copy-start(bf16[256,2048]{1,0:T(8,128)(2,1)} %copy-done.34) | copy-start | bytes 3145732
  295.9 37.1 %copy-start.37 = (bf16[256,2048]{1,0:T(8,128)(2,1)S(1)}, bf16[256,2048]{1,0:T(8,128)(2,1)}, u32[]{:S(2)}) copy-start(bf16[256,2048]{1,0:T(8,128)(2,1)} %copy-done.36) | copy-start | bytes 3145732
  334.4 28.1 %copy-start.75 = (bf16[64,2048]{1,0:T(8,128)(2,1)S(1)}, bf16[64,2048]{1,0:T(8,128)(2,1)}, u32[]{:S(2)}) copy-start(bf16[64,2048]{1,0:T(8,128)(2,1)} %copy-done.74) | copy-start | bytes 786436
  334.4 10.7 %collective-permute-start.36 = (bf16[128,2048]{1,0:T(8,128)(2,1)S(1)}, bf16[128,2048]{1,0:T(8,128)(2,1)S(1)}, u32[]{:S(2)}, u32[]{:S(2)}) collective-permute-start(bf16[128,2048]{1,0:T(8,128)(2,1)S(1)} %get-tuple-element.336), channel_id=1, source_target_pairs={{0,4},{2,6},{4,0},{6,2},{8,12},{10,14},{12,8},{14,10},{16,20},{18,... | collective-permute-start | bytes 1572872 | tf_op jit(solution)/shard_map/ppermute | solution.py:30
  335.6 10.9 %collective-permute-start.37 = (bf16[128,2048]{1,0:T(8,128)(2,1)S(1)}, bf16[128,2048]{1,0:T(8,128)(2,1)S(1)}, u32[]{:S(2)}, u32[]{:S(2)}) collective-permute-start(bf16[128,2048]{1,0:T(8,128)(2,1)S(1)} %get-tuple-element.337), channel_id=1, source_target_pairs={{0,2},{2,0},{4,6},{6,4},{8,10},{10,8},{12,14},{14,12},{16,18},{18,... | collective-permute-start | bytes 1572872 | tf_op jit(solution)/shard_map/ppermute | solution.py:30
  337.4 10.0 %collective-permute-start.38 = (bf16[64,2048]{1,0:T(8,128)(2,1)S(1)}, bf16[64,2048]{1,0:T(8,128)(2,1)S(1)}, u32[]{:S(2)}, u32[]{:S(2)}) collective-permute-start(bf16[64,2048]{1,0:T(8,128)(2,1)S(1)} %get-tuple-element.345), channel_id=1, source_target_pairs={{0,8},{2,10},{4,12},{6,14},{8,0},{10,2},{12,4},{14,6},{16,24},{18,... | collective-permute-start | bytes 786440 | tf_op jit(solution)/shard_map/ppermute | solution.py:30
  337.4 10.0 %collective-permute-start.39 = (bf16[64,2048]{1,0:T(8,128)(2,1)S(1)}, bf16[64,2048]{1,0:T(8,128)(2,1)S(1)}, u32[]{:S(2)}, u32[]{:S(2)}) collective-permute-start(bf16[64,2048]{1,0:T(8,128)(2,1)S(1)} %get-tuple-element.346), channel_id=1, source_target_pairs={{0,16},{2,18},{4,20},{6,22},{8,24},{10,26},{12,28},{14,30},{16,0},... | collective-permute-start | bytes 786440 | tf_op jit(solution)/shard_map/ppermute | solution.py:30
  337.4 25.1 %collective-permute-start.40 = (bf16[64,2048]{1,0:T(8,128)(2,1)S(1)}, bf16[64,2048]{1,0:T(8,128)(2,1)S(1)}, u32[]{:S(2)}, u32[]{:S(2)}) collective-permute-start(bf16[64,2048]{1,0:T(8,128)(2,1)S(1)} %get-tuple-element.347), channel_id=1, source_target_pairs={{0,24},{2,26},{4,28},{6,30},{8,16},{10,18},{12,20},{14,22},{16,8},... | collective-permute-start | bytes 786440 | tf_op jit(solution)/shard_map/ppermute | solution.py:30
  362.8 2.9 collective-permute-start.41
  367.6 27.4 %copy-start.77 = (bf16[64,2048]{1,0:T(8,128)(2,1)S(1)}, bf16[64,2048]{1,0:T(8,128)(2,1)}, u32[]{:S(2)}) copy-start(bf16[64,2048]{1,0:T(8,128)(2,1)} %copy-done.76) | copy-start | bytes 786436
  367.6 3.1 collective-permute-start.42
  368.1 9.3 %collective-permute-start.43 = (bf16[64,2048]{1,0:T(8,128)(2,1)S(1)}, bf16[64,2048]{1,0:T(8,128)(2,1)S(1)}, u32[]{:S(2)}, u32[]{:S(2)}) collective-permute-start(bf16[64,2048]{1,0:T(8,128)(2,1)S(1)} %get-tuple-element.357), channel_id=1, source_target_pairs={{0,8},{2,10},{4,12},{6,14},{8,0},{10,2},{12,4},{14,6},{16,24},{18,... | collective-permute-start | bytes 786440 | tf_op jit(solution)/shard_map/ppermute | solution.py:30
  368.1 12.4 %collective-permute-start.44 = (bf16[64,2048]{1,0:T(8,128)(2,1)S(1)}, bf16[64,2048]{1,0:T(8,128)(2,1)S(1)}, u32[]{:S(2)}, u32[]{:S(2)}) collective-permute-start(bf16[64,2048]{1,0:T(8,128)(2,1)S(1)} %get-tuple-element.358), channel_id=1, source_target_pairs={{0,16},{2,18},{4,20},{6,22},{8,24},{10,26},{12,28},{14,30},{16,0},... | collective-permute-start | bytes 786440 | tf_op jit(solution)/shard_map/ppermute | solution.py:30
  368.5 25.2 %collective-permute-start.45 = (bf16[64,2048]{1,0:T(8,128)(2,1)S(1)}, bf16[64,2048]{1,0:T(8,128)(2,1)}, u32[]{:S(2)}, u32[]{:S(2)}) collective-permute-start(bf16[64,2048]{1,0:T(8,128)(2,1)S(1)} %get-tuple-element.359), channel_id=1, source_target_pairs={{0,24},{2,26},{4,28},{6,30},{8,16},{10,18},{12,20},{14,22},{16,8},... | collective-permute-start | bytes 786440 | tf_op jit(solution)/shard_map/ppermute | solution.py:30
  396.4 4.8 %collective-permute-start.46 = (bf16[64,2048]{1,0:T(8,128)(2,1)S(1)}, bf16[64,2048]{1,0:T(8,128)(2,1)S(1)}, u32[]{:S(2)}, u32[]{:S(2)}) collective-permute-start(bf16[64,2048]{1,0:T(8,128)(2,1)S(1)} %fusion.8), channel_id=1, source_target_pairs={{0,1},{1,0},{2,3},{3,2},{4,5},{5,4},{6,7},{7,6},{8,9},{9,8},{10,11... | collective-permute-start | bytes 786440 | tf_op jit(solution)/shard_map/ppermute | solution.py:25
  (77 other events, 474.9 us)
